TPU v7x, 32 devices: a whole 2x2x4 slice. The times are simulated.
32 devices in a mesh: batch: 16 (over z, y, x), tensor: 2 (over core).
Axes of the slice: x: 2, y: 2, z: 4, core: 2. Of those that a mesh axis runs over, the one named last changes fastest.
Arguments:
- images: bfloat16 [128, 256, 256], P('batch', 'tensor'), may hold values from -6 to 6
- timesteps: int32 [128], P('batch'), may hold values from 0 to 1023
- embed_table: bfloat16 [1024, 512], replicated, may hold values from -6 to 6
- first_gain: float32 [256], P('tensor'), may hold values from 0.5 to 1.5
- first_shift: float32 [256], P('tensor'), may hold values from -3 to 3
- first_conv: bfloat16 [9, 256, 256], P(None, None, 'tensor'), may hold values from -0.125 to 0.125
- first_bias: float32 [256], P('tensor'), may hold values from -3 to 3
- time_weight: bfloat16 [512, 256], P(None, 'tensor'), may hold values from -0.25 to 0.25
- time_bias: float32 [256], P('tensor'), may hold values from -3 to 3
- second_gain: float32 [256], P('tensor'), may hold values from 0.5 to 1.5
- second_shift: float32 [256], P('tensor'), may hold values from -3 to 3
- second_conv: bfloat16 [9, 256, 256], P(None, 'tensor'), may hold values from -0.125 to 0.125
- second_bias: float32 [256], P('tensor'), may hold values from -3 to 3
- third_gain: float32 [256], P('tensor'), may hold values from 0.5 to 1.5
- third_shift: float32 [256], P('tensor'), may hold values from -3 to 3
- project_in: bfloat16 [3, 256, 256], P(None, None, 'tensor'), may hold values from -0.5 to 0.5
- query_bias: float32 [256], P('tensor'), may hold values from -3 to 3
- value_bias: float32 [256], P('tensor'), may hold values from -3 to 3
- project_out: bfloat16 [256, 256], P('tensor'), may hold values from -1.5 to 1.5
- output_bias: float32 [256], P('tensor'), may hold values from -3 to 3
- cotangent: bfloat16 [128, 256, 256], P('batch', 'tensor'), may hold values from -6 to 6
Outputs:
- block_out: float32 [128, 256, 256], P('batch', 'tensor')
- images_grad: float32 [128, 256, 256], P('batch', 'tensor')
- table_grad: float32 [1024, 512], replicated
- first_gain_grad: float32 [256], P('tensor')
- first_shift_grad: float32 [256], P('tensor')
- first_conv_grad: float32 [9, 256, 256], P(None, None, 'tensor')
- first_bias_grad: float32 [256], P('tensor')
- time_weight_grad: float32 [512, 256], P(None, 'tensor')
- time_bias_grad: float32 [256], P('tensor')
- second_gain_grad: float32 [256], P('tensor')
- second_shift_grad: float32 [256], P('tensor')
- second_conv_grad: float32 [9, 256, 256], P(None, 'tensor')
- second_bias_grad: float32 [256], P('tensor')
- third_gain_grad: float32 [256], P('tensor')
- third_shift_grad: float32 [256], P('tensor')
- project_in_grad: float32 [3, 256, 256], P(None, None, 'tensor')
- query_bias_grad: float32 [256], P('tensor')
- value_bias_grad: float32 [256], P('tensor')
- project_out_grad: float32 [256, 256], P('tensor')
- output_bias_grad: float32 [256], P('tensor')
All inputs are finite; a program needn't handle non-finite values.
Results may differ from a plain program's by a relative error of at most 0.017.
Values may be sent and summed in bfloat16 or wider, within the bound.
No kernel may reach another device: no remote copies, remote signals or barrier semaphores. Data moves between devices by JAX's collectives and lax.ppermute only.
A program may use at most 128 MiB of HBM per device.

v0:
```python
import math

import jax
import jax.numpy as jnp
from jax import lax
from jax.sharding import PartitionSpec as P

C = 256
GROUPS = 32


norm_eps = 1e-06


def shifted_taps(values, sign):
    side = math.isqrt(values.shape[-1])
    lead = values.shape[:-1]
    grid = values.reshape(lead + (side, side))
    padded = jnp.pad(grid, [(0, 0)] * len(lead) + [(1, 1), (1, 1)])
    pieces = []
    for row_off in (-1, 0, 1):
        for col_off in (-1, 0, 1):
            top = 1 + sign * row_off
            left = 1 + sign * col_off
            pieces.append(padded[..., top : top + side, left : left + side].reshape(values.shape))
    return jnp.stack(pieces, 0)


def conv_apply(values, weight):
    return jnp.einsum(
        "kio,kbip->bop", weight, shifted_taps(values, 1), preferred_element_type=jnp.float32
    )


def conv_back(grads, weight):
    return jnp.einsum(
        "kio,kbop->bip", weight, shifted_taps(grads, -1), preferred_element_type=jnp.float32
    )


def conv_weight_grad(values, grads):
    return jnp.einsum(
        "kbip,bop->kio", shifted_taps(values, 1), grads, preferred_element_type=jnp.float32
    )


def group_moments(values, width):
    count, chans, points = values.shape
    grouped = values.reshape(count, chans // width, width, points)
    center = jnp.mean(grouped, axis=(2, 3), keepdims=True)
    spread = jnp.mean(jnp.square(grouped - center), axis=(2, 3), keepdims=True)
    return (center, lax.rsqrt(spread + norm_eps))


def group_apply(values, moments, width):
    count, chans, points = values.shape
    grouped = values.reshape(count, chans // width, width, points)
    return ((grouped - moments[0]) * moments[1]).reshape(values.shape)


def group_back(grad_hat, hat, moments, width):
    count, chans, points = hat.shape
    grad_grouped = grad_hat.reshape(count, chans // width, width, points)
    hat_grouped = hat.reshape(count, chans // width, width, points)
    first_mean = jnp.mean(grad_grouped, axis=(2, 3), keepdims=True)
    second_mean = jnp.mean(grad_grouped * hat_grouped, axis=(2, 3), keepdims=True)
    return (moments[1] * (grad_grouped - first_mean - hat_grouped * second_mean)).reshape(hat.shape)


def silu_slope(pre):
    sigma = jax.nn.sigmoid(pre)
    return sigma * (1.0 + pre * (1.0 - sigma))


def per_channel(vector):
    return vector[None, :, None]


def channel_total(values):
    return jnp.sum(values, axis=(0, 2))


def front_part(inputs_f, moments_one, first_gain, first_shift, first_conv, bias_add, width):
    hat_one = group_apply(inputs_f, moments_one, width)
    pre_one = hat_one * per_channel(first_gain) + per_channel(first_shift)
    act_one = jax.nn.silu(pre_one).astype(jnp.bfloat16)
    act_full = lax.all_gather(act_one, "tensor", axis=1, tiled=True)
    sum_one = conv_apply(act_full, first_conv) + bias_add
    return (hat_one, pre_one, act_full, sum_one)


def middle_part(sum_one, moments_two, second_gain, second_shift, width):
    hat_two = group_apply(sum_one, moments_two, width)
    pre_two = hat_two * per_channel(second_gain) + per_channel(second_shift)
    return (hat_two, pre_two, jax.nn.silu(pre_two).astype(jnp.bfloat16))


def attention_scores(query, keys, scale):
    partial_raw = jnp.einsum("bcp,bcq->bpq", query, keys, preferred_element_type=jnp.float32)
    raw = lax.psum(partial_raw, "tensor")
    return raw * scale


def weight_grads(grad_mixed, values):
    partial_grad = jnp.einsum(
        "bcp,bcq->bpq", grad_mixed, values, preferred_element_type=jnp.float32
    )
    result = lax.psum(partial_grad, "tensor")
    return result


def per_device(
    images,
    timesteps,
    embed_table,
    first_gain,
    first_shift,
    first_conv,
    first_bias,
    time_weight,
    time_bias,
    second_gain,
    second_shift,
    second_conv,
    second_bias,
    third_gain,
    third_shift,
    project_in,
    query_bias,
    value_bias,
    project_out,
    output_bias,
    cotangent,
):
    highest = lax.Precision.HIGHEST
    width = C // GROUPS
    scale = C ** (-0.5)
    inputs_f = images.astype(jnp.float32)
    table_rows = embed_table.shape[0]
    row_ids = jnp.arange(table_rows, dtype=jnp.int32)
    one_hot = (timesteps[:, None] == row_ids[None, :]).astype(jnp.float32)
    embed_rows = jnp.dot(one_hot, embed_table.astype(jnp.float32), precision=highest)
    embed_act = jax.nn.silu(embed_rows).astype(jnp.bfloat16)
    time_add = (
        jnp.dot(embed_act, time_weight, preferred_element_type=jnp.float32) + time_bias[None, :]
    )
    bias_add = per_channel(first_bias) + time_add[:, :, None]
    moments_one = group_moments(inputs_f, width)
    hat_one, pre_one, act_full, sum_one = front_part(
        inputs_f, moments_one, first_gain, first_shift, first_conv, bias_add, width
    )
    moments_two = group_moments(sum_one, width)
    hat_two, pre_two, act_two = middle_part(sum_one, moments_two, second_gain, second_shift, width)
    conv_partial = jnp.einsum(
        "kio,kbip->bop", second_conv, shifted_taps(act_two, 1), preferred_element_type=jnp.float32
    )
    conv_two = lax.psum_scatter(conv_partial, "tensor", scatter_dimension=1, tiled=True)
    resid = inputs_f + conv_two + per_channel(second_bias)
    moments_three = group_moments(resid, width)
    hat_three = group_apply(resid, moments_three, width)
    normed = (hat_three * per_channel(third_gain) + per_channel(third_shift)).astype(jnp.bfloat16)
    normed_full = lax.all_gather(normed, "tensor", axis=1, tiled=True)
    linear = jnp.einsum(
        "jio,bip->jbop", project_in, normed_full, preferred_element_type=jnp.float32
    )
    query = (linear[0] + per_channel(query_bias)).astype(jnp.bfloat16)
    keys = linear[1].astype(jnp.bfloat16)
    values = (linear[2] + per_channel(value_bias)).astype(jnp.bfloat16)
    scores = attention_scores(query, keys, scale)
    row_max = jnp.max(scores, axis=-1, keepdims=True)
    expo = jnp.exp(scores - row_max)
    row_total = jnp.sum(expo, axis=-1, keepdims=True)
    log_total = row_max + jnp.log(row_total)
    weights = (expo / row_total).astype(jnp.bfloat16)
    mixed = jnp.einsum("bcq,bpq->bcp", values, weights, preferred_element_type=jnp.float32).astype(
        jnp.bfloat16
    )
    proj_partial = jnp.einsum("io,bip->bop", project_out, mixed, preferred_element_type=jnp.float32)
    projected = lax.psum_scatter(proj_partial, "tensor", scatter_dimension=1, tiled=True)
    block_out = resid + projected + per_channel(output_bias)
    grad_out = cotangent.astype(jnp.float32)
    grad_full = lax.all_gather(cotangent, "tensor", axis=1, tiled=True)
    output_bias_grad = channel_total(grad_out)
    project_out_grad = jnp.einsum(
        "bip,bop->io", mixed, grad_full, preferred_element_type=jnp.float32
    )
    grad_mixed = jnp.einsum(
        "io,bop->bip", project_out, grad_full, preferred_element_type=jnp.float32
    ).astype(jnp.bfloat16)
    scores_again = attention_scores(query, keys, scale)
    probs = jnp.exp(scores_again - log_total)
    grad_weights = weight_grads(grad_mixed, values)
    grad_values = jnp.einsum(
        "bcp,bpq->bcq", grad_mixed, weights, preferred_element_type=jnp.float32
    ).astype(jnp.bfloat16)
    grad_scores = (
        probs * (grad_weights - jnp.sum(probs * grad_weights, axis=-1, keepdims=True))
    ).astype(jnp.bfloat16)
    grad_query = (
        jnp.einsum("bcq,bpq->bcp", keys, grad_scores, preferred_element_type=jnp.float32) * scale
    ).astype(jnp.bfloat16)
    grad_keys = (
        jnp.einsum("bcp,bpq->bcq", query, grad_scores, preferred_element_type=jnp.float32) * scale
    ).astype(jnp.bfloat16)
    query_bias_grad = channel_total(grad_query.astype(jnp.float32))
    value_bias_grad = channel_total(grad_values.astype(jnp.float32))
    grad_linear = jnp.stack([grad_query, grad_keys, grad_values], 0)
    project_in_grad = jnp.einsum(
        "jbop,bip->jio", grad_linear, normed_full, preferred_element_type=jnp.float32
    )
    normed_partial = jnp.einsum(
        "jio,jbop->bip", project_in, grad_linear, preferred_element_type=jnp.float32
    )
    grad_normed = lax.psum_scatter(normed_partial, "tensor", scatter_dimension=1, tiled=True)
    third_gain_grad = channel_total(grad_normed * hat_three)
    third_shift_grad = channel_total(grad_normed)
    grad_resid = grad_out + group_back(
        grad_normed * per_channel(third_gain), hat_three, moments_three, width
    )
    second_bias_grad = channel_total(grad_resid)
    grad_conv_two = grad_resid.astype(jnp.bfloat16)
    resid_full = lax.all_gather(grad_conv_two, "tensor", axis=1, tiled=True)
    hat_one, pre_one, act_full, sum_one = front_part(
        inputs_f, moments_one, first_gain, first_shift, first_conv, bias_add, width
    )
    hat_two, pre_two, act_two = middle_part(sum_one, moments_two, second_gain, second_shift, width)
    second_conv_grad = conv_weight_grad(act_two, resid_full)
    grad_act_two = conv_back(resid_full, second_conv)
    grad_pre_two = grad_act_two * silu_slope(pre_two)
    second_gain_grad = channel_total(grad_pre_two * hat_two)
    second_shift_grad = channel_total(grad_pre_two)
    grad_sum_one = group_back(grad_pre_two * per_channel(second_gain), hat_two, moments_two, width)
    first_bias_grad = channel_total(grad_sum_one)
    grad_time = jnp.sum(grad_sum_one, axis=2)
    time_bias_grad = jnp.sum(grad_time, axis=0)
    time_weight_grad = jnp.dot(embed_act.astype(jnp.float32).T, grad_time, precision=highest)
    grad_embed = jnp.dot(
        grad_time, time_weight.astype(jnp.float32).T, precision=highest
    ) * silu_slope(embed_rows)
    table_partial = jnp.dot(one_hot.T, grad_embed, precision=highest)
    table_grad = lax.psum(table_partial, ("batch", "tensor"))
    grad_conv_one = grad_sum_one.astype(jnp.bfloat16)
    first_conv_grad = conv_weight_grad(act_full, grad_conv_one)
    act_partial = conv_back(grad_conv_one, first_conv)
    grad_act_one = lax.psum_scatter(act_partial, "tensor", scatter_dimension=1, tiled=True)
    grad_pre_one = grad_act_one * silu_slope(pre_one)
    first_gain_grad = channel_total(grad_pre_one * hat_one)
    first_shift_grad = channel_total(grad_pre_one)
    images_grad = grad_resid + group_back(
        grad_pre_one * per_channel(first_gain), hat_one, moments_one, width
    )
    summed = lax.psum(
        (
            first_gain_grad,
            first_shift_grad,
            first_conv_grad,
            first_bias_grad,
            time_weight_grad,
            time_bias_grad,
            second_gain_grad,
            second_shift_grad,
            second_conv_grad,
            second_bias_grad,
            third_gain_grad,
            third_shift_grad,
            project_in_grad,
            query_bias_grad,
            value_bias_grad,
            project_out_grad,
            output_bias_grad,
        ),
        "batch",
    )
    return (block_out, images_grad, table_grad) + tuple(summed)


def solution(mesh):
    in_specs = (
        P("batch", "tensor", None),
        P("batch"),
        P(),
        P("tensor"),
        P("tensor"),
        P(None, None, "tensor"),
        P("tensor"),
        P(None, "tensor"),
        P("tensor"),
        P("tensor"),
        P("tensor"),
        P(None, "tensor", None),
        P("tensor"),
        P("tensor"),
        P("tensor"),
        P(None, None, "tensor"),
        P("tensor"),
        P("tensor"),
        P("tensor", None),
        P("tensor"),
        P("batch", "tensor", None),
    )
    out_specs = (
        P("batch", "tensor", None),
        P("batch", "tensor", None),
        P(),
        P("tensor"),
        P("tensor"),
        P(None, None, "tensor"),
        P("tensor"),
        P(None, "tensor"),
        P("tensor"),
        P("tensor"),
        P("tensor"),
        P(None, "tensor", None),
        P("tensor"),
        P("tensor"),
        P("tensor"),
        P(None, None, "tensor"),
        P("tensor"),
        P("tensor"),
        P("tensor", None),
        P("tensor"),
    )
    return jax.shard_map(
        per_device, mesh=mesh, in_specs=in_specs, out_specs=out_specs, check_vma=False
    )
```

profile of v0, /device:TPU:0, one launch (start us, length us, event | category | flops | bytes accessed | tf_op | source)
XLA Modules:
  0.0 516.7 jit_solution(14788391389325860543)
XLA Ops:
  7.3 1.4 copy.63
  9.7 1.9 fusion.21
  12.7 10.7 %all-gather.5.cloned.1.call-done = bf16[8,256,256]{1,2,0:T(8,128)(2,1)} async-done(((bf16[8,128,256]{1,2,0:T(8,128)(2,1)}), bf16[8,256,256]{1,2,0:T(8,128)(2,1)}) %all-gather.5.cloned.1.call-update) | async-done | bytes 1048592 | tf_op jit(solution)/shard_map/all_gather | solution.py:87
  23.4 5.8 %pad_slice_fusion.8 = (bf16[8,256,16,16]{1,3,2,0:T(8,128)(2,1)S(1)}, bf16[8,256,16,16]{1,3,2,0:T(8,128)(2,1)S(1)}, bf16[8,256,16,16]{1,3,2,0:T(8,128)(2,1)S(1)},...) fusion(bf16[8,256,16,16]{1,3,2,0:T(8,128)(2,1)} %bitcast.183), kind=kLoop, calls=%fused_computation.8 | loop fusion | bytes 9437184 | tf_op jit(solution)/shard_map/slice | solution.py:25
  31.6 2.7 fusion.69
  36.5 1.0 pad_slice_fusion.24
  40.9 1.2 bitcast_dynamic-update-slice_fusion.3
  45.5 5.2 %convolution_bitcast_fusion.3 = f32[8,256,256]{1,2,0:T(8,128)} fusion(bf16[9,8,128,256]{2,3,1,0:T(8,128)(2,1)} %constant_dynamic-update-slice_fusion.8, bf16[9,128,256]{2,1,0:T(8,128)(2,1)S(1)} %copy-done.64), kind=kOutput, calls=%fused_computation.25 | convolution fusion | flops 1207959552 | bytes 7405568 | tf_op jit(solution)/shard_map/kio,kbip->bop/dot_general | solution.py:154
  51.9 9.8 %reduce-scatter.5.cloned.1.call-done = f32[8,128,256]{1,2,0:T(8,128)} async-done(((f32[8,256,256]{1,2,0:T(8,128)}), f32[8,128,256]{1,2,0:T(8,128)}) %reduce-scatter.5.cloned.1.call-update) | async-done | bytes 1048592 | tf_op jit(solution)/shard_map/reduce_scatter | solution.py:157
  61.7 1.4 fusion.67
  65.2 8.9 %all-gather.9.cloned.1.call-done = bf16[8,256,256]{1,2,0:T(8,128)(2,1)} async-done(((bf16[8,128,256]{1,2,0:T(8,128)(2,1)}), bf16[8,256,256]{1,2,0:T(8,128)(2,1)}) %all-gather.9.cloned.1.call-update) | async-done | bytes 1048592 | tf_op jit(solution)/shard_map/all_gather | solution.py:182
  74.1 2.5 convolution_convert_fusion
  76.6 9.8 %all-gather.7.cloned.1.call-done = bf16[8,256,256]{1,2,0:T(8,128)(2,1)} async-done(((bf16[8,128,256]{1,2,0:T(8,128)(2,1)}), bf16[8,256,256]{1,2,0:T(8,128)(2,1)}) %all-gather.7.cloned.1.call-update) | async-done | bytes 1048592 | tf_op jit(solution)/shard_map/all_gather | solution.py:162
  86.4 2.0 convolution_bitcast_fusion
  88.4 2.4 fusion.46
  90.8 2.5 fusion.50
  93.3 29.8 %all-reduce.15.cloned.1.call-done = (f32[8,256,256]{2,1,0:T(8,128)}, f32[8,256,256]{2,1,0:T(8,128)}) async-done(((f32[8,256,256]{2,1,0:T(8,128)}, f32[8,256,256]{2,1,0:T(8,128)}), (f32[8,256,256]{2,1,0:T(8,128)}, f32[8,256,256]{2,1,0:T(8,128)})) %all-reduce.15.cloned.1.call-update) | async-done | bytes 4194320 | tf_op jit(solution)/shard_map/psum | solution.py:100
  123.2 2.1 multiply_reduce_fusion.1
  125.3 2.3 fusion
  128.4 1.4 multiply_convert_fusion
  130.2 1.1 convert_reduce_fusion.3
  133.1 2.1 convolution_bitcast_fusion.2
  135.3 1.7 convolution_convert_fusion.2
  137.8 1.8 convolution_bitcast_fusion.4
  139.6 6.5 %reduce-scatter.9.cloned.1.call-done = f32[8,128,256]{1,2,0:T(8,128)} async-done(((f32[8,256,256]{1,2,0:T(8,128)}), f32[8,128,256]{1,2,0:T(8,128)}) %reduce-scatter.9.cloned.1.call-update) | async-done | bytes 1048592 | tf_op jit(solution)/shard_map/reduce_scatter | solution.py:214
  146.1 1.6 multiply_reduce_fusion.2
  148.5 10.8 %reduce-scatter.7.cloned.1.call-done = f32[8,128,256]{1,2,0:T(8,128)} async-done(((f32[8,256,256]{1,2,0:T(8,128)}), f32[8,128,256]{1,2,0:T(8,128)}) %reduce-scatter.7.cloned.1.call-update) | async-done | bytes 1048592 | tf_op jit(solution)/shard_map/reduce_scatter | solution.py:179
  159.3 3.0 fusion.65
  163.4 10.1 %all-gather.11.cloned.1.call-done = bf16[8,256,256]{1,2,0:T(8,128)(2,1)} async-done(((bf16[8,128,256]{1,2,0:T(8,128)(2,1)}), bf16[8,256,256]{1,2,0:T(8,128)(2,1)}) %all-gather.11.cloned.1.call-update) | async-done | bytes 1048592 | tf_op jit(solution)/shard_map/all_gather | solution.py:222
  173.5 6.2 %pad_slice_fusion = (bf16[8,256,16,16]{1,3,2,0:T(8,128)(2,1)S(1)}, bf16[8,256,16,16]{1,3,2,0:T(8,128)(2,1)S(1)}, bf16[8,256,16,16]{1,3,2,0:T(8,128)(2,1)S(1)}, b...) fusion(bf16[8,256,16,16]{1,3,2,0:T(8,128)(2,1)} %bitcast.181), kind=kLoop, calls=%fused_computation | loop fusion | bytes 9437184 | tf_op jit(solution)/shard_map/slice | solution.py:25
  182.5 3.9 multiply_reduce_fusion.3
  187.1 1.6 fusion.64
  188.7 1.0 pad_slice_fusion.16
  190.8 2.9 convolution_bitcast_fusion.1
  193.8 2.2 convolution_bitcast_fusion.10
  196.0 3.0 convolution_bitcast_fusion.9
  199.2 1.1 fusion.63
  200.3 2.4 fusion.57
  203.1 5.0 convolution_bitcast_fusion.5
  208.1 7.4 %convolution_bitcast_fusion.6 = f32[9,256,128]{2,1,0:T(8,128)} fusion(bf16[9,8,256,256]{2,3,0,1:T(8,128)(2,1)} %copy-done.34, bf16[8,128,256]{1,2,0:T(8,128)(2,1)S(1)} %copy-done.13), kind=kOutput, calls=%fused_computation.49 | convolution fusion | flops 1207959552 | bytes 11141120 | tf_op jit(solution)/shard_map/kbip,bop->kio/dot_general | solution.py:42
  215.6 1.3 copy.83
  217.0 2.0 fusion.29
  219.0 43.3 %all-reduce.4 = (f32[128]{0:T(128)}, f32[128]{0:T(128)}, f32[128]{0:T(128)S(1)}, f32[128]{0:T(128)}, f32[128]{0:T(128)}, /*index=5*/f32[128]{0:T(128)}, f32[128]...) all-reduce(f32[128]{0:T(128)S(1)} %get-tuple-element.64, ...), channel_id=1, replica_groups=mesh['batch'=16,'tensor'=2] {'batch'}, use_global_device_ids=true, to_apply=%region_36.37 | all-reduce | flops 1408 | bytes 11264 | tf_op jit(solution)/shard_map/psum | solution.py:252
  263.0 1.3 fusion.28
  264.3 2.6 copy.84
  266.9 79.2 %all-reduce.11.cloned.1.call-done = f32[1024,512]{1,0:T(8,128)} async-done(((f32[1024,512]{1,0:T(8,128)}), f32[1024,512]{1,0:T(8,128)}) %all-reduce.11.cloned.1.call-update) | async-done | bytes 2097168 | tf_op jit(solution)/shard_map/psum | solution.py:241
  346.1 155.6 %all-reduce.13.cloned.1.call-done = (f32[9,256,128]{2,1,0:T(8,128)}, f32[512,128]{1,0:T(8,128)}, f32[9,128,256]{2,1,0:T(8,128)}, f32[3,256,128]{2,1,0:T(8,128)}, f32[128,256]{1,0:T(8,128)}) async-done(((f32[9,256,128]{2,1,0:T(8,128)}, f32[512,128]{1,0:T(8,128)}, f32[9,128,256]{2,1,0:T(8,128)}, f32[3,256,128]{2,1,0:T(8,128)}, f32[128,256]{1,0:T(8,128)}), (f32[9,256,128]{2,1,0:T(8,128)}, ...) | async-done | bytes 3145744 | tf_op jit(solution)/shard_map/psum | solution.py:252
  502.2 3.3 copy.155
  (277 shorter events, 32.5 us)
Async XLA Ops:
  7.2 5.4 %copy-start.26 = (bf16[512,128]{1,0:T(8,128)(2,1)S(1)}, bf16[512,128]{1,0:T(8,128)(2,1)}, u32[]{:S(2)}) copy-start(bf16[512,128]{1,0:T(8,128)(2,1)} %param.28) | copy-start | bytes 393220
  7.2 5.4 %copy-start.59 = (f32[128]{0:T(128)S(1)}, f32[128]{0:T(128)}, u32[]{:S(2)}) copy-start(f32[128]{0:T(128)} %param.29) | copy-start | bytes 1540
  7.2 5.4 %copy-start.60 = (f32[128]{0:T(128)S(1)}, f32[128]{0:T(128)}, u32[]{:S(2)}) copy-start(f32[128]{0:T(128)} %param.27) | copy-start | bytes 1540
  7.2 16.2 %all-gather.5.cloned.1.call-start = ((), (), s32[]{:S(2)}) async-start(), calls=%async_computation.4 | async-start | bytes 1572864 | tf_op jit(solution)/shard_map/all_gather | solution.py:87
  8.7 53.0 %copy-start.5 = (bf16[8,128,256]{1,2,0:T(8,128)(2,1)}, bf16[8,128,256]{1,2,0:T(8,128)(2,1)S(1)}, u32[]{:S(2)}) copy-start(bf16[8,128,256]{1,2,0:T(8,128)(2,1)S(1)} %copy.63) | copy-start | bytes 1572868
  9.2 20.1 %copy-start.37 = (f32[8,128]{1,0:T(8,128)}, f32[8,128]{1,0:T(8,128)S(1)}, u32[]{:S(2)}) copy-start(f32[8,128]{1,0:T(8,128)S(1)} %sub.153) | copy-start | bytes 12292
  9.7 19.5 %copy-start.43 = (f32[8,128]{1,0:T(8,128)}, f32[8,128]{1,0:T(8,128)S(1)}, u32[]{:S(2)}) copy-start(f32[8,128]{1,0:T(8,128)S(1)} %mul.241) | copy-start | bytes 12292
  11.6 50.1 %reduce-scatter.5.cloned.1.call-start = ((), (), s32[]{:S(2)}) async-start(), calls=%async_computation.5 | async-start | bytes 3145728 | tf_op jit(solution)/shard_map/reduce_scatter | solution.py:157
  31.6 4.5 copy-start.47
  31.6 4.6 copy-start.53
  35.3 5.7 %copy-start.7 = (f32[8,128,256]{1,2,0:T(8,128)}, f32[8,128,256]{1,2,0:T(8,128)S(1)}, u32[]{:S(2)}) copy-start(f32[8,128,256]{1,2,0:T(8,128)S(1)} %get-tuple-element.135) | copy-start | bytes 3145732
  35.6 5.3 %copy-start.35 = (f32[8,128]{1,0:T(8,128)}, f32[8,128]{1,0:T(8,128)S(1)}, u32[]{:S(2)}) copy-start(f32[8,128]{1,0:T(8,128)S(1)} %sub.157) | copy-start | bytes 12292
  36.2 4.8 copy-start.41
  38.4 7.1 %copy-start.64 = (bf16[9,128,256]{2,1,0:T(8,128)(2,1)S(1)}, bf16[9,128,256]{2,1,0:T(8,128)(2,1)}, u32[]{:S(2)}) copy-start(bf16[9,128,256]{2,1,0:T(8,128)(2,1)} %param.32) | copy-start | bytes 1769476
  45.5 5.3 %copy-start.25 = (bf16[8,128,256]{2,1,0:T(8,128)(2,1)S(1)}, bf16[8,128,256]{2,1,0:T(8,128)(2,1)}, u32[]{:S(2)}) copy-start(bf16[8,128,256]{2,1,0:T(8,128)(2,1)} %param.41) | copy-start | bytes 1572868
  45.5 16.3 %copy-start.62 = (f32[128]{0:T(128)S(1)}, f32[128]{0:T(128)}, u32[]{:S(2)}) copy-start(f32[128]{0:T(128)} %param.33) | copy-start | bytes 1540
  50.7 13.3 %copy-start.50 = (f32[128]{0:T(128)S(1)}, f32[128]{0:T(128)}, u32[]{:S(2)}) copy-start(f32[128]{0:T(128)} %param.34) | copy-start | bytes 1540
  50.7 13.3 %copy-start.61 = (f32[128]{0:T(128)S(1)}, f32[128]{0:T(128)}, u32[]{:S(2)}) copy-start(f32[128]{0:T(128)} %param.35) | copy-start | bytes 1540
  50.7 23.4 %copy-start.31 = (bf16[128,256]{1,0:T(8,128)(2,1)S(1)}, bf16[128,256]{1,0:T(8,128)(2,1)}, u32[]{:S(2)}) copy-start(bf16[128,256]{1,0:T(8,128)(2,1)} %param.39) | copy-start | bytes 196612
  50.7 35.6 %copy-start.32 = (bf16[3,256,128]{2,1,0:T(8,128)(2,1)S(1)}, bf16[3,256,128]{2,1,0:T(8,128)(2,1)}, u32[]{:S(2)}) copy-start(bf16[3,256,128]{2,1,0:T(8,128)(2,1)} %param.36) | copy-start | bytes 589828
  50.7 23.4 %all-gather.9.cloned.1.call-start = ((), (), s32[]{:S(2)}) async-start(), calls=%async_computation.8 | async-start | bytes 1572864 | tf_op jit(solution)/shard_map/all_gather | solution.py:182
  51.8 34.5 %all-gather.7.cloned.1.call-start = ((), (), s32[]{:S(2)}) async-start(), calls=%async_computation.6 | async-start | bytes 1572864 | tf_op jit(solution)/shard_map/all_gather | solution.py:162
  63.1 13.5 %copy-start.3 = (f32[8,128,256]{1,2,0:T(8,128)}, f32[8,128,256]{1,2,0:T(8,128)S(1)}, u32[]{:S(2)}) copy-start(f32[8,128,256]{1,2,0:T(8,128)S(1)} %get-tuple-element.97) | copy-start | bytes 3145732
  63.5 13.1 %copy-start.39 = (f32[8,128]{1,0:T(8,128)}, f32[8,128]{1,0:T(8,128)S(1)}, u32[]{:S(2)}) copy-start(f32[8,128]{1,0:T(8,128)S(1)} %sub.161) | copy-start | bytes 12292
  64.0 12.6 %copy-start.45 = (f32[8,128]{1,0:T(8,128)}, f32[8,128]{1,0:T(8,128)S(1)}, u32[]{:S(2)}) copy-start(f32[8,128]{1,0:T(8,128)S(1)} %mul.256) | copy-start | bytes 12292
  65.0 58.2 %all-reduce.15.cloned.1.call-start = ((), (), s32[]{:S(2)}) async-start(), calls=%async_computation.14 | async-start | bytes 8388608 | tf_op jit(solution)/shard_map/psum | solution.py:100
  93.3 52.9 %reduce-scatter.9.cloned.1.call-start = ((), (), s32[]{:S(2)}) async-start(), calls=%async_computation.9 | async-start | bytes 3145728 | tf_op jit(solution)/shard_map/reduce_scatter | solution.py:214
  135.2 11.0 %copy-start.40 = (f32[8,128]{1,0:T(8,128)S(1)}, f32[8,128]{1,0:T(8,128)}, u32[]{:S(2)}) copy-start(f32[8,128]{1,0:T(8,128)} %copy-done.39) | copy-start | bytes 12292
  135.2 11.0 %copy-start.46 = (f32[8,128]{1,0:T(8,128)S(1)}, f32[8,128]{1,0:T(8,128)}, u32[]{:S(2)}) copy-start(f32[8,128]{1,0:T(8,128)} %copy-done.45) | copy-start | bytes 12292
  135.2 11.0 %copy-start.51 = (f32[128]{0:T(128)S(1)}, f32[128]{0:T(128)}, u32[]{:S(2)}) copy-start(f32[128]{0:T(128)} %param.34) | copy-start | bytes 1540
  135.2 24.1 %copy-start.63 = (f32[128]{0:T(128)S(1)}, f32[128]{0:T(128)}, u32[]{:S(2)}) copy-start(f32[128]{0:T(128)} %param.40) | copy-start | bytes 1540
  135.2 24.1 %reduce-scatter.7.cloned.1.call-start = ((), (), s32[]{:S(2)}) async-start(), calls=%async_computation.7 | async-start | bytes 3145728 | tf_op jit(solution)/shard_map/reduce_scatter | solution.py:179
  137.8 8.4 %copy-start.4 = (f32[8,128,256]{1,2,0:T(8,128)S(1)}, f32[8,128,256]{1,2,0:T(8,128)}, u32[]{:S(2)}) copy-start(f32[8,128,256]{1,2,0:T(8,128)} %copy-done.3) | copy-start | bytes 3145732
  137.8 21.5 %copy-start.18 = (bf16[8,128,256]{1,2,0:T(8,128)(2,1)S(1)}, bf16[8,128,256]{1,2,0:T(8,128)(2,1)}, u32[]{:S(2)}) copy-start(bf16[8,128,256]{1,2,0:T(8,128)(2,1)} %copy.68) | copy-start | bytes 1572868
  139.6 33.9 %all-gather.11.cloned.1.call-start = ((), (), s32[]{:S(2)}) async-start(), calls=%async_computation.10 | async-start | bytes 1572864 | tf_op jit(solution)/shard_map/all_gather | solution.py:222
  163.2 53.8 %reduce-scatter.11.cloned.1.call-start = ((), (), s32[]{:S(2)}) async-start(), calls=%async_computation.11 | async-start | bytes 3145728 | tf_op jit(solution)/shard_map/reduce_scatter | solution.py:245
  190.8 5.2 %copy-start.24 = (bf16[8,128,256]{2,1,0:T(8,128)(2,1)S(1)}, bf16[8,128,256]{2,1,0:T(8,128)(2,1)}, u32[]{:S(2)}) copy-start(bf16[8,128,256]{2,1,0:T(8,128)(2,1)} %copy-done.23) | copy-start | bytes 1572868
  193.8 6.5 %copy-start.55 = (s32[8]{0:T(128)S(1)}, s32[8]{0:T(128)}, u32[]{:S(2)}) copy-start(s32[8]{0:T(128)} %param.22) | copy-start | bytes 100
  193.8 152.4 %all-reduce.11.cloned.1.call-start = ((), (), s32[]{:S(2)}) async-start(), calls=%async_computation.12 | async-start | bytes 4194304 | tf_op jit(solution)/shard_map/psum | solution.py:241
  202.7 5.3 %copy-start.13 = (bf16[8,128,256]{1,2,0:T(8,128)(2,1)S(1)}, bf16[8,128,256]{1,2,0:T(8,128)(2,1)}, u32[]{:S(2)}) copy-start(bf16[8,128,256]{1,2,0:T(8,128)(2,1)} %copy-done.12) | copy-start | bytes 1572868
  202.8 298.9 %all-reduce.13.cloned.1.call-start = ((), (), s32[]{:S(2)}) async-start(), calls=%async_computation.13 | async-start | bytes 6291456 | tf_op jit(solution)/shard_map/psum | solution.py:252
  208.1 7.5 %copy-start.20 = (f32[8,128,256]{1,2,0:T(8,128)S(1)}, f32[8,128,256]{1,2,0:T(8,128)}, u32[]{:S(2)}) copy-start(f32[8,128,256]{1,2,0:T(8,128)} %get-tuple-element.108) | copy-start | bytes 3145732
  262.3 243.2 %copy-start.68 = (f32[128]{0:T(128)}, f32[128]{0:T(128)S(1)}, u32[]{:S(2)}) copy-start(f32[128]{0:T(128)S(1)} %get-tuple-element.190) | copy-start | bytes 1540
  501.7 4.9 copy-start.30
  501.7 5.6 %copy-start.21 = (f32[9,128,256]{2,1,0:T(8,128)S(1)}, f32[9,128,256]{2,1,0:T(8,128)}, u32[]{:S(2)}) copy-start(f32[9,128,256]{2,1,0:T(8,128)} %get-tuple-element.195) | copy-start | bytes 3538948
  501.7 8.0 %copy-start.1 = (bf16[1024,512]{1,0:T(8,128)(2,1)S(1)}, bf16[1024,512]{1,0:T(8,128)(2,1)}, u32[]{:S(2)}) copy-start(bf16[1024,512]{1,0:T(8,128)(2,1)} %param.23) | copy-start | bytes 3145732
  502.2 6.1 %copy-start.29 = (f32[3,256,128]{2,1,0:T(8,128)S(1)}, f32[3,256,128]{2,1,0:T(8,128)}, u32[]{:S(2)}) copy-start(f32[3,256,128]{2,1,0:T(8,128)} %get-tuple-element.199) | copy-start | bytes 1179652
  502.2 6.8 %copy-start.33 = (f32[128,256]{1,0:T(8,128)S(1)}, f32[128,256]{1,0:T(8,128)}, u32[]{:S(2)}) copy-start(f32[128,256]{1,0:T(8,128)} %get-tuple-element.202) | copy-start | bytes 393220
  (32 other events, 66.8 us)
Sparse Core Ops, SparseCore 0:
  11.7 11.6 all-gather.4
  50.9 10.8 reduce-scatter.4
  63.9 10.1 all-gather.8
  76.1 10.1 all-gather.6
  93.4 29.7 all-reduce.14
  135.3 10.7 reduce-scatter.8
  148.5 10.7 reduce-scatter.6
  163.3 10.1 all-gather.10
  193.9 10.7 reduce-scatter.10
  210.8 135.3 all-reduce.10
  354.1 147.5 all-reduce.12
where the time goes:
time: 525 us; the launch traced here: 517 us
  waiting for transfers between devices  331 us (63%)
  matrix products  54.5 us (10%)
  local copies, waits for them, and re-layouts  46.7 us (9%)
  blocking collectives  43.3 us (8%)
  other arithmetic  24.2 us (5%)
  between operations  15.5 us (3%)
    psum x1, waiting for transfers between devices, per_device(): lax.psum((first_gain_grad, first_shift_grad, first_conv_grad, first_bias_...  156 us
    psum x1, waiting for transfers between devices, per_device(): table_grad = lax.psum(table_partial, ('batch', 'tensor'))  79.2 us
    psum x1, blocking collectives, per_device(): lax.psum((first_gain_grad, first_shift_grad, first_conv_grad, first_bias_...  43.3 us
    psum x1, waiting for transfers between devices, attention_scores(): raw = lax.psum(partial_raw, 'tensor')  29.8 us
    unnamed x180, local copies, waits for them, and re-layouts  28.6 us
    slice x4, local copies, waits for them, and re-layouts, shifted_taps(): padded[..., top:top + side, left:left + side].reshape(values.shape)  14.1 us
    dot_general x2, matrix products, conv_weight_grad(): jnp.einsum('kbip,bop->kio', shifted_taps(values, 1), grads, preferred_ele...  12.5 us
    reduce_scatter x1, waiting for transfers between devices, per_device(): lax.psum_scatter(proj_partial, 'tensor', scatter_dimension=1, tiled=True)  10.8 us
  transfers between devices with their start and end apart: 11, of which 10 were waited for; matrix products, arithmetic and copies ran while one was open for 8% of the time, Pallas kernels for 0%

commit v1 on v0

v1 whole, which is shorter than its diff:
```python
import functools
import math

import jax
import jax.numpy as jnp
from jax import lax
from jax.experimental import pallas as pl
from jax.experimental.pallas import tpu as pltpu
from jax.sharding import PartitionSpec as P

GROUPS = 32
EPS = 1e-06
VMEM_LIMIT = 56 * 1024 * 1024
ANY = pl.BlockSpec(memory_space=pl.ANY)
VMEM = pl.BlockSpec(memory_space=pltpu.VMEM)
SMEM = pl.BlockSpec(memory_space=pltpu.SMEM)
f32 = jnp.float32
bf16 = jnp.bfloat16

(
    FIRST_GAIN,
    FIRST_SHIFT,
    FIRST_BIAS,
    TIME_BIAS,
    SECOND_GAIN,
    SECOND_SHIFT,
    SECOND_BIAS,
    THIRD_GAIN,
    THIRD_SHIFT,
    QUERY_BIAS,
    VALUE_BIAS,
    OUTPUT_BIAS,
) = range(12)


def nn(a, b):
    return lax.dot_general(a, b, (((1,), (0,)), ((), ())), preferred_element_type=f32)


def nt(a, b):
    return lax.dot_general(a, b, (((1,), (1,)), ((), ())), preferred_element_type=f32)


def sigmoid(v):
    return 0.5 * jnp.tanh(0.5 * v) + 0.5


def silu_slope(v, sig):
    return sig * (1.0 + v * (1.0 - sig))


def col_sum(v):
    return jnp.sum(v, axis=0, keepdims=True)


def lane_groups(v, width):
    lanes = v.shape[1]
    lane = lax.broadcasted_iota(jnp.int32, v.shape, 1)
    step = 1
    while step < width:
        up = pltpu.roll(v, step, 1)
        down = pltpu.roll(v, lanes - step, 1)
        v = v + jnp.where((lane & step) != 0, up, down)
        step *= 2
    return v


def fill_shift(shift_ref, side):
    points = shift_ref.shape[1]
    to = lax.broadcasted_iota(jnp.int32, (points, points), 0)
    of = lax.broadcasted_iota(jnp.int32, (points, points), 1)
    for d in range(3):
        s = d - 1
        col = (to & (side - 1)) + s
        hit = (of == to + s) & (col >= 0) & (col < side)
        shift_ref[d * points : (d + 1) * points, :] = jnp.where(hit, 1.0, 0.0).astype(bf16)


def zero_pads(pad_ref, side, points):
    images, chans = pad_ref.shape[1], pad_ref.shape[3]
    for d in range(3):
        for b in range(images):
            pad_ref[d, b, 0:side, :] = jnp.zeros((side, chans), bf16)
            pad_ref[d, b, side + points : 2 * side + points, :] = jnp.zeros((side, chans), bf16)


def put_pads(pad_ref, b, moved, side, points):
    for d in range(3):
        pad_ref[d, b, side : side + points, :] = moved[d * points : (d + 1) * points]


def taps(pad_ref, b, sign, side, points):
    out = []
    for dr in (-1, 0, 1):
        for dc in (-1, 0, 1):
            top = side + sign * dr * side
            out.append(pad_ref[1 + sign * dc, b, top : top + points, :])
    return out


class Copies:
    def __init__(self, sems):
        self.sems = sems
        self.used = 0

    def start(self, src, dst):
        copy = pltpu.make_async_copy(src, dst, self.sems.at[self.used])
        self.used += 1
        copy.start()
        return copy


def wait_all(copies):
    for c in copies:
        c.wait()


def side_of(points):
    return math.isqrt(points)


def load_split(cps, refs, dst, axis, places):
    out = []
    for ref, place in zip(refs, places, strict=True):
        size = ref.shape[axis]
        idx = [slice(None)] * len(ref.shape)
        idx[axis] = pl.ds(pl.multiple_of(place * size, size), size)
        out.append(cps.start(ref, dst.at[tuple(idx)]))
    return out


def load_images(cps, refs, dst, places, count):
    out = []
    for j, (ref, place) in enumerate(zip(refs, places, strict=True)):
        size = ref.shape[1]
        first = pl.multiple_of(places[0] * count, count) if j == 0 else 0
        out.append(
            cps.start(
                ref.at[pl.ds(first, count)],
                dst.at[:, pl.ds(pl.multiple_of(place * size, size), size), :],
            )
        )
    return out


def places_of(pieces):
    if pieces == 1:
        return [0]
    me = lax.axis_index("tensor")
    return [me, 1 - me]


def split_store(own_ref, send_ref, at, value, axis, places):
    if send_ref is None:
        own_ref[at] = value.astype(own_ref.dtype)
        return
    half = value.shape[axis] // 2
    low = lax.slice_in_dim(value, 0, half, axis=axis)
    high = lax.slice_in_dim(value, half, 2 * half, axis=axis)
    first = places[0] == 0
    own_ref[at] = jnp.where(first, low, high).astype(own_ref.dtype)
    send_ref[at] = jnp.where(first, high, low).astype(send_ref.dtype)


def front_kernel(pieces, count, *refs):
    it = iter(refs)

    def take(n):
        return [next(it) for _ in range(n)]

    x_in, g_in, w1_in, w2_in, pi_in, po_in, tw_in, vec_in = (take(pieces) for _ in range(8))
    steps_ref, table_ref = take(2)
    dw2_own, dpo_own, dpi_own = take(3)
    dw2_send, dpo_send, dpi_send = take(3) if pieces == 2 else (None, None, None)
    vec_out, stat_out = take(2)
    gpad_out, sum_out, a1t_out, resid_out, gres_out, mix_out = take(6)
    xin, gin, w1, w2, pi, po, tw, vec, rows = take(9)
    shift, apad, gpad, sum_one, a1t, resid, gres, mix = take(8)
    a2t, nmt, gl = take(3)
    sems = next(it)

    cps = Copies(sems)
    places = places_of(pieces)
    chans, points = xin.shape[1], xin.shape[2]
    side = side_of(points)
    width = chans // GROUPS
    size = float(width * points)
    scale = chans ** (-0.5)

    x_cp = load_images(cps, x_in, xin, places, count)
    vec_cp = load_split(cps, vec_in, vec, 1, places)
    row_cp = []
    for b in range(count):
        step = steps_ref[places[0] * count + b]
        row_cp.append(
            cps.start(table_ref.at[pl.ds(pl.multiple_of(step // 16 * 16, 16), 16), :], rows.at[b])
        )
    tw_cp = load_split(cps, tw_in, tw, 1, places)
    w1_cp = load_split(cps, w1_in, w1, 2, places)
    w2_cp = load_split(cps, w2_in, w2, 1, places)
    pi_cp = load_split(cps, pi_in, pi, 2, places)
    po_cp = load_split(cps, po_in, po, 0, places)
    g_cp = load_images(cps, g_in, gin, places, count)

    fill_shift(shift, side)
    zero_pads(apad, side, points)
    zero_pads(gpad, side, points)
    eye = shift[points : 2 * points, :]

    wait_all(vec_cp)
    vcols = jnp.transpose(vec[...])

    def col(j):
        return vcols[:, j : j + 1]

    def row(j):
        return vec[j : j + 1, :]

    wait_all(x_cp)
    for b in range(count):
        x3 = xin[b].astype(f32).reshape(GROUPS, width, points)
        mean = jnp.sum(jnp.sum(x3, axis=2, keepdims=True), axis=1, keepdims=True) / size
        off = x3 - mean
        var = jnp.sum(jnp.sum(off * off, axis=2, keepdims=True), axis=1, keepdims=True) / size
        hat = (off * lax.rsqrt(var + EPS)).reshape(chans, points)
        pre = hat * col(FIRST_GAIN) + col(FIRST_SHIFT)
        act = (pre * sigmoid(pre)).astype(bf16)
        a1t[b] = act
        put_pads(apad, b, nt(shift[...], act).astype(bf16), side, points)
    outs = [cps.start(a1t, a1t_out)]

    wait_all(row_cp)
    wait_all(tw_cp)
    picked = []
    for b in range(count):
        step = steps_ref[places[0] * count + b]
        r = lax.broadcasted_iota(jnp.int32, (16, rows.shape[2]), 0)
        picked.append(
            col_sum(jnp.where(r == lax.rem(step, 16), rows[b].astype(f32), 0.0))
        )
    emb = jnp.concatenate(picked + picked[:1] * (8 - count), axis=0)
    time_add = nn((emb * sigmoid(emb)).astype(bf16), tw[...]) + row(TIME_BIAS)

    wait_all(w1_cp)
    w1_rows = w1[...].reshape(9 * chans, chans)
    sums = []
    for b in range(count):
        lhs = jnp.concatenate(taps(apad, b, 1, side, points), axis=1)
        val = nn(lhs, w1_rows) + (row(FIRST_BIAS) + time_add[b : b + 1])
        sum_one[b] = val
        sums.append(col_sum(val))
    outs.append(cps.start(sum_one, sum_out))
    mean2 = lane_groups(jnp.concatenate(sums, axis=0), width) / size
    sums = []
    for b in range(count):
        off = sum_one[b] - mean2[b : b + 1]
        sums.append(col_sum(off * off))
    rstd2 = lax.rsqrt(lane_groups(jnp.concatenate(sums, axis=0), width) / size + EPS)
    stat_out[0, 0:count, :] = mean2
    stat_out[1, 0:count, :] = rstd2
    for b in range(count):
        hat = (sum_one[b] - mean2[b : b + 1]) * rstd2[b : b + 1]
        pre = hat * row(SECOND_GAIN) + row(SECOND_SHIFT)
        act = (pre * sigmoid(pre)).astype(bf16)
        a2t[b] = nt(eye, act).astype(bf16)
        put_pads(apad, b, nn(shift[...], act).astype(bf16), side, points)

    wait_all(w2_cp)
    w2_rows = w2[...].reshape(9 * chans, chans)
    sums = []
    for b in range(count):
        lhs = jnp.concatenate(taps(apad, b, 1, side, points), axis=1)
        val = nn(lhs, w2_rows) + row(SECOND_BIAS) + nt(eye, xin[b])
        resid[b] = val
        sums.append(col_sum(val))
    outs.append(cps.start(resid, resid_out))
    mean3 = lane_groups(jnp.concatenate(sums, axis=0), width) / size
    sums = []
    for b in range(count):
        off = resid[b] - mean3[b : b + 1]
        sums.append(col_sum(off * off))
    rstd3 = lax.rsqrt(lane_groups(jnp.concatenate(sums, axis=0), width) / size + EPS)

    wait_all(pi_cp)
    wait_all(po_cp)
    wait_all(g_cp)
    pi_q, pi_k, pi_v = pi[0], pi[1], pi[2]
    pi_row = jnp.concatenate([pi_q, pi_k, pi_v], axis=1)
    pi_kt = nt(eye, pi_k).astype(bf16) if chans == points else jnp.transpose(pi_k)
    pi_vt = nt(eye, pi_v).astype(bf16) if chans == points else jnp.transpose(pi_v)
    zero = jnp.zeros((1, chans), f32)
    qb_grad, vb_grad, ob_grad = zero, zero, zero
    gain3, shift3 = [], []
    dpo = None
    for b in range(count):
        hat = (resid[b] - mean3[b : b + 1]) * rstd3[b : b + 1]
        normed = (hat * row(THIRD_GAIN) + row(THIRD_SHIFT)).astype(bf16)
        nmt[b] = nt(eye, normed).astype(bf16)
        lin = nn(normed, pi_row)
        q = (lin[:, :chans] + row(QUERY_BIAS)).astype(bf16)
        k = lin[:, chans : 2 * chans].astype(bf16)
        v = (lin[:, 2 * chans :] + row(VALUE_BIAS)).astype(bf16)
        kt = nt(pi_kt, normed).astype(bf16)
        vt = (nt(pi_vt, normed) + col(VALUE_BIAS)).astype(bf16)
        scores = nt(k, q) * scale
        expo = jnp.exp(scores - jnp.max(scores, axis=0, keepdims=True))
        probs = expo * (1.0 / jnp.sum(expo, axis=0, keepdims=True))
        weights = probs.astype(bf16)
        mixed = nn(vt, weights).astype(bf16)
        mix[b] = mixed
        grad = gin[b]
        part = nt(mixed, grad)
        dpo = part if dpo is None else dpo + part
        grad_mixed = nn(po[...], grad).astype(bf16)
        grad_w = nn(v, grad_mixed)
        grad_v = nt(weights, grad_mixed).astype(bf16)
        inner = probs * grad_w
        grad_s = (inner - probs * jnp.sum(inner, axis=0, keepdims=True)).astype(bf16)
        grad_qt = (nn(kt, grad_s) * scale).astype(bf16)
        grad_q = nt(eye, grad_qt).astype(bf16)
        grad_k = (nn(grad_s, q) * scale).astype(bf16)
        qb_grad = qb_grad + col_sum(grad_q.astype(f32))
        vb_grad = vb_grad + col_sum(grad_v.astype(f32))
        lhs = jnp.concatenate([grad_q, grad_k, grad_v], axis=1)
        gl[b] = lhs
        grad_n = nt(lhs, pi_row)
        gres[b] = grad_n
        gain3.append(col_sum(grad_n * hat))
        shift3.append(col_sum(grad_n))
    outs.append(cps.start(mix, mix_out))
    split_store(dpo_own, dpo_send, ..., dpo, 0, places)
    gain3 = jnp.concatenate(gain3, axis=0)
    shift3 = jnp.concatenate(shift3, axis=0)
    first_mean = lane_groups(shift3 * row(THIRD_GAIN), width) / size
    second_mean = lane_groups(gain3 * row(THIRD_GAIN), width) / size
    sb_grad = zero
    for b in range(count):
        hat = (resid[b] - mean3[b : b + 1]) * rstd3[b : b + 1]
        h = gres[b] * row(THIRD_GAIN)
        grad_out = nt(eye, gin[b])
        ob_grad = ob_grad + col_sum(grad_out)
        val = grad_out + rstd3[b : b + 1] * (
            h - first_mean[b : b + 1] - hat * second_mean[b : b + 1]
        )
        gres[b] = val
        sb_grad = sb_grad + col_sum(val)
        put_pads(gpad, b, nn(shift[...], val.astype(bf16)).astype(bf16), side, points)
    outs.append(cps.start(gres, gres_out))
    outs.append(cps.start(gpad, gpad_out))

    nm_all = jnp.concatenate([nmt[b] for b in range(count)], axis=1)
    gl_all = jnp.concatenate([gl[b] for b in range(count)], axis=0)
    for j in range(3):
        val = nn(nm_all, gl_all[:, j * chans : (j + 1) * chans])
        split_store(dpi_own, dpi_send, j, val, 1, places)
    a_all = jnp.concatenate([a2t[b] for b in range(count)], axis=1)
    moved = [taps(gpad, b, -1, side, points) for b in range(count)]
    for tap in range(9):
        val = nn(a_all, jnp.concatenate([moved[b][tap] for b in range(count)], axis=0))
        split_store(dw2_own, dw2_send, tap, val, 0, places)

    vec_out[...] = jnp.concatenate(
        [sb_grad, col_sum(gain3), col_sum(shift3), qb_grad, vb_grad, ob_grad, zero, zero], axis=0
    )
    wait_all(outs)


def middle_kernel(pieces, count, *refs):
    it = iter(refs)

    def take(n):
        return [next(it) for _ in range(n)]

    w2_in, vec_in = (take(pieces) for _ in range(2))
    gpad_in, sum_in, a1t_in, stat = take(4)
    dw1_own = next(it)
    dw1_send = next(it) if pieces == 2 else None
    vec_out, time_out, hpad_out = take(3)
    w2, vec, gpad, sum_one, a1t, shift, hpad, grad = take(8)
    sems = next(it)
    cps = Copies(sems)
    places = places_of(pieces)
    chans, points = a1t.shape[1], a1t.shape[2]
    side = side_of(points)
    width = chans // GROUPS
    size = float(width * points)

    vec_cp = load_split(cps, vec_in, vec, 1, places)
    w2_cp = load_split(cps, w2_in, w2, 1, places)
    gpad_cp = cps.start(gpad_in, gpad)
    sum_cp = cps.start(sum_in, sum_one)
    a1t_cp = cps.start(a1t_in, a1t)
    fill_shift(shift, side)
    zero_pads(hpad, side, points)
    wait_all(vec_cp)

    def row(j):
        return vec[j : j + 1, :]

    wait_all(w2_cp)
    gpad_cp.wait()
    sum_cp.wait()
    mean2, rstd2 = stat[0], stat[1]
    w2_cols = jnp.concatenate([w2[k] for k in range(9)], axis=1)
    gain, shift_g = [], []
    for b in range(count):
        back = nt(jnp.concatenate(taps(gpad, b, -1, side, points), axis=1), w2_cols)
        hat = (sum_one[b] - mean2[b : b + 1]) * rstd2[b : b + 1]
        pre = hat * row(SECOND_GAIN) + row(SECOND_SHIFT)
        val = back * silu_slope(pre, sigmoid(pre))
        grad[b] = val
        gain.append(col_sum(val * hat))
        shift_g.append(col_sum(val))
    gain = jnp.concatenate(gain, axis=0)
    shift_g = jnp.concatenate(shift_g, axis=0)
    first_mean = lane_groups(shift_g * row(SECOND_GAIN), width) / size
    second_mean = lane_groups(gain * row(SECOND_GAIN), width) / size
    times = []
    for b in range(count):
        hat = (sum_one[b] - mean2[b : b + 1]) * rstd2[b : b + 1]
        val = rstd2[b : b + 1] * (
            grad[b] * row(SECOND_GAIN) - first_mean[b : b + 1] - hat * second_mean[b : b + 1]
        )
        times.append(col_sum(val))
        put_pads(hpad, b, nn(shift[...], val.astype(bf16)).astype(bf16), side, points)
    out_cp = cps.start(hpad, hpad_out)
    times = jnp.concatenate(times, axis=0)
    time_out[0:count, :] = times
    zero = jnp.zeros((1, chans), f32)
    vec_out[...] = jnp.concatenate(
        [col_sum(gain), col_sum(shift_g), col_sum(times)] + [zero] * 5, axis=0
    )
    a1t_cp.wait()
    a_all = jnp.concatenate([a1t[b] for b in range(count)], axis=1)
    moved = [taps(hpad, b, -1, side, points) for b in range(count)]
    for tap in range(9):
        val = nn(a_all, jnp.concatenate([moved[b][tap] for b in range(count)], axis=0))
        split_store(dw1_own, dw1_send, tap, val, 1, places)
    out_cp.wait()


def last_kernel(pieces, count, *refs):
    it = iter(refs)

    def take(n):
        return [next(it) for _ in range(n)]

    x_in, w1_in, po_in, vec_in = (take(pieces) for _ in range(4))
    hpad_in, resid_in, gres_in, mix_in = take(4)
    block_own, image_own = take(2)
    block_send, image_send = take(2) if pieces == 2 else (None, None)
    vec_out = next(it)
    xin, w1, po, vec, hpad, resid, gres, mix = take(8)
    sems = next(it)
    cps = Copies(sems)
    places = places_of(pieces)
    chans, points = xin.shape[1], xin.shape[2]
    side = side_of(points)
    width = chans // GROUPS
    size = float(width * points)

    vec_cp = load_split(cps, vec_in, vec, 1, places)
    po_cp = load_split(cps, po_in, po, 0, places)
    mix_cp = cps.start(mix_in, mix)
    resid_cp = cps.start(resid_in, resid)
    x_cp = load_images(cps, x_in, xin, places, count)
    w1_cp = load_split(cps, w1_in, w1, 2, places)
    hpad_cp = cps.start(hpad_in, hpad)
    gres_cp = cps.start(gres_in, gres)
    wait_all(vec_cp)
    vcols = jnp.transpose(vec[...])

    def col(j):
        return vcols[:, j : j + 1]

    wait_all(po_cp)
    mix_cp.wait()
    resid_cp.wait()
    po_t = jnp.transpose(po[...].astype(f32)).astype(bf16)
    for b in range(count):
        val = jnp.transpose(resid[b]) + nn(po_t, mix[b]) + col(OUTPUT_BIAS)
        split_store(block_own, block_send, b, val, 0, places)

    wait_all(x_cp)
    wait_all(w1_cp)
    hpad_cp.wait()
    gres_cp.wait()
    w1_cols = jnp.concatenate([w1[k] for k in range(9)], axis=1)
    zero = jnp.zeros((chans, 1), f32)
    gain_sum, shift_sum = zero, zero

    def groups(v):
        total = jnp.sum(v.reshape(GROUPS, width, 1), axis=1, keepdims=True) / size
        return jnp.broadcast_to(total, (GROUPS, width, 1)).reshape(chans, 1)

    for b in range(count):
        back = nt(w1_cols, jnp.concatenate(taps(hpad, b, -1, side, points), axis=1))
        x3 = xin[b].astype(f32).reshape(GROUPS, width, points)
        mean = jnp.sum(jnp.sum(x3, axis=2, keepdims=True), axis=1, keepdims=True) / size
        off = x3 - mean
        var = jnp.sum(jnp.sum(off * off, axis=2, keepdims=True), axis=1, keepdims=True) / size
        rstd = lax.rsqrt(var + EPS)
        hat = (off * rstd).reshape(chans, points)
        rstd = jnp.broadcast_to(rstd, (GROUPS, width, 1)).reshape(chans, 1)
        pre = hat * col(FIRST_GAIN) + col(FIRST_SHIFT)
        val = back * silu_slope(pre, sigmoid(pre))
        gain = jnp.sum(val * hat, axis=1, keepdims=True)
        shift_g = jnp.sum(val, axis=1, keepdims=True)
        gain_sum = gain_sum + gain
        shift_sum = shift_sum + shift_g
        first_mean = groups(shift_g * col(FIRST_GAIN))
        second_mean = groups(gain * col(FIRST_GAIN))
        val = rstd * (val * col(FIRST_GAIN) - first_mean - hat * second_mean)
        val = val + jnp.transpose(gres[b])
        split_store(image_own, image_send, b, val, 0, places)
    lane = lax.broadcasted_iota(jnp.int32, (chans, 128), 1)
    both = jnp.where(lane == 0, gain_sum, 0.0) + jnp.where(lane == 1, shift_sum, 0.0)
    vec_out[...] = jnp.transpose(both)[0:8]


def swap(value, axis, size, bit):
    return lax.ppermute(value, axis, [(i, i ^ bit) for i in range(size)])


def phases_of(size):
    bits = size.bit_length() - 1
    out = []
    low = 0
    while low < bits:
        out.append((low, min(2, bits - low)))
        low += 2
    return out


def scatter_sum(total, batch):
    me = lax.axis_index("batch")
    for low, bits in phases_of(batch):
        m = 1 << bits
        mine = (me >> low) & (m - 1)
        parts = total.reshape(m, total.shape[0] // m, total.shape[1])
        got = [
            swap(
                lax.dynamic_index_in_dim(parts, mine ^ j, 0, False).astype(bf16),
                "batch",
                batch,
                j << low,
            )
            for j in range(1, m)
        ]
        total = lax.dynamic_index_in_dim(parts, mine, 0, False).astype(f32)
        for g in got:
            total = total + g.astype(f32)
    return total


def gather_all(piece, extra, batch):
    me = lax.axis_index("batch")
    rows = piece.shape[0]
    for low, bits in reversed(phases_of(batch)):
        m = 1 << bits
        mine = (me >> low) & (m - 1)
        both = jnp.concatenate([piece, extra], axis=0)
        all_of = [both] + [swap(both, "batch", batch, j << low) for j in range(1, m)]
        extra = jnp.concatenate([a[rows:] for a in all_of], axis=0)
        parts = jnp.stack([a[:rows] for a in all_of], axis=0)
        for i in range(bits):
            shape = parts.shape
            split = parts.reshape((1 << (bits - 1 - i), 2, 1 << i) + shape[1:])
            turned = jnp.flip(split, axis=1)
            parts = jnp.where(((mine >> i) & 1) == 1, turned, split).reshape(shape)
        piece = parts.reshape(m * rows, piece.shape[1])
        rows = piece.shape[0]
    return piece, extra


def pack(arrays, unit):
    flat = jnp.concatenate([a.reshape(-1, 128) for a in arrays], axis=0)
    pad = -flat.shape[0] % unit
    return jnp.pad(flat, ((0, pad), (0, 0)))


def unpack(flat, shapes):
    out = []
    at = 0
    for shape in shapes:
        n = math.prod(shape) // 128
        out.append(flat[at : at + n].reshape(shape).astype(f32))
        at += n
    return out


def per_device(
    batch,
    tensor,
    images,
    timesteps,
    embed_table,
    first_gain,
    first_shift,
    first_conv,
    first_bias,
    time_weight,
    time_bias,
    second_gain,
    second_shift,
    second_conv,
    second_bias,
    third_gain,
    third_shift,
    project_in,
    query_bias,
    value_bias,
    project_out,
    output_bias,
    cotangent,
):
    per_batch, local, points = images.shape
    chans = local * tensor
    count = per_batch // tensor
    steps, embed = embed_table.shape
    pieces = 2 if tensor == 2 else 1
    me = lax.axis_index("tensor")
    vec = jnp.stack(
        [
            first_gain,
            first_shift,
            first_bias,
            time_bias,
            second_gain,
            second_shift,
            second_bias,
            third_gain,
            third_shift,
            query_bias,
            value_bias,
            output_bias,
        ]
        + [output_bias] * 4,
        axis=0,
    )

    def other_half(array):
        parts = array.reshape((2, count) + array.shape[1:])
        return lax.dynamic_index_in_dim(parts, 1 - me, 0, False)

    def images_of(array):
        if pieces == 2:
            return [array, swap(other_half(array), "tensor", 2, 1)]
        return [lax.all_to_all(array, "tensor", 0, 1, tiled=True)]

    def whole(array, axis):
        if pieces == 2:
            return [array, swap(array, "tensor", 2, 1)]
        return [lax.all_gather(array, "tensor", axis=axis, tiled=True)]

    x_in = images_of(images)
    vec_in = whole(vec, 1)
    tw_in = whole(time_weight, 1)
    w1_in = whole(first_conv, 2)
    w2_in = whole(second_conv, 1)
    pi_in = whole(project_in, 2)
    po_in = whole(project_out, 0)
    g_in = images_of(cotangent)
    my_steps = timesteps if pieces == 2 else lax.dynamic_slice_in_dim(timesteps, me * count, count)

    side = side_of(points)
    image_b = (count, chans, points)
    image_p = (count, points, chans)
    pads = (3, count, points + 2 * side, chans)

    def shape(s, d):
        return jax.ShapeDtypeStruct(s, d)

    def grads(full, axis):
        if pieces == 1:
            return [shape(full, f32)]
        half = full[:axis] + (full[axis] // 2,) + full[axis + 1 :]
        return [shape(half, bf16), shape(half, bf16)]

    dw2_t, dpo_t = grads((9, chans, chans), 1), grads((chans, chans), 0)
    dpi_t, dw1_t = grads((3, chans, chans), 2), grads((9, chans, chans), 2)
    params = pltpu.CompilerParams(vmem_limit_bytes=VMEM_LIMIT)
    n_grad = 3 * pieces
    front = pl.pallas_call(
        functools.partial(front_kernel, pieces, count),
        out_shape=[g[0] for g in (dw2_t, dpo_t, dpi_t)]
        + ([g[1] for g in (dw2_t, dpo_t, dpi_t)] if pieces == 2 else [])
        + [
            shape((8, chans), f32),
            shape((2, count, chans), f32),
            shape(pads, bf16),
            shape(image_p, f32),
            shape(image_b, bf16),
            shape(image_p, f32),
            shape(image_p, f32),
            shape(image_b, bf16),
        ],
        in_specs=[ANY] * (8 * pieces) + [SMEM, ANY],
        out_specs=[VMEM] * (n_grad + 2) + [ANY] * 6,
        scratch_shapes=[
            pltpu.VMEM(image_b, bf16),
            pltpu.VMEM(image_b, bf16),
            pltpu.VMEM((9, chans, chans), bf16),
            pltpu.VMEM((9, chans, chans), bf16),
            pltpu.VMEM((3, chans, chans), bf16),
            pltpu.VMEM((chans, chans), bf16),
            pltpu.VMEM((embed, chans), bf16),
            pltpu.VMEM((16, chans), f32),
            pltpu.VMEM((count, 16, embed), bf16),
            pltpu.VMEM((3 * points, points), bf16),
            pltpu.VMEM(pads, bf16),
            pltpu.VMEM(pads, bf16),
            pltpu.VMEM(image_p, f32),
            pltpu.VMEM(image_b, bf16),
            pltpu.VMEM(image_p, f32),
            pltpu.VMEM(image_p, f32),
            pltpu.VMEM(image_b, bf16),
            pltpu.VMEM(image_b, bf16),
            pltpu.VMEM(image_b, bf16),
            pltpu.VMEM((count, points, 3 * chans), bf16),
            pltpu.SemaphoreType.DMA((8 * pieces + count + 6,)),
        ],
        compiler_params=params,
        name="front",
    )(*x_in, *g_in, *w1_in, *w2_in, *pi_in, *po_in, *tw_in, *vec_in, my_steps, embed_table)
    g_front = front[:n_grad]
    vec_a, stat, gpad, sum_one, a1t, resid, gres, mix = front[n_grad:]

    middle = pl.pallas_call(
        functools.partial(middle_kernel, pieces, count),
        out_shape=dw1_t + [shape((8, chans), f32), shape((count, chans), f32), shape(pads, bf16)],
        in_specs=[ANY] * (2 * pieces + 3) + [VMEM],
        out_specs=[VMEM] * (pieces + 2) + [ANY],
        scratch_shapes=[
            pltpu.VMEM((9, chans, chans), bf16),
            pltpu.VMEM((16, chans), f32),
            pltpu.VMEM(pads, bf16),
            pltpu.VMEM(image_p, f32),
            pltpu.VMEM(image_b, bf16),
            pltpu.VMEM((3 * points, points), bf16),
            pltpu.VMEM(pads, bf16),
            pltpu.VMEM(image_p, f32),
            pltpu.SemaphoreType.DMA((2 * pieces + 4,)),
        ],
        compiler_params=params,
        name="middle",
    )(*w2_in, *vec_in, gpad, sum_one, a1t, stat)
    g_middle = middle[:pieces]
    vec_b, times, hpad = middle[pieces:]

    if pieces == 2:
        half = (count, chans // 2, points)
        out_t = [shape(half, f32)] * 2 + [shape(half, bf16)] * 2
    else:
        out_t = [shape(image_b, f32)] * 2
    last = pl.pallas_call(
        functools.partial(last_kernel, pieces, count),
        out_shape=out_t + [shape((8, chans), f32)],
        in_specs=[ANY] * (4 * pieces + 4),
        out_specs=[VMEM] * (2 * pieces + 1),
        scratch_shapes=[
            pltpu.VMEM(image_b, bf16),
            pltpu.VMEM((9, chans, chans), bf16),
            pltpu.VMEM((chans, chans), bf16),
            pltpu.VMEM((16, chans), f32),
            pltpu.VMEM(pads, bf16),
            pltpu.VMEM(image_p, f32),
            pltpu.VMEM(image_p, f32),
            pltpu.VMEM(image_b, bf16),
            pltpu.SemaphoreType.DMA((4 * pieces + 4,)),
        ],
        compiler_params=params,
        name="last",
    )(*x_in, *w1_in, *po_in, *vec_in, hpad, resid, gres, mix)
    block, image = last[0], last[1]
    vec_c = last[-1]

    def placed(own, send):
        if pieces == 2:
            got = swap(send, "tensor", 2, 1).astype(f32)
            low = jnp.where(me == 0, own, got)
            high = jnp.where(me == 0, got, own)
            return jnp.concatenate([low, high], axis=0)
        return lax.all_to_all(own, "tensor", 1, 0, tiled=True)

    block_out = placed(block, last[pieces])
    images_grad = placed(image, last[pieces + 1])

    unit = 16 * batch

    def over_tensor(own, send, axis):
        if pieces == 2:
            return own.astype(f32) + swap(send, "tensor", 2, 1).astype(f32)
        return lax.psum_scatter(own, "tensor", scatter_dimension=axis, tiled=True)

    dw2 = over_tensor(g_front[0], g_front[-3], 1)
    dpo = over_tensor(g_front[1], g_front[-2], 0)
    dpi = over_tensor(g_front[2], g_front[-1], 2)
    dw1 = over_tensor(g_middle[0], g_middle[-1], 2)
    shapes_a = [dw2.shape, dpo.shape, dpi.shape]
    piece_a = scatter_sum(pack([dw2, dpo, dpi], unit), batch)
    piece_b = scatter_sum(pack([dw1], unit), batch)

    vecs = jnp.concatenate([vec_a, vec_b, vec_c], axis=0)
    if pieces == 2:
        vecs = vecs + swap(vecs, "tensor", 2, 1)
        theirs = swap(times, "tensor", 2, 1)
        times = jnp.concatenate(
            [jnp.where(me == 0, times, theirs), jnp.where(me == 0, theirs, times)], axis=0
        )
    else:
        vecs = lax.psum(vecs, "tensor")
        times = lax.all_gather(times, "tensor", axis=0, tiled=True)
    stamp = jnp.zeros((8, chans), f32)
    stamp = stamp.at[:per_batch, 0].set((timesteps >> 5).astype(f32))
    stamp = stamp.at[:per_batch, 1].set((timesteps & 31).astype(f32))
    small = jnp.concatenate([vecs, times, stamp], axis=0)
    n_small = small.shape[0]
    small = small.reshape(-1, 128).astype(bf16)
    done_a, _ = gather_all(piece_a.astype(bf16), small[:0], batch)
    done_b, small = gather_all(piece_b.astype(bf16), small, batch)
    second_conv_grad, project_out_grad, project_in_grad = unpack(done_a, shapes_a)
    (first_conv_grad,) = unpack(done_b, [dw1.shape])

    small = small.reshape(batch, n_small, chans)
    sums = jnp.sum(small[:, :24].astype(f32), axis=0)
    mine = lax.dynamic_slice_in_dim(sums, me * local, local, axis=1)
    all_times = small[:, 24 : 24 + per_batch].reshape(batch * per_batch, chans)
    stamps = small[:, 24 + per_batch :].astype(jnp.int32)[:, :per_batch]
    all_steps = (stamps[:, :, 0] * 32 + stamps[:, :, 1]).reshape(batch * per_batch)
    one_hot = (all_steps[:, None] == jnp.arange(steps, dtype=jnp.int32)[None, :]).astype(bf16)
    emb = nn(one_hot, embed_table)
    sig = sigmoid(emb)
    act = (emb * sig).astype(bf16)
    my_times = lax.dynamic_slice_in_dim(all_times, me * local, local, axis=1)
    time_weight_grad = lax.dot_general(
        act, my_times, (((0,), (0,)), ((), ())), preferred_element_type=f32
    )
    if pieces == 2:
        tw = jnp.where(
            me == 0, jnp.concatenate(tw_in, axis=1), jnp.concatenate(tw_in[::-1], axis=1)
        )
    else:
        tw = tw_in[0]
    grad_emb = (nt(all_times, tw) * silu_slope(emb, sig)).astype(bf16)
    table_grad = lax.dot_general(
        one_hot, grad_emb, (((0,), (0,)), ((), ())), preferred_element_type=f32
    )
    return (
        block_out,
        images_grad,
        table_grad,
        mine[16],
        mine[17],
        first_conv_grad,
        mine[10],
        time_weight_grad,
        mine[10],
        mine[8],
        mine[9],
        second_conv_grad,
        mine[0],
        mine[1],
        mine[2],
        project_in_grad,
        mine[3],
        mine[4],
        project_out_grad,
        mine[5],
    )


def solution(mesh):
    in_specs = (
        P("batch", "tensor", None),
        P("batch"),
        P(),
        P("tensor"),
        P("tensor"),
        P(None, None, "tensor"),
        P("tensor"),
        P(None, "tensor"),
        P("tensor"),
        P("tensor"),
        P("tensor"),
        P(None, "tensor", None),
        P("tensor"),
        P("tensor"),
        P("tensor"),
        P(None, None, "tensor"),
        P("tensor"),
        P("tensor"),
        P("tensor", None),
        P("tensor"),
        P("batch", "tensor", None),
    )
    out_specs = (
        P("batch", "tensor", None),
        P("batch", "tensor", None),
        P(),
        P("tensor"),
        P("tensor"),
        P(None, None, "tensor"),
        P("tensor"),
        P(None, "tensor"),
        P("tensor"),
        P("tensor"),
        P("tensor"),
        P(None, "tensor", None),
        P("tensor"),
        P("tensor"),
        P("tensor"),
        P(None, None, "tensor"),
        P("tensor"),
        P("tensor"),
        P("tensor", None),
        P("tensor"),
    )
    sizes = dict(mesh.shape)
    return jax.shard_map(
        functools.partial(per_device, sizes["batch"], sizes["tensor"]),
        mesh=mesh,
        in_specs=in_specs,
        out_specs=out_specs,
        check_vma=False,
    )
```

time: 525 us -> 127 us (0.24); the launches traced: 517 us -> 126 us
  waiting for transfers between devices: 331 us -> 24.6 us
  matrix products: 54.5 us -> 3.25 us
  blocking collectives: 43.3 us -> 0 us
  starting transfers between devices: 1.09 us -> 37.9 us
  local copies, waits for them, and re-layouts: 46.7 us -> 12.6 us
  Pallas kernels: 0 us -> 32 us
  between operations: 15.5 us -> 1.33 us
  other arithmetic: 24.2 us -> 14.5 us
    psum x3 -> x0, waiting for transfers between devices: 265 us -> none  [the longest x1 156 us: per_device(): lax.psum((first_gain_grad, first_shift_grad, first_conv_grad, first_bias_...]
    dot_general x23 -> x3, matrix products: 54.5 us -> 3.25 us  [the longest x1 1.97 us: per_device(): lax.dot_general(one_hot, grad_emb, (((0,), (0,)), ((), ())), preferred_el...]
    psum x1 -> x0, blocking collectives: 43.3 us -> none  [per_device(): lax.psum((first_gain_grad, first_shift_grad, first_conv_grad, first_bias_...]
    all_gather x4 -> x0, waiting for transfers between devices: 39.4 us -> none  [the longest x1 10.7 us: front_part(): act_full = lax.all_gather(act_one, 'tensor', axis=1, tiled=True)]
    ppermute x0 -> x40, starting transfers between devices: none -> 37.9 us  [swap(): return lax.ppermute(value, axis, [(i, i ^ bit) for i in range(size)])]
    pallas_call x0 -> x3, Pallas kernels: none -> 32 us  [the longest x1 17.3 us: per_device(): pl.pallas_call(functools.partial(front_kernel, pieces, count), out_shape=...]
    reduce_scatter x4 -> x0, waiting for transfers between devices: 27.1 us -> none  [the longest x1 10.8 us: per_device(): lax.psum_scatter(proj_partial, 'tensor', scatter_dimension=1, tiled=True)]
    unnamed x180 -> x61, local copies, waits for them, and re-layouts: 28.6 us -> 2.83 us
  transfers between devices with their start and end apart: 11 -> 40, of which waited for: 10 -> 14; matrix products, arithmetic and copies ran while one was open for 8% -> 18% of each run, Pallas kernels for 0% -> 0%
where the time goes in v1:
time: 127 us; the launch traced here: 126 us
  starting transfers between devices  37.9 us (30%)
  Pallas kernels  32 us (25%)
  waiting for transfers between devices  24.6 us (19%)
  other arithmetic  14.5 us (11%)
  local copies, waits for them, and re-layouts  12.6 us (10%)
  matrix products  3.25 us (3%)
  between operations  1.33 us (1%)
    ppermute x40, starting transfers between devices, swap(): return lax.ppermute(value, axis, [(i, i ^ bit) for i in range(size)])  37.9 us
    ppermute x40, waiting for transfers between devices, swap(): return lax.ppermute(value, axis, [(i, i ^ bit) for i in range(size)])  24.6 us
    pallas_call x1, Pallas kernels, per_device(): pl.pallas_call(functools.partial(front_kernel, pieces, count), out_shape=...  17.3 us
    pallas_call x1, Pallas kernels, per_device(): pl.pallas_call(functools.partial(middle_kernel, pieces, count), out_shape...  8.42 us
    pallas_call x1, Pallas kernels, per_device(): pl.pallas_call(functools.partial(last_kernel, pieces, count), out_shape=o...  6.28 us
    another operation x5, other arithmetic  3.24 us
    unnamed x61, local copies, waits for them, and re-layouts  2.83 us
  transfers between devices with their start and end apart: 40, of which 14 were waited for; matrix products, arithmetic and copies ran while one was open for 18% of the time, Pallas kernels for 0%

profile of v1, /device:TPU:0, one launch (start us, length us, event | category | flops | bytes accessed | tf_op | source)
XLA Modules:
  0.0 126.2 jit_solution(16179385567251472760)
XLA Ops:
  1.7 1.6 %stack.109.refs_14_.refs_2_.refs_6_ = f32[16,128]{1,0:T(8,128)S(1)} concatenate(f32[1,128]{1,0:T(1,128)} %bitcast.185, f32[1,128]{1,0:T(1,128)} %bitcast.186, f32[1,128]{1,0:T(1,128)} %bitcast.187, f32[1,128]{1,0:T(1,128)} %bitcast.188, f32[1,128]{1,0:T(1,128)} %bitcast.189, f32[1,128]{1,0:T(1,128)} %bitcast.190, f32[1,128]{1,0:T(1,128)} %bitcast.191, f32[1,128]{1,0:T(1,128)} %bitcast.192, ...), dimensions={0} | concatenate | bytes 16384 | tf_op jit(solution)/shard_map/stack | solution.py:623
  3.9 1.0 dynamic-slice_bitcast_fusion.1
  4.9 1.0 dynamic-slice_bitcast_fusion
  7.8 2.0 %fusion.55 = (bf16[8,1]{0,1:T(2,128)(2,1)S(1)}, bf16[8,1]{0,1:T(2,128)(2,1)S(1)}) fusion(pred[]{:T(512)} %compare_reduce_fusion, s32[8]{0:T(128)} %refs_16_.1, pred[]{:T(512)} %compare_reduce_fusion.1), kind=kLoop, calls=%fused_computation.133 | loop fusion | flops 48 | bytes 66 | tf_op jit(solution)/shard_map/reshape.99
  11.2 0.8 copy-done.2
  12.0 17.3 %front.1 = (bf16[9,128,256]{2,1,0:T(8,128)(2,1)}, bf16[128,256]{1,0:T(8,128)(2,1)}, bf16[3,256,128]{2,1,0:T(8,128)(2,1)}, bf16[9,128,256]{2,1,0:T(8,128)(2,1)}, ...) custom-call(bf16[8,128,256]{2,1,0:T(8,128)(2,1)} %refs_0_.5, ...), custom_call_target="tpu_custom_call" | custom-call | tf_op jit(solution)/shard_map/front/pallas_call | solution.py:684
  29.3 8.4 %middle.1 = (bf16[9,256,128]{2,1,0:T(8,128)(2,1)}, bf16[9,256,128]{2,1,0:T(8,128)(2,1)}, f32[8,256]{1,0:T(8,128)}, f32[4,256]{1,0:T(4,128)}, bf16[3,4,288,256]{3,2,1,0:T(8,128)(2,1)}) custom-call(bf16[9,128,256]{2,1,0:T(8,128)(2,1)} %refs_0_.4, bf16[9,128,256]{2,1,0:T(8,128)(2,1)} %copy-done.2, f32[16,128]{1,0:T(8,128)} %copy-done.16, f32[16,128]{1,0:T(8,128)} %copy-done.17, ...), custom_call_target="tpu_custom_call" | custom-call | tf_op jit(solution)/shard_map/middle/pallas_call | solution.py:729
  37.8 6.3 %last.1 = (f32[4,128,256]{2,1,0:T(8,128)}, f32[4,128,256]{2,1,0:T(8,128)}, bf16[4,128,256]{2,1,0:T(8,128)(2,1)}, bf16[4,128,256]{2,1,0:T(8,128)(2,1)}, f32[8,256]{1,0:T(8,128)}) custom-call(bf16[8,128,256]{2,1,0:T(8,128)(2,1)} %refs_0_.5, bf16[4,128,256]{2,1,0:T(8,128)(2,1)} %copy-done.3, bf16[9,256,128]{2,1,0:T(8,128)(2,1)} %refs_2_.3, ...), custom_call_target="tpu_custom_call" | custom-call | tf_op jit(solution)/shard_map/last/pallas_call | solution.py:756
  45.1 0.7 constant_dynamic-update-slice_fusion
  48.7 0.7 reshape.189
  49.4 0.8 convert_add_fusion.2
  50.7 1.1 pad_maximum_fusion.1
  51.8 1.1 pad_maximum_fusion.2
  53.1 0.8 fusion.32
  53.9 3.6 %collective-permute-start.15 = (bf16[576,128]{1,0:T(8,128)(2,1)}, bf16[576,128]{1,0:T(8,128)(2,1)}, u32[]{:S(2)}, u32[]{:S(2)}) collective-permute-start(bf16[576,128]{1,0:T(8,128)(2,1)} %get-tuple-element.96), channel_id=1, source_target_pairs={{0,6},{2,4},{4,2},{6,0},{8,14},{10,12},{12,10},{14,8},{16,22},{18,... | collective-permute-start | bytes 442376 | tf_op jit(solution)/shard_map/ppermute | solution.py:522
  58.1 1.2 convert_add_fusion
  59.4 1.1 pad_maximum_fusion
  60.5 2.0 %collective-permute-done.15 = bf16[576,128]{1,0:T(8,128)(2,1)} collective-permute-done((bf16[576,128]{1,0:T(8,128)(2,1)}, bf16[576,128]{1,0:T(8,128)(2,1)}, u32[]{:S(2)}, u32[]{:S(2)}) %collective-permute-start.15) | collective-permute-done | bytes 147488 | tf_op jit(solution)/shard_map/ppermute | solution.py:522
  62.5 2.8 %collective-permute-done.14 = bf16[576,128]{1,0:T(8,128)(2,1)} collective-permute-done((bf16[576,128]{1,0:T(8,128)(2,1)}, bf16[576,128]{1,0:T(8,128)(2,1)}, u32[]{:S(2)}, u32[]{:S(2)}) %collective-permute-start.14) | collective-permute-done | bytes 147488 | tf_op jit(solution)/shard_map/ppermute | solution.py:522
  65.6 1.1 fusion.8
  66.8 3.6 %collective-permute-start.18 = (bf16[144,128]{1,0:T(8,128)(2,1)S(1)}, bf16[144,128]{1,0:T(8,128)(2,1)S(1)}, u32[]{:S(2)}, u32[]{:S(2)}) collective-permute-start(bf16[144,128]{1,0:T(8,128)(2,1)S(1)} %get-tuple-element.108), channel_id=1, source_target_pairs={{0,24},{2,26},{4,28},{6,30},{8,16},{10,18},{12,20},{14,22},{16,8},... | collective-permute-start | bytes 110600 | tf_op jit(solution)/shard_map/ppermute | solution.py:522
  70.4 0.8 collective-permute-start.16
  71.3 1.5 %collective-permute-start.30 = (bf16[832,128]{1,0:T(8,128)(2,1)S(1)}, bf16[832,128]{1,0:T(8,128)(2,1)S(1)}, u32[]{:S(2)}, u32[]{:S(2)}) collective-permute-start(bf16[832,128]{1,0:T(8,128)(2,1)S(1)} %get-tuple-element.93), channel_id=1, source_target_pairs={{0,6},{2,4},{4,2},{6,0},{8,14},{10,12},{12,10},{14,8},{16,22},{18,... | collective-permute-start | bytes 638984 | tf_op jit(solution)/shard_map/ppermute | solution.py:522
  72.8 1.5 %collective-permute-start.29 = (bf16[832,128]{1,0:T(8,128)(2,1)S(1)}, bf16[832,128]{1,0:T(8,128)(2,1)S(1)}, u32[]{:S(2)}, u32[]{:S(2)}) collective-permute-start(bf16[832,128]{1,0:T(8,128)(2,1)S(1)} %get-tuple-element.94), channel_id=1, source_target_pairs={{0,4},{2,6},{4,0},{6,2},{8,12},{10,14},{12,8},{14,10},{16,20},{18,... | collective-permute-start | bytes 638984 | tf_op jit(solution)/shard_map/ppermute | solution.py:522
  75.3 3.2 %collective-permute-start.21 = (bf16[224,128]{1,0:T(8,128)(2,1)S(1)}, bf16[224,128]{1,0:T(8,128)(2,1)S(1)}, u32[]{:S(2)}, u32[]{:S(2)}) collective-permute-start(bf16[224,128]{1,0:T(8,128)(2,1)S(1)} %pad_maximum_fusion.7), channel_id=1, source_target_pairs={{0,24},{2,26},{4,28},{6,30},{8,16},{10,18},{12,20},{14,22},{16,8},... | collective-permute-start | bytes 172040 | tf_op jit(solution)/shard_map/ppermute | solution.py:522
  78.5 1.9 %collective-permute-done.30 = bf16[832,128]{1,0:T(8,128)(2,1)S(1)} collective-permute-done((bf16[832,128]{1,0:T(8,128)(2,1)S(1)}, bf16[832,128]{1,0:T(8,128)(2,1)S(1)}, u32[]{:S(2)}, u32[]{:S(2)}) %collective-permute-start.30) | collective-permute-done | bytes 213024 | tf_op jit(solution)/shard_map/ppermute | solution.py:522
  80.5 1.2 collective-permute-start.19
  81.7 1.5 %collective-permute-done.29 = bf16[832,128]{1,0:T(8,128)(2,1)S(1)} collective-permute-done((bf16[832,128]{1,0:T(8,128)(2,1)S(1)}, bf16[832,128]{1,0:T(8,128)(2,1)S(1)}, u32[]{:S(2)}, u32[]{:S(2)}) %collective-permute-start.29) | collective-permute-done | bytes 213024 | tf_op jit(solution)/shard_map/ppermute | solution.py:522
  83.4 3.5 %collective-permute-start.33 = (bf16[208,128]{1,0:T(8,128)(2,1)S(1)}, bf16[208,128]{1,0:T(8,128)(2,1)S(1)}, u32[]{:S(2)}, u32[]{:S(2)}) collective-permute-start(bf16[208,128]{1,0:T(8,128)(2,1)S(1)} %get-tuple-element.103), channel_id=1, source_target_pairs={{0,24},{2,26},{4,28},{6,30},{8,16},{10,18},{12,20},{14,22},{16,8},... | collective-permute-start | bytes 159752 | tf_op jit(solution)/shard_map/ppermute | solution.py:522
  86.9 0.9 collective-permute-start.31
  88.1 1.9 %collective-permute-done.33 = bf16[208,128]{1,0:T(8,128)(2,1)S(1)} collective-permute-done((bf16[208,128]{1,0:T(8,128)(2,1)S(1)}, bf16[208,128]{1,0:T(8,128)(2,1)S(1)}, u32[]{:S(2)}, u32[]{:S(2)}) %collective-permute-start.33) | collective-permute-done | bytes 53280 | tf_op jit(solution)/shard_map/ppermute | solution.py:522
  90.0 2.1 %collective-permute-done.32 = bf16[208,128]{1,0:T(8,128)(2,1)S(1)} collective-permute-done((bf16[208,128]{1,0:T(8,128)(2,1)S(1)}, bf16[208,128]{1,0:T(8,128)(2,1)S(1)}, u32[]{:S(2)}, u32[]{:S(2)}) %collective-permute-start.32) | collective-permute-done | bytes 53280 | tf_op jit(solution)/shard_map/ppermute | solution.py:522
  92.1 2.2 %collective-permute-start.36 = (bf16[208,128]{1,0:T(8,128)(2,1)S(1)}, bf16[208,128]{1,0:T(8,128)(2,1)S(1)}, u32[]{:S(2)}, u32[]{:S(2)}) collective-permute-start(bf16[208,128]{1,0:T(8,128)(2,1)S(1)} %fusion.41), channel_id=1, source_target_pairs={{0,24},{2,26},{4,28},{6,30},{8,16},{10,18},{12,20},{14,22},{16,8},... | collective-permute-start | bytes 159752 | tf_op jit(solution)/shard_map/ppermute | solution.py:522
  94.5 2.1 %collective-permute-start.34 = (bf16[208,128]{1,0:T(8,128)(2,1)S(1)}, bf16[208,128]{1,0:T(8,128)(2,1)S(1)}, u32[]{:S(2)}, u32[]{:S(2)}) collective-permute-start(bf16[208,128]{1,0:T(8,128)(2,1)S(1)} %fusion.41), channel_id=1, source_target_pairs={{0,8},{2,10},{4,12},{6,14},{8,0},{10,2},{12,4},{14,6},{16,24},{18,... | collective-permute-start | bytes 159752 | tf_op jit(solution)/shard_map/ppermute | solution.py:522
  96.6 1.5 %collective-permute-start.22 = (bf16[896,128]{1,0:T(8,128)(2,1)S(1)}, bf16[896,128]{1,0:T(8,128)(2,1)S(1)}, u32[]{:S(2)}, u32[]{:S(2)}) collective-permute-start(bf16[896,128]{1,0:T(8,128)(2,1)S(1)} %get-tuple-element.110), channel_id=1, source_target_pairs={{0,2},{2,0},{4,6},{6,4},{8,10},{10,8},{12,14},{14,12},{16,18},{18,... | collective-permute-start | bytes 688136 | tf_op jit(solution)/shard_map/ppermute | solution.py:522
  98.5 1.5 %collective-permute-start.24 = (bf16[896,128]{1,0:T(8,128)(2,1)S(1)}, bf16[896,128]{1,0:T(8,128)(2,1)S(1)}, u32[]{:S(2)}, u32[]{:S(2)}) collective-permute-start(bf16[896,128]{1,0:T(8,128)(2,1)S(1)} %get-tuple-element.110), channel_id=1, source_target_pairs={{0,6},{2,4},{4,2},{6,0},{8,14},{10,12},{12,10},{14,8},{16,22},{18,... | collective-permute-start | bytes 688136 | tf_op jit(solution)/shard_map/ppermute | solution.py:522
  100.2 1.4 %collective-permute-start.39 = (bf16[832,128]{1,0:T(8,128)(2,1)S(1)}, bf16[832,128]{1,0:T(8,128)(2,1)S(1)}, u32[]{:S(2)}, u32[]{:S(2)}) collective-permute-start(bf16[832,128]{1,0:T(8,128)(2,1)S(1)} %bitcast.164), channel_id=1, source_target_pairs={{0,6},{2,4},{4,2},{6,0},{8,14},{10,12},{12,10},{14,8},{16,22},{18,... | collective-permute-start | bytes 638984 | tf_op jit(solution)/shard_map/ppermute | solution.py:522
  101.7 1.6 %collective-permute-start.38 = (bf16[832,128]{1,0:T(8,128)(2,1)S(1)}, bf16[832,128]{1,0:T(8,128)(2,1)S(1)}, u32[]{:S(2)}, u32[]{:S(2)}) collective-permute-start(bf16[832,128]{1,0:T(8,128)(2,1)S(1)} %bitcast.165), channel_id=1, source_target_pairs={{0,4},{2,6},{4,0},{6,2},{8,12},{10,14},{12,8},{14,10},{16,20},{18,... | collective-permute-start | bytes 638984 | tf_op jit(solution)/shard_map/ppermute | solution.py:522
  103.2 1.9 %collective-permute-done.22 = bf16[896,128]{1,0:T(8,128)(2,1)S(1)} collective-permute-done((bf16[896,128]{1,0:T(8,128)(2,1)S(1)}, bf16[896,128]{1,0:T(8,128)(2,1)S(1)}, u32[]{:S(2)}, u32[]{:S(2)}) %collective-permute-start.22) | collective-permute-done | bytes 229408 | tf_op jit(solution)/shard_map/ppermute | solution.py:522
  105.1 1.5 %collective-permute-start.37 = (bf16[832,128]{1,0:T(8,128)(2,1)S(1)}, bf16[832,128]{1,0:T(8,128)(2,1)}, u32[]{:S(2)}, u32[]{:S(2)}) collective-permute-start(bf16[832,128]{1,0:T(8,128)(2,1)S(1)} %bitcast.166), channel_id=1, source_target_pairs={{0,2},{2,0},{4,6},{6,4},{8,10},{10,8},{12,14},{14,12},{16,18},{18,... | collective-permute-start | bytes 638984 | tf_op jit(solution)/shard_map/ppermute | solution.py:522
  106.6 8.6 %collective-permute-done.23 = bf16[896,128]{1,0:T(8,128)(2,1)S(1)} collective-permute-done((bf16[896,128]{1,0:T(8,128)(2,1)S(1)}, bf16[896,128]{1,0:T(8,128)(2,1)S(1)}, u32[]{:S(2)}, u32[]{:S(2)}) %collective-permute-start.23) | collective-permute-done | bytes 229408 | tf_op jit(solution)/shard_map/ppermute | solution.py:522
  116.7 1.1 convert.20
  118.5 2.0 %fusion.1 = f32[1024,512]{1,0:T(8,128)} fusion(bf16[512,128]{1,0:T(8,128)(2,1)S(1)} %copy-done.8, bf16[512,128]{1,0:T(8,128)(2,1)S(1)} %copy-done.6, f32[128,512]{1,0:T(8,128)S(1)} %fusion.4, s32[128]{0:T(128)S(1)} %add.137, pred[]{:T(512)S(6)} %eq.16, bf16[16,40,256]{2,1,0:T(8,128)(2,1)S(1)} %reshape.185), kind=kOutput, calls=%fused_computation.7 | convolution fusion | flops 169672704 | bytes 2687489 | tf_op jit(solution)/shard_map/dot_general | solution.py:846
  120.4 0.9 fusion.35
  121.4 1.0 pad_maximum_fusion.3
  122.9 1.3 %reshape.196 = f32[9,128,256]{2,1,0:T(8,128)} reshape(f32[2304,128]{1,0:T(8,128)S(1)} %slice_convert_fusion) | data formatting | bytes 2359296 | tf_op jit(solution)/shard_map/convert_element_type | solution.py:587
  124.3 0.8 convert.21
  125.0 0.7 reshape.198
  (168 shorter events, 15.7 us)
Async XLA Ops:
  0.7 9.5 %collective-permute-start.1 = (bf16[9,256,128]{2,1,0:T(8,128)(2,1)}, bf16[9,256,128]{2,1,0:T(8,128)(2,1)S(1)}, u32[]{:S(2)}, u32[]{:S(2)}) collective-permute-start(bf16[9,256,128]{2,1,0:T(8,128)(2,1)} %refs_2_.3), channel_id=1, source_target_pairs={{0,1},{1,0},{2,3},{3,2},{4,5},{5,4},{6,7},{7,6},{8,9},{9,8},{10,11... | collective-permute-start | bytes 1769480 | tf_op jit(solution)/shard_map/ppermute | solution.py:522
  1.2 9.0 %collective-permute-start.4 = (bf16[9,128,256]{2,1,0:T(8,128)(2,1)}, bf16[9,128,256]{2,1,0:T(8,128)(2,1)S(1)}, u32[]{:S(2)}, u32[]{:S(2)}) collective-permute-start(bf16[9,128,256]{2,1,0:T(8,128)(2,1)} %refs_0_.4), channel_id=1, source_target_pairs={{0,1},{1,0},{2,3},{3,2},{4,5},{5,4},{6,7},{7,6},{8,9},{9,8},{10,11... | collective-permute-start | bytes 1769480 | tf_op jit(solution)/shard_map/ppermute | solution.py:522
  1.3 4.8 %collective-permute-start.2 = (bf16[128,256]{1,0:T(8,128)(2,1)}, bf16[128,256]{1,0:T(8,128)(2,1)S(1)}, u32[]{:S(2)}, u32[]{:S(2)}) collective-permute-start(bf16[128,256]{1,0:T(8,128)(2,1)} %refs_4_.3), channel_id=1, source_target_pairs={{0,1},{1,0},{2,3},{3,2},{4,5},{5,4},{6,7},{7,6},{8,9},{9,8},{10,11... | collective-permute-start | bytes 196616 | tf_op jit(solution)/shard_map/ppermute | solution.py:522
  3.3 2.5 %collective-permute-start.3 = (f32[16,128]{1,0:T(8,128)S(1)}, f32[16,128]{1,0:T(8,128)S(1)}, u32[]{:S(2)}, u32[]{:S(2)}) collective-permute-start(f32[16,128]{1,0:T(8,128)S(1)} %stack.109.refs_14_.refs_2_.refs_6_), channel_id=1, source_target_pairs={{0,1},{1,0},{2,3},{3,2},{4,5},{5,4},{6,7},{7,6},{8,9},{9,8},{10,11... | collective-permute-start | bytes 24584 | tf_op jit(solution)/shard_map/ppermute | solution.py:522
  3.5 4.3 %collective-permute-start.7 = (bf16[512,128]{1,0:T(8,128)(2,1)}, bf16[512,128]{1,0:T(8,128)(2,1)S(1)}, u32[]{:S(2)}, u32[]{:S(2)}) collective-permute-start(bf16[512,128]{1,0:T(8,128)(2,1)} %refs_12_.1), channel_id=1, source_target_pairs={{0,1},{1,0},{2,3},{3,2},{4,5},{5,4},{6,7},{7,6},{8,9},{9,8},{10,11... | collective-permute-start | bytes 393224 | tf_op jit(solution)/shard_map/ppermute | solution.py:522
  5.9 4.2 %collective-permute-start = (bf16[4,128,256]{2,1,0:T(8,128)(2,1)S(1)}, bf16[4,128,256]{2,1,0:T(8,128)(2,1)S(1)}, u32[]{:S(2)}, u32[]{:S(2)}) collective-permute-start(bf16[4,128,256]{2,1,0:T(8,128)(2,1)S(1)} %dynamic-slice_bitcast_fusion.1), channel_id=1, source_target_pairs={{0,1},{1,0},{2,3},{3,2},{4,5},{5,4},{6,7},{7,6},{8,9},{9,8},{10,11... | collective-permute-start | bytes 786440 | tf_op jit(solution)/shard_map/ppermute | solution.py:522
  6.0 4.1 %collective-permute-start.5 = (bf16[4,128,256]{2,1,0:T(8,128)(2,1)S(1)}, bf16[4,128,256]{2,1,0:T(8,128)(2,1)S(1)}, u32[]{:S(2)}, u32[]{:S(2)}) collective-permute-start(bf16[4,128,256]{2,1,0:T(8,128)(2,1)S(1)} %dynamic-slice_bitcast_fusion), channel_id=1, source_target_pairs={{0,1},{1,0},{2,3},{3,2},{4,5},{5,4},{6,7},{7,6},{8,9},{9,8},{10,11... | collective-permute-start | bytes 786440 | tf_op jit(solution)/shard_map/ppermute | solution.py:522
  7.7 2.3 %collective-permute-start.6 = (bf16[3,256,128]{2,1,0:T(8,128)(2,1)}, bf16[3,256,128]{2,1,0:T(8,128)(2,1)S(1)}, u32[]{:S(2)}, u32[]{:S(2)}) collective-permute-start(bf16[3,256,128]{2,1,0:T(8,128)(2,1)} %refs_8_.1), channel_id=1, source_target_pairs={{0,1},{1,0},{2,3},{3,2},{4,5},{5,4},{6,7},{7,6},{8,9},{9,8},{10,11... | collective-permute-start | bytes 589832 | tf_op jit(solution)/shard_map/ppermute | solution.py:522
  37.7 7.4 %copy-start.20 = (f32[8,256]{1,0:T(8,128)S(1)}, f32[8,256]{1,0:T(8,128)}, u32[]{:S(2)}) copy-start(f32[8,256]{1,0:T(8,128)} %get-tuple-element.80) | copy-start | bytes 24580
  37.8 8.6 %copy-start.24 = (bf16[3,256,128]{2,1,0:T(8,128)(2,1)S(1)}, bf16[3,256,128]{2,1,0:T(8,128)(2,1)}, u32[]{:S(2)}) copy-start(bf16[3,256,128]{2,1,0:T(8,128)(2,1)} %get-tuple-element.91) | copy-start | bytes 589828
  37.8 9.3 %copy-start.25 = (bf16[128,256]{1,0:T(8,128)(2,1)S(1)}, bf16[128,256]{1,0:T(8,128)(2,1)}, u32[]{:S(2)}) copy-start(bf16[128,256]{1,0:T(8,128)(2,1)} %get-tuple-element.89) | copy-start | bytes 196612
  37.8 10.6 %copy-start.23 = (bf16[9,128,256]{2,1,0:T(8,128)(2,1)S(1)}, bf16[9,128,256]{2,1,0:T(8,128)(2,1)}, u32[]{:S(2)}) copy-start(bf16[9,128,256]{2,1,0:T(8,128)(2,1)} %get-tuple-element.87) | copy-start | bytes 1769476
  37.8 10.9 %copy-start.18 = (bf16[128,256]{1,0:T(8,128)(2,1)S(1)}, bf16[128,256]{1,0:T(8,128)(2,1)}, u32[]{:S(2)}) copy-start(bf16[128,256]{1,0:T(8,128)(2,1)} %get-tuple-element.88) | copy-start | bytes 196612
  37.8 11.6 %copy-start.14 = (bf16[3,256,128]{2,1,0:T(8,128)(2,1)S(1)}, bf16[3,256,128]{2,1,0:T(8,128)(2,1)}, u32[]{:S(2)}) copy-start(bf16[3,256,128]{2,1,0:T(8,128)(2,1)} %get-tuple-element.90) | copy-start | bytes 589828
  44.1 6.1 %collective-permute-start.8 = (bf16[4,128,256]{2,1,0:T(8,128)(2,1)}, bf16[4,128,256]{2,1,0:T(8,128)(2,1)S(1)}, u32[]{:S(2)}, u32[]{:S(2)}) collective-permute-start(bf16[4,128,256]{2,1,0:T(8,128)(2,1)} %get-tuple-element.77), channel_id=1, source_target_pairs={{0,1},{1,0},{2,3},{3,2},{4,5},{5,4},{6,7},{7,6},{8,9},{9,8},{10,11... | collective-permute-start | bytes 786440 | tf_op jit(solution)/shard_map/ppermute | solution.py:522
  44.6 5.7 %collective-permute-start.9 = (bf16[4,128,256]{2,1,0:T(8,128)(2,1)}, bf16[4,128,256]{2,1,0:T(8,128)(2,1)S(1)}, u32[]{:S(2)}, u32[]{:S(2)}) collective-permute-start(bf16[4,128,256]{2,1,0:T(8,128)(2,1)} %get-tuple-element.79), channel_id=1, source_target_pairs={{0,1},{1,0},{2,3},{3,2},{4,5},{5,4},{6,7},{7,6},{8,9},{9,8},{10,11... | collective-permute-start | bytes 786440 | tf_op jit(solution)/shard_map/ppermute | solution.py:522
  44.7 1.6 %collective-permute-start.11 = (bf16[4,256]{1,0:T(4,128)(2,1)S(1)}, bf16[4,256]{1,0:T(4,128)(2,1)S(1)}, u32[]{:S(2)}, u32[]{:S(2)}) collective-permute-start(bf16[4,256]{1,0:T(4,128)(2,1)S(1)} %convert.25), channel_id=1, source_target_pairs={{0,1},{1,0},{2,3},{3,2},{4,5},{5,4},{6,7},{7,6},{8,9},{9,8},{10,11... | collective-permute-start | bytes 6152 | tf_op jit(solution)/shard_map/ppermute | solution.py:522
  45.8 1.2 collective-permute-start.10
  45.9 6.9 %collective-permute-start.12 = (bf16[9,256,128]{2,1,0:T(8,128)(2,1)}, bf16[9,256,128]{2,1,0:T(8,128)(2,1)S(1)}, u32[]{:S(2)}, u32[]{:S(2)}) collective-permute-start(bf16[9,256,128]{2,1,0:T(8,128)(2,1)} %get-tuple-element.85), channel_id=1, source_target_pairs={{0,1},{1,0},{2,3},{3,2},{4,5},{5,4},{6,7},{7,6},{8,9},{9,8},{10,11... | collective-permute-start | bytes 1769480 | tf_op jit(solution)/shard_map/ppermute | solution.py:522
  46.3 3.1 %collective-permute-start.27 = (bf16[3,256,128]{2,1,0:T(8,128)(2,1)S(1)}, bf16[3,256,128]{2,1,0:T(8,128)(2,1)S(1)}, u32[]{:S(2)}, u32[]{:S(2)}) collective-permute-start(bf16[3,256,128]{2,1,0:T(8,128)(2,1)S(1)} %copy-done.24), channel_id=1, source_target_pairs={{0,1},{1,0},{2,3},{3,2},{4,5},{5,4},{6,7},{7,6},{8,9},{9,8},{10,11... | collective-permute-start | bytes 589832 | tf_op jit(solution)/shard_map/ppermute | solution.py:522
  47.0 1.3 %collective-permute-start.26 = (bf16[128,256]{1,0:T(8,128)(2,1)S(1)}, bf16[128,256]{1,0:T(8,128)(2,1)S(1)}, u32[]{:S(2)}, u32[]{:S(2)}) collective-permute-start(bf16[128,256]{1,0:T(8,128)(2,1)S(1)} %copy-done.25), channel_id=1, source_target_pairs={{0,1},{1,0},{2,3},{3,2},{4,5},{5,4},{6,7},{7,6},{8,9},{9,8},{10,11... | collective-permute-start | bytes 196616 | tf_op jit(solution)/shard_map/ppermute | solution.py:522
  48.4 9.7 %collective-permute-start.25 = (bf16[9,128,256]{2,1,0:T(8,128)(2,1)S(1)}, bf16[9,128,256]{2,1,0:T(8,128)(2,1)}, u32[]{:S(2)}, u32[]{:S(2)}) collective-permute-start(bf16[9,128,256]{2,1,0:T(8,128)(2,1)S(1)} %copy-done.23), channel_id=1, source_target_pairs={{0,1},{1,0},{2,3},{3,2},{4,5},{5,4},{6,7},{7,6},{8,9},{9,8},{10,11... | collective-permute-start | bytes 1769480 | tf_op jit(solution)/shard_map/ppermute | solution.py:522
  53.9 8.6 %collective-permute-start.15 = (bf16[576,128]{1,0:T(8,128)(2,1)}, bf16[576,128]{1,0:T(8,128)(2,1)}, u32[]{:S(2)}, u32[]{:S(2)}) collective-permute-start(bf16[576,128]{1,0:T(8,128)(2,1)} %get-tuple-element.96), channel_id=1, source_target_pairs={{0,6},{2,4},{4,2},{6,0},{8,14},{10,12},{12,10},{14,8},{16,22},{18,... | collective-permute-start | bytes 442376 | tf_op jit(solution)/shard_map/ppermute | solution.py:522
  57.5 7.8 %collective-permute-start.14 = (bf16[576,128]{1,0:T(8,128)(2,1)}, bf16[576,128]{1,0:T(8,128)(2,1)}, u32[]{:S(2)}, u32[]{:S(2)}) collective-permute-start(bf16[576,128]{1,0:T(8,128)(2,1)} %get-tuple-element.97), channel_id=1, source_target_pairs={{0,4},{2,6},{4,0},{6,2},{8,12},{10,14},{12,8},{14,10},{16,20},{18,... | collective-permute-start | bytes 442376 | tf_op jit(solution)/shard_map/ppermute | solution.py:522
  58.0 7.6 %collective-permute-start.13 = (bf16[576,128]{1,0:T(8,128)(2,1)}, bf16[576,128]{1,0:T(8,128)(2,1)}, u32[]{:S(2)}, u32[]{:S(2)}) collective-permute-start(bf16[576,128]{1,0:T(8,128)(2,1)} %get-tuple-element.95), channel_id=1, source_target_pairs={{0,2},{2,0},{4,6},{6,4},{8,10},{10,8},{12,14},{14,12},{16,18},{18,... | collective-permute-start | bytes 442376 | tf_op jit(solution)/shard_map/ppermute | solution.py:522
  60.5 14.8 %copy-start.15 = (bf16[80,128]{1,0:T(8,128)(2,1)S(1)}, bf16[80,128]{1,0:T(8,128)(2,1)}, u32[]{:S(2)}) copy-start(bf16[80,128]{1,0:T(8,128)(2,1)} %convert_element_type.195) | copy-start | bytes 61444
  66.8 7.6 %collective-permute-start.18 = (bf16[144,128]{1,0:T(8,128)(2,1)S(1)}, bf16[144,128]{1,0:T(8,128)(2,1)S(1)}, u32[]{:S(2)}, u32[]{:S(2)}) collective-permute-start(bf16[144,128]{1,0:T(8,128)(2,1)S(1)} %get-tuple-element.108), channel_id=1, source_target_pairs={{0,24},{2,26},{4,28},{6,30},{8,16},{10,18},{12,20},{14,22},{16,8},... | collective-permute-start | bytes 110600 | tf_op jit(solution)/shard_map/ppermute | solution.py:522
  70.4 4.9 %collective-permute-start.17 = (bf16[144,128]{1,0:T(8,128)(2,1)S(1)}, bf16[144,128]{1,0:T(8,128)(2,1)S(1)}, u32[]{:S(2)}, u32[]{:S(2)}) collective-permute-start(bf16[144,128]{1,0:T(8,128)(2,1)S(1)} %get-tuple-element.109), channel_id=1, source_target_pairs={{0,16},{2,18},{4,20},{6,22},{8,24},{10,26},{12,28},{14,30},{16,0},... | collective-permute-start | bytes 110600 | tf_op jit(solution)/shard_map/ppermute | solution.py:522
  70.4 4.9 %collective-permute-start.16 = (bf16[144,128]{1,0:T(8,128)(2,1)S(1)}, bf16[144,128]{1,0:T(8,128)(2,1)S(1)}, u32[]{:S(2)}, u32[]{:S(2)}) collective-permute-start(bf16[144,128]{1,0:T(8,128)(2,1)S(1)} %get-tuple-element.107), channel_id=1, source_target_pairs={{0,8},{2,10},{4,12},{6,14},{8,0},{10,2},{12,4},{14,6},{16,24},{18,... | collective-permute-start | bytes 110600 | tf_op jit(solution)/shard_map/ppermute | solution.py:522
  71.3 9.2 %collective-permute-start.30 = (bf16[832,128]{1,0:T(8,128)(2,1)S(1)}, bf16[832,128]{1,0:T(8,128)(2,1)S(1)}, u32[]{:S(2)}, u32[]{:S(2)}) collective-permute-start(bf16[832,128]{1,0:T(8,128)(2,1)S(1)} %get-tuple-element.93), channel_id=1, source_target_pairs={{0,6},{2,4},{4,2},{6,0},{8,14},{10,12},{12,10},{14,8},{16,22},{18,... | collective-permute-start | bytes 638984 | tf_op jit(solution)/shard_map/ppermute | solution.py:522
  72.8 10.3 %collective-permute-start.29 = (bf16[832,128]{1,0:T(8,128)(2,1)S(1)}, bf16[832,128]{1,0:T(8,128)(2,1)S(1)}, u32[]{:S(2)}, u32[]{:S(2)}) collective-permute-start(bf16[832,128]{1,0:T(8,128)(2,1)S(1)} %get-tuple-element.94), channel_id=1, source_target_pairs={{0,4},{2,6},{4,0},{6,2},{8,12},{10,14},{12,8},{14,10},{16,20},{18,... | collective-permute-start | bytes 638984 | tf_op jit(solution)/shard_map/ppermute | solution.py:522
  74.3 8.9 %collective-permute-start.28 = (bf16[832,128]{1,0:T(8,128)(2,1)S(1)}, bf16[832,128]{1,0:T(8,128)(2,1)S(1)}, u32[]{:S(2)}, u32[]{:S(2)}) collective-permute-start(bf16[832,128]{1,0:T(8,128)(2,1)S(1)} %get-tuple-element.92), channel_id=1, source_target_pairs={{0,2},{2,0},{4,6},{6,4},{8,10},{10,8},{12,14},{14,12},{16,18},{18,... | collective-permute-start | bytes 638984 | tf_op jit(solution)/shard_map/ppermute | solution.py:522
  75.3 11.6 %collective-permute-start.21 = (bf16[224,128]{1,0:T(8,128)(2,1)S(1)}, bf16[224,128]{1,0:T(8,128)(2,1)S(1)}, u32[]{:S(2)}, u32[]{:S(2)}) collective-permute-start(bf16[224,128]{1,0:T(8,128)(2,1)S(1)} %pad_maximum_fusion.7), channel_id=1, source_target_pairs={{0,24},{2,26},{4,28},{6,30},{8,16},{10,18},{12,20},{14,22},{16,8},... | collective-permute-start | bytes 172040 | tf_op jit(solution)/shard_map/ppermute | solution.py:522
  78.5 9.3 %collective-permute-start.20 = (bf16[224,128]{1,0:T(8,128)(2,1)S(1)}, bf16[224,128]{1,0:T(8,128)(2,1)S(1)}, u32[]{:S(2)}, u32[]{:S(2)}) collective-permute-start(bf16[224,128]{1,0:T(8,128)(2,1)S(1)} %pad_maximum_fusion.7), channel_id=1, source_target_pairs={{0,16},{2,18},{4,20},{6,22},{8,24},{10,26},{12,28},{14,30},{16,0},... | collective-permute-start | bytes 172040 | tf_op jit(solution)/shard_map/ppermute | solution.py:522
  80.5 7.4 %collective-permute-start.19 = (bf16[224,128]{1,0:T(8,128)(2,1)S(1)}, bf16[224,128]{1,0:T(8,128)(2,1)S(1)}, u32[]{:S(2)}, u32[]{:S(2)}) collective-permute-start(bf16[224,128]{1,0:T(8,128)(2,1)S(1)} %pad_maximum_fusion.7), channel_id=1, source_target_pairs={{0,8},{2,10},{4,12},{6,14},{8,0},{10,2},{12,4},{14,6},{16,24},{18,... | collective-permute-start | bytes 172040 | tf_op jit(solution)/shard_map/ppermute | solution.py:522
  83.4 6.6 %collective-permute-start.33 = (bf16[208,128]{1,0:T(8,128)(2,1)S(1)}, bf16[208,128]{1,0:T(8,128)(2,1)S(1)}, u32[]{:S(2)}, u32[]{:S(2)}) collective-permute-start(bf16[208,128]{1,0:T(8,128)(2,1)S(1)} %get-tuple-element.103), channel_id=1, source_target_pairs={{0,24},{2,26},{4,28},{6,30},{8,16},{10,18},{12,20},{14,22},{16,8},... | collective-permute-start | bytes 159752 | tf_op jit(solution)/shard_map/ppermute | solution.py:522
  86.9 5.1 %collective-permute-start.32 = (bf16[208,128]{1,0:T(8,128)(2,1)S(1)}, bf16[208,128]{1,0:T(8,128)(2,1)S(1)}, u32[]{:S(2)}, u32[]{:S(2)}) collective-permute-start(bf16[208,128]{1,0:T(8,128)(2,1)S(1)} %get-tuple-element.104), channel_id=1, source_target_pairs={{0,16},{2,18},{4,20},{6,22},{8,24},{10,26},{12,28},{14,30},{16,0},... | collective-permute-start | bytes 159752 | tf_op jit(solution)/shard_map/ppermute | solution.py:522
  86.9 5.1 %collective-permute-start.31 = (bf16[208,128]{1,0:T(8,128)(2,1)S(1)}, bf16[208,128]{1,0:T(8,128)(2,1)S(1)}, u32[]{:S(2)}, u32[]{:S(2)}) collective-permute-start(bf16[208,128]{1,0:T(8,128)(2,1)S(1)} %get-tuple-element.102), channel_id=1, source_target_pairs={{0,8},{2,10},{4,12},{6,14},{8,0},{10,2},{12,4},{14,6},{16,24},{18,... | collective-permute-start | bytes 159752 | tf_op jit(solution)/shard_map/ppermute | solution.py:522
  92.1 6.4 %collective-permute-start.36 = (bf16[208,128]{1,0:T(8,128)(2,1)S(1)}, bf16[208,128]{1,0:T(8,128)(2,1)S(1)}, u32[]{:S(2)}, u32[]{:S(2)}) collective-permute-start(bf16[208,128]{1,0:T(8,128)(2,1)S(1)} %fusion.41), channel_id=1, source_target_pairs={{0,24},{2,26},{4,28},{6,30},{8,16},{10,18},{12,20},{14,22},{16,8},... | collective-permute-start | bytes 159752 | tf_op jit(solution)/shard_map/ppermute | solution.py:522
  94.3 5.7 %collective-permute-start.35 = (bf16[208,128]{1,0:T(8,128)(2,1)S(1)}, bf16[208,128]{1,0:T(8,128)(2,1)S(1)}, u32[]{:S(2)}, u32[]{:S(2)}) collective-permute-start(bf16[208,128]{1,0:T(8,128)(2,1)S(1)} %fusion.41), channel_id=1, source_target_pairs={{0,16},{2,18},{4,20},{6,22},{8,24},{10,26},{12,28},{14,30},{16,0},... | collective-permute-start | bytes 159752 | tf_op jit(solution)/shard_map/ppermute | solution.py:522
  94.5 5.6 %collective-permute-start.34 = (bf16[208,128]{1,0:T(8,128)(2,1)S(1)}, bf16[208,128]{1,0:T(8,128)(2,1)S(1)}, u32[]{:S(2)}, u32[]{:S(2)}) collective-permute-start(bf16[208,128]{1,0:T(8,128)(2,1)S(1)} %fusion.41), channel_id=1, source_target_pairs={{0,8},{2,10},{4,12},{6,14},{8,0},{10,2},{12,4},{14,6},{16,24},{18,... | collective-permute-start | bytes 159752 | tf_op jit(solution)/shard_map/ppermute | solution.py:522
  96.6 8.5 %collective-permute-start.22 = (bf16[896,128]{1,0:T(8,128)(2,1)S(1)}, bf16[896,128]{1,0:T(8,128)(2,1)S(1)}, u32[]{:S(2)}, u32[]{:S(2)}) collective-permute-start(bf16[896,128]{1,0:T(8,128)(2,1)S(1)} %get-tuple-element.110), channel_id=1, source_target_pairs={{0,2},{2,0},{4,6},{6,4},{8,10},{10,8},{12,14},{14,12},{16,18},{18,... | collective-permute-start | bytes 688136 | tf_op jit(solution)/shard_map/ppermute | solution.py:522
  98.0 17.2 %collective-permute-start.23 = (bf16[896,128]{1,0:T(8,128)(2,1)S(1)}, bf16[896,128]{1,0:T(8,128)(2,1)S(1)}, u32[]{:S(2)}, u32[]{:S(2)}) collective-permute-start(bf16[896,128]{1,0:T(8,128)(2,1)S(1)} %get-tuple-element.110), channel_id=1, source_target_pairs={{0,4},{2,6},{4,0},{6,2},{8,12},{10,14},{12,8},{14,10},{16,20},{18,... | collective-permute-start | bytes 688136 | tf_op jit(solution)/shard_map/ppermute | solution.py:522
  98.5 16.7 %collective-permute-start.24 = (bf16[896,128]{1,0:T(8,128)(2,1)S(1)}, bf16[896,128]{1,0:T(8,128)(2,1)S(1)}, u32[]{:S(2)}, u32[]{:S(2)}) collective-permute-start(bf16[896,128]{1,0:T(8,128)(2,1)S(1)} %get-tuple-element.110), channel_id=1, source_target_pairs={{0,6},{2,4},{4,2},{6,0},{8,14},{10,12},{12,10},{14,8},{16,22},{18,... | collective-permute-start | bytes 688136 | tf_op jit(solution)/shard_map/ppermute | solution.py:522
  100.2 15.8 %copy-start = (bf16[1024,512]{1,0:T(8,128)(2,1)S(1)}, bf16[1024,512]{1,0:T(8,128)(2,1)}, u32[]{:S(2)}) copy-start(bf16[1024,512]{1,0:T(8,128)(2,1)} %refs_17_.1) | copy-start | bytes 3145732
  100.2 21.1 %collective-permute-start.39 = (bf16[832,128]{1,0:T(8,128)(2,1)S(1)}, bf16[832,128]{1,0:T(8,128)(2,1)S(1)}, u32[]{:S(2)}, u32[]{:S(2)}) collective-permute-start(bf16[832,128]{1,0:T(8,128)(2,1)S(1)} %bitcast.164), channel_id=1, source_target_pairs={{0,6},{2,4},{4,2},{6,0},{8,14},{10,12},{12,10},{14,8},{16,22},{18,... | collective-permute-start | bytes 638984 | tf_op jit(solution)/shard_map/ppermute | solution.py:522
  101.7 19.7 %collective-permute-start.38 = (bf16[832,128]{1,0:T(8,128)(2,1)S(1)}, bf16[832,128]{1,0:T(8,128)(2,1)S(1)}, u32[]{:S(2)}, u32[]{:S(2)}) collective-permute-start(bf16[832,128]{1,0:T(8,128)(2,1)S(1)} %bitcast.165), channel_id=1, source_target_pairs={{0,4},{2,6},{4,0},{6,2},{8,12},{10,14},{12,8},{14,10},{16,20},{18,... | collective-permute-start | bytes 638984 | tf_op jit(solution)/shard_map/ppermute | solution.py:522
  105.1 16.3 %collective-permute-start.37 = (bf16[832,128]{1,0:T(8,128)(2,1)S(1)}, bf16[832,128]{1,0:T(8,128)(2,1)}, u32[]{:S(2)}, u32[]{:S(2)}) collective-permute-start(bf16[832,128]{1,0:T(8,128)(2,1)S(1)} %bitcast.166), channel_id=1, source_target_pairs={{0,2},{2,0},{4,6},{6,4},{8,10},{10,8},{12,14},{14,12},{16,18},{18,... | collective-permute-start | bytes 638984 | tf_op jit(solution)/shard_map/ppermute | solution.py:522
  (18 other events, 60.5 us)

commit v2 on v1

--- a/solution.py
+++ b/solution.py
@@ -9,6 +9,8 @@
 from jax.sharding import PartitionSpec as P
 
 GROUPS = 32
+LANES = 128
+BLOCK = 32
 EPS = 1e-06
 VMEM_LIMIT = 56 * 1024 * 1024
 ANY = pl.BlockSpec(memory_space=pl.ANY)
@@ -162,6 +164,22 @@
     send_ref[at] = jnp.where(first, high, low).astype(send_ref.dtype)
 
 
+def pack_store(own_ref, send_ref, at, value, axis, places):
+    half = value.shape[axis] // 2
+    low = lax.slice_in_dim(value, 0, half, axis=axis)
+    high = lax.slice_in_dim(value, half, 2 * half, axis=axis)
+    first = places[0] == 0
+    own = jnp.where(first, low, high).astype(own_ref.dtype)
+    send = jnp.where(first, high, low).astype(send_ref.dtype)
+    rows = own.shape[0]
+    for i in range(own.shape[1] // LANES):
+        lanes = slice(i * LANES, (i + 1) * LANES)
+        own_ref[at : at + rows, :] = own[:, lanes]
+        send_ref[at : at + rows, :] = send[:, lanes]
+        at += rows
+    return at
+
+
 def front_kernel(pieces, count, *refs):
     it = iter(refs)
 
@@ -170,8 +188,10 @@
 
     x_in, g_in, w1_in, w2_in, pi_in, po_in, tw_in, vec_in = (take(pieces) for _ in range(8))
     steps_ref, table_ref = take(2)
-    dw2_own, dpo_own, dpi_own = take(3)
-    dw2_send, dpo_send, dpi_send = take(3) if pieces == 2 else (None, None, None)
+    if pieces == 2:
+        own, send = take(2)
+    else:
+        dw2_own, dpo_own, dpi_own = take(3)
     vec_out, stat_out = take(2)
     gpad_out, sum_out, a1t_out, resid_out, gres_out, mix_out = take(6)
     xin, gin, w1, w2, pi, po, tw, vec, rows = take(9)
@@ -328,7 +348,11 @@
         gain3.append(col_sum(grad_n * hat))
         shift3.append(col_sum(grad_n))
     outs.append(cps.start(mix, mix_out))
-    split_store(dpo_own, dpo_send, ..., dpo, 0, places)
+    at = 0
+    if pieces == 2:
+        at = pack_store(own, send, at, dpo, 0, places)
+    else:
+        dpo_own[...] = dpo
     gain3 = jnp.concatenate(gain3, axis=0)
     shift3 = jnp.concatenate(shift3, axis=0)
     first_mean = lane_groups(shift3 * row(THIRD_GAIN), width) / size
@@ -352,12 +376,18 @@
     gl_all = jnp.concatenate([gl[b] for b in range(count)], axis=0)
     for j in range(3):
         val = nn(nm_all, gl_all[:, j * chans : (j + 1) * chans])
-        split_store(dpi_own, dpi_send, j, val, 1, places)
+        if pieces == 2:
+            at = pack_store(own, send, at, val, 1, places)
+        else:
+            dpi_own[j] = val
     a_all = jnp.concatenate([a2t[b] for b in range(count)], axis=1)
     moved = [taps(gpad, b, -1, side, points) for b in range(count)]
     for tap in range(9):
         val = nn(a_all, jnp.concatenate([moved[b][tap] for b in range(count)], axis=0))
-        split_store(dw2_own, dw2_send, tap, val, 0, places)
+        if pieces == 2:
+            at = pack_store(own, send, at, val, 0, places)
+        else:
+            dw2_own[tap] = val
 
     vec_out[...] = jnp.concatenate(
         [sb_grad, col_sum(gain3), col_sum(shift3), qb_grad, vb_grad, ob_grad, zero, zero], axis=0
@@ -372,15 +402,15 @@
         return [next(it) for _ in range(n)]
 
     w2_in, vec_in = (take(pieces) for _ in range(2))
-    gpad_in, sum_in, a1t_in, stat = take(4)
-    dw1_own = next(it)
-    dw1_send = next(it) if pieces == 2 else None
-    vec_out, time_out, hpad_out = take(3)
+    gpad_in, sum_in, a1t_in, stat, vec_a, steps_ref = take(6)
+    own = next(it)
+    send = next(it) if pieces == 2 else None
+    block_out, hpad_out = take(2)
     w2, vec, gpad, sum_one, a1t, shift, hpad, grad = take(8)
     sems = next(it)
     cps = Copies(sems)
     places = places_of(pieces)
-    chans, points = a1t.shape[1], a1t.shape[2]
+    points, chans = sum_one.shape[1], sum_one.shape[2]
     side = side_of(points)
     width = chans // GROUPS
     size = float(width * points)
@@ -424,19 +454,62 @@
         times.append(col_sum(val))
         put_pads(hpad, b, nn(shift[...], val.astype(bf16)).astype(bf16), side, points)
     out_cp = cps.start(hpad, hpad_out)
-    times = jnp.concatenate(times, axis=0)
-    time_out[0:count, :] = times
-    zero = jnp.zeros((1, chans), f32)
-    vec_out[...] = jnp.concatenate(
-        [col_sum(gain), col_sum(shift_g), col_sum(times)] + [zero] * 5, axis=0
-    )
+
+    rows = [vec_a[j : j + 1, :] for j in range(6)]
+    rows += [col_sum(gain), col_sum(shift_g), col_sum(jnp.concatenate(times, axis=0))]
+    lane = lax.broadcasted_iota(jnp.int32, (1, LANES), 1)
+    stamp = jnp.zeros((1, LANES), f32)
+    for b in range(count):
+        step = jnp.full((1, LANES), steps_ref[places[0] * count + b], jnp.int32)
+        stamp = jnp.where(lane == b, (step >> 5).astype(f32), stamp)
+        stamp = jnp.where(lane == LANES // 2 + b, (step & 31).astype(f32), stamp)
+    flat = []
+    for r in rows + times:
+        flat += [r[:, i * LANES : (i + 1) * LANES] for i in range(chans // LANES)]
+    flat.append(stamp)
+    flat += [jnp.zeros((1, LANES), f32)] * (BLOCK - len(flat))
+    block_out[...] = jnp.concatenate(flat, axis=0).astype(bf16)
+
     a1t_cp.wait()
     a_all = jnp.concatenate([a1t[b] for b in range(count)], axis=1)
     moved = [taps(hpad, b, -1, side, points) for b in range(count)]
+    at = 0
     for tap in range(9):
         val = nn(a_all, jnp.concatenate([moved[b][tap] for b in range(count)], axis=0))
-        split_store(dw1_own, dw1_send, tap, val, 1, places)
+        if pieces == 2:
+            at = pack_store(own, send, at, val, 1, places)
+        else:
+            own[tap] = val
     out_cp.wait()
+
+
+def block_kernel(pieces, count, *refs):
+    it = iter(refs)
+
+    def take(n):
+        return [next(it) for _ in range(n)]
+
+    po_in, vec_in = (take(pieces) for _ in range(2))
+    resid_in, mix_in = take(2)
+    own = next(it)
+    send = next(it) if pieces == 2 else None
+    po, vec, resid, mix = take(4)
+    sems = next(it)
+    cps = Copies(sems)
+    places = places_of(pieces)
+    vec_cp = load_split(cps, vec_in, vec, 1, places)
+    po_cp = load_split(cps, po_in, po, 0, places)
+    mix_cp = cps.start(mix_in, mix)
+    resid_cp = cps.start(resid_in, resid)
+    wait_all(vec_cp)
+    bias = jnp.transpose(vec[...])[:, OUTPUT_BIAS : OUTPUT_BIAS + 1]
+    wait_all(po_cp)
+    mix_cp.wait()
+    resid_cp.wait()
+    po_t = jnp.transpose(po[...].astype(f32)).astype(bf16)
+    for b in range(count):
+        val = jnp.transpose(resid[b]) + nn(po_t, mix[b]) + bias
+        split_store(own, send, b, val, 0, places)
 
 
 def last_kernel(pieces, count, *refs):
@@ -445,12 +518,12 @@
     def take(n):
         return [next(it) for _ in range(n)]
 
-    x_in, w1_in, po_in, vec_in = (take(pieces) for _ in range(4))
-    hpad_in, resid_in, gres_in, mix_in = take(4)
-    block_own, image_own = take(2)
-    block_send, image_send = take(2) if pieces == 2 else (None, None)
+    x_in, w1_in, vec_in = (take(pieces) for _ in range(3))
+    hpad_in, gres_in = take(2)
+    image_own = next(it)
+    image_send = next(it) if pieces == 2 else None
     vec_out = next(it)
-    xin, w1, po, vec, hpad, resid, gres, mix = take(8)
+    xin, w1, vec, hpad, gres = take(5)
     sems = next(it)
     cps = Copies(sems)
     places = places_of(pieces)
@@ -460,9 +533,6 @@
     size = float(width * points)
 
     vec_cp = load_split(cps, vec_in, vec, 1, places)
-    po_cp = load_split(cps, po_in, po, 0, places)
-    mix_cp = cps.start(mix_in, mix)
-    resid_cp = cps.start(resid_in, resid)
     x_cp = load_images(cps, x_in, xin, places, count)
     w1_cp = load_split(cps, w1_in, w1, 2, places)
     hpad_cp = cps.start(hpad_in, hpad)
@@ -472,14 +542,6 @@
 
     def col(j):
         return vcols[:, j : j + 1]
-
-    wait_all(po_cp)
-    mix_cp.wait()
-    resid_cp.wait()
-    po_t = jnp.transpose(po[...].astype(f32)).astype(bf16)
-    for b in range(count):
-        val = jnp.transpose(resid[b]) + nn(po_t, mix[b]) + col(OUTPUT_BIAS)
-        split_store(block_own, block_send, b, val, 0, places)
 
     wait_all(x_cp)
     wait_all(w1_cp)
@@ -522,61 +584,62 @@
     return lax.ppermute(value, axis, [(i, i ^ bit) for i in range(size)])
 
 
-def phases_of(size):
-    bits = size.bit_length() - 1
-    out = []
-    low = 0
-    while low < bits:
-        out.append((low, min(2, bits - low)))
-        low += 2
-    return out
-
-
-def scatter_sum(total, batch):
+def near_parts(part):
+    me = lax.axis_index("batch") & 3
+    return [part(me ^ j).astype(bf16) for j in range(1, 4)]
+
+
+def after(values, *others):
+    done = lax.optimization_barrier((tuple(values), others))
+    return list(done[0])
+
+
+def send_near(sent, batch):
+    return [swap(v, "batch", batch, j + 1) for j, v in enumerate(sent)]
+
+
+def sum_near(got, part):
+    total = part(lax.axis_index("batch") & 3).astype(f32)
+    for g in got:
+        total = total + g.astype(f32)
+    return total.astype(bf16)
+
+
+def far_steps(batch):
+    return batch.bit_length() - 3
+
+
+def send_far(piece, extra, step, batch):
+    steps = far_steps(batch)
+    mine = piece if extra is None else jnp.concatenate([piece, extra], axis=0)
+    tensor = lax.axis_size("tensor")
+    pairs = []
+    for i in range(batch):
+        for core in range(tensor):
+            bit = 4 << (step if core % 2 == 0 else steps - 1 - step)
+            pairs.append((i * tensor + core, (i ^ bit) * tensor + core))
+    return lax.ppermute(mine, ("batch", "tensor"), pairs)
+
+
+def sum_far(piece, extra, got):
+    rows = piece.shape[0]
+    piece = (piece.astype(f32) + got[:rows].astype(f32)).astype(bf16)
+    if extra is not None:
+        extra = jnp.concatenate([extra, got[rows:]], axis=0)
+    return piece, extra
+
+
+def gather_near(piece, batch):
+    return [piece] + [swap(piece, "batch", batch, j) for j in range(1, 4)]
+
+
+def in_order(pieces):
     me = lax.axis_index("batch")
-    for low, bits in phases_of(batch):
-        m = 1 << bits
-        mine = (me >> low) & (m - 1)
-        parts = total.reshape(m, total.shape[0] // m, total.shape[1])
-        got = [
-            swap(
-                lax.dynamic_index_in_dim(parts, mine ^ j, 0, False).astype(bf16),
-                "batch",
-                batch,
-                j << low,
-            )
-            for j in range(1, m)
-        ]
-        total = lax.dynamic_index_in_dim(parts, mine, 0, False).astype(f32)
-        for g in got:
-            total = total + g.astype(f32)
-    return total
-
-
-def gather_all(piece, extra, batch):
-    me = lax.axis_index("batch")
-    rows = piece.shape[0]
-    for low, bits in reversed(phases_of(batch)):
-        m = 1 << bits
-        mine = (me >> low) & (m - 1)
-        both = jnp.concatenate([piece, extra], axis=0)
-        all_of = [both] + [swap(both, "batch", batch, j << low) for j in range(1, m)]
-        extra = jnp.concatenate([a[rows:] for a in all_of], axis=0)
-        parts = jnp.stack([a[:rows] for a in all_of], axis=0)
-        for i in range(bits):
-            shape = parts.shape
-            split = parts.reshape((1 << (bits - 1 - i), 2, 1 << i) + shape[1:])
-            turned = jnp.flip(split, axis=1)
-            parts = jnp.where(((mine >> i) & 1) == 1, turned, split).reshape(shape)
-        piece = parts.reshape(m * rows, piece.shape[1])
-        rows = piece.shape[0]
-    return piece, extra
-
-
-def pack(arrays, unit):
-    flat = jnp.concatenate([a.reshape(-1, 128) for a in arrays], axis=0)
-    pad = -flat.shape[0] % unit
-    return jnp.pad(flat, ((0, pad), (0, 0)))
+    parts = jnp.stack(pieces, axis=0)
+    parts = parts.reshape((2, 2) + parts.shape[1:])
+    parts = jnp.where((me & 1) == 1, jnp.flip(parts, axis=1), parts)
+    parts = jnp.where((me & 2) == 2, jnp.flip(parts, axis=0), parts)
+    return parts.reshape((-1, LANES))
 
 
 def unpack(flat, shapes):
@@ -671,20 +734,25 @@
     def shape(s, d):
         return jax.ShapeDtypeStruct(s, d)
 
-    def grads(full, axis):
-        if pieces == 1:
-            return [shape(full, f32)]
-        half = full[:axis] + (full[axis] // 2,) + full[axis + 1 :]
-        return [shape(half, bf16), shape(half, bf16)]
-
-    dw2_t, dpo_t = grads((9, chans, chans), 1), grads((chans, chans), 0)
-    dpi_t, dw1_t = grads((3, chans, chans), 2), grads((9, chans, chans), 2)
     params = pltpu.CompilerParams(vmem_limit_bytes=VMEM_LIMIT)
-    n_grad = 3 * pieces
+
+    def cost(units, moved):
+        flops = 2 * units * count * points * chans * chans
+        return pl.CostEstimate(flops=flops, bytes_accessed=moved, transcendentals=0)
+
+    half_b = 9 * chans * chans // 2 // LANES
+    half_a = half_b + 4 * chans * chans // 2 // LANES
+    if pieces == 2:
+        grads_a = [shape((half_a, LANES), bf16)] * 2
+        grads_b = [shape((half_b, LANES), bf16)] * 2
+    else:
+        grads_a = [shape((9, chans, chans), f32), shape((chans, chans), f32)]
+        grads_a.append(shape((3, chans, chans), f32))
+        grads_b = [shape((9, chans, chans), f32)]
+    n_grad = len(grads_a)
     front = pl.pallas_call(
         functools.partial(front_kernel, pieces, count),
-        out_shape=[g[0] for g in (dw2_t, dpo_t, dpi_t)]
-        + ([g[1] for g in (dw2_t, dpo_t, dpi_t)] if pieces == 2 else [])
+        out_shape=grads_a
         + [
             shape((8, chans), f32),
             shape((2, count, chans), f32),
@@ -721,16 +789,68 @@
             pltpu.SemaphoreType.DMA((8 * pieces + count + 6,)),
         ],
         compiler_params=params,
+        cost_estimate=cost(54, 12 << 20),
         name="front",
     )(*x_in, *g_in, *w1_in, *w2_in, *pi_in, *po_in, *tw_in, *vec_in, my_steps, embed_table)
-    g_front = front[:n_grad]
+    sums_a = front[:n_grad]
     vec_a, stat, gpad, sum_one, a1t, resid, gres, mix = front[n_grad:]
 
-    middle = pl.pallas_call(
+    if pieces == 2:
+        half = (count, chans // 2, points)
+        out_t = [shape(half, f32), shape(half, bf16)]
+    else:
+        out_t = [shape(image_b, f32)]
+    block_part = pl.pallas_call(
+        functools.partial(block_kernel, pieces, count),
+        out_shape=out_t,
+        in_specs=[ANY] * (2 * pieces + 2),
+        out_specs=[VMEM] * pieces,
+        scratch_shapes=[
+            pltpu.VMEM((chans, chans), bf16),
+            pltpu.VMEM((16, chans), f32),
+            pltpu.VMEM(image_p, f32),
+            pltpu.VMEM(image_b, bf16),
+            pltpu.SemaphoreType.DMA((2 * pieces + 2,)),
+        ],
+        compiler_params=params,
+        cost_estimate=cost(3, 5 << 20),
+        name="block",
+    )(*po_in, *vec_in, resid, mix)
+
+    def quarters(sums, axes, beside=None):
+        if pieces == 2:
+            got = swap(sums[1], "tensor", 2, 1)
+            if beside is not None:
+                (got,) = after([got], beside)
+            rows = got.shape[0] // 4
+            own4, got4 = (v.reshape(4, rows, LANES) for v in (sums[0], got))
+
+            def part(q):
+                pair = [lax.dynamic_index_in_dim(v, q, 0, False).astype(f32) for v in (own4, got4)]
+                return pair[0] + pair[1]
+
+            return part
+        done = [
+            lax.psum_scatter(v, "tensor", scatter_dimension=axis, tiled=True)
+            for v, axis in zip(sums, axes, strict=True)
+        ]
+        flat = jnp.concatenate([v.reshape(-1, LANES) for v in done], axis=0)
+        flat = jnp.pad(flat, ((0, -flat.shape[0] % 64), (0, 0)))
+        rows = flat.shape[0] // 4
+        flat = flat.reshape(4, rows, LANES)
+        return lambda q: lax.dynamic_index_in_dim(flat, q, 0, False)
+
+    part_a = quarters(sums_a, (1, 0, 2), block_part[0])
+    sent_a = near_parts(part_a)
+
+    got_a = send_near(sent_a, batch)
+    gpad, sum_one = after([gpad, sum_one], *sent_a)
+
+    *sums_b, block, hpad = pl.pallas_call(
         functools.partial(middle_kernel, pieces, count),
-        out_shape=dw1_t + [shape((8, chans), f32), shape((count, chans), f32), shape(pads, bf16)],
-        in_specs=[ANY] * (2 * pieces + 3) + [VMEM],
-        out_specs=[VMEM] * (pieces + 2) + [ANY],
+        out_shape=grads_b + [shape((BLOCK, LANES), bf16), shape(pads, bf16)],
+        in_specs=[ANY] * (2 * pieces + 3) + [VMEM, VMEM, SMEM],
+        out_specs=[VMEM] * (pieces + 1) + [ANY],
         scratch_shapes=[
             pltpu.VMEM((9, chans, chans), bf16),
             pltpu.VMEM((16, chans), f32),
@@ -743,37 +863,39 @@
             pltpu.SemaphoreType.DMA((2 * pieces + 4,)),
         ],
         compiler_params=params,
+        cost_estimate=cost(21, 7 << 20),
         name="middle",
-    )(*w2_in, *vec_in, gpad, sum_one, a1t, stat)
-    g_middle = middle[:pieces]
-    vec_b, times, hpad = middle[pieces:]
-
-    if pieces == 2:
-        half = (count, chans // 2, points)
-        out_t = [shape(half, f32)] * 2 + [shape(half, bf16)] * 2
-    else:
-        out_t = [shape(image_b, f32)] * 2
-    last = pl.pallas_call(
+    )(*w2_in, *vec_in, gpad, sum_one, a1t, stat, vec_a, my_steps)
+    got_a = after(got_a, block)
+    sums_b = after(sums_b, *got_a)
+    piece_a = sum_near(got_a, part_a)
+    part_b = quarters(sums_b, (2,))
+    sent_b = near_parts(part_b)
+    got_b = send_near(sent_b, batch)
+    far_a = send_far(piece_a, block, 0, batch)
+    hpad, gres = after([hpad, gres], piece_a, *sent_b)
+
+    image_grad = pl.pallas_call(
         functools.partial(last_kernel, pieces, count),
         out_shape=out_t + [shape((8, chans), f32)],
-        in_specs=[ANY] * (4 * pieces + 4),
-        out_specs=[VMEM] * (2 * pieces + 1),
+        in_specs=[ANY] * (3 * pieces + 2),
+        out_specs=[VMEM] * (pieces + 1),
         scratch_shapes=[
             pltpu.VMEM(image_b, bf16),
             pltpu.VMEM((9, chans, chans), bf16),
-            pltpu.VMEM((chans, chans), bf16),
             pltpu.VMEM((16, chans), f32),
             pltpu.VMEM(pads, bf16),
             pltpu.VMEM(image_p, f32),
-            pltpu.VMEM(image_p, f32),
-            pltpu.VMEM(image_b, bf16),
-            pltpu.SemaphoreType.DMA((4 * pieces + 4,)),
+            pltpu.SemaphoreType.DMA((3 * pieces + 2,)),
         ],
         compiler_params=params,
+        cost_estimate=cost(9, 8 << 20),
         name="last",
-    )(*x_in, *w1_in, *po_in, *vec_in, hpad, resid, gres, mix)
-    block, image = last[0], last[1]
-    vec_c = last[-1]
+    )(*x_in, *w1_in, *vec_in, hpad, gres)
+    got_b = after(got_b, image_grad[-1])
+    *image_grad, far_a = after([*image_grad, far_a], *got_b)
+    block_part = after(block_part, image_grad[-1])
+    vec_c = image_grad[-1][:2].reshape(-1, LANES)
 
     def placed(own, send):
         if pieces == 2:
@@ -783,51 +905,62 @@
             return jnp.concatenate([low, high], axis=0)
         return lax.all_to_all(own, "tensor", 1, 0, tiled=True)
 
-    block_out = placed(block, last[pieces])
-    images_grad = placed(image, last[pieces + 1])
-
-    unit = 16 * batch
-
-    def over_tensor(own, send, axis):
-        if pieces == 2:
-            return own.astype(f32) + swap(send, "tensor", 2, 1).astype(f32)
-        return lax.psum_scatter(own, "tensor", scatter_dimension=axis, tiled=True)
-
-    dw2 = over_tensor(g_front[0], g_front[-3], 1)
-    dpo = over_tensor(g_front[1], g_front[-2], 0)
-    dpi = over_tensor(g_front[2], g_front[-1], 2)
-    dw1 = over_tensor(g_middle[0], g_middle[-1], 2)
-    shapes_a = [dw2.shape, dpo.shape, dpi.shape]
-    piece_a = scatter_sum(pack([dw2, dpo, dpi], unit), batch)
-    piece_b = scatter_sum(pack([dw1], unit), batch)
-
-    vecs = jnp.concatenate([vec_a, vec_b, vec_c], axis=0)
+    block_out = placed(block_part[0], block_part[-1])
+    images_grad = placed(image_grad[0], image_grad[1])
+
+    piece_a, blocks = sum_far(piece_a, block, far_a)
+    for step in range(1, far_steps(batch)):
+        piece_a, blocks = sum_far(piece_a, blocks, send_far(piece_a, blocks, step, batch))
+
+    piece_b = sum_near(got_b, part_b)
+    vec_c = jnp.pad(vec_c, ((0, 16 - vec_c.shape[0]), (0, 0))).astype(bf16)
+    piece_b = jnp.concatenate([piece_b, vec_c], axis=0)
+    for step in range(far_steps(batch)):
+        piece_b, _ = sum_far(piece_b, None, send_far(piece_b, None, step, batch))
+    rows_a = piece_a.shape[0]
+    got_a = gather_near(jnp.concatenate([piece_a, blocks], axis=0), batch)
+    done_a = in_order([g[:rows_a] for g in got_a])
+    blocks = jnp.concatenate([g[rows_a:] for g in got_a], axis=0)
+    got_b = gather_near(piece_b, batch)
+    rows_b = piece_b.shape[0] - 16
+    done_b = in_order([g[:rows_b] for g in got_b])
+    vec_c = sum(g[rows_b:].astype(f32) for g in got_b)[: 2 * chans // LANES].reshape(2, chans)
     if pieces == 2:
-        vecs = vecs + swap(vecs, "tensor", 2, 1)
-        theirs = swap(times, "tensor", 2, 1)
-        times = jnp.concatenate(
-            [jnp.where(me == 0, times, theirs), jnp.where(me == 0, theirs, times)], axis=0
+        vec_c = vec_c + swap(vec_c, "tensor", 2, 1)
+    else:
+        vec_c = lax.psum(vec_c, "tensor")
+
+    half = local
+    if pieces == 2:
+        n = chans * chans // 2 // LANES
+        project_out_grad = done_a[:n].reshape(2, local, LANES)
+        project_out_grad = jnp.concatenate([project_out_grad[0], project_out_grad[1]], axis=1)
+        project_in_grad = done_a[n : 4 * n].reshape(3, chans, local)
+        taps_grad = done_a[4 * n :].reshape(9, 2, local, LANES)
+        second_conv_grad = jnp.concatenate([taps_grad[:, 0], taps_grad[:, 1]], axis=2)
+        first_conv_grad = done_b.reshape(9, chans, local)
+    else:
+        second_conv_grad, project_out_grad, project_in_grad = unpack(
+            done_a, [(9, half, chans), (half, chans), (3, chans, half)]
         )
+        (first_conv_grad,) = unpack(done_b, [(9, chans, half)])
+
+    if pieces == 2:
+        blocks = jnp.concatenate([blocks, swap(blocks, "tensor", 2, 1)], axis=0)
+        two = blocks.reshape(2, batch, BLOCK, LANES)
+        blocks = jnp.where(me == 0, two, jnp.flip(two, axis=0))
     else:
-        vecs = lax.psum(vecs, "tensor")
-        times = lax.all_gather(times, "tensor", axis=0, tiled=True)
-    stamp = jnp.zeros((8, chans), f32)
-    stamp = stamp.at[:per_batch, 0].set((timesteps >> 5).astype(f32))
-    stamp = stamp.at[:per_batch, 1].set((timesteps & 31).astype(f32))
-    small = jnp.concatenate([vecs, times, stamp], axis=0)
-    n_small = small.shape[0]
-    small = small.reshape(-1, 128).astype(bf16)
-    done_a, _ = gather_all(piece_a.astype(bf16), small[:0], batch)
-    done_b, small = gather_all(piece_b.astype(bf16), small, batch)
-    second_conv_grad, project_out_grad, project_in_grad = unpack(done_a, shapes_a)
-    (first_conv_grad,) = unpack(done_b, [dw1.shape])
-
-    small = small.reshape(batch, n_small, chans)
-    sums = jnp.sum(small[:, :24].astype(f32), axis=0)
+        blocks = lax.all_gather(blocks, "tensor", axis=0, tiled=True)
+    blocks = blocks.reshape(batch * tensor, BLOCK, LANES)
+    wide = chans // LANES
+    n_vec = 9 * wide
+    sums = jnp.sum(blocks[:, :n_vec].astype(f32), axis=0).reshape(9, chans)
+    sums = jnp.concatenate([sums, vec_c], axis=0)
     mine = lax.dynamic_slice_in_dim(sums, me * local, local, axis=1)
-    all_times = small[:, 24 : 24 + per_batch].reshape(batch * per_batch, chans)
-    stamps = small[:, 24 + per_batch :].astype(jnp.int32)[:, :per_batch]
-    all_steps = (stamps[:, :, 0] * 32 + stamps[:, :, 1]).reshape(batch * per_batch)
+    all_times = blocks[:, n_vec : n_vec + wide * count].reshape(-1, chans)
+    stamps = blocks[:, n_vec + wide * count].astype(jnp.int32)
+    all_steps = stamps[:, :count] * 32 + stamps[:, LANES // 2 : LANES // 2 + count]
+    all_steps = all_steps.reshape(-1)
     one_hot = (all_steps[:, None] == jnp.arange(steps, dtype=jnp.int32)[None, :]).astype(bf16)
     emb = nn(one_hot, embed_table)
     sig = sigmoid(emb)
@@ -850,22 +983,22 @@
         block_out,
         images_grad,
         table_grad,
-        mine[16],
-        mine[17],
-        first_conv_grad,
+        mine[9],
         mine[10],
+        first_conv_grad.astype(f32),
+        mine[8],
         time_weight_grad,
-        mine[10],
         mine[8],
-        mine[9],
-        second_conv_grad,
+        mine[6],
+        mine[7],
+        second_conv_grad.astype(f32),
         mine[0],
         mine[1],
         mine[2],
-        project_in_grad,
+        project_in_grad.astype(f32),
         mine[3],
         mine[4],
-        project_out_grad,
+        project_out_grad.astype(f32),
         mine[5],
     )
 

time: 127 us -> 104 us (0.82); the launches traced: 126 us -> 102 us
  starting transfers between devices: 37.9 us -> 27.5 us
  waiting for transfers between devices: 24.6 us -> 17.4 us
  other arithmetic: 14.5 us -> 8.83 us
  local copies, waits for them, and re-layouts: 12.6 us -> 9.23 us
  Pallas kernels: 32 us -> 34.2 us
    ppermute x40 -> x26, starting transfers between devices: 37.9 us -> 18.1 us  [swap(): return lax.ppermute(value, axis, [(i, i ^ bit) for i in range(size)])]
    ppermute x40 -> x26, waiting for transfers between devices: 24.6 us -> 12.3 us  [swap(): return lax.ppermute(value, axis, [(i, i ^ bit) for i in range(size)])]
    ppermute x0 -> x4, starting transfers between devices: none -> 9.4 us  [send_far(): return lax.ppermute(mine, ('batch', 'tensor'), pairs)]
    ppermute x0 -> x4, waiting for transfers between devices: none -> 5.1 us  [send_far(): return lax.ppermute(mine, ('batch', 'tensor'), pairs)]
    another operation x13 -> x2, other arithmetic: 4.79 us -> 0.19 us  [in_order(): parts = jnp.stack(pieces, axis=0)]
    add x7 -> x3, other arithmetic: 3.74 us -> 0.09 us  [the longest x1 0.07 us: per_device(): stamps[:, :count] * 32 + stamps[:, LANES // 2:LANES // 2 + count]]
    convert_element_type x7 -> x0, local copies, waits for them, and re-layouts: 3.58 us -> none  [the longest x2 2.03 us: unpack(): out.append(flat[at:at + n].reshape(shape).astype(f32))]
    convert_element_type x6 -> x13, other arithmetic: 2.02 us -> 5.47 us  [the longest x2 1.3 us: sum_near(): return total.astype(bf16)]
  transfers between devices with their start and end apart: 40 -> 30, of which waited for: 14 -> 7; matrix products, arithmetic and copies ran while one was open for 18% -> 12% of each run, Pallas kernels for 0% -> 16%
where the time goes in v2:
time: 104 us; the launch traced here: 102 us
  Pallas kernels  34.2 us (33%)
  starting transfers between devices  27.5 us (26%)
  waiting for transfers between devices  17.4 us (17%)
  local copies, waits for them, and re-layouts  9.23 us (9%)
  other arithmetic  8.83 us (8%)
  matrix products  3.25 us (3%)
  between operations  1.26 us (1%)
    ppermute x26, starting transfers between devices, swap(): return lax.ppermute(value, axis, [(i, i ^ bit) for i in range(size)])  18.1 us
    pallas_call x1, Pallas kernels, per_device(): pl.pallas_call(functools.partial(front_kernel, pieces, count), out_shape=...  17.5 us
    ppermute x26, waiting for transfers between devices, swap(): return lax.ppermute(value, axis, [(i, i ^ bit) for i in range(size)])  12.3 us
    ppermute x4, starting transfers between devices, send_far(): return lax.ppermute(mine, ('batch', 'tensor'), pairs)  9.4 us
    pallas_call x1, Pallas kernels, per_device(): pl.pallas_call(functools.partial(middle_kernel, pieces, count), out_shape...  8.27 us
    pallas_call x1, Pallas kernels, per_device(): pl.pallas_call(functools.partial(last_kernel, pieces, count), out_shape=o...  5.49 us
    ppermute x4, waiting for transfers between devices, send_far(): return lax.ppermute(mine, ('batch', 'tensor'), pairs)  5.1 us
    unnamed x46, local copies, waits for them, and re-layouts  3.96 us
  transfers between devices with their start and end apart: 30, of which 7 were waited for; matrix products, arithmetic and copies ran while one was open for 12% of the time, Pallas kernels for 16%

profile of v2, /device:TPU:0, one launch (start us, length us, event | category | flops | bytes accessed | tf_op | source)
XLA Modules:
  0.0 101.6 jit_solution(12119493432839427932)
XLA Ops:
  0.7 0.5 collective-permute-start.4
  1.3 0.4 collective-permute-start
  1.7 1.6 %stack.85.refs_14_.refs_2_.refs_4_ = f32[16,128]{1,0:T(8,128)S(1)} concatenate(f32[1,128]{1,0:T(1,128)} %bitcast.137, f32[1,128]{1,0:T(1,128)} %bitcast.138, f32[1,128]{1,0:T(1,128)} %bitcast.139, f32[1,128]{1,0:T(1,128)} %bitcast.140, f32[1,128]{1,0:T(1,128)} %bitcast.141, f32[1,128]{1,0:T(1,128)} %bitcast.142, f32[1,128]{1,0:T(1,128)} %bitcast.143, f32[1,128]{1,0:T(1,128)} %bitcast.144, ...), dimensions={0} | concatenate | bytes 16384 | tf_op jit(solution)/shard_map/stack | solution.py:686
  3.5 0.4 collective-permute-start.7
  3.9 1.0 dynamic-slice_bitcast_fusion.1
  4.9 1.0 dynamic-slice_bitcast_fusion
  6.0 0.4 collective-permute-start.3
  6.6 1.8 %collective-permute-done.6.refs_9_ = bf16[3,256,128]{2,1,0:T(8,128)(2,1)S(1)} collective-permute-done((bf16[3,256,128]{2,1,0:T(8,128)(2,1)}, bf16[3,256,128]{2,1,0:T(8,128)(2,1)S(1)}, u32[]{:S(2)}, u32[]{:S(2)}) %collective-permute-start.6) | collective-permute-done | bytes 196640 | tf_op jit(solution)/shard_map/ppermute | solution.py:584
  8.4 0.6 copy-done.19
  9.4 0.8 copy-done.17
  10.2 17.5 %front.1 = (bf16[3328,128]{1,0:T(8,128)(2,1)}, bf16[3328,128]{1,0:T(8,128)(2,1)}, f32[8,256]{1,0:T(8,128)}, f32[2,4,256]{2,1,0:T(4,128)}, bf16[3,4,288,256]{3,2,...) custom-call(bf16[8,128,256]{2,1,0:T(8,128)(2,1)} %refs_0_.7, ...), custom_call_target="tpu_custom_call" | custom-call | flops 7247757312 | bytes 12582912 | tf_op jit(solution)/shard_map/front/pallas_call | solution.py:753
  28.0 2.9 %block.1 = (f32[4,128,256]{2,1,0:T(8,128)}, bf16[4,128,256]{2,1,0:T(8,128)(2,1)}) custom-call(bf16[128,256]{1,0:T(8,128)(2,1)} %refs_0_.5, bf16[128,256]{1,0:T(8,128)(2,1)} %copy-done.14, f32[16,128]{1,0:T(8,128)} %copy-done.13, f32[16,128]{1,0:T(8,128)} %copy-done.15, f32[4,256,256]{2,1,0:T(8,128)} %get-tuple-element.58.refs_4_, ...), custom_call_target="tpu_custom_call" | custom-call | flops 402653184 | bytes 5242880 | tf_op jit(solution)/shard_map/block/pallas_call | solution.py:803
  31.1 2.9 %collective-permute-start.9 = (bf16[832,128]{1,0:T(8,128)(2,1)S(1)}, bf16[832,128]{1,0:T(8,128)(2,1)S(1)}, u32[]{:S(2)}, u32[]{:S(2)}) collective-permute-start(bf16[832,128]{1,0:T(8,128)(2,1)S(1)} %get-tuple-element.98), channel_id=1, source_target_pairs={{0,2},{2,0},{4,6},{6,4},{8,10},{10,8},{12,14},{14,12},{16,18},{18,... | collective-permute-start | bytes 638984 | tf_op jit(solution)/shard_map/ppermute | solution.py:584
  34.0 1.5 %collective-permute-start.10 = (bf16[832,128]{1,0:T(8,128)(2,1)S(1)}, bf16[832,128]{1,0:T(8,128)(2,1)S(1)}, u32[]{:S(2)}, u32[]{:S(2)}) collective-permute-start(bf16[832,128]{1,0:T(8,128)(2,1)S(1)} %get-tuple-element.97), channel_id=1, source_target_pairs={{0,4},{2,6},{4,0},{6,2},{8,12},{10,14},{12,8},{14,10},{16,20},{18,... | collective-permute-start | bytes 638984 | tf_op jit(solution)/shard_map/ppermute | solution.py:584
  35.5 8.3 %middle.1 = (bf16[2304,128]{1,0:T(8,128)(2,1)}, bf16[2304,128]{1,0:T(8,128)(2,1)}, bf16[32,128]{1,0:T(8,128)(2,1)}, bf16[3,4,288,256]{3,2,1,0:T(8,128)(2,1)}) custom-call(bf16[9,128,256]{2,1,0:T(8,128)(2,1)} %refs_0_.6, bf16[9,128,256]{2,1,0:T(8,128)(2,1)} %copy-done.17, f32[16,128]{1,0:T(8,128)} %copy-done.13, f32[16,128]{1,0:T(8,128)} %copy-done.15, ...), custom_call_target="tpu_custom_call" | custom-call | flops 2818572288 | bytes 7340032 | tf_op jit(solution)/shard_map/middle/pallas_call | solution.py:849
  43.8 1.8 %collective-permute-done.10 = bf16[832,128]{1,0:T(8,128)(2,1)S(1)} collective-permute-done((bf16[832,128]{1,0:T(8,128)(2,1)S(1)}, bf16[832,128]{1,0:T(8,128)(2,1)S(1)}, u32[]{:S(2)}, u32[]{:S(2)}) %collective-permute-start.10) | collective-permute-done | bytes 213024 | tf_op jit(solution)/shard_map/ppermute | solution.py:584
  45.6 0.7 copy-done.8
  46.3 0.7 constant_dynamic-update-slice_fusion.2
  47.0 1.2 %fusion.5 = bf16[832,128]{1,0:T(8,128)(2,1)S(1)} fusion(bf16[832,128]{1,0:T(8,128)(2,1)} %copy-done.8, bf16[832,128]{1,0:T(8,128)(2,1)} %copy-done.7, bf16[832,128]{1,0:T(8,128)(2,1)S(1)} %collective-permute-done.9, bf16[4,832,128]{2,1,0:T(8,128)(2,1)S(1)} %bitcast.123, s32[]{:T(128)S(6)} %select_n.104, bf16[4,832,128]{2,1,0:T(8,128)(2,1)S(1)} %bitcast.121), kind=kLoop, calls=%fused_computation.21 | loop fusion | flops 1064960 | bytes 1277956 | tf_op jit(solution)/shard_map/convert_element_type | solution.py:605
  48.6 1.3 %collective-permute-start.14 = (bf16[576,128]{1,0:T(8,128)(2,1)S(1)}, bf16[576,128]{1,0:T(8,128)(2,1)S(1)}, u32[]{:S(2)}, u32[]{:S(2)}) collective-permute-start(bf16[576,128]{1,0:T(8,128)(2,1)S(1)} %get-tuple-element.101), channel_id=1, source_target_pairs={{0,2},{2,0},{4,6},{6,4},{8,10},{10,8},{12,14},{14,12},{16,18},{18,... | collective-permute-start | bytes 442376 | tf_op jit(solution)/shard_map/ppermute | solution.py:584
  49.9 0.9 collective-permute-start.15
  50.8 1.4 %collective-permute-start.16 = (bf16[576,128]{1,0:T(8,128)(2,1)S(1)}, bf16[576,128]{1,0:T(8,128)(2,1)S(1)}, u32[]{:S(2)}, u32[]{:S(2)}) collective-permute-start(bf16[576,128]{1,0:T(8,128)(2,1)S(1)} %get-tuple-element.99), channel_id=1, source_target_pairs={{0,6},{2,4},{4,2},{6,0},{8,14},{10,12},{12,10},{14,8},{16,22},{18,... | collective-permute-start | bytes 442376 | tf_op jit(solution)/shard_map/ppermute | solution.py:584
  52.2 1.6 %collective-permute-start.13 = (bf16[864,128]{1,0:T(8,128)(2,1)S(1)}, bf16[864,128]{1,0:T(8,128)(2,1)S(1)}, u32[]{:S(2)}, u32[]{:S(2)}) collective-permute-start(bf16[864,128]{1,0:T(8,128)(2,1)S(1)} %pad_maximum_fusion.6), channel_id=1, source_target_pairs={{0,8},{1,17},{2,10},{3,19},{4,12},{5,21},{6,14},{7,23},{8,0},{9,25... | collective-permute-start | bytes 663560 | tf_op jit(solution)/shard_map/ppermute | solution.py:621
  53.9 5.5 %last.1 = (f32[4,128,256]{2,1,0:T(8,128)}, bf16[4,128,256]{2,1,0:T(8,128)(2,1)}, f32[8,256]{1,0:T(8,128)}) custom-call(bf16[8,128,256]{2,1,0:T(8,128)(2,1)} %refs_0_.7, bf16[4,128,256]{2,1,0:T(8,128)(2,1)} %copy-done.6, bf16[9,256,128]{2,1,0:T(8,128)(2,1)} %refs_2_.3, bf16[9,256,128]{2,1,0:T(8,128)(2,1)} %copy-done.2, f32[16,128]{1,0:T(8,128)} %copy-done.13, ...), custom_call_target="tpu_custom_call" | custom-call | flops 1207959552 | bytes 8388608 | tf_op jit(solution)/shard_map/last/pallas_call | solution.py:878
  59.5 0.7 slice.261
  60.8 2.1 %collective-permute-start.24 = (bf16[592,128]{1,0:T(8,128)(2,1)S(1)}, bf16[592,128]{1,0:T(8,128)(2,1)S(1)}, u32[]{:S(2)}, u32[]{:S(2)}) collective-permute-start(bf16[592,128]{1,0:T(8,128)(2,1)S(1)} %fusion.31), channel_id=1, source_target_pairs={{0,8},{1,17},{2,10},{3,19},{4,12},{5,21},{6,14},{7,23},{8,0},{9,25... | collective-permute-start | bytes 454664 | tf_op jit(solution)/shard_map/ppermute | solution.py:621
  63.0 3.1 %collective-permute-start.19 = (bf16[896,128]{1,0:T(8,128)(2,1)S(1)}, bf16[896,128]{1,0:T(8,128)(2,1)S(1)}, u32[]{:S(2)}, u32[]{:S(2)}) collective-permute-start(bf16[896,128]{1,0:T(8,128)(2,1)S(1)} %pad_maximum_fusion.5), channel_id=1, source_target_pairs={{0,16},{1,9},{2,18},{3,11},{4,20},{5,13},{6,22},{7,15},{8,24},{9,1... | collective-permute-start | bytes 688136 | tf_op jit(solution)/shard_map/ppermute | solution.py:621
  66.1 5.1 %collective-permute-done.24 = bf16[592,128]{1,0:T(8,128)(2,1)S(1)} collective-permute-done((bf16[592,128]{1,0:T(8,128)(2,1)S(1)}, bf16[592,128]{1,0:T(8,128)(2,1)S(1)}, u32[]{:S(2)}, u32[]{:S(2)}) %collective-permute-start.24) | collective-permute-done | bytes 151584 | tf_op jit(solution)/shard_map/ppermute | solution.py:621
  71.2 2.5 %collective-permute-start.25 = (bf16[592,128]{1,0:T(8,128)(2,1)S(1)}, bf16[592,128]{1,0:T(8,128)(2,1)S(1)}, u32[]{:S(2)}, u32[]{:S(2)}) collective-permute-start(bf16[592,128]{1,0:T(8,128)(2,1)S(1)} %add_convert_fusion.6), channel_id=1, source_target_pairs={{0,16},{1,9},{2,18},{3,11},{4,20},{5,13},{6,22},{7,15},{8,24},{9,1... | collective-permute-start | bytes 454664 | tf_op jit(solution)/shard_map/ppermute | solution.py:621
  73.9 1.3 %collective-permute-start.20 = (bf16[960,128]{1,0:T(8,128)(2,1)S(1)}, bf16[960,128]{1,0:T(8,128)(2,1)S(1)}, u32[]{:S(2)}, u32[]{:S(2)}) collective-permute-start(bf16[960,128]{1,0:T(8,128)(2,1)S(1)} %pad_maximum_fusion.4), channel_id=1, source_target_pairs={{0,2},{2,0},{4,6},{6,4},{8,10},{10,8},{12,14},{14,12},{16,18},{18,... | collective-permute-start | bytes 737288 | tf_op jit(solution)/shard_map/ppermute | solution.py:584
  75.1 0.8 collective-permute-start.21
  76.2 1.0 %pad_maximum_fusion = f32[8,128,256]{2,1,0:T(8,128)} fusion(f32[4,128,256]{2,1,0:T(8,128)S(1)} %get-tuple-element.107, f32[4,128,256]{2,1,0:T(8,128)S(1)} %get-tuple-element.106), kind=kLoop, calls=%fused_computation.5 | loop fusion | flops 262144 | bytes 2097152 | tf_op jit(solution)/shard_map/concatenate | solution.py:905
  77.3 1.0 %pad_maximum_fusion.1 = f32[8,128,256]{2,1,0:T(8,128)} fusion(f32[4,128,256]{2,1,0:T(8,128)S(1)} %get-tuple-element.105, f32[4,128,256]{2,1,0:T(8,128)S(1)} %get-tuple-element.104), kind=kLoop, calls=%fused_computation.6 | loop fusion | flops 262144 | bytes 2097152 | tf_op jit(solution)/shard_map/concatenate | solution.py:905
  78.3 1.5 %collective-permute-start.28 = (bf16[592,128]{1,0:T(8,128)(2,1)S(1)}, bf16[592,128]{1,0:T(8,128)(2,1)S(1)}, u32[]{:S(2)}, u32[]{:S(2)}) collective-permute-start(bf16[592,128]{1,0:T(8,128)(2,1)S(1)} %add_convert_fusion.5), channel_id=1, source_target_pairs={{0,6},{2,4},{4,2},{6,0},{8,14},{10,12},{12,10},{14,8},{16,22},{18,... | collective-permute-start | bytes 454664 | tf_op jit(solution)/shard_map/ppermute | solution.py:584
  79.9 1.5 %collective-permute-start.27 = (bf16[592,128]{1,0:T(8,128)(2,1)S(1)}, bf16[592,128]{1,0:T(8,128)(2,1)S(1)}, u32[]{:S(2)}, u32[]{:S(2)}) collective-permute-start(bf16[592,128]{1,0:T(8,128)(2,1)S(1)} %add_convert_fusion.5), channel_id=1, source_target_pairs={{0,4},{2,6},{4,0},{6,2},{8,12},{10,14},{12,8},{14,10},{16,20},{18,... | collective-permute-start | bytes 454664 | tf_op jit(solution)/shard_map/ppermute | solution.py:584
  81.4 0.5 collective-permute-start.26
  81.9 4.3 %collective-permute-done.28 = bf16[592,128]{1,0:T(8,128)(2,1)S(1)} collective-permute-done((bf16[592,128]{1,0:T(8,128)(2,1)S(1)}, bf16[592,128]{1,0:T(8,128)(2,1)S(1)}, u32[]{:S(2)}, u32[]{:S(2)}) %collective-permute-start.28) | collective-permute-done | bytes 151584 | tf_op jit(solution)/shard_map/ppermute | solution.py:584
  86.2 1.3 %collective-permute-start.22 = (bf16[960,128]{1,0:T(8,128)(2,1)S(1)}, bf16[960,128]{1,0:T(8,128)(2,1)S(1)}, u32[]{:S(2)}, u32[]{:S(2)}) collective-permute-start(bf16[960,128]{1,0:T(8,128)(2,1)S(1)} %pad_maximum_fusion.4), channel_id=1, source_target_pairs={{0,6},{2,4},{4,2},{6,0},{8,14},{10,12},{12,10},{14,8},{16,22},{18,... | collective-permute-start | bytes 737288 | tf_op jit(solution)/shard_map/ppermute | solution.py:584
  87.5 1.5 %collective-permute-done.27 = bf16[592,128]{1,0:T(8,128)(2,1)S(1)} collective-permute-done((bf16[592,128]{1,0:T(8,128)(2,1)S(1)}, bf16[592,128]{1,0:T(8,128)(2,1)S(1)}, u32[]{:S(2)}, u32[]{:S(2)}) %collective-permute-start.27) | collective-permute-done | bytes 151584 | tf_op jit(solution)/shard_map/ppermute | solution.py:584
  89.5 1.1 %convert.10 = f32[9,256,128]{2,1,0:T(8,128)} convert(bf16[9,256,128]{2,1,0:T(8,128)(2,1)S(1)} %bitcast.112) | non-fusion elementwise | flops 294912 | bytes 1769472 | tf_op jit(solution)/shard_map/convert_element_type | solution.py:988
  90.6 2.7 %collective-permute-done.22 = bf16[960,128]{1,0:T(8,128)(2,1)S(1)} collective-permute-done((bf16[960,128]{1,0:T(8,128)(2,1)S(1)}, bf16[960,128]{1,0:T(8,128)(2,1)S(1)}, u32[]{:S(2)}, u32[]{:S(2)}) %collective-permute-start.22) | collective-permute-done | bytes 245792 | tf_op jit(solution)/shard_map/ppermute | solution.py:584
  94.1 0.8 convert.11
  94.9 0.7 maximum_convert_fusion.1
  95.6 1.1 %maximum_convert_fusion = f32[9,128,256]{2,1,0:T(8,128)} fusion(bf16[9,128,128]{2,1,0:T(8,128)(2,1)S(1)} %get-tuple-element.109, bf16[9,128,128]{2,1,0:T(8,128)(2,1)S(1)} %get-tuple-element.108), kind=kLoop, calls=%fused_computation.15 | loop fusion | flops 1179648 | bytes 1769472 | tf_op jit(solution)/shard_map/convert_element_type | solution.py:994
  97.7 0.6 slice_bitcast_fusion.9
  98.2 0.9 fusion.35
  99.2 2.0 %fusion.1 = f32[1024,512]{1,0:T(8,128)} fusion(bf16[128,256]{1,0:T(8,128)(2,1)S(1)} %reshape.140, bf16[512,128]{1,0:T(8,128)(2,1)S(1)} %copy-done.12, bf16[512,128]{1,0:T(8,128)(2,1)S(1)} %copy-done.10, f32[128,512]{1,0:T(8,128)S(1)} %fusion.2, s32[128]{0:T(128)S(1)} %eq.15, pred[]{:T(512)S(6)} %eq.14), kind=kOutput, calls=%fused_computation.4 | convolution fusion | flops 169672704 | bytes 2687489 | tf_op jit(solution)/shard_map/dot_general | solution.py:979
  101.1 0.5 copy.61
  (126 shorter events, 5.0 us)
Async XLA Ops:
  0.7 7.7 %collective-permute-start.4 = (bf16[9,256,128]{2,1,0:T(8,128)(2,1)}, bf16[9,256,128]{2,1,0:T(8,128)(2,1)S(1)}, u32[]{:S(2)}, u32[]{:S(2)}) collective-permute-start(bf16[9,256,128]{2,1,0:T(8,128)(2,1)} %refs_2_.3), channel_id=1, source_target_pairs={{0,1},{1,0},{2,3},{3,2},{4,5},{5,4},{6,7},{7,6},{8,9},{9,8},{10,11... | collective-permute-start | bytes 1769480 | tf_op jit(solution)/shard_map/ppermute | solution.py:584
  1.2 7.2 %collective-permute-start.5 = (bf16[9,128,256]{2,1,0:T(8,128)(2,1)}, bf16[9,128,256]{2,1,0:T(8,128)(2,1)S(1)}, u32[]{:S(2)}, u32[]{:S(2)}) collective-permute-start(bf16[9,128,256]{2,1,0:T(8,128)(2,1)} %refs_0_.6), channel_id=1, source_target_pairs={{0,1},{1,0},{2,3},{3,2},{4,5},{5,4},{6,7},{7,6},{8,9},{9,8},{10,11... | collective-permute-start | bytes 1769480 | tf_op jit(solution)/shard_map/ppermute | solution.py:584
  1.3 4.8 %collective-permute-start = (bf16[128,256]{1,0:T(8,128)(2,1)}, bf16[128,256]{1,0:T(8,128)(2,1)S(1)}, u32[]{:S(2)}, u32[]{:S(2)}) collective-permute-start(bf16[128,256]{1,0:T(8,128)(2,1)} %refs_0_.5), channel_id=1, source_target_pairs={{0,1},{1,0},{2,3},{3,2},{4,5},{5,4},{6,7},{7,6},{8,9},{9,8},{10,11... | collective-permute-start | bytes 196616 | tf_op jit(solution)/shard_map/ppermute | solution.py:584
  3.3 5.1 %copy-start.13 = (f32[16,128]{1,0:T(8,128)}, f32[16,128]{1,0:T(8,128)S(1)}, u32[]{:S(2)}) copy-start(f32[16,128]{1,0:T(8,128)S(1)} %stack.85.refs_14_.refs_2_.refs_4_) | copy-start | bytes 24580
  3.3 2.5 %collective-permute-start.1 = (f32[16,128]{1,0:T(8,128)S(1)}, f32[16,128]{1,0:T(8,128)S(1)}, u32[]{:S(2)}, u32[]{:S(2)}) collective-permute-start(f32[16,128]{1,0:T(8,128)S(1)} %stack.85.refs_14_.refs_2_.refs_4_), channel_id=1, source_target_pairs={{0,1},{1,0},{2,3},{3,2},{4,5},{5,4},{6,7},{7,6},{8,9},{9,8},{10,11... | collective-permute-start | bytes 24584 | tf_op jit(solution)/shard_map/ppermute | solution.py:584
  3.5 3.0 %collective-permute-start.7 = (bf16[512,128]{1,0:T(8,128)(2,1)}, bf16[512,128]{1,0:T(8,128)(2,1)S(1)}, u32[]{:S(2)}, u32[]{:S(2)}) collective-permute-start(bf16[512,128]{1,0:T(8,128)(2,1)} %refs_12_.1), channel_id=1, source_target_pairs={{0,1},{1,0},{2,3},{3,2},{4,5},{5,4},{6,7},{7,6},{8,9},{9,8},{10,11... | collective-permute-start | bytes 393224 | tf_op jit(solution)/shard_map/ppermute | solution.py:584
  5.9 2.5 %copy-start.15 = (f32[16,128]{1,0:T(8,128)}, f32[16,128]{1,0:T(8,128)S(1)}, u32[]{:S(2)}) copy-start(f32[16,128]{1,0:T(8,128)S(1)} %collective-permute-done.1.refs_15_.refs_3_.refs_5_) | copy-start | bytes 24580
  5.9 2.5 %collective-permute-start.2 = (bf16[4,128,256]{2,1,0:T(8,128)(2,1)S(1)}, bf16[4,128,256]{2,1,0:T(8,128)(2,1)S(1)}, u32[]{:S(2)}, u32[]{:S(2)}) collective-permute-start(bf16[4,128,256]{2,1,0:T(8,128)(2,1)S(1)} %dynamic-slice_bitcast_fusion.1), channel_id=1, source_target_pairs={{0,1},{1,0},{2,3},{3,2},{4,5},{5,4},{6,7},{7,6},{8,9},{9,8},{10,11... | collective-permute-start | bytes 786440 | tf_op jit(solution)/shard_map/ppermute | solution.py:584
  6.0 2.4 %copy-start.14 = (bf16[128,256]{1,0:T(8,128)(2,1)}, bf16[128,256]{1,0:T(8,128)(2,1)S(1)}, u32[]{:S(2)}) copy-start(bf16[128,256]{1,0:T(8,128)(2,1)S(1)} %collective-permute-done.refs_11_.refs_1_) | copy-start | bytes 196612
  6.0 2.3 %collective-permute-start.3 = (bf16[4,128,256]{2,1,0:T(8,128)(2,1)S(1)}, bf16[4,128,256]{2,1,0:T(8,128)(2,1)S(1)}, u32[]{:S(2)}, u32[]{:S(2)}) collective-permute-start(bf16[4,128,256]{2,1,0:T(8,128)(2,1)S(1)} %dynamic-slice_bitcast_fusion), channel_id=1, source_target_pairs={{0,1},{1,0},{2,3},{3,2},{4,5},{5,4},{6,7},{7,6},{8,9},{9,8},{10,11... | collective-permute-start | bytes 786440 | tf_op jit(solution)/shard_map/ppermute | solution.py:584
  6.5 2.0 %copy-start.11 = (bf16[512,128]{1,0:T(8,128)(2,1)}, bf16[512,128]{1,0:T(8,128)(2,1)S(1)}, u32[]{:S(2)}) copy-start(bf16[512,128]{1,0:T(8,128)(2,1)S(1)} %collective-permute-done.7.refs_13_) | copy-start | bytes 393220
  6.5 1.9 %collective-permute-start.6 = (bf16[3,256,128]{2,1,0:T(8,128)(2,1)}, bf16[3,256,128]{2,1,0:T(8,128)(2,1)S(1)}, u32[]{:S(2)}, u32[]{:S(2)}) collective-permute-start(bf16[3,256,128]{2,1,0:T(8,128)(2,1)} %refs_8_.1), channel_id=1, source_target_pairs={{0,1},{1,0},{2,3},{3,2},{4,5},{5,4},{6,7},{7,6},{8,9},{9,8},{10,11... | collective-permute-start | bytes 589832 | tf_op jit(solution)/shard_map/ppermute | solution.py:584
  8.4 0.8 copy-start.6
  8.4 0.8 copy-start.18
  8.4 1.0 %copy-start.2 = (bf16[9,256,128]{2,1,0:T(8,128)(2,1)}, bf16[9,256,128]{2,1,0:T(8,128)(2,1)S(1)}, u32[]{:S(2)}) copy-start(bf16[9,256,128]{2,1,0:T(8,128)(2,1)S(1)} %collective-permute-done.4.refs_5_.refs_3_) | copy-start | bytes 1769476
  9.4 0.8 copy-start.17
  27.7 3.2 %copy-start.1 = (bf16[3328,128]{1,0:T(8,128)(2,1)S(1)}, bf16[3328,128]{1,0:T(8,128)(2,1)}, u32[]{:S(2)}) copy-start(bf16[3328,128]{1,0:T(8,128)(2,1)} %get-tuple-element.64) | copy-start | bytes 2555908
  27.7 3.1 %collective-permute-start.8 = (bf16[3328,128]{1,0:T(8,128)(2,1)}, bf16[3328,128]{1,0:T(8,128)(2,1)S(1)}, u32[]{:S(2)}, u32[]{:S(2)}) collective-permute-start(bf16[3328,128]{1,0:T(8,128)(2,1)} %get-tuple-element.65), channel_id=1, source_target_pairs={{0,1},{1,0},{2,3},{3,2},{4,5},{5,4},{6,7},{7,6},{8,9},{9,8},{10,11... | collective-permute-start | bytes 2555912 | tf_op jit(solution)/shard_map/ppermute | solution.py:584
  31.1 12.7 %collective-permute-start.9 = (bf16[832,128]{1,0:T(8,128)(2,1)S(1)}, bf16[832,128]{1,0:T(8,128)(2,1)S(1)}, u32[]{:S(2)}, u32[]{:S(2)}) collective-permute-start(bf16[832,128]{1,0:T(8,128)(2,1)S(1)} %get-tuple-element.98), channel_id=1, source_target_pairs={{0,2},{2,0},{4,6},{6,4},{8,10},{10,8},{12,14},{14,12},{16,18},{18,... | collective-permute-start | bytes 638984 | tf_op jit(solution)/shard_map/ppermute | solution.py:584
  34.0 11.6 %collective-permute-start.10 = (bf16[832,128]{1,0:T(8,128)(2,1)S(1)}, bf16[832,128]{1,0:T(8,128)(2,1)S(1)}, u32[]{:S(2)}, u32[]{:S(2)}) collective-permute-start(bf16[832,128]{1,0:T(8,128)(2,1)S(1)} %get-tuple-element.97), channel_id=1, source_target_pairs={{0,4},{2,6},{4,0},{6,2},{8,12},{10,14},{12,8},{14,10},{16,20},{18,... | collective-permute-start | bytes 638984 | tf_op jit(solution)/shard_map/ppermute | solution.py:584
  35.5 10.1 %collective-permute-start.11 = (bf16[832,128]{1,0:T(8,128)(2,1)S(1)}, bf16[832,128]{1,0:T(8,128)(2,1)S(1)}, u32[]{:S(2)}, u32[]{:S(2)}) collective-permute-start(bf16[832,128]{1,0:T(8,128)(2,1)S(1)} %get-tuple-element.96), channel_id=1, source_target_pairs={{0,6},{2,4},{4,2},{6,0},{8,14},{10,12},{12,10},{14,8},{16,22},{18,... | collective-permute-start | bytes 638984 | tf_op jit(solution)/shard_map/ppermute | solution.py:584
  43.8 4.7 %copy-start.3 = (bf16[2304,128]{1,0:T(8,128)(2,1)S(1)}, bf16[2304,128]{1,0:T(8,128)(2,1)}, u32[]{:S(2)}) copy-start(bf16[2304,128]{1,0:T(8,128)(2,1)} %get-tuple-element.80) | copy-start | bytes 1769476
  45.6 0.8 copy-start.7
  46.3 2.2 %collective-permute-start.12 = (bf16[2304,128]{1,0:T(8,128)(2,1)}, bf16[2304,128]{1,0:T(8,128)(2,1)S(1)}, u32[]{:S(2)}, u32[]{:S(2)}) collective-permute-start(bf16[2304,128]{1,0:T(8,128)(2,1)} %get-tuple-element.81), channel_id=1, source_target_pairs={{0,1},{1,0},{2,3},{3,2},{4,5},{5,4},{6,7},{7,6},{8,9},{9,8},{10,11... | collective-permute-start | bytes 1769480 | tf_op jit(solution)/shard_map/ppermute | solution.py:584
  47.0 5.2 %copy-start.9 = (bf16[32,128]{1,0:T(8,128)(2,1)S(1)}, bf16[32,128]{1,0:T(8,128)(2,1)}, u32[]{:S(2)}) copy-start(bf16[32,128]{1,0:T(8,128)(2,1)} %get-tuple-element.74) | copy-start | bytes 24580
  48.6 10.7 %collective-permute-start.14 = (bf16[576,128]{1,0:T(8,128)(2,1)S(1)}, bf16[576,128]{1,0:T(8,128)(2,1)S(1)}, u32[]{:S(2)}, u32[]{:S(2)}) collective-permute-start(bf16[576,128]{1,0:T(8,128)(2,1)S(1)} %get-tuple-element.101), channel_id=1, source_target_pairs={{0,2},{2,0},{4,6},{6,4},{8,10},{10,8},{12,14},{14,12},{16,18},{18,... | collective-permute-start | bytes 442376 | tf_op jit(solution)/shard_map/ppermute | solution.py:584
  49.9 9.5 %collective-permute-start.15 = (bf16[576,128]{1,0:T(8,128)(2,1)S(1)}, bf16[576,128]{1,0:T(8,128)(2,1)S(1)}, u32[]{:S(2)}, u32[]{:S(2)}) collective-permute-start(bf16[576,128]{1,0:T(8,128)(2,1)S(1)} %get-tuple-element.100), channel_id=1, source_target_pairs={{0,4},{2,6},{4,0},{6,2},{8,12},{10,14},{12,8},{14,10},{16,20},{18,... | collective-permute-start | bytes 442376 | tf_op jit(solution)/shard_map/ppermute | solution.py:584
  50.8 8.6 %collective-permute-start.16 = (bf16[576,128]{1,0:T(8,128)(2,1)S(1)}, bf16[576,128]{1,0:T(8,128)(2,1)S(1)}, u32[]{:S(2)}, u32[]{:S(2)}) collective-permute-start(bf16[576,128]{1,0:T(8,128)(2,1)S(1)} %get-tuple-element.99), channel_id=1, source_target_pairs={{0,6},{2,4},{4,2},{6,0},{8,14},{10,12},{12,10},{14,8},{16,22},{18,... | collective-permute-start | bytes 442376 | tf_op jit(solution)/shard_map/ppermute | solution.py:584
  52.2 7.3 %collective-permute-start.13 = (bf16[864,128]{1,0:T(8,128)(2,1)S(1)}, bf16[864,128]{1,0:T(8,128)(2,1)S(1)}, u32[]{:S(2)}, u32[]{:S(2)}) collective-permute-start(bf16[864,128]{1,0:T(8,128)(2,1)S(1)} %pad_maximum_fusion.6), channel_id=1, source_target_pairs={{0,8},{1,17},{2,10},{3,19},{4,12},{5,21},{6,14},{7,23},{8,0},{9,25... | collective-permute-start | bytes 663560 | tf_op jit(solution)/shard_map/ppermute | solution.py:621
  60.2 15.8 %collective-permute-start.17 = (bf16[4,128,256]{2,1,0:T(8,128)(2,1)}, bf16[4,128,256]{2,1,0:T(8,128)(2,1)S(1)}, u32[]{:S(2)}, u32[]{:S(2)}) collective-permute-start(bf16[4,128,256]{2,1,0:T(8,128)(2,1)} %get-tuple-element.92), channel_id=1, source_target_pairs={{0,1},{1,0},{2,3},{3,2},{4,5},{5,4},{6,7},{7,6},{8,9},{9,8},{10,11... | collective-permute-start | bytes 786440 | tf_op jit(solution)/shard_map/ppermute | solution.py:584
  60.4 15.7 %collective-permute-start.18 = (bf16[4,128,256]{2,1,0:T(8,128)(2,1)}, bf16[4,128,256]{2,1,0:T(8,128)(2,1)S(1)}, u32[]{:S(2)}, u32[]{:S(2)}) collective-permute-start(bf16[4,128,256]{2,1,0:T(8,128)(2,1)} %get-tuple-element.94), channel_id=1, source_target_pairs={{0,1},{1,0},{2,3},{3,2},{4,5},{5,4},{6,7},{7,6},{8,9},{9,8},{10,11... | collective-permute-start | bytes 786440 | tf_op jit(solution)/shard_map/ppermute | solution.py:584
  60.8 15.2 %copy-start.4 = (f32[4,128,256]{2,1,0:T(8,128)S(1)}, f32[4,128,256]{2,1,0:T(8,128)}, u32[]{:S(2)}) copy-start(f32[4,128,256]{2,1,0:T(8,128)} %get-tuple-element.91) | copy-start | bytes 1572868
  60.8 10.3 %collective-permute-start.24 = (bf16[592,128]{1,0:T(8,128)(2,1)S(1)}, bf16[592,128]{1,0:T(8,128)(2,1)S(1)}, u32[]{:S(2)}, u32[]{:S(2)}) collective-permute-start(bf16[592,128]{1,0:T(8,128)(2,1)S(1)} %fusion.31), channel_id=1, source_target_pairs={{0,8},{1,17},{2,10},{3,19},{4,12},{5,21},{6,14},{7,23},{8,0},{9,25... | collective-permute-start | bytes 454664 | tf_op jit(solution)/shard_map/ppermute | solution.py:621
  63.0 10.8 %collective-permute-start.19 = (bf16[896,128]{1,0:T(8,128)(2,1)S(1)}, bf16[896,128]{1,0:T(8,128)(2,1)S(1)}, u32[]{:S(2)}, u32[]{:S(2)}) collective-permute-start(bf16[896,128]{1,0:T(8,128)(2,1)S(1)} %pad_maximum_fusion.5), channel_id=1, source_target_pairs={{0,16},{1,9},{2,18},{3,11},{4,20},{5,13},{6,22},{7,15},{8,24},{9,1... | collective-permute-start | bytes 688136 | tf_op jit(solution)/shard_map/ppermute | solution.py:621
  71.2 7.1 %collective-permute-start.25 = (bf16[592,128]{1,0:T(8,128)(2,1)S(1)}, bf16[592,128]{1,0:T(8,128)(2,1)S(1)}, u32[]{:S(2)}, u32[]{:S(2)}) collective-permute-start(bf16[592,128]{1,0:T(8,128)(2,1)S(1)} %add_convert_fusion.6), channel_id=1, source_target_pairs={{0,16},{1,9},{2,18},{3,11},{4,20},{5,13},{6,22},{7,15},{8,24},{9,1... | collective-permute-start | bytes 454664 | tf_op jit(solution)/shard_map/ppermute | solution.py:621
  73.8 2.3 %copy-start.5 = (f32[4,128,256]{2,1,0:T(8,128)S(1)}, f32[4,128,256]{2,1,0:T(8,128)}, u32[]{:S(2)}) copy-start(f32[4,128,256]{2,1,0:T(8,128)} %get-tuple-element.93) | copy-start | bytes 1572868
  73.9 19.5 %collective-permute-start.20 = (bf16[960,128]{1,0:T(8,128)(2,1)S(1)}, bf16[960,128]{1,0:T(8,128)(2,1)S(1)}, u32[]{:S(2)}, u32[]{:S(2)}) collective-permute-start(bf16[960,128]{1,0:T(8,128)(2,1)S(1)} %pad_maximum_fusion.4), channel_id=1, source_target_pairs={{0,2},{2,0},{4,6},{6,4},{8,10},{10,8},{12,14},{14,12},{16,18},{18,... | collective-permute-start | bytes 737288 | tf_op jit(solution)/shard_map/ppermute | solution.py:584
  75.1 18.2 %collective-permute-start.21 = (bf16[960,128]{1,0:T(8,128)(2,1)S(1)}, bf16[960,128]{1,0:T(8,128)(2,1)S(1)}, u32[]{:S(2)}, u32[]{:S(2)}) collective-permute-start(bf16[960,128]{1,0:T(8,128)(2,1)S(1)} %pad_maximum_fusion.4), channel_id=1, source_target_pairs={{0,4},{2,6},{4,0},{6,2},{8,12},{10,14},{12,8},{14,10},{16,20},{18,... | collective-permute-start | bytes 737288 | tf_op jit(solution)/shard_map/ppermute | solution.py:584
  78.3 7.8 %collective-permute-start.28 = (bf16[592,128]{1,0:T(8,128)(2,1)S(1)}, bf16[592,128]{1,0:T(8,128)(2,1)S(1)}, u32[]{:S(2)}, u32[]{:S(2)}) collective-permute-start(bf16[592,128]{1,0:T(8,128)(2,1)S(1)} %add_convert_fusion.5), channel_id=1, source_target_pairs={{0,6},{2,4},{4,2},{6,0},{8,14},{10,12},{12,10},{14,8},{16,22},{18,... | collective-permute-start | bytes 454664 | tf_op jit(solution)/shard_map/ppermute | solution.py:584
  79.9 9.1 %collective-permute-start.27 = (bf16[592,128]{1,0:T(8,128)(2,1)S(1)}, bf16[592,128]{1,0:T(8,128)(2,1)S(1)}, u32[]{:S(2)}, u32[]{:S(2)}) collective-permute-start(bf16[592,128]{1,0:T(8,128)(2,1)S(1)} %add_convert_fusion.5), channel_id=1, source_target_pairs={{0,4},{2,6},{4,0},{6,2},{8,12},{10,14},{12,8},{14,10},{16,20},{18,... | collective-permute-start | bytes 454664 | tf_op jit(solution)/shard_map/ppermute | solution.py:584
  81.4 7.6 %collective-permute-start.26 = (bf16[592,128]{1,0:T(8,128)(2,1)S(1)}, bf16[592,128]{1,0:T(8,128)(2,1)S(1)}, u32[]{:S(2)}, u32[]{:S(2)}) collective-permute-start(bf16[592,128]{1,0:T(8,128)(2,1)S(1)} %add_convert_fusion.5), channel_id=1, source_target_pairs={{0,2},{2,0},{4,6},{6,4},{8,10},{10,8},{12,14},{14,12},{16,18},{18,... | collective-permute-start | bytes 454664 | tf_op jit(solution)/shard_map/ppermute | solution.py:584
  86.2 7.1 %collective-permute-start.22 = (bf16[960,128]{1,0:T(8,128)(2,1)S(1)}, bf16[960,128]{1,0:T(8,128)(2,1)S(1)}, u32[]{:S(2)}, u32[]{:S(2)}) collective-permute-start(bf16[960,128]{1,0:T(8,128)(2,1)S(1)} %pad_maximum_fusion.4), channel_id=1, source_target_pairs={{0,6},{2,4},{4,2},{6,0},{8,14},{10,12},{12,10},{14,8},{16,22},{18,... | collective-permute-start | bytes 737288 | tf_op jit(solution)/shard_map/ppermute | solution.py:584
  89.0 1.6 %collective-permute-start.29 = (f32[2,256]{1,0:T(2,128)S(1)}, f32[2,256]{1,0:T(2,128)S(1)}, u32[]{:S(2)}, u32[]{:S(2)}) collective-permute-start(f32[2,256]{1,0:T(2,128)S(1)} %reshape.143), channel_id=1, source_target_pairs={{0,1},{1,0},{2,3},{3,2},{4,5},{5,4},{6,7},{7,6},{8,9},{9,8},{10,11... | collective-permute-start | bytes 6152 | tf_op jit(solution)/shard_map/ppermute | solution.py:584
  94.0 2.7 %collective-permute-start.23 = (bf16[512,128]{1,0:T(8,128)(2,1)S(1)}, bf16[512,128]{1,0:T(8,128)(2,1)S(1)}, u32[]{:S(2)}, u32[]{:S(2)}) collective-permute-start(bf16[512,128]{1,0:T(8,128)(2,1)S(1)} %get-tuple-element.110), channel_id=1, source_target_pairs={{0,1},{1,0},{2,3},{3,2},{4,5},{5,4},{6,7},{7,6},{8,9},{9,8},{10,11... | collective-permute-start | bytes 393224 | tf_op jit(solution)/shard_map/ppermute | solution.py:584
  95.6 1.7 %copy-start = (bf16[1024,512]{1,0:T(8,128)(2,1)S(1)}, bf16[1024,512]{1,0:T(8,128)(2,1)}, u32[]{:S(2)}) copy-start(bf16[1024,512]{1,0:T(8,128)(2,1)} %refs_17_.1) | copy-start | bytes 3145732
  96.8 2.3 %copy-start.10 = (bf16[512,128]{1,0:T(8,128)(2,1)S(1)}, bf16[512,128]{1,0:T(8,128)(2,1)}, u32[]{:S(2)}) copy-start(bf16[512,128]{1,0:T(8,128)(2,1)} %refs_12_.1) | copy-start | bytes 393220
  96.8 2.3 %copy-start.12 = (bf16[512,128]{1,0:T(8,128)(2,1)S(1)}, bf16[512,128]{1,0:T(8,128)(2,1)}, u32[]{:S(2)}) copy-start(bf16[512,128]{1,0:T(8,128)(2,1)} %copy-done.11) | copy-start | bytes 393220
  98.2 2.9 %copy-start.16 = (f32[128]{0:T(128)}, f32[128]{0:T(128)S(1)}, u32[]{:S(2)}) copy-start(f32[128]{0:T(128)S(1)} %get-tuple-element.163) | copy-start | bytes 1540
  (2 other events, 1.4 us)

commit v3 on v2

v3 whole, which is shorter than its diff:
```python
import functools
import math

import jax
import jax.numpy as jnp
from jax import lax
from jax.experimental import pallas as pl
from jax.experimental.pallas import tpu as pltpu
from jax.sharding import PartitionSpec as P

GROUPS = 32
LANES = 128
BLOCK = 32
EPS = 1e-06
MIB = 1024 * 1024
ANY = pl.BlockSpec(memory_space=pl.ANY)
VMEM = pl.BlockSpec(memory_space=pltpu.VMEM)
SMEM = pl.BlockSpec(memory_space=pltpu.SMEM)
f32 = jnp.float32
bf16 = jnp.bfloat16

(
    FIRST_GAIN,
    FIRST_SHIFT,
    FIRST_BIAS,
    TIME_BIAS,
    SECOND_GAIN,
    SECOND_SHIFT,
    SECOND_BIAS,
    THIRD_GAIN,
    THIRD_SHIFT,
    QUERY_BIAS,
    VALUE_BIAS,
    OUTPUT_BIAS,
) = range(12)


def nn(a, b):
    return lax.dot_general(a, b, (((1,), (0,)), ((), ())), preferred_element_type=f32)


def nt(a, b):
    return lax.dot_general(a, b, (((1,), (1,)), ((), ())), preferred_element_type=f32)


def sigmoid(v):
    return 0.5 * jnp.tanh(0.5 * v) + 0.5


def silu_slope(v, sig):
    return sig * (1.0 + v * (1.0 - sig))


def col_sum(v):
    return jnp.sum(v, axis=0, keepdims=True)


def lane_groups(v, width):
    lanes = v.shape[1]
    lane = lax.broadcasted_iota(jnp.int32, v.shape, 1)
    step = 1
    while step < width:
        up = pltpu.roll(v, step, 1)
        down = pltpu.roll(v, lanes - step, 1)
        v = v + jnp.where((lane & step) != 0, up, down)
        step *= 2
    return v


def fill_shift(shift_ref, side):
    points = shift_ref.shape[1]
    to = lax.broadcasted_iota(jnp.int32, (points, points), 0)
    of = lax.broadcasted_iota(jnp.int32, (points, points), 1)
    for d in range(3):
        s = d - 1
        col = (to & (side - 1)) + s
        hit = (of == to + s) & (col >= 0) & (col < side)
        shift_ref[d * points : (d + 1) * points, :] = jnp.where(hit, 1.0, 0.0).astype(bf16)


def zero_pads(pad_ref, side, points):
    images, chans = pad_ref.shape[1], pad_ref.shape[3]
    for d in range(3):
        for b in range(images):
            pad_ref[d, b, 0:side, :] = jnp.zeros((side, chans), bf16)
            pad_ref[d, b, side + points : 2 * side + points, :] = jnp.zeros((side, chans), bf16)


def put_moved(pad_ref, b, value, side, points):
    chans = value.shape[1]
    column = lax.broadcasted_iota(jnp.int32, (side, chans), 0)
    for d, edge in ((0, 0), (1, None), (2, side - 1)):
        moved = value
        if edge is not None:
            moved = pltpu.roll(value, (1 - d) % points, 0).reshape(side, side, chans)
            moved = jnp.where((column == edge)[None], 0.0, moved).reshape(points, chans)
        pad_ref[d, b, side : side + points, :] = moved.astype(bf16)


def put_pads(pad_ref, b, moved, side, points):
    for d in range(3):
        pad_ref[d, b, side : side + points, :] = moved[d * points : (d + 1) * points]


def taps(pad_ref, b, sign, side, points):
    out = []
    for dr in (-1, 0, 1):
        for dc in (-1, 0, 1):
            top = side + sign * dr * side
            out.append(pad_ref[1 + sign * dc, b, top : top + points, :])
    return out


class Copies:
    def __init__(self, sems):
        self.sems = sems
        self.used = 0

    def start(self, src, dst):
        copy = pltpu.make_async_copy(src, dst, self.sems.at[self.used])
        self.used += 1
        copy.start()
        return copy


def wait_all(copies):
    for c in copies:
        c.wait()


def side_of(points):
    return math.isqrt(points)


def load_split(cps, refs, dst, axis, places):
    out = []
    for ref, place in zip(refs, places, strict=True):
        size = ref.shape[axis]
        idx = [slice(None)] * len(ref.shape)
        idx[axis] = pl.ds(pl.multiple_of(place * size, size), size)
        out.append(cps.start(ref, dst.at[tuple(idx)]))
    return out


def load_images(cps, refs, dst, places, count):
    out = []
    for j, (ref, place) in enumerate(zip(refs, places, strict=True)):
        size = ref.shape[1]
        first = pl.multiple_of(places[0] * count, count) if j == 0 else 0
        out.append(
            cps.start(
                ref.at[pl.ds(first, count)],
                dst.at[:, pl.ds(pl.multiple_of(place * size, size), size), :],
            )
        )
    return out


def places_of(pieces):
    if pieces == 1:
        return [0]
    me = lax.axis_index("tensor")
    return [me, 1 - me]


def split_store(own_ref, send_ref, at, value, axis, places):
    if send_ref is None:
        own_ref[at] = value.astype(own_ref.dtype)
        return
    half = value.shape[axis] // 2
    low = lax.slice_in_dim(value, 0, half, axis=axis)
    high = lax.slice_in_dim(value, half, 2 * half, axis=axis)
    first = places[0] == 0
    own_ref[at] = jnp.where(first, low, high).astype(own_ref.dtype)
    send_ref[at] = jnp.where(first, high, low).astype(send_ref.dtype)


def pack_store(own_ref, send_ref, at, value, axis, places):
    half = value.shape[axis] // 2
    low = lax.slice_in_dim(value, 0, half, axis=axis)
    high = lax.slice_in_dim(value, half, 2 * half, axis=axis)
    first = places[0] == 0
    own = jnp.where(first, low, high).astype(own_ref.dtype)
    send = jnp.where(first, high, low).astype(send_ref.dtype)
    rows = own.shape[0]
    for i in range(own.shape[1] // LANES):
        lanes = slice(i * LANES, (i + 1) * LANES)
        own_ref[at : at + rows, :] = own[:, lanes]
        send_ref[at : at + rows, :] = send[:, lanes]
        at += rows
    return at


def pack_kernel(n_vec, *refs):
    vectors, arrays = refs[:n_vec], refs[n_vec : n_vec + 2]
    vec, x_half, g_half, sems = refs[n_vec + 2 :]
    cps = Copies(sems)
    count = x_half.shape[0]
    first = pl.multiple_of((1 - lax.axis_index("tensor")) * count, count)
    copies = [
        cps.start(src.at[pl.ds(first, count)], dst)
        for src, dst in zip(arrays, (x_half, g_half), strict=True)
    ]
    copies += [cps.start(v, vec.at[j]) for j, v in enumerate(vectors)]
    vec[n_vec:, :] = jnp.zeros((16 - n_vec, vec.shape[1]), f32)
    wait_all(copies)


def part(value, b, points):
    return value[b * points : (b + 1) * points]


def lane_part(value, b, points):
    return value[:, b * points : (b + 1) * points]


def norm_first(x, size, width):
    x3 = x.astype(f32).reshape(GROUPS, width, x.shape[1])
    mean = jnp.sum(jnp.sum(x3, axis=2, keepdims=True), axis=1, keepdims=True) / size
    off = x3 - mean
    var = jnp.sum(jnp.sum(off * off, axis=2, keepdims=True), axis=1, keepdims=True) / size
    rstd = lax.rsqrt(var + EPS)
    return (off * rstd).reshape(x.shape), rstd


def moments(value, width, size):
    mean = lane_groups(col_sum(value), width) / size
    off = value - mean
    return mean, lax.rsqrt(lane_groups(col_sum(off * off), width) / size + EPS)


def pipelined(stages, count):
    for t in range(count + len(stages) - 1):
        for i in reversed(range(len(stages))):
            if 0 <= t - i < count:
                stages[i](t - i)


def front_kernel(pieces, count, *refs):
    it = iter(refs)

    def take(n):
        return [next(it) for _ in range(n)]

    x_in, g_in, w1_in, w2_in, pi_in, po_in, tw_in, vec_in = (take(pieces) for _ in range(8))
    steps_ref, table_ref = take(2)
    if pieces == 2:
        own_out, send_out = take(2)
    else:
        dw2_own, dpo_own, dpi_own = take(3)
    vec_out, stat_out = take(2)
    w1_out, w2_out, po_out, all_vec_out, x_out = take(5)
    gpad_out, sum_out, a1t_out, resid_out, gres_out, mix_out = take(6)
    if pieces == 2:
        own, send = take(2)
    w1, w2, po, vec, xin = take(5)
    gpad, sum_one, a1t, resid, gres, mix = take(6)
    gin, pi, tw, rows, shift, apad, bpad = take(7)
    sems = next(it)

    cps = Copies(sems)
    places = places_of(pieces)
    chans, points = xin.shape[1], xin.shape[2]
    side = side_of(points)
    width = chans // GROUPS
    size = float(width * points)
    scale = chans ** (-0.5)
    images = range(count)

    x_cp = load_images(cps, x_in, xin, places, count)
    vec_cp = load_split(cps, vec_in, vec, 1, places)
    w1_cp = load_split(cps, w1_in, w1, 2, places)
    row_cp = []
    for b in images:
        step = steps_ref[places[0] * count + b]
        row_cp.append(
            cps.start(table_ref.at[pl.ds(pl.multiple_of(step // 16 * 16, 16), 16), :], rows.at[b])
        )
    tw_cp = load_split(cps, tw_in, tw, 1, places)
    w2_cp = load_split(cps, w2_in, w2, 1, places)
    pi_cp = load_split(cps, pi_in, pi, 2, places)
    po_cp = load_split(cps, po_in, po, 0, places)
    g_cp = load_images(cps, g_in, gin, places, count)

    fill_shift(shift, side)
    zero_pads(apad, side, points)
    zero_pads(bpad, side, points)
    zero_pads(gpad, side, points)
    eye = shift[points : 2 * points, :]

    wait_all(vec_cp)
    vcols = jnp.transpose(vec[...])

    def col(j):
        return vcols[:, j : j + 1]

    def row(j):
        return vec[j : j + 1, :]

    wait_all(x_cp)
    wait_all(row_cp)
    wait_all(tw_cp)
    wait_all(w1_cp)
    outs = [cps.start(vec, all_vec_out), cps.start(xin, x_out), cps.start(w1, w1_out)]
    picked = []
    for b in images:
        step = steps_ref[places[0] * count + b]
        r = lax.broadcasted_iota(jnp.int32, (16, rows.shape[2]), 0)
        picked.append(col_sum(jnp.where(r == lax.rem(step, 16), rows[b].astype(f32), 0.0)))
    emb = jnp.concatenate(picked + picked[:1] * (8 - count), axis=0)
    time_add = nn((emb * sigmoid(emb)).astype(bf16), tw[...]) + row(TIME_BIAS) + row(FIRST_BIAS)

    stats2, stats3 = [], []
    act_t = [None] * count

    def norm_one(b):
        hat, _ = norm_first(xin[b], size, width)
        pre = hat * col(FIRST_GAIN) + col(FIRST_SHIFT)
        act = (pre * sigmoid(pre)).astype(bf16)
        a1t[b] = act
        put_pads(apad, b, nt(shift[...], act).astype(bf16), side, points)

    def conv_one(b):
        lhs = jnp.concatenate(taps(apad, b, 1, side, points), axis=1)
        sum_one[b] = nn(lhs, w1[...].reshape(9 * chans, chans)) + time_add[b : b + 1]

    def norm_two(b):
        mean, rstd = moments(sum_one[b], width, size)
        stats2.append((mean, rstd))
        hat = (sum_one[b] - mean) * rstd
        pre = hat * row(SECOND_GAIN) + row(SECOND_SHIFT)
        act = pre * sigmoid(pre)
        act_t[b] = jnp.transpose(act.astype(bf16))
        put_moved(bpad, b, act, side, points)

    def conv_two(b):
        if b == 0:
            wait_all(w2_cp)
        lhs = jnp.concatenate(taps(bpad, b, 1, side, points), axis=1)
        val = nn(lhs, w2[...].reshape(9 * chans, chans)) + row(SECOND_BIAS)
        resid[b] = val + nt(eye, xin[b])

    normed = []

    def norm_three(b):
        mean, rstd = moments(resid[b], width, size)
        stats3.append((mean, rstd))
        hat = (resid[b] - mean) * rstd
        normed.append((hat * row(THIRD_GAIN) + row(THIRD_SHIFT)).astype(bf16))

    pipelined([norm_one, conv_one, norm_two, conv_two, norm_three], count)
    outs += [cps.start(a1t, a1t_out), cps.start(sum_one, sum_out), cps.start(resid, resid_out)]
    stat_out[0, 0:count, :] = jnp.concatenate([m for m, _ in stats2], axis=0)
    stat_out[1, 0:count, :] = jnp.concatenate([r for _, r in stats2], axis=0)

    wait_all(pi_cp)
    wait_all(po_cp)
    wait_all(g_cp)
    outs += [cps.start(w2, w2_out), cps.start(po, po_out)]
    pi_row = jnp.concatenate([pi[0], pi[1], pi[2]], axis=1)
    pi_t = jnp.concatenate([jnp.transpose(pi[1]), jnp.transpose(pi[2])], axis=0)
    zero = jnp.zeros((1, chans), f32)
    normed_t = jnp.concatenate([jnp.transpose(v) for v in normed], axis=1)
    normed = jnp.concatenate(normed, axis=0)
    lin = nn(normed, pi_row)
    q = (lin[:, :chans] + row(QUERY_BIAS)).astype(bf16)
    k = lin[:, chans : 2 * chans].astype(bf16)
    v = (lin[:, 2 * chans :] + row(VALUE_BIAS)).astype(bf16)
    lin_t = nn(pi_t, normed_t)
    kt = lin_t[:chans].astype(bf16)
    vt = (lin_t[chans:] + col(VALUE_BIAS)).astype(bf16)
    grad_all = jnp.concatenate([gin[b] for b in images], axis=1)
    grad_mixed = nn(po[...], grad_all).astype(bf16)
    scores = [nt(part(k, b, points), part(q, b, points)) for b in images]
    grad_w = [nn(part(v, b, points), lane_part(grad_mixed, b, points)) for b in images]
    weights, grad_s = [], []
    for b in images:
        top = scores[b] * scale
        expo = jnp.exp(top - jnp.max(top, axis=0, keepdims=True))
        probs = expo * (1.0 / jnp.sum(expo, axis=0, keepdims=True))
        weights.append(probs.astype(bf16))
        inner = probs * grad_w[b]
        grad_s.append((inner - probs * jnp.sum(inner, axis=0, keepdims=True)).astype(bf16))
    mixed = []
    for b in images:
        mixed.append(nn(lane_part(vt, b, points), weights[b]).astype(bf16))
        mix[b] = mixed[b]
    outs.append(cps.start(mix, mix_out))
    grad_qt = [nn(lane_part(kt, b, points), grad_s[b]) * scale for b in images]
    grad_q = [jnp.transpose(t.astype(bf16)) for t in grad_qt]
    grad_k = [(nn(grad_s[b], part(q, b, points)) * scale).astype(bf16) for b in images]
    grad_v = [nt(weights[b], lane_part(grad_mixed, b, points)).astype(bf16) for b in images]
    lin_grad = jnp.concatenate(
        [jnp.concatenate([grad_q[b], grad_k[b], grad_v[b]], axis=1) for b in images], axis=0
    )
    qb_grad = col_sum(sum(t.astype(f32) for t in grad_q))
    vb_grad = col_sum(sum(t.astype(f32) for t in grad_v))
    dpo = nt(jnp.concatenate(mixed, axis=1), grad_all)
    grad_normed = nt(lin_grad, pi_row)

    gain3, shift3, means = [], [], []
    for b in images:
        hat = (resid[b] - stats3[b][0]) * stats3[b][1]
        val = part(grad_normed, b, points)
        gain3.append(col_sum(val * hat))
        shift3.append(col_sum(val))
        both = jnp.concatenate([shift3[b], gain3[b]], axis=0) * row(THIRD_GAIN)
        means.append(lane_groups(both, width) / size)
    sb_grad, ob_grad = zero, zero
    for b in images:
        hat = (resid[b] - stats3[b][0]) * stats3[b][1]
        h = part(grad_normed, b, points) * row(THIRD_GAIN)
        grad_out = nt(eye, gin[b])
        ob_grad = ob_grad + col_sum(grad_out)
        val = grad_out + stats3[b][1] * (h - means[b][0:1] - hat * means[b][1:2])
        gres[b] = val
        sb_grad = sb_grad + col_sum(val)
        put_moved(gpad, b, val, side, points)
    outs += [cps.start(gres, gres_out), cps.start(gpad, gpad_out)]

    dpi = nn(normed_t, lin_grad)
    at = 0
    if pieces == 2:
        at = pack_store(own, send, at, dpo, 0, places)
        for j in range(3):
            at = pack_store(own, send, at, dpi[:, j * chans : (j + 1) * chans], 1, places)
        outs += copy_rows(cps, [(send, send_out), (own, own_out)], 0, at)
    else:
        dpo_own[...] = dpo
        for j in range(3):
            dpi_own[j] = dpi[:, j * chans : (j + 1) * chans]

    a_all = jnp.concatenate(act_t, axis=1)
    moved = [taps(gpad, b, -1, side, points) for b in images]
    for tap in range(9):
        val = nn(a_all, jnp.concatenate([moved[b][tap] for b in images], axis=0))
        if pieces == 2:
            start = at if tap % 3 == 0 else start
            at = pack_store(own, send, at, val, 0, places)
            if tap % 3 == 2:
                outs += copy_rows(cps, [(send, send_out), (own, own_out)], start, at)
        else:
            dw2_own[tap] = val

    gain3 = jnp.concatenate(gain3, axis=0)
    shift3 = jnp.concatenate(shift3, axis=0)
    vec_out[...] = jnp.concatenate(
        [sb_grad, col_sum(gain3), col_sum(shift3), qb_grad, vb_grad, ob_grad, zero, zero], axis=0
    )
    wait_all(outs)


def copy_rows(cps, pairs, start, end):
    rows = slice(start, end)
    return [cps.start(src.at[rows], dst.at[rows]) for src, dst in pairs]


def back_kernel(pieces, count, *refs):
    it = iter(refs)

    def take(n):
        return [next(it) for _ in range(n)]

    kept = take(11)
    stat, vec_a, steps_ref = take(3)
    if pieces == 2:
        own_out, send_out, block_own_out, block_send_out, image_own_out, image_send_out = take(6)
    else:
        own, block_own_out, image_own_out = take(3)
        block_send_out = image_send_out = None
    small_out = next(it)
    w1, w2, po, vec, xin, gpad, sum_one, a1t, resid, gres, mix = take(11)
    if pieces == 2:
        own, send, block_own, block_send, image_own, image_send = take(6)
    else:
        block_own, image_own = take(2)
        block_send = image_send = None
    hpad, back, sems = take(3)
    cps = Copies(sems)
    places = places_of(pieces)
    points, chans = sum_one.shape[1], sum_one.shape[2]
    side = side_of(points)
    width = chans // GROUPS
    size = float(width * points)
    images = range(count)

    w1_in, w2_in, po_in, vec_in, x_in, gpad_in, sum_in, a1t_in, resid_in, gres_in, mix_in = kept
    w2_cp = cps.start(w2_in, w2)
    gpad_cp = [cps.start(gpad_in.at[:, b], gpad.at[:, b]) for b in images]
    vec_cp = cps.start(vec_in, vec)
    sum_cp = cps.start(sum_in, sum_one)
    a1t_cp = cps.start(a1t_in, a1t)
    later = [(w1_in, w1), (po_in, po), (x_in, xin), (resid_in, resid), (gres_in, gres), (mix_in, mix)]
    later = [cps.start(src, dst) for src, dst in later]

    def row(j):
        return vec[j : j + 1, :]

    zero_pads(hpad, side, points)
    w2_cp.wait()
    w2_cols = jnp.concatenate([w2[k] for k in range(9)], axis=1)
    gain, shift_g, times = [], [], []

    def conv_back(b):
        gpad_cp[b].wait()
        back[b] = nt(jnp.concatenate(taps(gpad, b, -1, side, points), axis=1), w2_cols)

    def norm_back(b):
        if b == 0:
            sum_cp.wait()
            vec_cp.wait()
        mean, rstd = stat[0, b : b + 1, :], stat[1, b : b + 1, :]
        hat = (sum_one[b] - mean) * rstd
        pre = hat * row(SECOND_GAIN) + row(SECOND_SHIFT)
        val = back[b] * silu_slope(pre, sigmoid(pre))
        gain.append(col_sum(val * hat))
        shift_g.append(col_sum(val))
        both = jnp.concatenate([shift_g[b], gain[b]], axis=0) * row(SECOND_GAIN)
        both = lane_groups(both, width) / size
        val = rstd * (val * row(SECOND_GAIN) - both[0:1] - hat * both[1:2])
        times.append(col_sum(val))
        put_moved(hpad, b, val, side, points)

    pipelined([conv_back, norm_back], count)

    a1t_cp.wait()
    a_all = jnp.concatenate([a1t[b] for b in images], axis=1)
    moved = [taps(hpad, b, -1, side, points) for b in images]
    at = 0
    outs = []
    for tap in range(9):
        val = nn(a_all, jnp.concatenate([moved[b][tap] for b in images], axis=0))
        if pieces == 2:
            start = at if tap % 3 == 0 else start
            at = pack_store(own, send, at, val, 1, places)
            if tap % 3 == 2:
                outs += copy_rows(cps, [(send, send_out), (own, own_out)], start, at)
        else:
            own[tap] = val

    wait_all(later)
    vcols = jnp.transpose(vec[...])

    def col(j):
        return vcols[:, j : j + 1]

    def put_out(own_ref, send_ref, own_dst, send_dst, b, val):
        split_store(own_ref, send_ref, b, val, 0, places)
        outs.append(cps.start(own_ref.at[b], own_dst.at[b]))
        if send_ref is not None:
            outs.append(cps.start(send_ref.at[b], send_dst.at[b]))

    proj = nn(jnp.transpose(po[...]), jnp.concatenate([mix[b] for b in images], axis=1))

    w1_cols = jnp.concatenate([w1[k] for k in range(9)], axis=1)
    zero = jnp.zeros((chans, 1), f32)
    gain_sum, shift_sum = [zero], [zero]
    first_back = [None] * count

    def groups(v):
        total = jnp.sum(v.reshape(GROUPS, width, 1), axis=1, keepdims=True) / size
        return jnp.broadcast_to(total, (GROUPS, width, 1)).reshape(chans, 1)

    def conv_first(b):
        first_back[b] = nt(w1_cols, jnp.concatenate(taps(hpad, b, -1, side, points), axis=1))

    def block_part(b):
        val = jnp.transpose(resid[b]) + lane_part(proj, b, points) + col(OUTPUT_BIAS)
        put_out(block_own, block_send, block_own_out, block_send_out, b, val)

    def norm_first_back(b):
        hat, rstd = norm_first(xin[b], size, width)
        rstd = jnp.broadcast_to(rstd, (GROUPS, width, 1)).reshape(chans, 1)
        pre = hat * col(FIRST_GAIN) + col(FIRST_SHIFT)
        val = first_back[b] * silu_slope(pre, sigmoid(pre))
        gain = jnp.sum(val * hat, axis=1, keepdims=True)
        shift = jnp.sum(val, axis=1, keepdims=True)
        gain_sum[0] = gain_sum[0] + gain
        shift_sum[0] = shift_sum[0] + shift
        first_mean = groups(shift * col(FIRST_GAIN))
        second_mean = groups(gain * col(FIRST_GAIN))
        val = rstd * (val * col(FIRST_GAIN) - first_mean - hat * second_mean)
        val = val + jnp.transpose(gres[b])
        put_out(image_own, image_send, image_own_out, image_send_out, b, val)

    pipelined([conv_first, block_part, norm_first_back], count)

    lane = lax.broadcasted_iota(jnp.int32, (chans, LANES), 1)
    both = jnp.where(lane == 0, gain_sum[0], 0.0) + jnp.where(lane == 1, shift_sum[0], 0.0)
    both = jnp.transpose(both)
    rows = [vec_a[j : j + 1, :] for j in range(6)]
    rows += [sum(gain), sum(shift_g), sum(times), both[0:1], both[1:2]]
    lane = lax.broadcasted_iota(jnp.int32, (1, LANES), 1)
    stamp = jnp.zeros((1, LANES), f32)
    for b in images:
        step = jnp.full((1, LANES), steps_ref[places[0] * count + b], jnp.int32)
        stamp = jnp.where(lane == b, (step >> 5).astype(f32), stamp)
        stamp = jnp.where(lane == LANES // 2 + b, (step & 31).astype(f32), stamp)
    flat = []
    for r in rows + times:
        flat += [r[:, i * LANES : (i + 1) * LANES] for i in range(chans // LANES)]
    flat.append(stamp)
    flat += [jnp.zeros((1, LANES), f32)] * (BLOCK - len(flat))
    small_out[...] = jnp.concatenate(flat, axis=0).astype(bf16)
    wait_all(outs)


def swap(value, axis, size, bit):
    return lax.ppermute(value, axis, [(i, i ^ bit) for i in range(size)])


def near_parts(part):
    me = lax.axis_index("batch") & 3
    return [part(me ^ j).astype(bf16) for j in range(1, 4)]


def after(values, *others):
    done = lax.optimization_barrier((tuple(values), others))
    return list(done[0])


def send_near(sent, batch):
    return [swap(v, "batch", batch, j + 1) for j, v in enumerate(sent)]


def sum_near(got, part):
    total = part(lax.axis_index("batch") & 3).astype(f32)
    for g in got:
        total = total + g.astype(f32)
    return total.astype(bf16)


def far_steps(batch):
    return batch.bit_length() - 3


def send_far(piece, extra, step, batch):
    steps = far_steps(batch)
    mine = piece if extra is None else jnp.concatenate([piece, extra], axis=0)
    tensor = lax.axis_size("tensor")
    pairs = []
    for i in range(batch):
        for core in range(tensor):
            bit = 4 << (step if core % 2 == 0 else steps - 1 - step)
            pairs.append((i * tensor + core, (i ^ bit) * tensor + core))
    return lax.ppermute(mine, ("batch", "tensor"), pairs)


def sum_far(piece, extra, got):
    rows = piece.shape[0]
    piece = (piece.astype(f32) + got[:rows].astype(f32)).astype(bf16)
    if extra is not None:
        extra = jnp.concatenate([extra, got[rows:]], axis=0)
    return piece, extra


def gather_near(piece, batch):
    return [piece] + [swap(piece, "batch", batch, j) for j in range(1, 4)]


def in_order(pieces):
    me = lax.axis_index("batch")
    parts = jnp.stack(pieces, axis=0)
    parts = parts.reshape((2, 2) + parts.shape[1:])
    parts = jnp.where((me & 1) == 1, jnp.flip(parts, axis=1), parts)
    parts = jnp.where((me & 2) == 2, jnp.flip(parts, axis=0), parts)
    return parts.reshape((-1, LANES))


def unpack(flat, shapes):
    out = []
    at = 0
    for shape in shapes:
        n = math.prod(shape) // 128
        out.append(flat[at : at + n].reshape(shape).astype(f32))
        at += n
    return out


def per_device(
    batch,
    tensor,
    images,
    timesteps,
    embed_table,
    first_gain,
    first_shift,
    first_conv,
    first_bias,
    time_weight,
    time_bias,
    second_gain,
    second_shift,
    second_conv,
    second_bias,
    third_gain,
    third_shift,
    project_in,
    query_bias,
    value_bias,
    project_out,
    output_bias,
    cotangent,
):
    per_batch, local, points = images.shape
    chans = local * tensor
    count = per_batch // tensor
    steps, embed = embed_table.shape
    pieces = 2 if tensor == 2 else 1
    me = lax.axis_index("tensor")
    vectors = [
        first_gain,
        first_shift,
        first_bias,
        time_bias,
        second_gain,
        second_shift,
        second_bias,
        third_gain,
        third_shift,
        query_bias,
        value_bias,
        output_bias,
    ]
    def in_hbm(array):
        return pltpu.with_memory_space_constraint(array, pltpu.HBM)

    n_vec = len(vectors)
    if pieces == 2:
        half = (count, local, points)
        vec, x_half, g_half = pl.pallas_call(
            functools.partial(pack_kernel, n_vec),
            out_shape=[
                jax.ShapeDtypeStruct((16, local), f32),
                jax.ShapeDtypeStruct(half, bf16),
                jax.ShapeDtypeStruct(half, bf16),
            ],
            in_specs=[ANY] * (n_vec + 2),
            out_specs=[VMEM] * 3,
            scratch_shapes=[pltpu.SemaphoreType.DMA((n_vec + 2,))],
            compiler_params=pltpu.CompilerParams(vmem_limit_bytes=4 * MIB),
            name="pack",
        )(*(in_hbm(v) for v in vectors + [images, cotangent]))
    else:
        vec = jnp.stack(vectors + [output_bias] * 4, axis=0)
        x_half = g_half = None

    def images_of(array, half):
        if pieces == 2:
            return [array, swap(half, "tensor", 2, 1)]
        return [lax.all_to_all(array, "tensor", 0, 1, tiled=True)]

    def whole(array, axis):
        if pieces == 2:
            return [array, swap(array, "tensor", 2, 1)]
        return [lax.all_gather(array, "tensor", axis=axis, tiled=True)]

    x_in = images_of(images, x_half)
    vec_in = whole(vec, 1)
    tw_in = whole(time_weight, 1)
    w1_in = whole(first_conv, 2)
    w2_in = whole(second_conv, 1)
    pi_in = whole(project_in, 2)
    po_in = whole(project_out, 0)
    g_in = images_of(cotangent, g_half)
    my_steps = timesteps if pieces == 2 else lax.dynamic_slice_in_dim(timesteps, me * count, count)

    side = side_of(points)
    image_b = (count, chans, points)
    image_p = (count, points, chans)
    pads = (3, count, points + 2 * side, chans)

    def shape(s, d):
        return jax.ShapeDtypeStruct(s, d)

    def params(mib):
        return pltpu.CompilerParams(vmem_limit_bytes=mib * MIB)

    def cost(units, moved):
        flops = 2 * units * count * points * chans * chans
        return pl.CostEstimate(flops=flops, bytes_accessed=moved, transcendentals=0)

    half_b = 9 * chans * chans // 2 // LANES
    half_a = half_b + 4 * chans * chans // 2 // LANES
    if pieces == 2:
        grads_a = [pltpu.HBM((half_a, LANES), bf16)] * 2
        grads_b = [pltpu.HBM((half_b, LANES), bf16)] * 2
    else:
        grads_a = [shape((9, chans, chans), f32), shape((chans, chans), f32)]
        grads_a.append(shape((3, chans, chans), f32))
        grads_b = [shape((9, chans, chans), f32)]
    n_grad = len(grads_a)
    steps_in = in_hbm(my_steps)
    kept = [
        ((9, chans, chans), bf16),
        ((9, chans, chans), bf16),
        ((chans, chans), bf16),
        ((16, chans), f32),
        (image_b, bf16),
        (pads, bf16),
        (image_p, f32),
        (image_b, bf16),
        (image_p, f32),
        (image_p, f32),
        (image_b, bf16),
    ]
    out_a = ANY if pieces == 2 else VMEM
    scratch_a = [pltpu.VMEM(v.shape, v.dtype) for v in grads_a] if pieces == 2 else []

    front = pl.pallas_call(
        functools.partial(front_kernel, pieces, count),
        out_shape=grads_a
        + [shape((8, chans), f32), shape((2, count, chans), f32)]
        + [pltpu.HBM(*v) for v in kept],
        in_specs=[ANY] * (8 * pieces) + [SMEM, ANY],
        out_specs=[out_a] * n_grad + [VMEM] * 2 + [ANY] * len(kept),
        scratch_shapes=scratch_a
        + [pltpu.VMEM(*v) for v in kept]
        + [
            pltpu.VMEM(image_b, bf16),
            pltpu.VMEM((3, chans, chans), bf16),
            pltpu.VMEM((embed, chans), bf16),
            pltpu.VMEM((count, 16, embed), bf16),
            pltpu.VMEM((3 * points, points), bf16),
            pltpu.VMEM(pads, bf16),
            pltpu.VMEM(pads, bf16),
            pltpu.SemaphoreType.DMA((8 * pieces + count + 19,)),
        ],
        compiler_params=params(32),
        cost_estimate=cost(54, 12 << 20),
        name="front",
    )(
        *(in_hbm(v) for v in x_in + g_in + w1_in + w2_in + pi_in + po_in + tw_in + vec_in),
        steps_in,
        in_hbm(embed_table),
    )
    sums_a = front[:n_grad]
    vec_a, stat, w1, w2, po, vec, xin = front[n_grad : n_grad + 7]
    gpad, sum_one, a1t, resid, gres, mix = front[n_grad + 7 :]

    def quarters(sums, axes):
        if pieces == 2:
            got = swap(sums[1], "tensor", 2, 1)
            rows = got.shape[0] // 4
            own4, got4 = (v.reshape(4, rows, LANES) for v in (sums[0], got))

            def part(q):
                pair = [lax.dynamic_index_in_dim(v, q, 0, False).astype(f32) for v in (own4, got4)]
                return pair[0] + pair[1]

            return part
        done = [
            lax.psum_scatter(v, "tensor", scatter_dimension=axis, tiled=True)
            for v, axis in zip(sums, axes, strict=True)
        ]
        flat = jnp.concatenate([v.reshape(-1, LANES) for v in done], axis=0)
        flat = jnp.pad(flat, ((0, -flat.shape[0] % 64), (0, 0)))
        rows = flat.shape[0] // 4
        flat = flat.reshape(4, rows, LANES)
        return lambda q: lax.dynamic_index_in_dim(flat, q, 0, False)

    part_a = quarters(sums_a, (1, 0, 2))
    sent_a = near_parts(part_a)

    got_a = send_near(sent_a, batch)
    (vec_a,) = after([vec_a], *sent_a)

    half = (count, chans // 2, points)
    if pieces == 2:
        outs_b = grads_b + [pltpu.HBM(half, f32), pltpu.HBM(half, bf16)] * 2
        scratch_b = [pltpu.VMEM(v.shape, v.dtype) for v in outs_b]
    else:
        outs_b = grads_b + [pltpu.HBM(image_b, f32)] * 2
        scratch_b = [pltpu.VMEM(image_b, f32)] * 2
    *outs_b, block = pl.pallas_call(
        functools.partial(back_kernel, pieces, count),
        out_shape=outs_b + [shape((BLOCK, LANES), bf16)],
        in_specs=[ANY] * len(kept) + [VMEM] * 2 + [SMEM],
        out_specs=[out_a] * pieces + [ANY] * (2 * pieces) + [VMEM],
        scratch_shapes=[pltpu.VMEM(*v) for v in kept]
        + scratch_b
        + [
            pltpu.VMEM(pads, bf16),
            pltpu.VMEM(image_p, f32),
            pltpu.SemaphoreType.DMA((6 + 5 * count + 10,)),
        ],
        compiler_params=params(36),
        cost_estimate=cost(33, 12 << 20),
        name="back",
    )(
        *(in_hbm(v) for v in (w1, w2, po, vec, xin, gpad, sum_one, a1t, resid, gres, mix)),
        stat,
        vec_a,
        steps_in,
    )
    sums_b, block_part, image_grad = outs_b[:pieces], outs_b[pieces : 2 * pieces], outs_b[2 * pieces :]
    got_a = after(got_a, block)
    sums_b = after(sums_b, *got_a)
    piece_a = sum_near(got_a, part_a)
    part_b = quarters(sums_b, (2,))
    sent_b = near_parts(part_b)
    got_b = send_near(sent_b, batch)
    (piece_a,) = after([piece_a], *sent_b)
    blocks = block
    for step in range(far_steps(batch)):
        piece_a, blocks = sum_far(piece_a, blocks, send_far(piece_a, blocks, step, batch))

    def placed(own, send):
        if pieces == 2:
            got = swap(send, "tensor", 2, 1).astype(f32)
            low = jnp.where(me == 0, own, got)
            high = jnp.where(me == 0, got, own)
            return jnp.concatenate([low, high], axis=0)
        return lax.all_to_all(own, "tensor", 1, 0, tiled=True)

    block_out = placed(block_part[0], block_part[-1])
    images_grad = placed(image_grad[0], image_grad[-1])

    piece_b = sum_near(got_b, part_b)
    for step in range(far_steps(batch)):
        piece_b, _ = sum_far(piece_b, None, send_far(piece_b, None, step, batch))
    rows_a = piece_a.shape[0]
    got_a = gather_near(jnp.concatenate([piece_a, blocks], axis=0), batch)
    got_a = after(got_a, piece_b)
    done_a = in_order([g[:rows_a] for g in got_a])
    blocks = jnp.concatenate([g[rows_a:] for g in got_a], axis=0)
    (piece_b,) = after([piece_b], *got_a)
    done_b = in_order(gather_near(piece_b, batch))

    if pieces == 2:
        n = chans * chans // 2 // LANES
        project_out_grad = done_a[:n].reshape(2, local, LANES)
        project_out_grad = jnp.concatenate([project_out_grad[0], project_out_grad[1]], axis=1)
        project_in_grad = done_a[n : 4 * n].reshape(3, chans, local)
        taps_grad = done_a[4 * n :].reshape(9, 2, local, LANES)
        second_conv_grad = jnp.concatenate([taps_grad[:, 0], taps_grad[:, 1]], axis=2)
        first_conv_grad = done_b.reshape(9, chans, local)
    else:
        second_conv_grad, project_out_grad, project_in_grad = unpack(
            done_a, [(9, local, chans), (local, chans), (3, chans, local)]
        )
        (first_conv_grad,) = unpack(done_b, [(9, chans, local)])

    if pieces == 2:
        blocks = jnp.concatenate([blocks, swap(blocks, "tensor", 2, 1)], axis=0)
        two = blocks.reshape(2, batch, BLOCK, LANES)
        blocks = jnp.where(me == 0, two, jnp.flip(two, axis=0))
    else:
        blocks = lax.all_gather(blocks, "tensor", axis=0, tiled=True)
    blocks = blocks.reshape(batch * tensor, BLOCK, LANES)
    wide = chans // LANES
    n_sum = 11 * wide
    sums = jnp.sum(blocks[:, :n_sum].astype(f32), axis=0).reshape(11, chans)
    mine = lax.dynamic_slice_in_dim(sums, me * local, local, axis=1)
    all_times = blocks[:, n_sum : n_sum + wide * count].reshape(-1, chans)
    stamps = blocks[:, n_sum + wide * count].astype(jnp.int32)
    all_steps = stamps[:, :count] * 32 + stamps[:, LANES // 2 : LANES // 2 + count]
    all_steps = all_steps.reshape(-1)
    one_hot = (all_steps[:, None] == jnp.arange(steps, dtype=jnp.int32)[None, :]).astype(bf16)
    emb = nn(one_hot, embed_table)
    sig = sigmoid(emb)
    act = (emb * sig).astype(bf16)
    my_times = lax.dynamic_slice_in_dim(all_times, me * local, local, axis=1)
    time_weight_grad = lax.dot_general(
        act, my_times, (((0,), (0,)), ((), ())), preferred_element_type=f32
    )
    if pieces == 2:
        tw = jnp.where(
            me == 0, jnp.concatenate(tw_in, axis=1), jnp.concatenate(tw_in[::-1], axis=1)
        )
    else:
        tw = tw_in[0]
    grad_emb = (nt(all_times, tw) * silu_slope(emb, sig)).astype(bf16)
    table_grad = lax.dot_general(
        one_hot, grad_emb, (((0,), (0,)), ((), ())), preferred_element_type=f32
    )
    return (
        block_out,
        images_grad,
        table_grad,
        mine[9],
        mine[10],
        first_conv_grad.astype(f32),
        mine[8],
        time_weight_grad,
        mine[8],
        mine[6],
        mine[7],
        second_conv_grad.astype(f32),
        mine[0],
        mine[1],
        mine[2],
        project_in_grad.astype(f32),
        mine[3],
        mine[4],
        project_out_grad.astype(f32),
        mine[5],
    )


def solution(mesh):
    in_specs = (
        P("batch", "tensor", None),
        P("batch"),
        P(),
        P("tensor"),
        P("tensor"),
        P(None, None, "tensor"),
        P("tensor"),
        P(None, "tensor"),
        P("tensor"),
        P("tensor"),
        P("tensor"),
        P(None, "tensor", None),
        P("tensor"),
        P("tensor"),
        P("tensor"),
        P(None, None, "tensor"),
        P("tensor"),
        P("tensor"),
        P("tensor", None),
        P("tensor"),
        P("batch", "tensor", None),
    )
    out_specs = (
        P("batch", "tensor", None),
        P("batch", "tensor", None),
        P(),
        P("tensor"),
        P("tensor"),
        P(None, None, "tensor"),
        P("tensor"),
        P(None, "tensor"),
        P("tensor"),
        P("tensor"),
        P("tensor"),
        P(None, "tensor", None),
        P("tensor"),
        P("tensor"),
        P("tensor"),
        P(None, None, "tensor"),
        P("tensor"),
        P("tensor"),
        P("tensor", None),
        P("tensor"),
    )
    sizes = dict(mesh.shape)
    return jax.shard_map(
        functools.partial(per_device, sizes["batch"], sizes["tensor"]),
        mesh=mesh,
        in_specs=in_specs,
        out_specs=out_specs,
        check_vma=False,
    )
```

time: 104 us -> 97.2 us (0.935); the launches traced: 102 us -> 96.9 us
  waiting for transfers between devices: 17.4 us -> 24.8 us
  Pallas kernels: 34.2 us -> 27.9 us
  local copies, waits for them, and re-layouts: 9.23 us -> 4.28 us
  starting transfers between devices: 27.5 us -> 25.7 us
    ppermute x26 -> x25, waiting for transfers between devices: 12.3 us -> 17.1 us  [swap(): return lax.ppermute(value, axis, [(i, i ^ bit) for i in range(size)])]
    pallas_call x3 -> x2, Pallas kernels: 16.7 us -> 13.2 us  [the longest x1 12 us: per_device(): pl.pallas_call(functools.partial(back_kernel, pieces, count), out_shape=o...]
    pallas_call x1, Pallas kernels: 17.5 us -> 14.6 us  [per_device(): pl.pallas_call(functools.partial(front_kernel, pieces, count), out_shape=...]
    ppermute x4, waiting for transfers between devices: 5.1 us -> 7.78 us  [send_far(): return lax.ppermute(mine, ('batch', 'tensor'), pairs)]
    ppermute x4, starting transfers between devices: 9.4 us -> 6.94 us  [send_far(): return lax.ppermute(mine, ('batch', 'tensor'), pairs)]
    squeeze x2 -> x0, local copies, waits for them, and re-layouts: 1.94 us -> none  [other_half(): return lax.dynamic_index_in_dim(parts, 1 - me, 0, False)]
    another operation x1 -> x0, local copies, waits for them, and re-layouts: 1.64 us -> none  [per_device(): jnp.stack([first_gain, first_shift, first_bias, time_bias, second_gain, s...]
    convert_element_type x2, other arithmetic: 0.3 us -> 1.42 us  [near_parts(): return [part(me ^ j).astype(bf16) for j in range(1, 4)]]
  transfers between devices with their start and end apart: 30 -> 29, of which waited for: 7 -> 11; matrix products, arithmetic and copies ran while one was open for 12% -> 11% of each run, Pallas kernels for 16% -> 14%
where the time goes in v3:
time: 97.2 us; the launch traced here: 96.9 us
  Pallas kernels  27.9 us (29%)
  starting transfers between devices  25.7 us (26%)
  waiting for transfers between devices  24.8 us (26%)
  other arithmetic  9.83 us (10%)
  local copies, waits for them, and re-layouts  4.28 us (4%)
  matrix products  3.25 us (3%)
  between operations  1.15 us (1%)
    ppermute x25, starting transfers between devices, swap(): return lax.ppermute(value, axis, [(i, i ^ bit) for i in range(size)])  18.7 us
    ppermute x25, waiting for transfers between devices, swap(): return lax.ppermute(value, axis, [(i, i ^ bit) for i in range(size)])  17.1 us
    pallas_call x1, Pallas kernels, per_device(): pl.pallas_call(functools.partial(front_kernel, pieces, count), out_shape=...  14.6 us
    pallas_call x1, Pallas kernels, per_device(): pl.pallas_call(functools.partial(back_kernel, pieces, count), out_shape=o...  12 us
    ppermute x4, waiting for transfers between devices, send_far(): return lax.ppermute(mine, ('batch', 'tensor'), pairs)  7.78 us
    ppermute x4, starting transfers between devices, send_far(): return lax.ppermute(mine, ('batch', 'tensor'), pairs)  6.94 us
    unnamed x33, local copies, waits for them, and re-layouts  3.24 us
    concatenate x2, other arithmetic, placed(): return jnp.concatenate([low, high], axis=0)  2.16 us
  transfers between devices with their start and end apart: 29, of which 11 were waited for; matrix products, arithmetic and copies ran while one was open for 11% of the time, Pallas kernels for 14%

profile of v3, /device:TPU:0, one launch (start us, length us, event | category | flops | bytes accessed | tf_op | source)
XLA Modules:
  0.0 96.9 jit_solution(7390236564244291220)
XLA Ops:
  0.7 0.5 collective-permute-start.2
  1.3 0.4 collective-permute-start.6
  1.8 1.2 %pack.1 = (f32[16,128]{1,0:T(8,128)S(1)}, bf16[4,128,256]{2,1,0:T(8,128)(2,1)S(1)}, bf16[4,128,256]{2,1,0:T(8,128)(2,1)S(1)}) custom-call(f32[128]{0:T(128)} %refs_0_.2, f32[128]{0:T(128)} %refs_1_.1, f32[128]{0:T(128)} %refs_2_.2, f32[128]{0:T(128)} %refs_3_.1, f32[128]{0:T(128)} %refs_4_.2, f32[128]{0:T(128)} %refs_5_.1, f32[128]{0:T(128)} %refs_6_.2, ...), custom_call_target="tpu_custom_call" | custom-call | tf_op jit(solution)/shard_map/pack/pallas_call | solution.py:731
  3.0 0.5 collective-permute-start.7
  3.5 0.8 collective-permute-done.7.refs_15_
  4.3 0.3 collective-permute-start
  4.8 0.3 collective-permute-start.4
  5.2 1.5 %collective-permute-done.4.refs_9_ = bf16[3,256,128]{2,1,0:T(8,128)(2,1)S(1)} collective-permute-done((bf16[3,256,128]{2,1,0:T(8,128)(2,1)}, bf16[3,256,128]{2,1,0:T(8,128)(2,1)S(1)}, u32[]{:S(2)}, u32[]{:S(2)}) %collective-permute-start.4) | collective-permute-done | bytes 196640 | tf_op jit(solution)/shard_map/ppermute | solution.py:609
  6.8 0.6 copy-done.13
  7.8 0.8 copy-done.10
  8.6 14.6 %front.1 = (bf16[3328,128]{1,0:T(8,128)(2,1)}, bf16[3328,128]{1,0:T(8,128)(2,1)}, f32[8,256]{1,0:T(8,128)S(1)}, f32[2,4,256]{2,1,0:T(4,128)S(1)}, bf16[9,256,256...) custom-call(bf16[8,128,256]{2,1,0:T(8,128)(2,1)} %refs_0_.3, ...), custom_call_target="tpu_custom_call" | custom-call | flops 7247757312 | bytes 12582912 | tf_op jit(solution)/shard_map/front/pallas_call | solution.py:810
  23.3 0.4 collective-permute-start.8
  23.7 2.2 %collective-permute-done.8 = bf16[3328,128]{1,0:T(8,128)(2,1)S(1)} collective-permute-done((bf16[3328,128]{1,0:T(8,128)(2,1)}, bf16[3328,128]{1,0:T(8,128)(2,1)S(1)}, u32[]{:S(2)}, u32[]{:S(2)}) %collective-permute-start.8) | collective-permute-done | bytes 852000 | tf_op jit(solution)/shard_map/ppermute | solution.py:609
  25.9 1.3 %fusion.29 = (bf16[832,128]{1,0:T(8,128)(2,1)S(1)}, bf16[832,128]{1,0:T(8,128)(2,1)S(1)}, bf16[832,128]{1,0:T(8,128)(2,1)S(1)}) fusion(bf16[4,832,128]{2,1,0:T(8,128)(2,1)S(1)} %bitcast.99, s32[]{:T(128)S(6)} %select_n.99, bf16[4,832,128]{2,1,0:T(8,128)(2,1)} %bitcast.97, s32[]{:T(128)S(6)} %select_n.98, s32[]{:T(128)S(6)} %select_n.97), kind=kLoop, calls=%fused_computation.60 | loop fusion | flops 1277952 | bytes 1916940 | tf_op jit(solution)/shard_map/convert_element_type | solution.py:614
  27.2 2.9 %collective-permute-start.11 = (bf16[832,128]{1,0:T(8,128)(2,1)S(1)}, bf16[832,128]{1,0:T(8,128)(2,1)S(1)}, u32[]{:S(2)}, u32[]{:S(2)}) collective-permute-start(bf16[832,128]{1,0:T(8,128)(2,1)S(1)} %get-tuple-element.96), channel_id=1, source_target_pairs={{0,2},{2,0},{4,6},{6,4},{8,10},{10,8},{12,14},{14,12},{16,18},{18,... | collective-permute-start | bytes 638984 | tf_op jit(solution)/shard_map/ppermute | solution.py:609
  30.1 1.5 %collective-permute-start.12 = (bf16[832,128]{1,0:T(8,128)(2,1)S(1)}, bf16[832,128]{1,0:T(8,128)(2,1)S(1)}, u32[]{:S(2)}, u32[]{:S(2)}) collective-permute-start(bf16[832,128]{1,0:T(8,128)(2,1)S(1)} %get-tuple-element.95), channel_id=1, source_target_pairs={{0,4},{2,6},{4,0},{6,2},{8,12},{10,14},{12,8},{14,10},{16,20},{18,... | collective-permute-start | bytes 638984 | tf_op jit(solution)/shard_map/ppermute | solution.py:609
  31.7 12.0 %back.1 = (bf16[2304,128]{1,0:T(8,128)(2,1)}, bf16[2304,128]{1,0:T(8,128)(2,1)}, f32[4,128,256]{2,1,0:T(8,128)}, bf16[4,128,256]{2,1,0:T(8,128)(2,1)}, f32[4,128...) custom-call(bf16[9,256,256]{2,1,0:T(8,128)(2,1)} %get-tuple-element.60.refs_0_, ...), custom_call_target="tpu_custom_call" | custom-call | flops 4429185024 | bytes 12582912 | tf_op jit(solution)/shard_map/back/pallas_call | solution.py:875
  43.8 0.5 collective-permute-start.9
  44.5 1.1 %fusion.5 = bf16[832,128]{1,0:T(8,128)(2,1)S(1)} fusion(bf16[832,128]{1,0:T(8,128)(2,1)S(1)} %collective-permute-done.13, bf16[832,128]{1,0:T(8,128)(2,1)S(1)} %collective-permute-done.12, bf16[832,128]{1,0:T(8,128)(2,1)S(1)} %collective-permute-done.11, bf16[4,832,128]{2,1,0:T(8,128)(2,1)S(1)} %bitcast.100, s32[]{:T(128)S(6)} %select_n.105, ...), kind=kLoop, calls=%fused_computation.21 | loop fusion | flops 1064960 | bytes 1277956 | tf_op jit(solution)/shard_map/convert_element_type | solution.py:630
  45.9 0.7 copy-done.3
  46.9 2.0 %collective-permute-start.20 = (bf16[576,128]{1,0:T(8,128)(2,1)S(1)}, bf16[576,128]{1,0:T(8,128)(2,1)S(1)}, u32[]{:S(2)}, u32[]{:S(2)}) collective-permute-start(bf16[576,128]{1,0:T(8,128)(2,1)S(1)} %get-tuple-element.99), channel_id=1, source_target_pairs={{0,2},{2,0},{4,6},{6,4},{8,10},{10,8},{12,14},{14,12},{16,18},{18,... | collective-permute-start | bytes 442376 | tf_op jit(solution)/shard_map/ppermute | solution.py:609
  48.9 1.5 %collective-permute-start.21 = (bf16[576,128]{1,0:T(8,128)(2,1)S(1)}, bf16[576,128]{1,0:T(8,128)(2,1)S(1)}, u32[]{:S(2)}, u32[]{:S(2)}) collective-permute-start(bf16[576,128]{1,0:T(8,128)(2,1)S(1)} %get-tuple-element.98), channel_id=1, source_target_pairs={{0,4},{2,6},{4,0},{6,2},{8,12},{10,14},{12,8},{14,10},{16,20},{18,... | collective-permute-start | bytes 442376 | tf_op jit(solution)/shard_map/ppermute | solution.py:609
  50.5 1.1 %pad_maximum_fusion.1 = f32[8,128,256]{2,1,0:T(8,128)} fusion(f32[4,128,256]{2,1,0:T(8,128)S(1)} %get-tuple-element.103, f32[4,128,256]{2,1,0:T(8,128)S(1)} %get-tuple-element.102), kind=kLoop, calls=%fused_computation.6 | loop fusion | flops 262144 | bytes 2097152 | tf_op jit(solution)/shard_map/concatenate | solution.py:913
  51.6 2.1 %collective-permute-start.15 = (bf16[864,128]{1,0:T(8,128)(2,1)S(1)}, bf16[864,128]{1,0:T(8,128)(2,1)S(1)}, u32[]{:S(2)}, u32[]{:S(2)}) collective-permute-start(bf16[864,128]{1,0:T(8,128)(2,1)S(1)} %pad_maximum_fusion.6), channel_id=1, source_target_pairs={{0,8},{1,17},{2,10},{3,19},{4,12},{5,21},{6,14},{7,23},{8,0},{9,25... | collective-permute-start | bytes 663560 | tf_op jit(solution)/shard_map/ppermute | solution.py:646
  53.7 4.3 %collective-permute-done.21 = bf16[576,128]{1,0:T(8,128)(2,1)S(1)} collective-permute-done((bf16[576,128]{1,0:T(8,128)(2,1)S(1)}, bf16[576,128]{1,0:T(8,128)(2,1)S(1)}, u32[]{:S(2)}, u32[]{:S(2)}) %collective-permute-start.21) | collective-permute-done | bytes 147488 | tf_op jit(solution)/shard_map/ppermute | solution.py:609
  58.1 1.6 %collective-permute-start.23 = (bf16[576,128]{1,0:T(8,128)(2,1)S(1)}, bf16[576,128]{1,0:T(8,128)(2,1)S(1)}, u32[]{:S(2)}, u32[]{:S(2)}) collective-permute-start(bf16[576,128]{1,0:T(8,128)(2,1)S(1)} %fusion.8), channel_id=1, source_target_pairs={{0,8},{1,17},{2,10},{3,19},{4,12},{5,21},{6,14},{7,23},{8,0},{9,25... | collective-permute-start | bytes 442376 | tf_op jit(solution)/shard_map/ppermute | solution.py:646
  59.9 2.7 %collective-permute-start.16 = (bf16[896,128]{1,0:T(8,128)(2,1)S(1)}, bf16[896,128]{1,0:T(8,128)(2,1)S(1)}, u32[]{:S(2)}, u32[]{:S(2)}) collective-permute-start(bf16[896,128]{1,0:T(8,128)(2,1)S(1)} %pad_maximum_fusion.5), channel_id=1, source_target_pairs={{0,16},{1,9},{2,18},{3,11},{4,20},{5,13},{6,22},{7,15},{8,24},{9,1... | collective-permute-start | bytes 688136 | tf_op jit(solution)/shard_map/ppermute | solution.py:646
  62.5 5.4 %collective-permute-done.23 = bf16[576,128]{1,0:T(8,128)(2,1)S(1)} collective-permute-done((bf16[576,128]{1,0:T(8,128)(2,1)S(1)}, bf16[576,128]{1,0:T(8,128)(2,1)S(1)}, u32[]{:S(2)}, u32[]{:S(2)}) %collective-permute-start.23) | collective-permute-done | bytes 147488 | tf_op jit(solution)/shard_map/ppermute | solution.py:646
  68.0 0.5 collective-permute-start.24
  68.9 1.4 %collective-permute-start.17 = (bf16[960,128]{1,0:T(8,128)(2,1)S(1)}, bf16[960,128]{1,0:T(8,128)(2,1)S(1)}, u32[]{:S(2)}, u32[]{:S(2)}) collective-permute-start(bf16[960,128]{1,0:T(8,128)(2,1)S(1)} %pad_maximum_fusion.4), channel_id=1, source_target_pairs={{0,2},{2,0},{4,6},{6,4},{8,10},{10,8},{12,14},{14,12},{16,18},{18,... | collective-permute-start | bytes 737288 | tf_op jit(solution)/shard_map/ppermute | solution.py:609
  70.3 1.1 %collective-permute-start.18 = (bf16[960,128]{1,0:T(8,128)(2,1)S(1)}, bf16[960,128]{1,0:T(8,128)(2,1)S(1)}, u32[]{:S(2)}, u32[]{:S(2)}) collective-permute-start(bf16[960,128]{1,0:T(8,128)(2,1)S(1)} %pad_maximum_fusion.4), channel_id=1, source_target_pairs={{0,4},{2,6},{4,0},{6,2},{8,12},{10,14},{12,8},{14,10},{16,20},{18,... | collective-permute-start | bytes 737288 | tf_op jit(solution)/shard_map/ppermute | solution.py:609
  71.4 1.1 %collective-permute-start.19 = (bf16[960,128]{1,0:T(8,128)(2,1)S(1)}, bf16[960,128]{1,0:T(8,128)(2,1)S(1)}, u32[]{:S(2)}, u32[]{:S(2)}) collective-permute-start(bf16[960,128]{1,0:T(8,128)(2,1)S(1)} %pad_maximum_fusion.4), channel_id=1, source_target_pairs={{0,6},{2,4},{4,2},{6,0},{8,14},{10,12},{12,10},{14,8},{16,22},{18,... | collective-permute-start | bytes 737288 | tf_op jit(solution)/shard_map/ppermute | solution.py:609
  72.5 1.1 %pad_maximum_fusion = f32[8,128,256]{2,1,0:T(8,128)} fusion(f32[4,128,256]{2,1,0:T(8,128)S(1)} %get-tuple-element.105, f32[4,128,256]{2,1,0:T(8,128)S(1)} %get-tuple-element.104), kind=kLoop, calls=%fused_computation.5 | loop fusion | flops 262144 | bytes 2097152 | tf_op jit(solution)/shard_map/concatenate | solution.py:913
  73.6 2.0 %collective-permute-done.24 = bf16[576,128]{1,0:T(8,128)(2,1)S(1)} collective-permute-done((bf16[576,128]{1,0:T(8,128)(2,1)S(1)}, bf16[576,128]{1,0:T(8,128)(2,1)S(1)}, u32[]{:S(2)}, u32[]{:S(2)}) %collective-permute-start.24) | collective-permute-done | bytes 147488 | tf_op jit(solution)/shard_map/ppermute | solution.py:646
  75.7 2.1 %collective-permute-done.17 = bf16[960,128]{1,0:T(8,128)(2,1)S(1)} collective-permute-done((bf16[960,128]{1,0:T(8,128)(2,1)S(1)}, bf16[960,128]{1,0:T(8,128)(2,1)S(1)}, u32[]{:S(2)}, u32[]{:S(2)}) %collective-permute-start.17) | collective-permute-done | bytes 245792 | tf_op jit(solution)/shard_map/ppermute | solution.py:609
  77.8 5.6 %collective-permute-done.18 = bf16[960,128]{1,0:T(8,128)(2,1)S(1)} collective-permute-done((bf16[960,128]{1,0:T(8,128)(2,1)S(1)}, bf16[960,128]{1,0:T(8,128)(2,1)S(1)}, u32[]{:S(2)}, u32[]{:S(2)}) %collective-permute-start.18) | collective-permute-done | bytes 245792 | tf_op jit(solution)/shard_map/ppermute | solution.py:609
  84.1 0.7 collective-permute-start.26
  84.8 1.4 %collective-permute-start.27 = (bf16[576,128]{1,0:T(8,128)(2,1)S(1)}, bf16[576,128]{1,0:T(8,128)(2,1)S(1)}, u32[]{:S(2)}, u32[]{:S(2)}) collective-permute-start(bf16[576,128]{1,0:T(8,128)(2,1)S(1)} %add_convert_fusion.5), channel_id=1, source_target_pairs={{0,4},{2,6},{4,0},{6,2},{8,12},{10,14},{12,8},{14,10},{16,20},{18,... | collective-permute-start | bytes 442376 | tf_op jit(solution)/shard_map/ppermute | solution.py:609
  86.2 1.5 %collective-permute-start.28 = (bf16[576,128]{1,0:T(8,128)(2,1)S(1)}, bf16[576,128]{1,0:T(8,128)(2,1)S(1)}, u32[]{:S(2)}, u32[]{:S(2)}) collective-permute-start(bf16[576,128]{1,0:T(8,128)(2,1)S(1)} %add_convert_fusion.5), channel_id=1, source_target_pairs={{0,6},{2,4},{4,2},{6,0},{8,14},{10,12},{12,10},{14,8},{16,22},{18,... | collective-permute-start | bytes 442376 | tf_op jit(solution)/shard_map/ppermute | solution.py:609
  87.7 0.8 convert.4
  88.6 0.7 maximum_convert_fusion.1
  89.3 1.1 %maximum_convert_fusion = f32[9,128,256]{2,1,0:T(8,128)} fusion(bf16[9,128,128]{2,1,0:T(8,128)(2,1)S(1)} %get-tuple-element.107, bf16[9,128,128]{2,1,0:T(8,128)(2,1)S(1)} %get-tuple-element.106), kind=kLoop, calls=%fused_computation.15 | loop fusion | flops 1179648 | bytes 1769472 | tf_op jit(solution)/shard_map/convert_element_type | solution.py:989
  90.9 0.3 fusion.2
  91.3 0.6 dynamic-slice_bitcast_fusion
  92.0 2.0 %fusion.1 = f32[1024,512]{1,0:T(8,128)} fusion(bf16[128,256]{1,0:T(8,128)(2,1)S(1)} %reshape.125, bf16[512,128]{1,0:T(8,128)(2,1)S(1)} %copy-done.7, bf16[512,128]{1,0:T(8,128)(2,1)S(1)} %copy-done.5, f32[128,512]{1,0:T(8,128)S(1)} %fusion.2, s32[128]{0:T(128)S(1)} %eq.15, pred[]{:T(512)S(6)} %eq.14), kind=kOutput, calls=%fused_computation.4 | convolution fusion | flops 169672704 | bytes 2687489 | tf_op jit(solution)/shard_map/dot_general | solution.py:974
  94.0 0.9 fusion.33
  95.3 1.1 %convert.3 = f32[9,256,128]{2,1,0:T(8,128)} convert(bf16[9,256,128]{2,1,0:T(8,128)(2,1)S(1)} %bitcast.91) | non-fusion elementwise | flops 294912 | bytes 1769472 | tf_op jit(solution)/shard_map/convert_element_type | solution.py:983
  96.4 0.5 copy.54
  (97 shorter events, 4.1 us)
Async XLA Ops:
  0.7 6.1 %collective-permute-start.2 = (bf16[9,256,128]{2,1,0:T(8,128)(2,1)}, bf16[9,256,128]{2,1,0:T(8,128)(2,1)S(1)}, u32[]{:S(2)}, u32[]{:S(2)}) collective-permute-start(bf16[9,256,128]{2,1,0:T(8,128)(2,1)} %refs_4_.3), channel_id=1, source_target_pairs={{0,1},{1,0},{2,3},{3,2},{4,5},{5,4},{6,7},{7,6},{8,9},{9,8},{10,11... | collective-permute-start | bytes 1769480 | tf_op jit(solution)/shard_map/ppermute | solution.py:609
  1.2 5.6 %collective-permute-start.3 = (bf16[9,128,256]{2,1,0:T(8,128)(2,1)}, bf16[9,128,256]{2,1,0:T(8,128)(2,1)S(1)}, u32[]{:S(2)}, u32[]{:S(2)}) collective-permute-start(bf16[9,128,256]{2,1,0:T(8,128)(2,1)} %refs_6_.3), channel_id=1, source_target_pairs={{0,1},{1,0},{2,3},{3,2},{4,5},{5,4},{6,7},{7,6},{8,9},{9,8},{10,11... | collective-permute-start | bytes 1769480 | tf_op jit(solution)/shard_map/ppermute | solution.py:609
  1.3 3.5 %collective-permute-start.6 = (bf16[512,128]{1,0:T(8,128)(2,1)}, bf16[512,128]{1,0:T(8,128)(2,1)S(1)}, u32[]{:S(2)}, u32[]{:S(2)}) collective-permute-start(bf16[512,128]{1,0:T(8,128)(2,1)} %refs_12_.3), channel_id=1, source_target_pairs={{0,1},{1,0},{2,3},{3,2},{4,5},{5,4},{6,7},{7,6},{8,9},{9,8},{10,11... | collective-permute-start | bytes 393224 | tf_op jit(solution)/shard_map/ppermute | solution.py:609
  1.7 2.9 %collective-permute-start.5 = (bf16[128,256]{1,0:T(8,128)(2,1)}, bf16[128,256]{1,0:T(8,128)(2,1)S(1)}, u32[]{:S(2)}, u32[]{:S(2)}) collective-permute-start(bf16[128,256]{1,0:T(8,128)(2,1)} %refs_10_.3), channel_id=1, source_target_pairs={{0,1},{1,0},{2,3},{3,2},{4,5},{5,4},{6,7},{7,6},{8,9},{9,8},{10,11... | collective-permute-start | bytes 196616 | tf_op jit(solution)/shard_map/ppermute | solution.py:609
  3.0 3.8 %copy-start = (f32[16,128]{1,0:T(8,128)}, f32[16,128]{1,0:T(8,128)S(1)}, u32[]{:S(2)}) copy-start(f32[16,128]{1,0:T(8,128)S(1)} %get-tuple-element.59.refs_14_) | copy-start | bytes 24580
  3.0 1.3 %collective-permute-start.7 = (f32[16,128]{1,0:T(8,128)S(1)}, f32[16,128]{1,0:T(8,128)S(1)}, u32[]{:S(2)}, u32[]{:S(2)}) collective-permute-start(f32[16,128]{1,0:T(8,128)S(1)} %get-tuple-element.59.refs_14_), channel_id=1, source_target_pairs={{0,1},{1,0},{2,3},{3,2},{4,5},{5,4},{6,7},{7,6},{8,9},{9,8},{10,11... | collective-permute-start | bytes 24584 | tf_op jit(solution)/shard_map/ppermute | solution.py:609
  4.3 2.5 %copy-start.15 = (f32[16,128]{1,0:T(8,128)}, f32[16,128]{1,0:T(8,128)S(1)}, u32[]{:S(2)}) copy-start(f32[16,128]{1,0:T(8,128)S(1)} %collective-permute-done.7.refs_15_) | copy-start | bytes 24580
  4.3 2.4 %collective-permute-start = (bf16[4,128,256]{2,1,0:T(8,128)(2,1)S(1)}, bf16[4,128,256]{2,1,0:T(8,128)(2,1)S(1)}, u32[]{:S(2)}, u32[]{:S(2)}) collective-permute-start(bf16[4,128,256]{2,1,0:T(8,128)(2,1)S(1)} %get-tuple-element.57), channel_id=1, source_target_pairs={{0,1},{1,0},{2,3},{3,2},{4,5},{5,4},{6,7},{7,6},{8,9},{9,8},{10,11... | collective-permute-start | bytes 786440 | tf_op jit(solution)/shard_map/ppermute | solution.py:609
  4.6 2.1 %copy-start.14 = (bf16[128,256]{1,0:T(8,128)(2,1)}, bf16[128,256]{1,0:T(8,128)(2,1)S(1)}, u32[]{:S(2)}) copy-start(bf16[128,256]{1,0:T(8,128)(2,1)S(1)} %collective-permute-done.5.refs_11_) | copy-start | bytes 196612
  4.6 2.1 %collective-permute-start.1 = (bf16[4,128,256]{2,1,0:T(8,128)(2,1)S(1)}, bf16[4,128,256]{2,1,0:T(8,128)(2,1)S(1)}, u32[]{:S(2)}, u32[]{:S(2)}) collective-permute-start(bf16[4,128,256]{2,1,0:T(8,128)(2,1)S(1)} %get-tuple-element.58), channel_id=1, source_target_pairs={{0,1},{1,0},{2,3},{3,2},{4,5},{5,4},{6,7},{7,6},{8,9},{9,8},{10,11... | collective-permute-start | bytes 786440 | tf_op jit(solution)/shard_map/ppermute | solution.py:609
  4.8 2.0 %copy-start.6 = (bf16[512,128]{1,0:T(8,128)(2,1)}, bf16[512,128]{1,0:T(8,128)(2,1)S(1)}, u32[]{:S(2)}) copy-start(bf16[512,128]{1,0:T(8,128)(2,1)S(1)} %collective-permute-done.6.refs_13_) | copy-start | bytes 393220
  4.8 1.9 %collective-permute-start.4 = (bf16[3,256,128]{2,1,0:T(8,128)(2,1)}, bf16[3,256,128]{2,1,0:T(8,128)(2,1)S(1)}, u32[]{:S(2)}, u32[]{:S(2)}) collective-permute-start(bf16[3,256,128]{2,1,0:T(8,128)(2,1)} %refs_8_.3), channel_id=1, source_target_pairs={{0,1},{1,0},{2,3},{3,2},{4,5},{5,4},{6,7},{7,6},{8,9},{9,8},{10,11... | collective-permute-start | bytes 589832 | tf_op jit(solution)/shard_map/ppermute | solution.py:609
  6.7 0.7 copy-start.13
  6.7 0.8 copy-start.11
  6.7 0.8 copy-start.12
  6.7 1.0 %copy-start.9 = (bf16[9,256,128]{2,1,0:T(8,128)(2,1)}, bf16[9,256,128]{2,1,0:T(8,128)(2,1)S(1)}, u32[]{:S(2)}) copy-start(bf16[9,256,128]{2,1,0:T(8,128)(2,1)S(1)} %collective-permute-done.2.refs_5_) | copy-start | bytes 1769476
  7.8 0.8 copy-start.10
  23.3 2.7 %collective-permute-start.8 = (bf16[3328,128]{1,0:T(8,128)(2,1)}, bf16[3328,128]{1,0:T(8,128)(2,1)S(1)}, u32[]{:S(2)}, u32[]{:S(2)}) collective-permute-start(bf16[3328,128]{1,0:T(8,128)(2,1)} %get-tuple-element.74), channel_id=1, source_target_pairs={{0,1},{1,0},{2,3},{3,2},{4,5},{5,4},{6,7},{7,6},{8,9},{9,8},{10,11... | collective-permute-start | bytes 2555912 | tf_op jit(solution)/shard_map/ppermute | solution.py:609
  27.2 17.1 %collective-permute-start.11 = (bf16[832,128]{1,0:T(8,128)(2,1)S(1)}, bf16[832,128]{1,0:T(8,128)(2,1)S(1)}, u32[]{:S(2)}, u32[]{:S(2)}) collective-permute-start(bf16[832,128]{1,0:T(8,128)(2,1)S(1)} %get-tuple-element.96), channel_id=1, source_target_pairs={{0,2},{2,0},{4,6},{6,4},{8,10},{10,8},{12,14},{14,12},{16,18},{18,... | collective-permute-start | bytes 638984 | tf_op jit(solution)/shard_map/ppermute | solution.py:609
  30.1 14.2 %collective-permute-start.12 = (bf16[832,128]{1,0:T(8,128)(2,1)S(1)}, bf16[832,128]{1,0:T(8,128)(2,1)S(1)}, u32[]{:S(2)}, u32[]{:S(2)}) collective-permute-start(bf16[832,128]{1,0:T(8,128)(2,1)S(1)} %get-tuple-element.95), channel_id=1, source_target_pairs={{0,4},{2,6},{4,0},{6,2},{8,12},{10,14},{12,8},{14,10},{16,20},{18,... | collective-permute-start | bytes 638984 | tf_op jit(solution)/shard_map/ppermute | solution.py:609
  31.6 12.7 %collective-permute-start.13 = (bf16[832,128]{1,0:T(8,128)(2,1)S(1)}, bf16[832,128]{1,0:T(8,128)(2,1)S(1)}, u32[]{:S(2)}, u32[]{:S(2)}) collective-permute-start(bf16[832,128]{1,0:T(8,128)(2,1)S(1)} %get-tuple-element.94), channel_id=1, source_target_pairs={{0,6},{2,4},{4,2},{6,0},{8,14},{10,12},{12,10},{14,8},{16,22},{18,... | collective-permute-start | bytes 638984 | tf_op jit(solution)/shard_map/ppermute | solution.py:609
  43.7 1.9 %copy-start.4 = (f32[4,128,256]{2,1,0:T(8,128)S(1)}, f32[4,128,256]{2,1,0:T(8,128)}, u32[]{:S(2)}) copy-start(f32[4,128,256]{2,1,0:T(8,128)} %get-tuple-element.78) | copy-start | bytes 1572868
  43.7 1.8 %collective-permute-start.10 = (bf16[4,128,256]{2,1,0:T(8,128)(2,1)}, bf16[4,128,256]{2,1,0:T(8,128)(2,1)S(1)}, u32[]{:S(2)}, u32[]{:S(2)}) collective-permute-start(bf16[4,128,256]{2,1,0:T(8,128)(2,1)} %get-tuple-element.79), channel_id=1, source_target_pairs={{0,1},{1,0},{2,3},{3,2},{4,5},{5,4},{6,7},{7,6},{8,9},{9,8},{10,11... | collective-permute-start | bytes 786440 | tf_op jit(solution)/shard_map/ppermute | solution.py:609
  43.8 2.1 %collective-permute-start.9 = (bf16[4,128,256]{2,1,0:T(8,128)(2,1)}, bf16[4,128,256]{2,1,0:T(8,128)(2,1)S(1)}, u32[]{:S(2)}, u32[]{:S(2)}) collective-permute-start(bf16[4,128,256]{2,1,0:T(8,128)(2,1)} %get-tuple-element.77), channel_id=1, source_target_pairs={{0,1},{1,0},{2,3},{3,2},{4,5},{5,4},{6,7},{7,6},{8,9},{9,8},{10,11... | collective-permute-start | bytes 786440 | tf_op jit(solution)/shard_map/ppermute | solution.py:609
  44.3 2.4 %collective-permute-start.14 = (bf16[2304,128]{1,0:T(8,128)(2,1)}, bf16[2304,128]{1,0:T(8,128)(2,1)S(1)}, u32[]{:S(2)}, u32[]{:S(2)}) collective-permute-start(bf16[2304,128]{1,0:T(8,128)(2,1)} %get-tuple-element.87), channel_id=1, source_target_pairs={{0,1},{1,0},{2,3},{3,2},{4,5},{5,4},{6,7},{7,6},{8,9},{9,8},{10,11... | collective-permute-start | bytes 1769480 | tf_op jit(solution)/shard_map/ppermute | solution.py:609
  45.5 1.0 %copy-start.3 = (f32[4,128,256]{2,1,0:T(8,128)S(1)}, f32[4,128,256]{2,1,0:T(8,128)}, u32[]{:S(2)}) copy-start(f32[4,128,256]{2,1,0:T(8,128)} %get-tuple-element.76) | copy-start | bytes 1572868
  45.7 1.1 %copy-start.2 = (bf16[2304,128]{1,0:T(8,128)(2,1)S(1)}, bf16[2304,128]{1,0:T(8,128)(2,1)}, u32[]{:S(2)}) copy-start(bf16[2304,128]{1,0:T(8,128)(2,1)} %get-tuple-element.86) | copy-start | bytes 1769476
  46.9 6.8 %collective-permute-start.20 = (bf16[576,128]{1,0:T(8,128)(2,1)S(1)}, bf16[576,128]{1,0:T(8,128)(2,1)S(1)}, u32[]{:S(2)}, u32[]{:S(2)}) collective-permute-start(bf16[576,128]{1,0:T(8,128)(2,1)S(1)} %get-tuple-element.99), channel_id=1, source_target_pairs={{0,2},{2,0},{4,6},{6,4},{8,10},{10,8},{12,14},{14,12},{16,18},{18,... | collective-permute-start | bytes 442376 | tf_op jit(solution)/shard_map/ppermute | solution.py:609
  48.9 9.1 %collective-permute-start.21 = (bf16[576,128]{1,0:T(8,128)(2,1)S(1)}, bf16[576,128]{1,0:T(8,128)(2,1)S(1)}, u32[]{:S(2)}, u32[]{:S(2)}) collective-permute-start(bf16[576,128]{1,0:T(8,128)(2,1)S(1)} %get-tuple-element.98), channel_id=1, source_target_pairs={{0,4},{2,6},{4,0},{6,2},{8,12},{10,14},{12,8},{14,10},{16,20},{18,... | collective-permute-start | bytes 442376 | tf_op jit(solution)/shard_map/ppermute | solution.py:609
  50.4 7.6 %collective-permute-start.22 = (bf16[576,128]{1,0:T(8,128)(2,1)S(1)}, bf16[576,128]{1,0:T(8,128)(2,1)S(1)}, u32[]{:S(2)}, u32[]{:S(2)}) collective-permute-start(bf16[576,128]{1,0:T(8,128)(2,1)S(1)} %get-tuple-element.97), channel_id=1, source_target_pairs={{0,6},{2,4},{4,2},{6,0},{8,14},{10,12},{12,10},{14,8},{16,22},{18,... | collective-permute-start | bytes 442376 | tf_op jit(solution)/shard_map/ppermute | solution.py:609
  51.6 8.2 %collective-permute-start.15 = (bf16[864,128]{1,0:T(8,128)(2,1)S(1)}, bf16[864,128]{1,0:T(8,128)(2,1)S(1)}, u32[]{:S(2)}, u32[]{:S(2)}) collective-permute-start(bf16[864,128]{1,0:T(8,128)(2,1)S(1)} %pad_maximum_fusion.6), channel_id=1, source_target_pairs={{0,8},{1,17},{2,10},{3,19},{4,12},{5,21},{6,14},{7,23},{8,0},{9,25... | collective-permute-start | bytes 663560 | tf_op jit(solution)/shard_map/ppermute | solution.py:646
  58.1 9.8 %collective-permute-start.23 = (bf16[576,128]{1,0:T(8,128)(2,1)S(1)}, bf16[576,128]{1,0:T(8,128)(2,1)S(1)}, u32[]{:S(2)}, u32[]{:S(2)}) collective-permute-start(bf16[576,128]{1,0:T(8,128)(2,1)S(1)} %fusion.8), channel_id=1, source_target_pairs={{0,8},{1,17},{2,10},{3,19},{4,12},{5,21},{6,14},{7,23},{8,0},{9,25... | collective-permute-start | bytes 442376 | tf_op jit(solution)/shard_map/ppermute | solution.py:646
  59.9 9.0 %collective-permute-start.16 = (bf16[896,128]{1,0:T(8,128)(2,1)S(1)}, bf16[896,128]{1,0:T(8,128)(2,1)S(1)}, u32[]{:S(2)}, u32[]{:S(2)}) collective-permute-start(bf16[896,128]{1,0:T(8,128)(2,1)S(1)} %pad_maximum_fusion.5), channel_id=1, source_target_pairs={{0,16},{1,9},{2,18},{3,11},{4,20},{5,13},{6,22},{7,15},{8,24},{9,1... | collective-permute-start | bytes 688136 | tf_op jit(solution)/shard_map/ppermute | solution.py:646
  68.0 7.6 %collective-permute-start.24 = (bf16[576,128]{1,0:T(8,128)(2,1)S(1)}, bf16[576,128]{1,0:T(8,128)(2,1)S(1)}, u32[]{:S(2)}, u32[]{:S(2)}) collective-permute-start(bf16[576,128]{1,0:T(8,128)(2,1)S(1)} %add_convert_fusion.6), channel_id=1, source_target_pairs={{0,16},{1,9},{2,18},{3,11},{4,20},{5,13},{6,22},{7,15},{8,24},{9,1... | collective-permute-start | bytes 442376 | tf_op jit(solution)/shard_map/ppermute | solution.py:646
  68.9 8.9 %collective-permute-start.17 = (bf16[960,128]{1,0:T(8,128)(2,1)S(1)}, bf16[960,128]{1,0:T(8,128)(2,1)S(1)}, u32[]{:S(2)}, u32[]{:S(2)}) collective-permute-start(bf16[960,128]{1,0:T(8,128)(2,1)S(1)} %pad_maximum_fusion.4), channel_id=1, source_target_pairs={{0,2},{2,0},{4,6},{6,4},{8,10},{10,8},{12,14},{14,12},{16,18},{18,... | collective-permute-start | bytes 737288 | tf_op jit(solution)/shard_map/ppermute | solution.py:609
  70.3 13.1 %collective-permute-start.18 = (bf16[960,128]{1,0:T(8,128)(2,1)S(1)}, bf16[960,128]{1,0:T(8,128)(2,1)S(1)}, u32[]{:S(2)}, u32[]{:S(2)}) collective-permute-start(bf16[960,128]{1,0:T(8,128)(2,1)S(1)} %pad_maximum_fusion.4), channel_id=1, source_target_pairs={{0,4},{2,6},{4,0},{6,2},{8,12},{10,14},{12,8},{14,10},{16,20},{18,... | collective-permute-start | bytes 737288 | tf_op jit(solution)/shard_map/ppermute | solution.py:609
  71.4 12.1 %collective-permute-start.19 = (bf16[960,128]{1,0:T(8,128)(2,1)S(1)}, bf16[960,128]{1,0:T(8,128)(2,1)S(1)}, u32[]{:S(2)}, u32[]{:S(2)}) collective-permute-start(bf16[960,128]{1,0:T(8,128)(2,1)S(1)} %pad_maximum_fusion.4), channel_id=1, source_target_pairs={{0,6},{2,4},{4,2},{6,0},{8,14},{10,12},{12,10},{14,8},{16,22},{18,... | collective-permute-start | bytes 737288 | tf_op jit(solution)/shard_map/ppermute | solution.py:609
  84.1 10.8 %collective-permute-start.26 = (bf16[576,128]{1,0:T(8,128)(2,1)S(1)}, bf16[576,128]{1,0:T(8,128)(2,1)S(1)}, u32[]{:S(2)}, u32[]{:S(2)}) collective-permute-start(bf16[576,128]{1,0:T(8,128)(2,1)S(1)} %add_convert_fusion.5), channel_id=1, source_target_pairs={{0,2},{2,0},{4,6},{6,4},{8,10},{10,8},{12,14},{14,12},{16,18},{18,... | collective-permute-start | bytes 442376 | tf_op jit(solution)/shard_map/ppermute | solution.py:609
  84.8 10.1 %collective-permute-start.27 = (bf16[576,128]{1,0:T(8,128)(2,1)S(1)}, bf16[576,128]{1,0:T(8,128)(2,1)S(1)}, u32[]{:S(2)}, u32[]{:S(2)}) collective-permute-start(bf16[576,128]{1,0:T(8,128)(2,1)S(1)} %add_convert_fusion.5), channel_id=1, source_target_pairs={{0,4},{2,6},{4,0},{6,2},{8,12},{10,14},{12,8},{14,10},{16,20},{18,... | collective-permute-start | bytes 442376 | tf_op jit(solution)/shard_map/ppermute | solution.py:609
  86.2 8.8 %collective-permute-start.28 = (bf16[576,128]{1,0:T(8,128)(2,1)S(1)}, bf16[576,128]{1,0:T(8,128)(2,1)S(1)}, u32[]{:S(2)}, u32[]{:S(2)}) collective-permute-start(bf16[576,128]{1,0:T(8,128)(2,1)S(1)} %add_convert_fusion.5), channel_id=1, source_target_pairs={{0,6},{2,4},{4,2},{6,0},{8,14},{10,12},{12,10},{14,8},{16,22},{18,... | collective-permute-start | bytes 442376 | tf_op jit(solution)/shard_map/ppermute | solution.py:609
  88.5 1.8 %collective-permute-start.25 = (bf16[512,128]{1,0:T(8,128)(2,1)S(1)}, bf16[512,128]{1,0:T(8,128)(2,1)S(1)}, u32[]{:S(2)}, u32[]{:S(2)}) collective-permute-start(bf16[512,128]{1,0:T(8,128)(2,1)S(1)} %pad_maximum_fusion.7), channel_id=1, source_target_pairs={{0,1},{1,0},{2,3},{3,2},{4,5},{5,4},{6,7},{7,6},{8,9},{9,8},{10,11... | collective-permute-start | bytes 393224 | tf_op jit(solution)/shard_map/ppermute | solution.py:609
  89.3 1.7 %copy-start.1 = (bf16[1024,512]{1,0:T(8,128)(2,1)S(1)}, bf16[1024,512]{1,0:T(8,128)(2,1)}, u32[]{:S(2)}) copy-start(bf16[1024,512]{1,0:T(8,128)(2,1)} %refs_17_.1) | copy-start | bytes 3145732
  90.4 1.6 %copy-start.5 = (bf16[512,128]{1,0:T(8,128)(2,1)S(1)}, bf16[512,128]{1,0:T(8,128)(2,1)}, u32[]{:S(2)}) copy-start(bf16[512,128]{1,0:T(8,128)(2,1)} %refs_12_.3) | copy-start | bytes 393220
  90.4 1.6 %copy-start.7 = (bf16[512,128]{1,0:T(8,128)(2,1)S(1)}, bf16[512,128]{1,0:T(8,128)(2,1)}, u32[]{:S(2)}) copy-start(bf16[512,128]{1,0:T(8,128)(2,1)} %copy-done.6) | copy-start | bytes 393220
  92.0 4.4 %copy-start.8 = (f32[128]{0:T(128)}, f32[128]{0:T(128)S(1)}, u32[]{:S(2)}) copy-start(f32[128]{0:T(128)S(1)} %get-tuple-element.159) | copy-start | bytes 1540

commit v4 on v3

--- a/solution.py
+++ b/solution.py
@@ -248,13 +248,14 @@
         own_out, send_out = take(2)
     else:
         dw2_own, dpo_own, dpi_own = take(3)
-    vec_out, stat_out = take(2)
     w1_out, w2_out, po_out, all_vec_out, x_out = take(5)
     gpad_out, sum_out, a1t_out, resid_out, gres_out, mix_out = take(6)
+    stat_out, sums_out = take(2)
     if pieces == 2:
         own, send = take(2)
     w1, w2, po, vec, xin = take(5)
     gpad, sum_one, a1t, resid, gres, mix = take(6)
+    stat, sums = take(2)
     gin, pi, tw, rows, shift, apad, bpad = take(7)
     sems = next(it)
 
@@ -350,8 +351,9 @@
 
     pipelined([norm_one, conv_one, norm_two, conv_two, norm_three], count)
     outs += [cps.start(a1t, a1t_out), cps.start(sum_one, sum_out), cps.start(resid, resid_out)]
-    stat_out[0, 0:count, :] = jnp.concatenate([m for m, _ in stats2], axis=0)
-    stat_out[1, 0:count, :] = jnp.concatenate([r for _, r in stats2], axis=0)
+    stat[0:count, :] = jnp.concatenate([m for m, _ in stats2], axis=0)
+    stat[count : 2 * count, :] = jnp.concatenate([r for _, r in stats2], axis=0)
+    outs.append(cps.start(stat, stat_out))
 
     wait_all(pi_cp)
     wait_all(po_cp)
@@ -416,7 +418,16 @@
         gres[b] = val
         sb_grad = sb_grad + col_sum(val)
         put_moved(gpad, b, val, side, points)
-    outs += [cps.start(gres, gres_out), cps.start(gpad, gpad_out)]
+    lane = lax.broadcasted_iota(jnp.int32, (1, chans), 1)
+    stamp = jnp.zeros((1, chans), f32)
+    for b in images:
+        step = jnp.full((1, chans), steps_ref[places[0] * count + b], jnp.int32)
+        stamp = jnp.where(lane == b, (step >> 5).astype(f32), stamp)
+        stamp = jnp.where(lane == LANES // 2 + b, (step & 31).astype(f32), stamp)
+    sums[...] = jnp.concatenate(
+        [sb_grad, sum(gain3), sum(shift3), qb_grad, vb_grad, ob_grad, stamp, zero], axis=0
+    )
+    outs += [cps.start(gres, gres_out), cps.start(gpad, gpad_out), cps.start(sums, sums_out)]
 
     dpi = nn(normed_t, lin_grad)
     at = 0
@@ -442,11 +453,6 @@
         else:
             dw2_own[tap] = val
 
-    gain3 = jnp.concatenate(gain3, axis=0)
-    shift3 = jnp.concatenate(shift3, axis=0)
-    vec_out[...] = jnp.concatenate(
-        [sb_grad, col_sum(gain3), col_sum(shift3), qb_grad, vb_grad, ob_grad, zero, zero], axis=0
-    )
     wait_all(outs)
 
 
@@ -461,21 +467,20 @@
     def take(n):
         return [next(it) for _ in range(n)]
 
-    kept = take(11)
-    stat, vec_a, steps_ref = take(3)
+    kept = take(13)
     if pieces == 2:
         own_out, send_out, block_own_out, block_send_out, image_own_out, image_send_out = take(6)
     else:
         own, block_own_out, image_own_out = take(3)
         block_send_out = image_send_out = None
     small_out = next(it)
-    w1, w2, po, vec, xin, gpad, sum_one, a1t, resid, gres, mix = take(11)
+    w1, w2, po, vec, xin, gpad, sum_one, a1t, resid, gres, mix, stat, front_sums = take(13)
     if pieces == 2:
         own, send, block_own, block_send, image_own, image_send = take(6)
     else:
         block_own, image_own = take(2)
         block_send = image_send = None
-    hpad, back, sems = take(3)
+    small, hpad, back, sems = take(4)
     cps = Copies(sems)
     places = places_of(pieces)
     points, chans = sum_one.shape[1], sum_one.shape[2]
@@ -484,10 +489,11 @@
     size = float(width * points)
     images = range(count)
 
-    w1_in, w2_in, po_in, vec_in, x_in, gpad_in, sum_in, a1t_in, resid_in, gres_in, mix_in = kept
+    w1_in, w2_in, po_in, vec_in, x_in, gpad_in, sum_in, a1t_in, resid_in, gres_in, mix_in = kept[:11]
     w2_cp = cps.start(w2_in, w2)
     gpad_cp = [cps.start(gpad_in.at[:, b], gpad.at[:, b]) for b in images]
-    vec_cp = cps.start(vec_in, vec)
+    small_cp = [(vec_in, vec), (kept[11], stat), (kept[12], front_sums)]
+    small_cp = [cps.start(src, dst) for src, dst in small_cp]
     sum_cp = cps.start(sum_in, sum_one)
     a1t_cp = cps.start(a1t_in, a1t)
     later = [(w1_in, w1), (po_in, po), (x_in, xin), (resid_in, resid), (gres_in, gres), (mix_in, mix)]
@@ -508,8 +514,8 @@
     def norm_back(b):
         if b == 0:
             sum_cp.wait()
-            vec_cp.wait()
-        mean, rstd = stat[0, b : b + 1, :], stat[1, b : b + 1, :]
+            wait_all(small_cp)
+        mean, rstd = stat[b : b + 1, :], stat[count + b : count + b + 1, :]
         hat = (sum_one[b] - mean) * rstd
         pre = hat * row(SECOND_GAIN) + row(SECOND_SHIFT)
         val = back[b] * silu_slope(pre, sigmoid(pre))
@@ -588,20 +594,63 @@
     lane = lax.broadcasted_iota(jnp.int32, (chans, LANES), 1)
     both = jnp.where(lane == 0, gain_sum[0], 0.0) + jnp.where(lane == 1, shift_sum[0], 0.0)
     both = jnp.transpose(both)
-    rows = [vec_a[j : j + 1, :] for j in range(6)]
+    rows = [front_sums[j : j + 1, :] for j in range(6)]
     rows += [sum(gain), sum(shift_g), sum(times), both[0:1], both[1:2]]
-    lane = lax.broadcasted_iota(jnp.int32, (1, LANES), 1)
-    stamp = jnp.zeros((1, LANES), f32)
-    for b in images:
-        step = jnp.full((1, LANES), steps_ref[places[0] * count + b], jnp.int32)
-        stamp = jnp.where(lane == b, (step >> 5).astype(f32), stamp)
-        stamp = jnp.where(lane == LANES // 2 + b, (step & 31).astype(f32), stamp)
     flat = []
     for r in rows + times:
         flat += [r[:, i * LANES : (i + 1) * LANES] for i in range(chans // LANES)]
-    flat.append(stamp)
+    flat.append(front_sums[6:7, :LANES])
     flat += [jnp.zeros((1, LANES), f32)] * (BLOCK - len(flat))
-    small_out[...] = jnp.concatenate(flat, axis=0).astype(bf16)
+    small[...] = jnp.concatenate(flat, axis=0).astype(bf16)
+    outs.append(cps.start(small, small_out))
+    wait_all(outs)
+
+
+def put_quarters(quarters, flat):
+    me = lax.axis_index("batch") & 3
+    rows = quarters[0].shape[0]
+    for j, ref in enumerate(quarters):
+        flat[pl.ds(pl.multiple_of((me ^ j) * rows, 16), rows), :] = ref[...]
+
+
+def unpack_first_kernel(*refs):
+    quarters = refs[:4]
+    dw1_out, flat, dw1, sems = refs[4:]
+    cps = Copies(sems)
+    put_quarters(quarters, flat)
+    outs = []
+    chans = dw1.shape[1]
+    for tap in range(dw1.shape[0]):
+        dw1[tap] = flat[tap * chans : (tap + 1) * chans, :].astype(f32)
+        if tap % 3 == 2:
+            part = slice(tap - 2, tap + 1)
+            outs.append(cps.start(dw1.at[part], dw1_out.at[part]))
+    wait_all(outs)
+
+
+def unpack_second_kernel(*refs):
+    quarters = refs[:4]
+    dw2_out, dpo_out, dpi_out, flat, dw2, dpo, dpi, sems = refs[4:]
+    cps = Copies(sems)
+    put_quarters(quarters, flat)
+    outs = []
+    chans = dpi.shape[1]
+    half = chans // 2
+    for i in range(2):
+        dpo[:, i * LANES : (i + 1) * LANES] = flat[i * half : (i + 1) * half, :].astype(f32)
+    outs.append(cps.start(dpo, dpo_out))
+    at = chans
+    for j in range(3):
+        dpi[j] = flat[at : at + chans, :].astype(f32)
+        at += chans
+    outs.append(cps.start(dpi, dpi_out))
+    for tap in range(dw2.shape[0]):
+        for i in range(2):
+            dw2[tap, :, i * LANES : (i + 1) * LANES] = flat[at : at + half, :].astype(f32)
+            at += half
+        if tap % 3 == 2:
+            part = slice(tap - 2, tap + 1)
+            outs.append(cps.start(dw2.at[part], dw2_out.at[part]))
     wait_all(outs)
 
 
@@ -803,6 +852,8 @@
         (image_p, f32),
         (image_p, f32),
         (image_b, bf16),
+        ((2 * count, chans), f32),
+        ((8, chans), f32),
     ]
     out_a = ANY if pieces == 2 else VMEM
     scratch_a = [pltpu.VMEM(v.shape, v.dtype) for v in grads_a] if pieces == 2 else []
@@ -810,10 +861,9 @@
     front = pl.pallas_call(
         functools.partial(front_kernel, pieces, count),
         out_shape=grads_a
-        + [shape((8, chans), f32), shape((2, count, chans), f32)]
         + [pltpu.HBM(*v) for v in kept],
-        in_specs=[ANY] * (8 * pieces) + [SMEM, ANY],
-        out_specs=[out_a] * n_grad + [VMEM] * 2 + [ANY] * len(kept),
+        in_specs=[ANY, VMEM][:pieces] * 8 + [SMEM, ANY],
+        out_specs=[out_a] * n_grad + [ANY] * len(kept),
         scratch_shapes=scratch_a
         + [pltpu.VMEM(*v) for v in kept]
         + [
@@ -824,23 +874,28 @@
             pltpu.VMEM((3 * points, points), bf16),
             pltpu.VMEM(pads, bf16),
             pltpu.VMEM(pads, bf16),
-            pltpu.SemaphoreType.DMA((8 * pieces + count + 19,)),
+            pltpu.SemaphoreType.DMA((8 * pieces + count + 21,)),
         ],
         compiler_params=params(32),
         cost_estimate=cost(54, 12 << 20),
         name="front",
     )(
-        *(in_hbm(v) for v in x_in + g_in + w1_in + w2_in + pi_in + po_in + tw_in + vec_in),
+        *(
+            place(v)
+            for pair in (x_in, g_in, w1_in, w2_in, pi_in, po_in, tw_in, vec_in)
+            for v, place in zip(pair, (in_hbm, lambda v: v))
+        ),
         steps_in,
         in_hbm(embed_table),
     )
     sums_a = front[:n_grad]
-    vec_a, stat, w1, w2, po, vec, xin = front[n_grad : n_grad + 7]
-    gpad, sum_one, a1t, resid, gres, mix = front[n_grad + 7 :]
-
-    def quarters(sums, axes):
+    kept_now = list(front[n_grad:])
+
+    def quarters(sums, axes, beside=None):
         if pieces == 2:
             got = swap(sums[1], "tensor", 2, 1)
+            if beside is not None:
+                (got,) = after([got], beside)
             rows = got.shape[0] // 4
             own4, got4 = (v.reshape(4, rows, LANES) for v in (sums[0], got))
 
@@ -863,7 +918,7 @@
     sent_a = near_parts(part_a)
 
     got_a = send_near(sent_a, batch)
-    (vec_a,) = after([vec_a], *sent_a)
+    kept_now[-2:] = after(kept_now[-2:], *sent_a)
 
     half = (count, chans // 2, points)
     if pieces == 2:
@@ -874,36 +929,37 @@
         scratch_b = [pltpu.VMEM(image_b, f32)] * 2
     *outs_b, block = pl.pallas_call(
         functools.partial(back_kernel, pieces, count),
-        out_shape=outs_b + [shape((BLOCK, LANES), bf16)],
-        in_specs=[ANY] * len(kept) + [VMEM] * 2 + [SMEM],
-        out_specs=[out_a] * pieces + [ANY] * (2 * pieces) + [VMEM],
+        out_shape=outs_b + [pltpu.HBM((BLOCK, LANES), bf16)],
+        in_specs=[ANY] * len(kept),
+        out_specs=[out_a] * pieces + [ANY] * (2 * pieces + 1),
         scratch_shapes=[pltpu.VMEM(*v) for v in kept]
         + scratch_b
         + [
+            pltpu.VMEM((BLOCK, LANES), bf16),
             pltpu.VMEM(pads, bf16),
             pltpu.VMEM(image_p, f32),
-            pltpu.SemaphoreType.DMA((6 + 5 * count + 10,)),
+            pltpu.SemaphoreType.DMA((6 + 5 * count + 13,)),
         ],
         compiler_params=params(36),
         cost_estimate=cost(33, 12 << 20),
         name="back",
-    )(
-        *(in_hbm(v) for v in (w1, w2, po, vec, xin, gpad, sum_one, a1t, resid, gres, mix)),
-        stat,
-        vec_a,
-        steps_in,
-    )
+    )(*(in_hbm(v) for v in kept_now))
     sums_b, block_part, image_grad = outs_b[:pieces], outs_b[pieces : 2 * pieces], outs_b[2 * pieces :]
     got_a = after(got_a, block)
     sums_b = after(sums_b, *got_a)
     piece_a = sum_near(got_a, part_a)
-    part_b = quarters(sums_b, (2,))
+    part_b = quarters(sums_b, (2,), piece_a)
     sent_b = near_parts(part_b)
-    got_b = send_near(sent_b, batch)
-    (piece_a,) = after([piece_a], *sent_b)
-    blocks = block
-    for step in range(far_steps(batch)):
-        piece_a, blocks = sum_far(piece_a, blocks, send_far(piece_a, blocks, step, batch))
+    got_b = send_near([jnp.concatenate([v, block], axis=0) for v in sent_b], batch)
+    piece_a, _ = sum_far(piece_a, None, send_far(piece_a, None, 0, batch))
+    got_b = after(got_b, piece_a)
+    rows_b = sent_b[0].shape[0]
+    blocks = jnp.concatenate([block] + [g[rows_b:] for g in got_b], axis=0)
+    piece_b = sum_near([g[:rows_b] for g in got_b], part_b)
+    for step in range(1, far_steps(batch)):
+        piece_a, _ = sum_far(piece_a, None, send_far(piece_a, None, step, batch))
+    block_part = after(block_part, piece_b)
+    image_grad = after(image_grad, piece_b)
 
     def placed(own, send):
         if pieces == 2:
@@ -916,30 +972,46 @@
     block_out = placed(block_part[0], block_part[-1])
     images_grad = placed(image_grad[0], image_grad[-1])
 
-    piece_b = sum_near(got_b, part_b)
+    got_a = gather_near(piece_a, batch)
     for step in range(far_steps(batch)):
-        piece_b, _ = sum_far(piece_b, None, send_far(piece_b, None, step, batch))
-    rows_a = piece_a.shape[0]
-    got_a = gather_near(jnp.concatenate([piece_a, blocks], axis=0), batch)
+        far_b = send_far(piece_b, blocks, step, batch)
+        if step > 0:
+            (far_b,) = after([far_b], got_a[0])
+        piece_b, blocks = sum_far(piece_b, blocks, far_b)
+    got_b = gather_near(piece_b, batch)
     got_a = after(got_a, piece_b)
-    done_a = in_order([g[:rows_a] for g in got_a])
-    blocks = jnp.concatenate([g[rows_a:] for g in got_a], axis=0)
-    (piece_b,) = after([piece_b], *got_a)
-    done_b = in_order(gather_near(piece_b, batch))
 
     if pieces == 2:
-        n = chans * chans // 2 // LANES
-        project_out_grad = done_a[:n].reshape(2, local, LANES)
-        project_out_grad = jnp.concatenate([project_out_grad[0], project_out_grad[1]], axis=1)
-        project_in_grad = done_a[n : 4 * n].reshape(3, chans, local)
-        taps_grad = done_a[4 * n :].reshape(9, 2, local, LANES)
-        second_conv_grad = jnp.concatenate([taps_grad[:, 0], taps_grad[:, 1]], axis=2)
-        first_conv_grad = done_b.reshape(9, chans, local)
+
+        def unpacked(kernel, name, got, rows, shapes):
+            outs = [shape(v, f32) for v in shapes]
+            return pl.pallas_call(
+                kernel,
+                out_shape=outs,
+                in_specs=[VMEM] * 4,
+                out_specs=[ANY] * len(outs),
+                scratch_shapes=[pltpu.VMEM((rows, LANES), bf16)]
+                + [pltpu.VMEM(v.shape, v.dtype) for v in outs]
+                + [pltpu.SemaphoreType.DMA((len(outs) + 2,))],
+                compiler_params=params(12),
+                name=name,
+            )(*got)
+
+        second_conv_grad, project_out_grad, project_in_grad = unpacked(
+            unpack_second_kernel,
+            "unpack_second",
+            got_a,
+            half_a,
+            [(9, local, chans), (local, chans), (3, chans, local)],
+        )
+        (first_conv_grad,) = unpacked(
+            unpack_first_kernel, "unpack_first", got_b, half_b, [(9, chans, local)]
+        )
     else:
         second_conv_grad, project_out_grad, project_in_grad = unpack(
-            done_a, [(9, local, chans), (local, chans), (3, chans, local)]
+            in_order(got_a), [(9, local, chans), (local, chans), (3, chans, local)]
         )
-        (first_conv_grad,) = unpack(done_b, [(9, chans, local)])
+        (first_conv_grad,) = unpack(in_order(got_b), [(9, chans, local)])
 
     if pieces == 2:
         blocks = jnp.concatenate([blocks, swap(blocks, "tensor", 2, 1)], axis=0)
@@ -951,6 +1023,7 @@
     wide = chans // LANES
     n_sum = 11 * wide
     sums = jnp.sum(blocks[:, :n_sum].astype(f32), axis=0).reshape(11, chans)
+    sums = jnp.concatenate([sums, sums[8:9]], axis=0)
     mine = lax.dynamic_slice_in_dim(sums, me * local, local, axis=1)
     all_times = blocks[:, n_sum : n_sum + wide * count].reshape(-1, chans)
     stamps = blocks[:, n_sum + wide * count].astype(jnp.int32)
@@ -980,20 +1053,20 @@
         table_grad,
         mine[9],
         mine[10],
-        first_conv_grad.astype(f32),
+        first_conv_grad,
         mine[8],
         time_weight_grad,
-        mine[8],
+        mine[11],
         mine[6],
         mine[7],
-        second_conv_grad.astype(f32),
+        second_conv_grad,
         mine[0],
         mine[1],
         mine[2],
-        project_in_grad.astype(f32),
+        project_in_grad,
         mine[3],
         mine[4],
-        project_out_grad.astype(f32),
+        project_out_grad,
         mine[5],
     )
 

time: 97.2 us -> 87.6 us (0.901)
  the two profiles are of different devices: /device:TPU:0 before, /device:TPU:8 now
where the time goes in v4:
time: 87.6 us; the launch traced here: 87.3 us
  Pallas kernels  29.4 us (34%)
  starting transfers between devices  25 us (29%)
  waiting for transfers between devices  22.1 us (25%)
  other arithmetic  5.49 us (6%)
  matrix products  3.25 us (4%)
  between operations  1.2 us (1%)
  local copies, waits for them, and re-layouts  0.91 us (1%)
    ppermute x25, starting transfers between devices, swap(): return lax.ppermute(value, axis, [(i, i ^ bit) for i in range(size)])  17 us
    pallas_call x1, Pallas kernels, per_device(): pl.pallas_call(functools.partial(front_kernel, pieces, count), out_shape=...  14.4 us
    ppermute x4, waiting for transfers between devices, send_far(): return lax.ppermute(mine, ('batch', 'tensor'), pairs)  11.8 us
    pallas_call x1, Pallas kernels, per_device(): pl.pallas_call(functools.partial(back_kernel, pieces, count), out_shape=o...  11.4 us
    ppermute x25, waiting for transfers between devices, swap(): return lax.ppermute(value, axis, [(i, i ^ bit) for i in range(size)])  10.3 us
    ppermute x4, starting transfers between devices, send_far(): return lax.ppermute(mine, ('batch', 'tensor'), pairs)  7.97 us
    pallas_call x2, Pallas kernels, unpacked(): pl.pallas_call(kernel, out_shape=outs, in_specs=[VMEM] * 4, out_specs=[AN...  2.41 us
    concatenate x2, other arithmetic, placed(): return jnp.concatenate([low, high], axis=0)  2.08 us
  transfers between devices with their start and end apart: 29, of which 11 were waited for; matrix products, arithmetic and copies ran while one was open for 10% of the time, Pallas kernels for 16%

profile of v4, /device:TPU:8, one launch (start us, length us, event | category | flops | bytes accessed | tf_op | source)
XLA Modules:
  0.0 87.3 jit_solution(6462907637922070674)
XLA Ops:
  0.7 0.5 collective-permute-start.3
  1.3 0.4 collective-permute-start.5
  1.7 1.2 %pack.1 = (f32[16,128]{1,0:T(8,128)S(1)}, bf16[4,128,256]{2,1,0:T(8,128)(2,1)S(1)}, bf16[4,128,256]{2,1,0:T(8,128)(2,1)S(1)}) custom-call(f32[128]{0:T(128)} %refs_0_.2, f32[128]{0:T(128)} %refs_1_.1, f32[128]{0:T(128)} %refs_2_.2, f32[128]{0:T(128)} %refs_3_.1, f32[128]{0:T(128)} %refs_4_.2, f32[128]{0:T(128)} %refs_5_.1, f32[128]{0:T(128)} %refs_6_.2, ...), custom_call_target="tpu_custom_call" | custom-call | tf_op jit(solution)/shard_map/pack/pallas_call | solution.py:780
  2.9 0.1 collective-permute-start.7
  3.1 1.1 %collective-permute-done.7.refs_15_ = f32[16,128]{1,0:T(8,128)S(1)} collective-permute-done((f32[16,128]{1,0:T(8,128)S(1)}, f32[16,128]{1,0:T(8,128)S(1)}, u32[]{:S(2)}, u32[]{:S(2)}) %collective-permute-start.7) | collective-permute-done | bytes 8224 | tf_op jit(solution)/shard_map/ppermute | solution.py:658
  4.2 0.2 collective-permute-start
  4.3 0.3 collective-permute-start.1
  4.7 0.2 collective-permute-start.4
  4.9 1.7 %collective-permute-done.4.refs_9_ = bf16[3,256,128]{2,1,0:T(8,128)(2,1)S(1)} collective-permute-done((bf16[3,256,128]{2,1,0:T(8,128)(2,1)}, bf16[3,256,128]{2,1,0:T(8,128)(2,1)S(1)}, u32[]{:S(2)}, u32[]{:S(2)}) %collective-permute-start.4) | collective-permute-done | bytes 196640 | tf_op jit(solution)/shard_map/ppermute | solution.py:658
  6.6 14.4 %front.1 = (bf16[3328,128]{1,0:T(8,128)(2,1)}, bf16[3328,128]{1,0:T(8,128)(2,1)}, bf16[9,256,256]{2,1,0:T(8,128)(2,1)}, bf16[9,256,256]{2,1,0:T(8,128)(2,1)}, bf...) custom-call(bf16[8,128,256]{2,1,0:T(8,128)(2,1)} %refs_0_.3, ...), custom_call_target="tpu_custom_call" | custom-call | flops 7247757312 | bytes 12582912 | tf_op jit(solution)/shard_map/front/pallas_call | solution.py:861
  21.1 0.2 collective-permute-start.8
  21.3 2.4 %collective-permute-done.8 = bf16[3328,128]{1,0:T(8,128)(2,1)S(1)} collective-permute-done((bf16[3328,128]{1,0:T(8,128)(2,1)}, bf16[3328,128]{1,0:T(8,128)(2,1)S(1)}, u32[]{:S(2)}, u32[]{:S(2)}) %collective-permute-start.8) | collective-permute-done | bytes 852000 | tf_op jit(solution)/shard_map/ppermute | solution.py:658
  23.7 1.3 %fusion.29 = (bf16[832,128]{1,0:T(8,128)(2,1)S(1)}, bf16[832,128]{1,0:T(8,128)(2,1)S(1)}, bf16[832,128]{1,0:T(8,128)(2,1)S(1)}) fusion(bf16[4,832,128]{2,1,0:T(8,128)(2,1)S(1)} %bitcast.68, s32[]{:T(128)S(6)} %select_n.71, bf16[4,832,128]{2,1,0:T(8,128)(2,1)} %bitcast.66, s32[]{:T(128)S(6)} %select_n.70, s32[]{:T(128)S(6)} %select_n.69), kind=kLoop, calls=%fused_computation.51 | loop fusion | flops 1277952 | bytes 1916940 | tf_op jit(solution)/shard_map/convert_element_type | solution.py:663
  25.0 1.6 %collective-permute-start.10 = (bf16[832,128]{1,0:T(8,128)(2,1)S(1)}, bf16[832,128]{1,0:T(8,128)(2,1)S(1)}, u32[]{:S(2)}, u32[]{:S(2)}) collective-permute-start(bf16[832,128]{1,0:T(8,128)(2,1)S(1)} %get-tuple-element.119), channel_id=1, source_target_pairs={{0,4},{2,6},{4,0},{6,2},{8,12},{10,14},{12,8},{14,10},{16,20},{18,... | collective-permute-start | bytes 638984 | tf_op jit(solution)/shard_map/ppermute | solution.py:658
  26.6 1.4 %collective-permute-start.11 = (bf16[832,128]{1,0:T(8,128)(2,1)S(1)}, bf16[832,128]{1,0:T(8,128)(2,1)S(1)}, u32[]{:S(2)}, u32[]{:S(2)}) collective-permute-start(bf16[832,128]{1,0:T(8,128)(2,1)S(1)} %get-tuple-element.118), channel_id=1, source_target_pairs={{0,6},{2,4},{4,2},{6,0},{8,14},{10,12},{12,10},{14,8},{16,22},{18,... | collective-permute-start | bytes 638984 | tf_op jit(solution)/shard_map/ppermute | solution.py:658
  28.0 0.5 collective-permute-start.9
  28.6 11.4 %back.1 = (bf16[2304,128]{1,0:T(8,128)(2,1)}, bf16[2304,128]{1,0:T(8,128)(2,1)}, f32[4,128,256]{2,1,0:T(8,128)}, bf16[4,128,256]{2,1,0:T(8,128)(2,1)}, f32[4,128...) custom-call(bf16[9,256,256]{2,1,0:T(8,128)(2,1)} %get-tuple-element.71.refs_0_, ...), custom_call_target="tpu_custom_call" | custom-call | flops 4429185024 | bytes 12582912 | tf_op jit(solution)/shard_map/back/pallas_call | solution.py:930
  40.1 1.1 %fusion.5 = bf16[832,128]{1,0:T(8,128)(2,1)S(1)} fusion(bf16[832,128]{1,0:T(8,128)(2,1)S(1)} %collective-permute-done.11, bf16[832,128]{1,0:T(8,128)(2,1)S(1)} %collective-permute-done.10, bf16[832,128]{1,0:T(8,128)(2,1)S(1)} %collective-permute-done.9, bf16[4,832,128]{2,1,0:T(8,128)(2,1)S(1)} %bitcast.69, s32[]{:T(128)S(6)} %select_n.72, ...), kind=kLoop, calls=%fused_computation.14 | loop fusion | flops 1064960 | bytes 1277956 | tf_op jit(solution)/shard_map/convert_element_type | solution.py:679
  41.4 1.0 %collective-permute-done.12 = bf16[2304,128]{1,0:T(8,128)(2,1)S(1)} collective-permute-done((bf16[2304,128]{1,0:T(8,128)(2,1)}, bf16[2304,128]{1,0:T(8,128)(2,1)S(1)}, u32[]{:S(2)}, u32[]{:S(2)}) %collective-permute-start.12) | collective-permute-done | bytes 589856 | tf_op jit(solution)/shard_map/ppermute | solution.py:658
  42.5 1.5 %collective-permute-start.13 = (bf16[608,128]{1,0:T(8,128)(2,1)S(1)}, bf16[608,128]{1,0:T(8,128)(2,1)S(1)}, u32[]{:S(2)}, u32[]{:S(2)}) collective-permute-start(bf16[608,128]{1,0:T(8,128)(2,1)S(1)} %get-tuple-element.159), channel_id=1, source_target_pairs={{0,2},{2,0},{4,6},{6,4},{8,10},{10,8},{12,14},{14,12},{16,18},{18,... | collective-permute-start | bytes 466952 | tf_op jit(solution)/shard_map/ppermute | solution.py:658
  44.1 1.5 %collective-permute-start.14 = (bf16[608,128]{1,0:T(8,128)(2,1)S(1)}, bf16[608,128]{1,0:T(8,128)(2,1)S(1)}, u32[]{:S(2)}, u32[]{:S(2)}) collective-permute-start(bf16[608,128]{1,0:T(8,128)(2,1)S(1)} %get-tuple-element.158), channel_id=1, source_target_pairs={{0,4},{2,6},{4,0},{6,2},{8,12},{10,14},{12,8},{14,10},{16,20},{18,... | collective-permute-start | bytes 466952 | tf_op jit(solution)/shard_map/ppermute | solution.py:658
  45.6 0.5 collective-permute-start.15
  46.1 3.0 %collective-permute-done.16 = bf16[832,128]{1,0:T(8,128)(2,1)S(1)} collective-permute-done((bf16[832,128]{1,0:T(8,128)(2,1)S(1)}, bf16[832,128]{1,0:T(8,128)(2,1)S(1)}, u32[]{:S(2)}, u32[]{:S(2)}) %collective-permute-start.16) | collective-permute-done | bytes 213024 | tf_op jit(solution)/shard_map/ppermute | solution.py:695
  49.1 2.7 %collective-permute-start.21 = (bf16[832,128]{1,0:T(8,128)(2,1)S(1)}, bf16[832,128]{1,0:T(8,128)(2,1)S(1)}, u32[]{:S(2)}, u32[]{:S(2)}) collective-permute-start(bf16[832,128]{1,0:T(8,128)(2,1)S(1)} %add_convert_fusion.1), channel_id=1, source_target_pairs={{0,16},{1,9},{2,18},{3,11},{4,20},{5,13},{6,22},{7,15},{8,24},{9,1... | collective-permute-start | bytes 638984 | tf_op jit(solution)/shard_map/ppermute | solution.py:695
  51.8 1.1 %collective-permute-done.14 = bf16[608,128]{1,0:T(8,128)(2,1)S(1)} collective-permute-done((bf16[608,128]{1,0:T(8,128)(2,1)S(1)}, bf16[608,128]{1,0:T(8,128)(2,1)S(1)}, u32[]{:S(2)}, u32[]{:S(2)}) %collective-permute-start.14) | collective-permute-done | bytes 155680 | tf_op jit(solution)/shard_map/ppermute | solution.py:658
  52.9 0.7 collective-permute-done.15
  53.7 1.8 %collective-permute-start.19 = (bf16[704,128]{1,0:T(8,128)(2,1)S(1)}, bf16[704,128]{1,0:T(8,128)(2,1)S(1)}, u32[]{:S(2)}, u32[]{:S(2)}) collective-permute-start(bf16[704,128]{1,0:T(8,128)(2,1)S(1)} %constant_dynamic-update-slice_fusion), channel_id=1, source_target_pairs={{0,8},{1,17},{2,10},{3,19},{4,12},{5,21},{6,14},{7,23},{8,0},{9,25... | collective-permute-start | bytes 540680 | tf_op jit(solution)/shard_map/ppermute | solution.py:695
  55.5 5.6 %collective-permute-done.21 = bf16[832,128]{1,0:T(8,128)(2,1)S(1)} collective-permute-done((bf16[832,128]{1,0:T(8,128)(2,1)S(1)}, bf16[832,128]{1,0:T(8,128)(2,1)S(1)}, u32[]{:S(2)}, u32[]{:S(2)}) %collective-permute-start.21) | collective-permute-done | bytes 213024 | tf_op jit(solution)/shard_map/ppermute | solution.py:695
  61.1 1.5 %collective-permute-start.26 = (bf16[832,128]{1,0:T(8,128)(2,1)S(1)}, bf16[832,128]{1,0:T(8,128)(2,1)S(1)}, u32[]{:S(2)}, u32[]{:S(2)}) collective-permute-start(bf16[832,128]{1,0:T(8,128)(2,1)S(1)} %add_convert_fusion.refs_0_), channel_id=1, source_target_pairs={{0,2},{2,0},{4,6},{6,4},{8,10},{10,8},{12,14},{14,12},{16,18},{18,... | collective-permute-start | bytes 638984 | tf_op jit(solution)/shard_map/ppermute | solution.py:658
  62.7 1.3 %collective-permute-start.27 = (bf16[832,128]{1,0:T(8,128)(2,1)S(1)}, bf16[832,128]{1,0:T(8,128)(2,1)S(1)}, u32[]{:S(2)}, u32[]{:S(2)}) collective-permute-start(bf16[832,128]{1,0:T(8,128)(2,1)S(1)} %add_convert_fusion.refs_0_), channel_id=1, source_target_pairs={{0,4},{2,6},{4,0},{6,2},{8,12},{10,14},{12,8},{14,10},{16,20},{18,... | collective-permute-start | bytes 638984 | tf_op jit(solution)/shard_map/ppermute | solution.py:658
  63.9 0.8 collective-permute-start.28
  64.7 0.5 collective-permute-start.18
  65.3 0.9 %collective-permute-done.17 = bf16[4,128,256]{2,1,0:T(8,128)(2,1)S(1)} collective-permute-done((bf16[4,128,256]{2,1,0:T(8,128)(2,1)S(1)}, bf16[4,128,256]{2,1,0:T(8,128)(2,1)S(1)}, u32[]{:S(2)}, u32[]{:S(2)}) %collective-permute-start.17) | collective-permute-done | bytes 262176 | tf_op jit(solution)/shard_map/ppermute | solution.py:658
  66.2 3.4 %collective-permute-start.20 = (bf16[832,128]{1,0:T(8,128)(2,1)S(1)}, bf16[832,128]{1,0:T(8,128)(2,1)S(1)}, u32[]{:S(2)}, u32[]{:S(2)}) collective-permute-start(bf16[832,128]{1,0:T(8,128)(2,1)S(1)} %get-tuple-element.132), channel_id=1, source_target_pairs={{0,16},{1,9},{2,18},{3,11},{4,20},{5,13},{6,22},{7,15},{8,24},{9,1... | collective-permute-start | bytes 638984 | tf_op jit(solution)/shard_map/ppermute | solution.py:695
  69.7 0.2 convert_select_fusion.1
  69.9 1.0 %pad_maximum_fusion.1 = f32[8,128,256]{2,1,0:T(8,128)} fusion(f32[4,128,256]{2,1,0:T(8,128)S(1)} %get-tuple-element.125, f32[4,128,256]{2,1,0:T(8,128)S(1)} %get-tuple-element.124), kind=kLoop, calls=%fused_computation.4 | loop fusion | flops 262144 | bytes 2097152 | tf_op jit(solution)/shard_map/concatenate | solution.py:969
  70.9 1.0 %pad_maximum_fusion = f32[8,128,256]{2,1,0:T(8,128)} fusion(f32[4,128,256]{2,1,0:T(8,128)S(1)} %get-tuple-element.160, f32[4,128,256]{2,1,0:T(8,128)S(1)} %get-tuple-element.161), kind=kLoop, calls=%fused_computation.3 | loop fusion | flops 262144 | bytes 2097152 | tf_op jit(solution)/shard_map/concatenate | solution.py:969
  72.0 3.2 %collective-permute-done.20 = bf16[832,128]{1,0:T(8,128)(2,1)S(1)} collective-permute-done((bf16[832,128]{1,0:T(8,128)(2,1)S(1)}, bf16[832,128]{1,0:T(8,128)(2,1)S(1)}, u32[]{:S(2)}, u32[]{:S(2)}) %collective-permute-start.20) | collective-permute-done | bytes 213024 | tf_op jit(solution)/shard_map/ppermute | solution.py:695
  75.4 1.5 %collective-permute-start.23 = (bf16[576,128]{1,0:T(8,128)(2,1)S(1)}, bf16[576,128]{1,0:T(8,128)(2,1)S(1)}, u32[]{:S(2)}, u32[]{:S(2)}) collective-permute-start(bf16[576,128]{1,0:T(8,128)(2,1)S(1)} %add_convert_fusion.5.refs_0_), channel_id=1, source_target_pairs={{0,2},{2,0},{4,6},{6,4},{8,10},{10,8},{12,14},{14,12},{16,18},{18,... | collective-permute-start | bytes 442376 | tf_op jit(solution)/shard_map/ppermute | solution.py:658
  76.9 1.2 %collective-permute-start.24 = (bf16[576,128]{1,0:T(8,128)(2,1)S(1)}, bf16[576,128]{1,0:T(8,128)(2,1)S(1)}, u32[]{:S(2)}, u32[]{:S(2)}) collective-permute-start(bf16[576,128]{1,0:T(8,128)(2,1)S(1)} %add_convert_fusion.5.refs_0_), channel_id=1, source_target_pairs={{0,4},{2,6},{4,0},{6,2},{8,12},{10,14},{12,8},{14,10},{16,20},{18,... | collective-permute-start | bytes 442376 | tf_op jit(solution)/shard_map/ppermute | solution.py:658
  78.1 0.8 collective-permute-start.25
  79.0 1.3 %unpack_second.1 = (f32[9,128,256]{2,1,0:T(8,128)}, f32[128,256]{1,0:T(8,128)}, f32[3,256,128]{2,1,0:T(8,128)}) custom-call(bf16[832,128]{1,0:T(8,128)(2,1)S(1)} %add_convert_fusion.refs_0_, bf16[832,128]{1,0:T(8,128)(2,1)S(1)} %collective-permute-done.26.refs_1_, bf16[832,128]{1,0:T(8,128)(2,1)S(1)} %collective-permute-done.27.refs_2_, ...), custom_call_target="tpu_custom_call" | custom-call | tf_op jit(solution)/shard_map/unpack_second/pallas_call | solution.py:988
  80.7 0.3 fusion.2
  81.1 0.9 %fusion.33 = f32[512,128]{1,0:T(8,128)} fusion(f32[128,512]{1,0:T(8,128)S(1)} %fusion.2, bf16[128,256]{1,0:T(8,128)(2,1)S(1)} %reshape.104, s32[]{:T(128)S(6)} %select_n.81), kind=kOutput, calls=%fused_computation.55 | convolution fusion | flops 17104896 | bytes 557060 | tf_op jit(solution)/shard_map/dot_general | solution.py:1037
  82.1 2.0 %fusion.1 = f32[1024,512]{1,0:T(8,128)} fusion(bf16[128,256]{1,0:T(8,128)(2,1)S(1)} %reshape.104, bf16[512,128]{1,0:T(8,128)(2,1)S(1)} %collective-permute-done.6.refs_13_, bf16[512,128]{1,0:T(8,128)(2,1)S(1)} %copy-done.5, f32[128,512]{1,0:T(8,128)S(1)} %fusion.2, s32[128]{0:T(128)S(1)} %eq.11, pred[]{:T(512)S(6)} %eq.10), kind=kOutput, calls=%fused_computation.2 | convolution fusion | flops 169672704 | bytes 2687489 | tf_op jit(solution)/shard_map/dot_general | solution.py:1047
  84.1 0.6 slice_bitcast_fusion
  84.7 1.4 %collective-permute-done.24.refs_2_ = bf16[576,128]{1,0:T(8,128)(2,1)S(1)} collective-permute-done((bf16[576,128]{1,0:T(8,128)(2,1)S(1)}, bf16[576,128]{1,0:T(8,128)(2,1)S(1)}, u32[]{:S(2)}, u32[]{:S(2)}) %collective-permute-start.24) | collective-permute-done | bytes 147488 | tf_op jit(solution)/shard_map/ppermute | solution.py:658
  86.1 1.1 %unpack_first.1 = f32[9,256,128]{2,1,0:T(8,128)} custom-call(bf16[576,128]{1,0:T(8,128)(2,1)S(1)} %add_convert_fusion.5.refs_0_, bf16[576,128]{1,0:T(8,128)(2,1)S(1)} %collective-permute-done.23.refs_1_, bf16[576,128]{1,0:T(8,128)(2,1)S(1)} %collective-permute-done.24.refs_2_, bf16[576,128]{1,0:T(8,128)(2,1)S(1)} %collective-permute-done.25.refs_3_), custom_call_target="tpu_custom_call" | custom-call | tf_op jit(solution)/shard_map/unpack_first/pallas_call | solution.py:988
  (70 shorter events, 1.5 us)
Async XLA Ops:
  0.7 5.9 %collective-permute-start.2 = (bf16[9,256,128]{2,1,0:T(8,128)(2,1)}, bf16[9,256,128]{2,1,0:T(8,128)(2,1)S(1)}, u32[]{:S(2)}, u32[]{:S(2)}) collective-permute-start(bf16[9,256,128]{2,1,0:T(8,128)(2,1)} %refs_4_.3), channel_id=1, source_target_pairs={{0,1},{1,0},{2,3},{3,2},{4,5},{5,4},{6,7},{7,6},{8,9},{9,8},{10,11... | collective-permute-start | bytes 1769480 | tf_op jit(solution)/shard_map/ppermute | solution.py:658
  0.7 5.9 %collective-permute-start.3 = (bf16[9,128,256]{2,1,0:T(8,128)(2,1)}, bf16[9,128,256]{2,1,0:T(8,128)(2,1)S(1)}, u32[]{:S(2)}, u32[]{:S(2)}) collective-permute-start(bf16[9,128,256]{2,1,0:T(8,128)(2,1)} %refs_6_.3), channel_id=1, source_target_pairs={{0,1},{1,0},{2,3},{3,2},{4,5},{5,4},{6,7},{7,6},{8,9},{9,8},{10,11... | collective-permute-start | bytes 1769480 | tf_op jit(solution)/shard_map/ppermute | solution.py:658
  1.2 3.5 %collective-permute-start.6 = (bf16[512,128]{1,0:T(8,128)(2,1)}, bf16[512,128]{1,0:T(8,128)(2,1)S(1)}, u32[]{:S(2)}, u32[]{:S(2)}) collective-permute-start(bf16[512,128]{1,0:T(8,128)(2,1)} %refs_12_.3), channel_id=1, source_target_pairs={{0,1},{1,0},{2,3},{3,2},{4,5},{5,4},{6,7},{7,6},{8,9},{9,8},{10,11... | collective-permute-start | bytes 393224 | tf_op jit(solution)/shard_map/ppermute | solution.py:658
  1.3 3.0 %collective-permute-start.5 = (bf16[128,256]{1,0:T(8,128)(2,1)}, bf16[128,256]{1,0:T(8,128)(2,1)S(1)}, u32[]{:S(2)}, u32[]{:S(2)}) collective-permute-start(bf16[128,256]{1,0:T(8,128)(2,1)} %refs_10_.3), channel_id=1, source_target_pairs={{0,1},{1,0},{2,3},{3,2},{4,5},{5,4},{6,7},{7,6},{8,9},{9,8},{10,11... | collective-permute-start | bytes 196616 | tf_op jit(solution)/shard_map/ppermute | solution.py:658
  2.9 3.7 %copy-start = (f32[16,128]{1,0:T(8,128)}, f32[16,128]{1,0:T(8,128)S(1)}, u32[]{:S(2)}) copy-start(f32[16,128]{1,0:T(8,128)S(1)} %get-tuple-element.70.refs_14_) | copy-start | bytes 24580
  2.9 1.2 %collective-permute-start.7 = (f32[16,128]{1,0:T(8,128)S(1)}, f32[16,128]{1,0:T(8,128)S(1)}, u32[]{:S(2)}, u32[]{:S(2)}) collective-permute-start(f32[16,128]{1,0:T(8,128)S(1)} %get-tuple-element.70.refs_14_), channel_id=1, source_target_pairs={{0,1},{1,0},{2,3},{3,2},{4,5},{5,4},{6,7},{7,6},{8,9},{9,8},{10,11... | collective-permute-start | bytes 24584 | tf_op jit(solution)/shard_map/ppermute | solution.py:658
  4.2 2.4 %collective-permute-start = (bf16[4,128,256]{2,1,0:T(8,128)(2,1)S(1)}, bf16[4,128,256]{2,1,0:T(8,128)(2,1)S(1)}, u32[]{:S(2)}, u32[]{:S(2)}) collective-permute-start(bf16[4,128,256]{2,1,0:T(8,128)(2,1)S(1)} %get-tuple-element.68), channel_id=1, source_target_pairs={{0,1},{1,0},{2,3},{3,2},{4,5},{5,4},{6,7},{7,6},{8,9},{9,8},{10,11... | collective-permute-start | bytes 786440 | tf_op jit(solution)/shard_map/ppermute | solution.py:658
  4.3 2.2 %collective-permute-start.1 = (bf16[4,128,256]{2,1,0:T(8,128)(2,1)S(1)}, bf16[4,128,256]{2,1,0:T(8,128)(2,1)S(1)}, u32[]{:S(2)}, u32[]{:S(2)}) collective-permute-start(bf16[4,128,256]{2,1,0:T(8,128)(2,1)S(1)} %get-tuple-element.69), channel_id=1, source_target_pairs={{0,1},{1,0},{2,3},{3,2},{4,5},{5,4},{6,7},{7,6},{8,9},{9,8},{10,11... | collective-permute-start | bytes 786440 | tf_op jit(solution)/shard_map/ppermute | solution.py:658
  4.7 1.9 %collective-permute-start.4 = (bf16[3,256,128]{2,1,0:T(8,128)(2,1)}, bf16[3,256,128]{2,1,0:T(8,128)(2,1)S(1)}, u32[]{:S(2)}, u32[]{:S(2)}) collective-permute-start(bf16[3,256,128]{2,1,0:T(8,128)(2,1)} %refs_8_.3), channel_id=1, source_target_pairs={{0,1},{1,0},{2,3},{3,2},{4,5},{5,4},{6,7},{7,6},{8,9},{9,8},{10,11... | collective-permute-start | bytes 589832 | tf_op jit(solution)/shard_map/ppermute | solution.py:658
  21.1 2.7 %collective-permute-start.8 = (bf16[3328,128]{1,0:T(8,128)(2,1)}, bf16[3328,128]{1,0:T(8,128)(2,1)S(1)}, u32[]{:S(2)}, u32[]{:S(2)}) collective-permute-start(bf16[3328,128]{1,0:T(8,128)(2,1)} %get-tuple-element.85), channel_id=1, source_target_pairs={{0,1},{1,0},{2,3},{3,2},{4,5},{5,4},{6,7},{7,6},{8,9},{9,8},{10,11... | collective-permute-start | bytes 2555912 | tf_op jit(solution)/shard_map/ppermute | solution.py:658
  25.0 15.0 %collective-permute-start.10 = (bf16[832,128]{1,0:T(8,128)(2,1)S(1)}, bf16[832,128]{1,0:T(8,128)(2,1)S(1)}, u32[]{:S(2)}, u32[]{:S(2)}) collective-permute-start(bf16[832,128]{1,0:T(8,128)(2,1)S(1)} %get-tuple-element.119), channel_id=1, source_target_pairs={{0,4},{2,6},{4,0},{6,2},{8,12},{10,14},{12,8},{14,10},{16,20},{18,... | collective-permute-start | bytes 638984 | tf_op jit(solution)/shard_map/ppermute | solution.py:658
  26.6 13.4 %collective-permute-start.11 = (bf16[832,128]{1,0:T(8,128)(2,1)S(1)}, bf16[832,128]{1,0:T(8,128)(2,1)S(1)}, u32[]{:S(2)}, u32[]{:S(2)}) collective-permute-start(bf16[832,128]{1,0:T(8,128)(2,1)S(1)} %get-tuple-element.118), channel_id=1, source_target_pairs={{0,6},{2,4},{4,2},{6,0},{8,14},{10,12},{12,10},{14,8},{16,22},{18,... | collective-permute-start | bytes 638984 | tf_op jit(solution)/shard_map/ppermute | solution.py:658
  28.0 12.0 %collective-permute-start.9 = (bf16[832,128]{1,0:T(8,128)(2,1)S(1)}, bf16[832,128]{1,0:T(8,128)(2,1)S(1)}, u32[]{:S(2)}, u32[]{:S(2)}) collective-permute-start(bf16[832,128]{1,0:T(8,128)(2,1)S(1)} %get-tuple-element.120), channel_id=1, source_target_pairs={{0,2},{2,0},{4,6},{6,4},{8,10},{10,8},{12,14},{14,12},{16,18},{18,... | collective-permute-start | bytes 638984 | tf_op jit(solution)/shard_map/ppermute | solution.py:658
  40.0 2.3 %copy-start.2 = (bf16[2304,128]{1,0:T(8,128)(2,1)S(1)}, bf16[2304,128]{1,0:T(8,128)(2,1)}, u32[]{:S(2)}) copy-start(bf16[2304,128]{1,0:T(8,128)(2,1)} %get-tuple-element.96) | copy-start | bytes 1769476
  40.0 2.3 %collective-permute-start.12 = (bf16[2304,128]{1,0:T(8,128)(2,1)}, bf16[2304,128]{1,0:T(8,128)(2,1)S(1)}, u32[]{:S(2)}, u32[]{:S(2)}) collective-permute-start(bf16[2304,128]{1,0:T(8,128)(2,1)} %get-tuple-element.97), channel_id=1, source_target_pairs={{0,1},{1,0},{2,3},{3,2},{4,5},{5,4},{6,7},{7,6},{8,9},{9,8},{10,11... | collective-permute-start | bytes 1769480 | tf_op jit(solution)/shard_map/ppermute | solution.py:658
  40.1 2.3 %copy-start.6 = (bf16[32,128]{1,0:T(8,128)(2,1)S(1)}, bf16[32,128]{1,0:T(8,128)(2,1)}, u32[]{:S(2)}) copy-start(bf16[32,128]{1,0:T(8,128)(2,1)} %get-tuple-element.92) | copy-start | bytes 24580
  41.3 7.8 %collective-permute-start.16 = (bf16[832,128]{1,0:T(8,128)(2,1)S(1)}, bf16[832,128]{1,0:T(8,128)(2,1)S(1)}, u32[]{:S(2)}, u32[]{:S(2)}) collective-permute-start(bf16[832,128]{1,0:T(8,128)(2,1)S(1)} %fusion.5), channel_id=1, source_target_pairs={{0,8},{1,17},{2,10},{3,19},{4,12},{5,21},{6,14},{7,23},{8,0},{9,25... | collective-permute-start | bytes 638984 | tf_op jit(solution)/shard_map/ppermute | solution.py:695
  42.5 9.3 %collective-permute-start.13 = (bf16[608,128]{1,0:T(8,128)(2,1)S(1)}, bf16[608,128]{1,0:T(8,128)(2,1)S(1)}, u32[]{:S(2)}, u32[]{:S(2)}) collective-permute-start(bf16[608,128]{1,0:T(8,128)(2,1)S(1)} %get-tuple-element.159), channel_id=1, source_target_pairs={{0,2},{2,0},{4,6},{6,4},{8,10},{10,8},{12,14},{14,12},{16,18},{18,... | collective-permute-start | bytes 466952 | tf_op jit(solution)/shard_map/ppermute | solution.py:658
  44.1 8.8 %collective-permute-start.14 = (bf16[608,128]{1,0:T(8,128)(2,1)S(1)}, bf16[608,128]{1,0:T(8,128)(2,1)S(1)}, u32[]{:S(2)}, u32[]{:S(2)}) collective-permute-start(bf16[608,128]{1,0:T(8,128)(2,1)S(1)} %get-tuple-element.158), channel_id=1, source_target_pairs={{0,4},{2,6},{4,0},{6,2},{8,12},{10,14},{12,8},{14,10},{16,20},{18,... | collective-permute-start | bytes 466952 | tf_op jit(solution)/shard_map/ppermute | solution.py:658
  45.6 19.1 %copy-start.8 = (bf16[4,128,256]{2,1,0:T(8,128)(2,1)S(1)}, bf16[4,128,256]{2,1,0:T(8,128)(2,1)}, u32[]{:S(2)}) copy-start(bf16[4,128,256]{2,1,0:T(8,128)(2,1)} %get-tuple-element.103) | copy-start | bytes 786436
  45.6 19.1 %copy-start.7 = (bf16[4,128,256]{2,1,0:T(8,128)(2,1)S(1)}, bf16[4,128,256]{2,1,0:T(8,128)(2,1)}, u32[]{:S(2)}) copy-start(bf16[4,128,256]{2,1,0:T(8,128)(2,1)} %get-tuple-element.107) | copy-start | bytes 786436
  45.6 8.0 %collective-permute-start.15 = (bf16[608,128]{1,0:T(8,128)(2,1)S(1)}, bf16[608,128]{1,0:T(8,128)(2,1)S(1)}, u32[]{:S(2)}, u32[]{:S(2)}) collective-permute-start(bf16[608,128]{1,0:T(8,128)(2,1)S(1)} %get-tuple-element.157), channel_id=1, source_target_pairs={{0,6},{2,4},{4,2},{6,0},{8,14},{10,12},{12,10},{14,8},{16,22},{18,... | collective-permute-start | bytes 466952 | tf_op jit(solution)/shard_map/ppermute | solution.py:658
  49.1 20.5 %copy-start.3 = (f32[4,128,256]{2,1,0:T(8,128)S(1)}, f32[4,128,256]{2,1,0:T(8,128)}, u32[]{:S(2)}) copy-start(f32[4,128,256]{2,1,0:T(8,128)} %get-tuple-element.102) | copy-start | bytes 1572868
  49.1 20.5 %copy-start.4 = (f32[4,128,256]{2,1,0:T(8,128)S(1)}, f32[4,128,256]{2,1,0:T(8,128)}, u32[]{:S(2)}) copy-start(f32[4,128,256]{2,1,0:T(8,128)} %get-tuple-element.106) | copy-start | bytes 1572868
  49.1 11.9 %collective-permute-start.21 = (bf16[832,128]{1,0:T(8,128)(2,1)S(1)}, bf16[832,128]{1,0:T(8,128)(2,1)S(1)}, u32[]{:S(2)}, u32[]{:S(2)}) collective-permute-start(bf16[832,128]{1,0:T(8,128)(2,1)S(1)} %add_convert_fusion.1), channel_id=1, source_target_pairs={{0,16},{1,9},{2,18},{3,11},{4,20},{5,13},{6,22},{7,15},{8,24},{9,1... | collective-permute-start | bytes 638984 | tf_op jit(solution)/shard_map/ppermute | solution.py:695
  53.7 11.0 %collective-permute-start.19 = (bf16[704,128]{1,0:T(8,128)(2,1)S(1)}, bf16[704,128]{1,0:T(8,128)(2,1)S(1)}, u32[]{:S(2)}, u32[]{:S(2)}) collective-permute-start(bf16[704,128]{1,0:T(8,128)(2,1)S(1)} %constant_dynamic-update-slice_fusion), channel_id=1, source_target_pairs={{0,8},{1,17},{2,10},{3,19},{4,12},{5,21},{6,14},{7,23},{8,0},{9,25... | collective-permute-start | bytes 540680 | tf_op jit(solution)/shard_map/ppermute | solution.py:695
  61.1 15.8 %collective-permute-start.26 = (bf16[832,128]{1,0:T(8,128)(2,1)S(1)}, bf16[832,128]{1,0:T(8,128)(2,1)S(1)}, u32[]{:S(2)}, u32[]{:S(2)}) collective-permute-start(bf16[832,128]{1,0:T(8,128)(2,1)S(1)} %add_convert_fusion.refs_0_), channel_id=1, source_target_pairs={{0,2},{2,0},{4,6},{6,4},{8,10},{10,8},{12,14},{14,12},{16,18},{18,... | collective-permute-start | bytes 638984 | tf_op jit(solution)/shard_map/ppermute | solution.py:658
  62.7 15.5 %collective-permute-start.27 = (bf16[832,128]{1,0:T(8,128)(2,1)S(1)}, bf16[832,128]{1,0:T(8,128)(2,1)S(1)}, u32[]{:S(2)}, u32[]{:S(2)}) collective-permute-start(bf16[832,128]{1,0:T(8,128)(2,1)S(1)} %add_convert_fusion.refs_0_), channel_id=1, source_target_pairs={{0,4},{2,6},{4,0},{6,2},{8,12},{10,14},{12,8},{14,10},{16,20},{18,... | collective-permute-start | bytes 638984 | tf_op jit(solution)/shard_map/ppermute | solution.py:658
  63.9 15.0 %collective-permute-start.28 = (bf16[832,128]{1,0:T(8,128)(2,1)S(1)}, bf16[832,128]{1,0:T(8,128)(2,1)S(1)}, u32[]{:S(2)}, u32[]{:S(2)}) collective-permute-start(bf16[832,128]{1,0:T(8,128)(2,1)S(1)} %add_convert_fusion.refs_0_), channel_id=1, source_target_pairs={{0,6},{2,4},{4,2},{6,0},{8,14},{10,12},{12,10},{14,8},{16,22},{18,... | collective-permute-start | bytes 638984 | tf_op jit(solution)/shard_map/ppermute | solution.py:658
  64.7 1.5 %collective-permute-start.17 = (bf16[4,128,256]{2,1,0:T(8,128)(2,1)S(1)}, bf16[4,128,256]{2,1,0:T(8,128)(2,1)S(1)}, u32[]{:S(2)}, u32[]{:S(2)}) collective-permute-start(bf16[4,128,256]{2,1,0:T(8,128)(2,1)S(1)} %copy-done.8), channel_id=1, source_target_pairs={{0,1},{1,0},{2,3},{3,2},{4,5},{5,4},{6,7},{7,6},{8,9},{9,8},{10,11... | collective-permute-start | bytes 786440 | tf_op jit(solution)/shard_map/ppermute | solution.py:658
  64.7 5.0 %collective-permute-start.18 = (bf16[4,128,256]{2,1,0:T(8,128)(2,1)S(1)}, bf16[4,128,256]{2,1,0:T(8,128)(2,1)S(1)}, u32[]{:S(2)}, u32[]{:S(2)}) collective-permute-start(bf16[4,128,256]{2,1,0:T(8,128)(2,1)S(1)} %copy-done.7), channel_id=1, source_target_pairs={{0,1},{1,0},{2,3},{3,2},{4,5},{5,4},{6,7},{7,6},{8,9},{9,8},{10,11... | collective-permute-start | bytes 786440 | tf_op jit(solution)/shard_map/ppermute | solution.py:658
  66.2 9.0 %collective-permute-start.20 = (bf16[832,128]{1,0:T(8,128)(2,1)S(1)}, bf16[832,128]{1,0:T(8,128)(2,1)S(1)}, u32[]{:S(2)}, u32[]{:S(2)}) collective-permute-start(bf16[832,128]{1,0:T(8,128)(2,1)S(1)} %get-tuple-element.132), channel_id=1, source_target_pairs={{0,16},{1,9},{2,18},{3,11},{4,20},{5,13},{6,22},{7,15},{8,24},{9,1... | collective-permute-start | bytes 638984 | tf_op jit(solution)/shard_map/ppermute | solution.py:695
  75.2 5.0 %collective-permute-start.22 = (bf16[512,128]{1,0:T(8,128)(2,1)S(1)}, bf16[512,128]{1,0:T(8,128)(2,1)S(1)}, u32[]{:S(2)}, u32[]{:S(2)}) collective-permute-start(bf16[512,128]{1,0:T(8,128)(2,1)S(1)} %get-tuple-element.128), channel_id=1, source_target_pairs={{0,1},{1,0},{2,3},{3,2},{4,5},{5,4},{6,7},{7,6},{8,9},{9,8},{10,11... | collective-permute-start | bytes 393224 | tf_op jit(solution)/shard_map/ppermute | solution.py:658
  75.4 5.3 %copy-start.1 = (bf16[1024,512]{1,0:T(8,128)(2,1)S(1)}, bf16[1024,512]{1,0:T(8,128)(2,1)}, u32[]{:S(2)}) copy-start(bf16[1024,512]{1,0:T(8,128)(2,1)} %refs_17_.1) | copy-start | bytes 3145732
  75.4 9.3 %collective-permute-start.23 = (bf16[576,128]{1,0:T(8,128)(2,1)S(1)}, bf16[576,128]{1,0:T(8,128)(2,1)S(1)}, u32[]{:S(2)}, u32[]{:S(2)}) collective-permute-start(bf16[576,128]{1,0:T(8,128)(2,1)S(1)} %add_convert_fusion.5.refs_0_), channel_id=1, source_target_pairs={{0,2},{2,0},{4,6},{6,4},{8,10},{10,8},{12,14},{14,12},{16,18},{18,... | collective-permute-start | bytes 442376 | tf_op jit(solution)/shard_map/ppermute | solution.py:658
  76.9 9.1 %collective-permute-start.24 = (bf16[576,128]{1,0:T(8,128)(2,1)S(1)}, bf16[576,128]{1,0:T(8,128)(2,1)S(1)}, u32[]{:S(2)}, u32[]{:S(2)}) collective-permute-start(bf16[576,128]{1,0:T(8,128)(2,1)S(1)} %add_convert_fusion.5.refs_0_), channel_id=1, source_target_pairs={{0,4},{2,6},{4,0},{6,2},{8,12},{10,14},{12,8},{14,10},{16,20},{18,... | collective-permute-start | bytes 442376 | tf_op jit(solution)/shard_map/ppermute | solution.py:658
  78.1 7.9 %collective-permute-start.25 = (bf16[576,128]{1,0:T(8,128)(2,1)S(1)}, bf16[576,128]{1,0:T(8,128)(2,1)S(1)}, u32[]{:S(2)}, u32[]{:S(2)}) collective-permute-start(bf16[576,128]{1,0:T(8,128)(2,1)S(1)} %add_convert_fusion.5.refs_0_), channel_id=1, source_target_pairs={{0,6},{2,4},{4,2},{6,0},{8,14},{10,12},{12,10},{14,8},{16,22},{18,... | collective-permute-start | bytes 442376 | tf_op jit(solution)/shard_map/ppermute | solution.py:658
  80.4 1.7 %copy-start.5 = (bf16[512,128]{1,0:T(8,128)(2,1)S(1)}, bf16[512,128]{1,0:T(8,128)(2,1)}, u32[]{:S(2)}) copy-start(bf16[512,128]{1,0:T(8,128)(2,1)} %refs_12_.3) | copy-start | bytes 393220

commit v5 on v4

--- a/solution.py
+++ b/solution.py
@@ -67,17 +67,6 @@
     return v
 
 
-def fill_shift(shift_ref, side):
-    points = shift_ref.shape[1]
-    to = lax.broadcasted_iota(jnp.int32, (points, points), 0)
-    of = lax.broadcasted_iota(jnp.int32, (points, points), 1)
-    for d in range(3):
-        s = d - 1
-        col = (to & (side - 1)) + s
-        hit = (of == to + s) & (col >= 0) & (col < side)
-        shift_ref[d * points : (d + 1) * points, :] = jnp.where(hit, 1.0, 0.0).astype(bf16)
-
-
 def zero_pads(pad_ref, side, points):
     images, chans = pad_ref.shape[1], pad_ref.shape[3]
     for d in range(3):
@@ -95,11 +84,6 @@
             moved = pltpu.roll(value, (1 - d) % points, 0).reshape(side, side, chans)
             moved = jnp.where((column == edge)[None], 0.0, moved).reshape(points, chans)
         pad_ref[d, b, side : side + points, :] = moved.astype(bf16)
-
-
-def put_pads(pad_ref, b, moved, side, points):
-    for d in range(3):
-        pad_ref[d, b, side : side + points, :] = moved[d * points : (d + 1) * points]
 
 
 def taps(pad_ref, b, sign, side, points):
@@ -193,13 +177,13 @@
 
 def pack_kernel(n_vec, *refs):
     vectors, arrays = refs[:n_vec], refs[n_vec : n_vec + 2]
-    vec, x_half, g_half, sems = refs[n_vec + 2 :]
+    vec, halves, sems = refs[n_vec + 2 :]
     cps = Copies(sems)
-    count = x_half.shape[0]
+    count = halves.shape[1]
     first = pl.multiple_of((1 - lax.axis_index("tensor")) * count, count)
     copies = [
-        cps.start(src.at[pl.ds(first, count)], dst)
-        for src, dst in zip(arrays, (x_half, g_half), strict=True)
+        cps.start(src.at[pl.ds(first, count)], halves.at[j])
+        for j, src in enumerate(arrays)
     ]
     copies += [cps.start(v, vec.at[j]) for j, v in enumerate(vectors)]
     vec[n_vec:, :] = jnp.zeros((16 - n_vec, vec.shape[1]), f32)
@@ -230,10 +214,9 @@
 
 
 def pipelined(stages, count):
-    for t in range(count + len(stages) - 1):
-        for i in reversed(range(len(stages))):
-            if 0 <= t - i < count:
-                stages[i](t - i)
+    for s in stages:
+        for b in range(count):
+            s(b)
 
 
 def front_kernel(pieces, count, *refs):
@@ -242,21 +225,22 @@
     def take(n):
         return [next(it) for _ in range(n)]
 
-    x_in, g_in, w1_in, w2_in, pi_in, po_in, tw_in, vec_in = (take(pieces) for _ in range(8))
+    x_in, g_in = take(pieces), take(1)
+    w1_in, w2_in, pi_in, po_in, tw_in, vec_in = (take(pieces) for _ in range(6))
+    if pieces == 2:
+        x_in, g_in = [x_in[0], x_in[1].at[0]], [g_in[0], x_in[1].at[1]]
     steps_ref, table_ref = take(2)
     if pieces == 2:
-        own_out, send_out = take(2)
+        own, send = take(2)
     else:
         dw2_own, dpo_own, dpi_own = take(3)
     w1_out, w2_out, po_out, all_vec_out, x_out = take(5)
     gpad_out, sum_out, a1t_out, resid_out, gres_out, mix_out = take(6)
     stat_out, sums_out = take(2)
-    if pieces == 2:
-        own, send = take(2)
     w1, w2, po, vec, xin = take(5)
     gpad, sum_one, a1t, resid, gres, mix = take(6)
     stat, sums = take(2)
-    gin, pi, tw, rows, shift, apad, bpad = take(7)
+    gin, pi, tw, rows, apad, bpad = take(6)
     sems = next(it)
 
     cps = Copies(sems)
@@ -283,11 +267,9 @@
     po_cp = load_split(cps, po_in, po, 0, places)
     g_cp = load_images(cps, g_in, gin, places, count)
 
-    fill_shift(shift, side)
     zero_pads(apad, side, points)
     zero_pads(bpad, side, points)
     zero_pads(gpad, side, points)
-    eye = shift[points : 2 * points, :]
 
     wait_all(vec_cp)
     vcols = jnp.transpose(vec[...])
@@ -299,10 +281,22 @@
         return vec[j : j + 1, :]
 
     wait_all(x_cp)
+    for b in images:
+        hat, _ = norm_first(xin[b], size, width)
+        pre = hat * col(FIRST_GAIN) + col(FIRST_SHIFT)
+        act = (pre * sigmoid(pre)).astype(bf16)
+        a1t[b] = act
+        put_moved(apad, b, jnp.transpose(act).astype(f32), side, points)
+
     wait_all(row_cp)
     wait_all(tw_cp)
     wait_all(w1_cp)
+    wait_all(w2_cp)
+    wait_all(pi_cp)
+    wait_all(po_cp)
+    wait_all(g_cp)
     outs = [cps.start(vec, all_vec_out), cps.start(xin, x_out), cps.start(w1, w1_out)]
+    outs += [cps.start(a1t, a1t_out), cps.start(w2, w2_out), cps.start(po, po_out)]
     picked = []
     for b in images:
         step = steps_ref[places[0] * count + b]
@@ -313,13 +307,6 @@
 
     stats2, stats3 = [], []
     act_t = [None] * count
-
-    def norm_one(b):
-        hat, _ = norm_first(xin[b], size, width)
-        pre = hat * col(FIRST_GAIN) + col(FIRST_SHIFT)
-        act = (pre * sigmoid(pre)).astype(bf16)
-        a1t[b] = act
-        put_pads(apad, b, nt(shift[...], act).astype(bf16), side, points)
 
     def conv_one(b):
         lhs = jnp.concatenate(taps(apad, b, 1, side, points), axis=1)
@@ -335,11 +322,9 @@
         put_moved(bpad, b, act, side, points)
 
     def conv_two(b):
-        if b == 0:
-            wait_all(w2_cp)
         lhs = jnp.concatenate(taps(bpad, b, 1, side, points), axis=1)
         val = nn(lhs, w2[...].reshape(9 * chans, chans)) + row(SECOND_BIAS)
-        resid[b] = val + nt(eye, xin[b])
+        resid[b] = val + jnp.transpose(xin[b]).astype(f32)
 
     normed = []
 
@@ -349,16 +334,12 @@
         hat = (resid[b] - mean) * rstd
         normed.append((hat * row(THIRD_GAIN) + row(THIRD_SHIFT)).astype(bf16))
 
-    pipelined([norm_one, conv_one, norm_two, conv_two, norm_three], count)
-    outs += [cps.start(a1t, a1t_out), cps.start(sum_one, sum_out), cps.start(resid, resid_out)]
+    pipelined([conv_one, norm_two, conv_two, norm_three], count)
+    outs += [cps.start(sum_one, sum_out), cps.start(resid, resid_out)]
     stat[0:count, :] = jnp.concatenate([m for m, _ in stats2], axis=0)
     stat[count : 2 * count, :] = jnp.concatenate([r for _, r in stats2], axis=0)
     outs.append(cps.start(stat, stat_out))
 
-    wait_all(pi_cp)
-    wait_all(po_cp)
-    wait_all(g_cp)
-    outs += [cps.start(w2, w2_out), cps.start(po, po_out)]
     pi_row = jnp.concatenate([pi[0], pi[1], pi[2]], axis=1)
     pi_t = jnp.concatenate([jnp.transpose(pi[1]), jnp.transpose(pi[2])], axis=0)
     zero = jnp.zeros((1, chans), f32)
@@ -412,12 +393,14 @@
     for b in images:
         hat = (resid[b] - stats3[b][0]) * stats3[b][1]
         h = part(grad_normed, b, points) * row(THIRD_GAIN)
-        grad_out = nt(eye, gin[b])
+        grad_out = jnp.transpose(gin[b]).astype(f32)
         ob_grad = ob_grad + col_sum(grad_out)
         val = grad_out + stats3[b][1] * (h - means[b][0:1] - hat * means[b][1:2])
         gres[b] = val
         sb_grad = sb_grad + col_sum(val)
         put_moved(gpad, b, val, side, points)
+        outs.append(cps.start(gres.at[b], gres_out.at[b]))
+        outs.append(cps.start(gpad.at[:, b], gpad_out.at[:, b]))
     lane = lax.broadcasted_iota(jnp.int32, (1, chans), 1)
     stamp = jnp.zeros((1, chans), f32)
     for b in images:
@@ -427,7 +410,7 @@
     sums[...] = jnp.concatenate(
         [sb_grad, sum(gain3), sum(shift3), qb_grad, vb_grad, ob_grad, stamp, zero], axis=0
     )
-    outs += [cps.start(gres, gres_out), cps.start(gpad, gpad_out), cps.start(sums, sums_out)]
+    outs.append(cps.start(sums, sums_out))
 
     dpi = nn(normed_t, lin_grad)
     at = 0
@@ -435,7 +418,6 @@
         at = pack_store(own, send, at, dpo, 0, places)
         for j in range(3):
             at = pack_store(own, send, at, dpi[:, j * chans : (j + 1) * chans], 1, places)
-        outs += copy_rows(cps, [(send, send_out), (own, own_out)], 0, at)
     else:
         dpo_own[...] = dpo
         for j in range(3):
@@ -446,10 +428,7 @@
     for tap in range(9):
         val = nn(a_all, jnp.concatenate([moved[b][tap] for b in images], axis=0))
         if pieces == 2:
-            start = at if tap % 3 == 0 else start
             at = pack_store(own, send, at, val, 0, places)
-            if tap % 3 == 2:
-                outs += copy_rows(cps, [(send, send_out), (own, own_out)], start, at)
         else:
             dw2_own[tap] = val
 
@@ -469,18 +448,18 @@
 
     kept = take(13)
     if pieces == 2:
-        own_out, send_out, block_own_out, block_send_out, image_own_out, image_send_out = take(6)
+        own, send_out, block_own_out, block_send_out, image_own_out, image_send_out = take(6)
     else:
         own, block_own_out, image_own_out = take(3)
         block_send_out = image_send_out = None
-    small_out = next(it)
+    small = next(it)
     w1, w2, po, vec, xin, gpad, sum_one, a1t, resid, gres, mix, stat, front_sums = take(13)
     if pieces == 2:
-        own, send, block_own, block_send, image_own, image_send = take(6)
+        send, block_own, block_send, image_own, image_send = take(5)
     else:
         block_own, image_own = take(2)
         block_send = image_send = None
-    small, hpad, back, sems = take(4)
+    hpad, back, first_hat, first_slope, sems = take(5)
     cps = Copies(sems)
     places = places_of(pieces)
     points, chans = sum_one.shape[1], sum_one.shape[2]
@@ -490,31 +469,46 @@
     images = range(count)
 
     w1_in, w2_in, po_in, vec_in, x_in, gpad_in, sum_in, a1t_in, resid_in, gres_in, mix_in = kept[:11]
+    early = [(vec_in, vec), (x_in, xin)]
+    early = [cps.start(src, dst) for src, dst in early]
     w2_cp = cps.start(w2_in, w2)
     gpad_cp = [cps.start(gpad_in.at[:, b], gpad.at[:, b]) for b in images]
-    small_cp = [(vec_in, vec), (kept[11], stat), (kept[12], front_sums)]
+    small_cp = [(kept[11], stat), (kept[12], front_sums)]
     small_cp = [cps.start(src, dst) for src, dst in small_cp]
     sum_cp = cps.start(sum_in, sum_one)
     a1t_cp = cps.start(a1t_in, a1t)
-    later = [(w1_in, w1), (po_in, po), (x_in, xin), (resid_in, resid), (gres_in, gres), (mix_in, mix)]
+    later = [(w1_in, w1), (po_in, po), (resid_in, resid), (gres_in, gres), (mix_in, mix)]
     later = [cps.start(src, dst) for src, dst in later]
 
     def row(j):
         return vec[j : j + 1, :]
 
     zero_pads(hpad, side, points)
+    wait_all(early)
+    vcols = jnp.transpose(vec[...])
+
+    def col(j):
+        return vcols[:, j : j + 1]
+
+    first_rstd = []
+    for b in images:
+        hat, rstd = norm_first(xin[b], size, width)
+        first_rstd.append(jnp.broadcast_to(rstd, (GROUPS, width, 1)).reshape(chans, 1))
+        pre = hat * col(FIRST_GAIN) + col(FIRST_SHIFT)
+        first_hat[b] = hat
+        first_slope[b] = silu_slope(pre, sigmoid(pre))
+
     w2_cp.wait()
+    wait_all(gpad_cp)
+    sum_cp.wait()
+    wait_all(small_cp)
     w2_cols = jnp.concatenate([w2[k] for k in range(9)], axis=1)
     gain, shift_g, times = [], [], []
 
     def conv_back(b):
-        gpad_cp[b].wait()
         back[b] = nt(jnp.concatenate(taps(gpad, b, -1, side, points), axis=1), w2_cols)
 
     def norm_back(b):
-        if b == 0:
-            sum_cp.wait()
-            wait_all(small_cp)
         mean, rstd = stat[b : b + 1, :], stat[count + b : count + b + 1, :]
         hat = (sum_one[b] - mean) * rstd
         pre = hat * row(SECOND_GAIN) + row(SECOND_SHIFT)
@@ -528,27 +522,10 @@
         put_moved(hpad, b, val, side, points)
 
     pipelined([conv_back, norm_back], count)
-
     a1t_cp.wait()
-    a_all = jnp.concatenate([a1t[b] for b in images], axis=1)
-    moved = [taps(hpad, b, -1, side, points) for b in images]
-    at = 0
+    wait_all(later)
     outs = []
-    for tap in range(9):
-        val = nn(a_all, jnp.concatenate([moved[b][tap] for b in images], axis=0))
-        if pieces == 2:
-            start = at if tap % 3 == 0 else start
-            at = pack_store(own, send, at, val, 1, places)
-            if tap % 3 == 2:
-                outs += copy_rows(cps, [(send, send_out), (own, own_out)], start, at)
-        else:
-            own[tap] = val
-
-    wait_all(later)
-    vcols = jnp.transpose(vec[...])
-
-    def col(j):
-        return vcols[:, j : j + 1]
+
 
     def put_out(own_ref, send_ref, own_dst, send_dst, b, val):
         split_store(own_ref, send_ref, b, val, 0, places)
@@ -557,6 +534,23 @@
             outs.append(cps.start(send_ref.at[b], send_dst.at[b]))
 
     proj = nn(jnp.transpose(po[...]), jnp.concatenate([mix[b] for b in images], axis=1))
+    a_all = jnp.concatenate([a1t[b] for b in images], axis=1)
+    moved = [taps(hpad, b, -1, side, points) for b in images]
+    at = 0
+    for tap in range(9):
+        val = nn(a_all, jnp.concatenate([moved[b][tap] for b in images], axis=0))
+        if pieces == 2:
+            at = pack_store(own, send, at, val, 1, places)
+        else:
+            own[tap] = val
+        if tap % 2 == 1 and tap // 2 < count:
+            b = tap // 2
+            val = jnp.transpose(resid[b]) + lane_part(proj, b, points) + col(OUTPUT_BIAS)
+            split_store(block_own, block_send, b, val, 0, places)
+    if pieces == 2:
+        outs += copy_rows(cps, [(send, send_out)], 0, at)
+        outs.append(cps.start(block_send, block_send_out))
+    outs.append(cps.start(block_own, block_own_out))
 
     w1_cols = jnp.concatenate([w1[k] for k in range(9)], axis=1)
     zero = jnp.zeros((chans, 1), f32)
@@ -570,15 +564,9 @@
     def conv_first(b):
         first_back[b] = nt(w1_cols, jnp.concatenate(taps(hpad, b, -1, side, points), axis=1))
 
-    def block_part(b):
-        val = jnp.transpose(resid[b]) + lane_part(proj, b, points) + col(OUTPUT_BIAS)
-        put_out(block_own, block_send, block_own_out, block_send_out, b, val)
-
     def norm_first_back(b):
-        hat, rstd = norm_first(xin[b], size, width)
-        rstd = jnp.broadcast_to(rstd, (GROUPS, width, 1)).reshape(chans, 1)
-        pre = hat * col(FIRST_GAIN) + col(FIRST_SHIFT)
-        val = first_back[b] * silu_slope(pre, sigmoid(pre))
+        hat, rstd = first_hat[b], first_rstd[b]
+        val = first_back[b] * first_slope[b]
         gain = jnp.sum(val * hat, axis=1, keepdims=True)
         shift = jnp.sum(val, axis=1, keepdims=True)
         gain_sum[0] = gain_sum[0] + gain
@@ -589,7 +577,7 @@
         val = val + jnp.transpose(gres[b])
         put_out(image_own, image_send, image_own_out, image_send_out, b, val)
 
-    pipelined([conv_first, block_part, norm_first_back], count)
+    pipelined([conv_first, norm_first_back], count)
 
     lane = lax.broadcasted_iota(jnp.int32, (chans, LANES), 1)
     both = jnp.where(lane == 0, gain_sum[0], 0.0) + jnp.where(lane == 1, shift_sum[0], 0.0)
@@ -602,20 +590,25 @@
     flat.append(front_sums[6:7, :LANES])
     flat += [jnp.zeros((1, LANES), f32)] * (BLOCK - len(flat))
     small[...] = jnp.concatenate(flat, axis=0).astype(bf16)
-    outs.append(cps.start(small, small_out))
     wait_all(outs)
 
 
 def put_quarters(quarters, flat):
     me = lax.axis_index("batch") & 3
     rows = quarters[0].shape[0]
-    for j, ref in enumerate(quarters):
-        flat[pl.ds(pl.multiple_of((me ^ j) * rows, 16), rows), :] = ref[...]
+    if len(quarters) == 4:
+        parts = [(j, ref, 0) for j, ref in enumerate(quarters)]
+    else:
+        odd = lax.axis_index("tensor") & 1
+        mine, first, both = quarters
+        parts = [(0, mine, 0), (1 + odd, first, 0), (2 - odd, both, 0), (3, both, rows)]
+    for j, ref, at in parts:
+        flat[pl.ds(pl.multiple_of((me ^ j) * rows, 16), rows), :] = ref[at : at + rows, :]
 
 
 def unpack_first_kernel(*refs):
-    quarters = refs[:4]
-    dw1_out, flat, dw1, sems = refs[4:]
+    quarters = refs[:-4]
+    dw1_out, flat, dw1, sems = refs[-4:]
     cps = Copies(sems)
     put_quarters(quarters, flat)
     outs = []
@@ -629,8 +622,8 @@
 
 
 def unpack_second_kernel(*refs):
-    quarters = refs[:4]
-    dw2_out, dpo_out, dpi_out, flat, dw2, dpo, dpi, sems = refs[4:]
+    quarters = refs[:-8]
+    dw2_out, dpo_out, dpi_out, flat, dw2, dpo, dpi, sems = refs[-8:]
     cps = Copies(sems)
     put_quarters(quarters, flat)
     outs = []
@@ -663,9 +656,8 @@
     return [part(me ^ j).astype(bf16) for j in range(1, 4)]
 
 
-def after(values, *others):
-    done = lax.optimization_barrier((tuple(values), others))
-    return list(done[0])
+def together(*groups):
+    return [list(g) for g in lax.optimization_barrier(tuple(tuple(g) for g in groups))]
 
 
 def send_near(sent, batch):
@@ -705,6 +697,26 @@
 
 def gather_near(piece, batch):
     return [piece] + [swap(piece, "batch", batch, j) for j in range(1, 4)]
+
+
+def plane_bit(step, core):
+    return 1 if step == core % 2 else 2
+
+
+def cross(value, step, batch):
+    tensor = lax.axis_size("tensor")
+    pairs = []
+    for i in range(batch):
+        for core in range(tensor):
+            pairs.append((i * tensor + core, (i ^ plane_bit(step, core)) * tensor + core))
+    return lax.ppermute(value, ("batch", "tensor"), pairs)
+
+
+def by_difference(mine, first, both):
+    rows = mine.shape[0]
+    odd = (lax.axis_index("tensor") & 1) == 1
+    near, far = both[:rows], both[rows:]
+    return [mine, jnp.where(odd, near, first), jnp.where(odd, first, near), far]
 
 
 def in_order(pieces):
@@ -754,7 +766,7 @@
     per_batch, local, points = images.shape
     chans = local * tensor
     count = per_batch // tensor
-    steps, embed = embed_table.shape
+    table_rows, embed = embed_table.shape
     pieces = 2 if tensor == 2 else 1
     me = lax.axis_index("tensor")
     vectors = [
@@ -776,42 +788,38 @@
 
     n_vec = len(vectors)
     if pieces == 2:
-        half = (count, local, points)
-        vec, x_half, g_half = pl.pallas_call(
+        vec, halves = pl.pallas_call(
             functools.partial(pack_kernel, n_vec),
             out_shape=[
                 jax.ShapeDtypeStruct((16, local), f32),
-                jax.ShapeDtypeStruct(half, bf16),
-                jax.ShapeDtypeStruct(half, bf16),
+                jax.ShapeDtypeStruct((2, count, local, points), bf16),
             ],
             in_specs=[ANY] * (n_vec + 2),
-            out_specs=[VMEM] * 3,
+            out_specs=[VMEM] * 2,
             scratch_shapes=[pltpu.SemaphoreType.DMA((n_vec + 2,))],
             compiler_params=pltpu.CompilerParams(vmem_limit_bytes=4 * MIB),
             name="pack",
         )(*(in_hbm(v) for v in vectors + [images, cotangent]))
     else:
         vec = jnp.stack(vectors + [output_bias] * 4, axis=0)
-        x_half = g_half = None
-
-    def images_of(array, half):
-        if pieces == 2:
-            return [array, swap(half, "tensor", 2, 1)]
-        return [lax.all_to_all(array, "tensor", 0, 1, tiled=True)]
 
     def whole(array, axis):
         if pieces == 2:
             return [array, swap(array, "tensor", 2, 1)]
         return [lax.all_gather(array, "tensor", axis=axis, tiled=True)]
 
-    x_in = images_of(images, x_half)
+    if pieces == 2:
+        x_in, g_in = [images, swap(halves, "tensor", 2, 1)], [cotangent]
+    else:
+        x_in, g_in = (
+            [lax.all_to_all(v, "tensor", 0, 1, tiled=True)] for v in (images, cotangent)
+        )
     vec_in = whole(vec, 1)
     tw_in = whole(time_weight, 1)
     w1_in = whole(first_conv, 2)
     w2_in = whole(second_conv, 1)
     pi_in = whole(project_in, 2)
     po_in = whole(project_out, 0)
-    g_in = images_of(cotangent, g_half)
     my_steps = timesteps if pieces == 2 else lax.dynamic_slice_in_dim(timesteps, me * count, count)
 
     side = side_of(points)
@@ -832,8 +840,8 @@
     half_b = 9 * chans * chans // 2 // LANES
     half_a = half_b + 4 * chans * chans // 2 // LANES
     if pieces == 2:
-        grads_a = [pltpu.HBM((half_a, LANES), bf16)] * 2
-        grads_b = [pltpu.HBM((half_b, LANES), bf16)] * 2
+        grads_a = [pltpu.VMEM((half_a, LANES), bf16)] * 2
+        grads_b = [pltpu.VMEM((half_b, LANES), bf16), pltpu.HBM((half_b, LANES), bf16)]
     else:
         grads_a = [shape((9, chans, chans), f32), shape((chans, chans), f32)]
         grads_a.append(shape((3, chans, chans), f32))
@@ -856,14 +864,14 @@
         ((8, chans), f32),
     ]
     out_a = ANY if pieces == 2 else VMEM
-    scratch_a = [pltpu.VMEM(v.shape, v.dtype) for v in grads_a] if pieces == 2 else []
+    scratch_a = []
 
     front = pl.pallas_call(
         functools.partial(front_kernel, pieces, count),
         out_shape=grads_a
         + [pltpu.HBM(*v) for v in kept],
-        in_specs=[ANY, VMEM][:pieces] * 8 + [SMEM, ANY],
-        out_specs=[out_a] * n_grad + [ANY] * len(kept),
+        in_specs=[ANY, VMEM][:pieces] + [ANY] + [ANY, VMEM][:pieces] * 6 + [SMEM, ANY],
+        out_specs=[VMEM] * n_grad + [ANY] * len(kept),
         scratch_shapes=scratch_a
         + [pltpu.VMEM(*v) for v in kept]
         + [
@@ -871,12 +879,11 @@
             pltpu.VMEM((3, chans, chans), bf16),
             pltpu.VMEM((embed, chans), bf16),
             pltpu.VMEM((count, 16, embed), bf16),
-            pltpu.VMEM((3 * points, points), bf16),
             pltpu.VMEM(pads, bf16),
             pltpu.VMEM(pads, bf16),
-            pltpu.SemaphoreType.DMA((8 * pieces + count + 21,)),
+            pltpu.SemaphoreType.DMA((8 * pieces + 3 * count + 19,)),
         ],
-        compiler_params=params(32),
+        compiler_params=params(28),
         cost_estimate=cost(54, 12 << 20),
         name="front",
     )(
@@ -895,7 +902,7 @@
         if pieces == 2:
             got = swap(sums[1], "tensor", 2, 1)
             if beside is not None:
-                (got,) = after([got], beside)
+                (got,), (beside,) = together([got], [beside])
             rows = got.shape[0] // 4
             own4, got4 = (v.reshape(4, rows, LANES) for v in (sums[0], got))
 
@@ -903,7 +910,7 @@
                 pair = [lax.dynamic_index_in_dim(v, q, 0, False).astype(f32) for v in (own4, got4)]
                 return pair[0] + pair[1]
 
-            return part
+            return part, beside
         done = [
             lax.psum_scatter(v, "tensor", scatter_dimension=axis, tiled=True)
             for v, axis in zip(sums, axes, strict=True)
@@ -912,54 +919,62 @@
         flat = jnp.pad(flat, ((0, -flat.shape[0] % 64), (0, 0)))
         rows = flat.shape[0] // 4
         flat = flat.reshape(4, rows, LANES)
-        return lambda q: lax.dynamic_index_in_dim(flat, q, 0, False)
-
-    part_a = quarters(sums_a, (1, 0, 2))
+        return (lambda q: lax.dynamic_index_in_dim(flat, q, 0, False)), beside
+
+    part_a, _ = quarters(sums_a, (1, 0, 2))
     sent_a = near_parts(part_a)
 
+    kept_now[-2:], sent_a = together(kept_now[-2:], sent_a)
     got_a = send_near(sent_a, batch)
-    kept_now[-2:] = after(kept_now[-2:], *sent_a)
 
     half = (count, chans // 2, points)
     if pieces == 2:
         outs_b = grads_b + [pltpu.HBM(half, f32), pltpu.HBM(half, bf16)] * 2
-        scratch_b = [pltpu.VMEM(v.shape, v.dtype) for v in outs_b]
+        scratch_b = [pltpu.VMEM(v.shape, v.dtype) for v in outs_b[1:]]
     else:
         outs_b = grads_b + [pltpu.HBM(image_b, f32)] * 2
         scratch_b = [pltpu.VMEM(image_b, f32)] * 2
     *outs_b, block = pl.pallas_call(
         functools.partial(back_kernel, pieces, count),
-        out_shape=outs_b + [pltpu.HBM((BLOCK, LANES), bf16)],
+        out_shape=outs_b + [pltpu.VMEM((BLOCK, LANES), bf16)],
         in_specs=[ANY] * len(kept),
-        out_specs=[out_a] * pieces + [ANY] * (2 * pieces + 1),
+        out_specs=[VMEM, out_a][:pieces] + [ANY] * (2 * pieces) + [VMEM],
         scratch_shapes=[pltpu.VMEM(*v) for v in kept]
         + scratch_b
         + [
-            pltpu.VMEM((BLOCK, LANES), bf16),
             pltpu.VMEM(pads, bf16),
             pltpu.VMEM(image_p, f32),
-            pltpu.SemaphoreType.DMA((6 + 5 * count + 13,)),
+            pltpu.VMEM(image_b, f32),
+            pltpu.VMEM(image_b, f32),
+            pltpu.SemaphoreType.DMA((16 + 3 * count,)),
         ],
-        compiler_params=params(36),
+        compiler_params=params(28),
         cost_estimate=cost(33, 12 << 20),
         name="back",
     )(*(in_hbm(v) for v in kept_now))
     sums_b, block_part, image_grad = outs_b[:pieces], outs_b[pieces : 2 * pieces], outs_b[2 * pieces :]
-    got_a = after(got_a, block)
-    sums_b = after(sums_b, *got_a)
+    got_a, sums_b, (block,) = together(got_a, sums_b, [block])
     piece_a = sum_near(got_a, part_a)
-    part_b = quarters(sums_b, (2,), piece_a)
+    steps = far_steps(batch)
+    far_a = send_far(piece_a, None, 0, batch) if steps > 0 else None
+    part_b, piece_a = quarters(sums_b, (2,), piece_a)
     sent_b = near_parts(part_b)
     got_b = send_near([jnp.concatenate([v, block], axis=0) for v in sent_b], batch)
-    piece_a, _ = sum_far(piece_a, None, send_far(piece_a, None, 0, batch))
-    got_b = after(got_b, piece_a)
+    if steps > 0:
+        piece_a, _ = sum_far(piece_a, None, far_a)
+    if steps > 1:
+        far_a = send_far(piece_a, None, 1, batch)
+    got_b, (piece_a,) = together(got_b, [piece_a])
     rows_b = sent_b[0].shape[0]
     blocks = jnp.concatenate([block] + [g[rows_b:] for g in got_b], axis=0)
     piece_b = sum_near([g[:rows_b] for g in got_b], part_b)
-    for step in range(1, far_steps(batch)):
-        piece_a, _ = sum_far(piece_a, None, send_far(piece_a, None, step, batch))
-    block_part = after(block_part, piece_b)
-    image_grad = after(image_grad, piece_b)
+    for step in range(1, steps):
+        if step > 1:
+            far_a = send_far(piece_a, None, step, batch)
+        piece_a, _ = sum_far(piece_a, None, far_a)
+    if steps > 0:
+        far_b = send_far(piece_b, blocks, 0, batch)
+    block_part, image_grad, (piece_b,) = together(block_part, image_grad, [piece_b])
 
     def placed(own, send):
         if pieces == 2:
@@ -972,14 +987,15 @@
     block_out = placed(block_part[0], block_part[-1])
     images_grad = placed(image_grad[0], image_grad[-1])
 
-    got_a = gather_near(piece_a, batch)
-    for step in range(far_steps(batch)):
-        far_b = send_far(piece_b, blocks, step, batch)
+    first_a = cross(piece_a, 0, batch)
+    both_a = cross(jnp.concatenate([piece_a, first_a], axis=0), 1, batch)
+    for step in range(steps):
         if step > 0:
-            (far_b,) = after([far_b], got_a[0])
+            far_b = send_far(piece_b, blocks, step, batch)
+            (far_b,), (first_a,) = together([far_b], [first_a])
         piece_b, blocks = sum_far(piece_b, blocks, far_b)
+    got_a = [piece_a, first_a, both_a]
     got_b = gather_near(piece_b, batch)
-    got_a = after(got_a, piece_b)
 
     if pieces == 2:
 
@@ -988,7 +1004,7 @@
             return pl.pallas_call(
                 kernel,
                 out_shape=outs,
-                in_specs=[VMEM] * 4,
+                in_specs=[VMEM] * len(got),
                 out_specs=[ANY] * len(outs),
                 scratch_shapes=[pltpu.VMEM((rows, LANES), bf16)]
                 + [pltpu.VMEM(v.shape, v.dtype) for v in outs]
@@ -1004,12 +1020,13 @@
             half_a,
             [(9, local, chans), (local, chans), (3, chans, local)],
         )
+        got_b, (second_conv_grad,) = together(got_b, [second_conv_grad])
         (first_conv_grad,) = unpacked(
             unpack_first_kernel, "unpack_first", got_b, half_b, [(9, chans, local)]
         )
     else:
         second_conv_grad, project_out_grad, project_in_grad = unpack(
-            in_order(got_a), [(9, local, chans), (local, chans), (3, chans, local)]
+            in_order(by_difference(*got_a)), [(9, local, chans), (local, chans), (3, chans, local)]
         )
         (first_conv_grad,) = unpack(in_order(got_b), [(9, chans, local)])
 
@@ -1029,7 +1046,7 @@
     stamps = blocks[:, n_sum + wide * count].astype(jnp.int32)
     all_steps = stamps[:, :count] * 32 + stamps[:, LANES // 2 : LANES // 2 + count]
     all_steps = all_steps.reshape(-1)
-    one_hot = (all_steps[:, None] == jnp.arange(steps, dtype=jnp.int32)[None, :]).astype(bf16)
+    one_hot = (all_steps[:, None] == jnp.arange(table_rows, dtype=jnp.int32)[None, :]).astype(bf16)
     emb = nn(one_hot, embed_table)
     sig = sigmoid(emb)
     act = (emb * sig).astype(bf16)

time: 87.6 us -> 79.7 us (0.910)
  the two profiles are of different devices: /device:TPU:8 before, /device:TPU:0 now
where the time goes in v5:
time: 79.7 us; the launch traced here: 79.4 us
  Pallas kernels  24.9 us (31%)
  starting transfers between devices  24 us (30%)
  waiting for transfers between devices  20.7 us (26%)
  other arithmetic  4.39 us (6%)
  matrix products  3.24 us (4%)
  between operations  1.18 us (1%)
  local copies, waits for them, and re-layouts  0.93 us (1%)
    ppermute x21, starting transfers between devices, swap(): return lax.ppermute(value, axis, [(i, i ^ bit) for i in range(size)])  14.7 us
    pallas_call x1, Pallas kernels, per_device(): pl.pallas_call(functools.partial(front_kernel, pieces, count), out_shape=...  12.5 us
    ppermute x4, waiting for transfers between devices, send_far(): return lax.ppermute(mine, ('batch', 'tensor'), pairs)  10.8 us
    ppermute x21, waiting for transfers between devices, swap(): return lax.ppermute(value, axis, [(i, i ^ bit) for i in range(size)])  9.91 us
    pallas_call x1, Pallas kernels, per_device(): pl.pallas_call(functools.partial(back_kernel, pieces, count), out_shape=o...  8.84 us
    ppermute x4, starting transfers between devices, send_far(): return lax.ppermute(mine, ('batch', 'tensor'), pairs)  6.39 us
    ppermute x2, starting transfers between devices, cross(): return lax.ppermute(value, ('batch', 'tensor'), pairs)  2.92 us
    pallas_call x2, Pallas kernels, unpacked(): pl.pallas_call(kernel, out_shape=outs, in_specs=[VMEM] * len(got), out_sp...  2.41 us
  transfers between devices with their start and end apart: 27, of which 10 were waited for; matrix products, arithmetic and copies ran while one was open for 10% of the time, Pallas kernels for 14%

profile of v5, /device:TPU:0, one launch (start us, length us, event | category | flops | bytes accessed | tf_op | source)
XLA Modules:
  0.0 79.4 jit_solution(9189509908027776002)
XLA Ops:
  0.7 0.5 collective-permute-start.1
  1.3 1.2 %pack.1 = (f32[16,128]{1,0:T(8,128)S(1)}, bf16[2,4,128,256]{3,2,1,0:T(8,128)(2,1)S(1)}) custom-call(f32[128]{0:T(128)} %refs_0_.2, f32[128]{0:T(128)} %refs_1_.1, f32[128]{0:T(128)} %refs_2_.2, f32[128]{0:T(128)} %refs_3_.2, f32[128]{0:T(128)} %refs_4_.1, f32[128]{0:T(128)} %refs_5_.2, f32[128]{0:T(128)} %refs_6_.1, f32[128]{0:T(128)} %refs_7_.2, ...), custom_call_target="tpu_custom_call" | custom-call | tf_op jit(solution)/shard_map/pack/pallas_call | solution.py:791
  2.5 0.5 collective-permute-start
  3.0 0.4 collective-permute-start.4
  3.5 1.0 %collective-permute-done.6.refs_14_ = f32[16,128]{1,0:T(8,128)S(1)} collective-permute-done((f32[16,128]{1,0:T(8,128)S(1)}, f32[16,128]{1,0:T(8,128)S(1)}, u32[]{:S(2)}, u32[]{:S(2)}) %collective-permute-start.6) | collective-permute-done | bytes 8224 | tf_op jit(solution)/shard_map/ppermute | solution.py:651
  4.5 0.4 collective-permute-start.3
  4.9 0.3 collective-permute-start.5
  5.2 1.3 %collective-permute-done.5.refs_12_ = bf16[512,128]{1,0:T(8,128)(2,1)S(1)} collective-permute-done((bf16[512,128]{1,0:T(8,128)(2,1)}, bf16[512,128]{1,0:T(8,128)(2,1)S(1)}, u32[]{:S(2)}, u32[]{:S(2)}) %collective-permute-start.5) | collective-permute-done | bytes 131104 | tf_op jit(solution)/shard_map/ppermute | solution.py:651
  6.5 12.5 %front.1 = (bf16[3328,128]{1,0:T(8,128)(2,1)S(1)}, bf16[3328,128]{1,0:T(8,128)(2,1)S(1)}, bf16[9,256,256]{2,1,0:T(8,128)(2,1)}, bf16[9,256,256]{2,1,0:T(8,128)(2...) custom-call(bf16[8,128,256]{2,1,0:T(8,128)(2,1)} %refs_0_.3, ...), custom_call_target="tpu_custom_call" | custom-call | flops 7247757312 | bytes 12582912 | tf_op jit(solution)/shard_map/front/pallas_call | solution.py:869
  19.0 0.4 collective-permute-start.7
  19.3 2.1 %collective-permute-done.7 = bf16[3328,128]{1,0:T(8,128)(2,1)S(1)} collective-permute-done((bf16[3328,128]{1,0:T(8,128)(2,1)S(1)}, bf16[3328,128]{1,0:T(8,128)(2,1)S(1)}, u32[]{:S(2)}, u32[]{:S(2)}) %collective-permute-start.7) | collective-permute-done | bytes 852000 | tf_op jit(solution)/shard_map/ppermute | solution.py:651
  21.4 0.2 fusion.29
  21.6 3.8 %collective-permute-start.10 = (bf16[832,128]{1,0:T(8,128)(2,1)S(1)}, bf16[832,128]{1,0:T(8,128)(2,1)S(1)}, u32[]{:S(2)}, u32[]{:S(2)}) collective-permute-start(bf16[832,128]{1,0:T(8,128)(2,1)S(1)} %get-tuple-element.101), channel_id=1, source_target_pairs={{0,6},{2,4},{4,2},{6,0},{8,14},{10,12},{12,10},{14,8},{16,22},{18,... | collective-permute-start | bytes 638984 | tf_op jit(solution)/shard_map/ppermute | solution.py:651
  25.4 0.5 collective-permute-start.8
  25.9 0.1 collective-permute-start.9
  26.0 8.8 %back.1 = (bf16[2304,128]{1,0:T(8,128)(2,1)S(1)}, bf16[2304,128]{1,0:T(8,128)(2,1)}, f32[4,128,256]{2,1,0:T(8,128)}, bf16[4,128,256]{2,1,0:T(8,128)(2,1)}, f32[4...) custom-call(bf16[9,256,256]{2,1,0:T(8,128)(2,1)} %get-tuple-element.78.refs_0_, ...), custom_call_target="tpu_custom_call" | custom-call | flops 4429185024 | bytes 12582912 | tf_op jit(solution)/shard_map/back/pallas_call | solution.py:937
  34.9 1.0 %collective-permute-done.8 = bf16[832,128]{1,0:T(8,128)(2,1)S(1)} collective-permute-done((bf16[832,128]{1,0:T(8,128)(2,1)S(1)}, bf16[832,128]{1,0:T(8,128)(2,1)S(1)}, u32[]{:S(2)}, u32[]{:S(2)}) %collective-permute-start.8) | collective-permute-done | bytes 213024 | tf_op jit(solution)/shard_map/ppermute | solution.py:651
  35.9 1.1 %fusion.5 = bf16[832,128]{1,0:T(8,128)(2,1)S(1)} fusion(bf16[832,128]{1,0:T(8,128)(2,1)S(1)} %collective-permute-done.10, bf16[832,128]{1,0:T(8,128)(2,1)} %collective-permute-done.9, bf16[832,128]{1,0:T(8,128)(2,1)S(1)} %collective-permute-done.8, bf16[4,832,128]{2,1,0:T(8,128)(2,1)S(1)} %bitcast.71, s32[]{:T(128)S(6)} %select_n.72, ...), kind=kLoop, calls=%fused_computation.15 | loop fusion | flops 1064960 | bytes 1277956 | tf_op jit(solution)/shard_map/convert_element_type | solution.py:671
  37.0 1.7 %collective-permute-start.15 = (bf16[832,128]{1,0:T(8,128)(2,1)S(1)}, bf16[832,128]{1,0:T(8,128)(2,1)S(1)}, u32[]{:S(2)}, u32[]{:S(2)}) collective-permute-start(bf16[832,128]{1,0:T(8,128)(2,1)S(1)} %fusion.5), channel_id=1, source_target_pairs={{0,8},{1,17},{2,10},{3,19},{4,12},{5,21},{6,14},{7,23},{8,0},{9,25... | collective-permute-start | bytes 638984 | tf_op jit(solution)/shard_map/ppermute | solution.py:687
  38.6 0.1 fusion.32
  38.8 1.6 %collective-permute-start.12 = (bf16[608,128]{1,0:T(8,128)(2,1)S(1)}, bf16[608,128]{1,0:T(8,128)(2,1)S(1)}, u32[]{:S(2)}, u32[]{:S(2)}) collective-permute-start(bf16[608,128]{1,0:T(8,128)(2,1)S(1)} %get-tuple-element.175), channel_id=1, source_target_pairs={{0,2},{2,0},{4,6},{6,4},{8,10},{10,8},{12,14},{14,12},{16,18},{18,... | collective-permute-start | bytes 466952 | tf_op jit(solution)/shard_map/ppermute | solution.py:651
  40.4 1.5 %collective-permute-start.13 = (bf16[608,128]{1,0:T(8,128)(2,1)S(1)}, bf16[608,128]{1,0:T(8,128)(2,1)S(1)}, u32[]{:S(2)}, u32[]{:S(2)}) collective-permute-start(bf16[608,128]{1,0:T(8,128)(2,1)S(1)} %get-tuple-element.174), channel_id=1, source_target_pairs={{0,4},{2,6},{4,0},{6,2},{8,12},{10,14},{12,8},{14,10},{16,20},{18,... | collective-permute-start | bytes 466952 | tf_op jit(solution)/shard_map/ppermute | solution.py:651
  41.9 0.5 collective-permute-start.14
  42.4 2.7 %collective-permute-done.15 = bf16[832,128]{1,0:T(8,128)(2,1)S(1)} collective-permute-done((bf16[832,128]{1,0:T(8,128)(2,1)S(1)}, bf16[832,128]{1,0:T(8,128)(2,1)S(1)}, u32[]{:S(2)}, u32[]{:S(2)}) %collective-permute-start.15) | collective-permute-done | bytes 213024 | tf_op jit(solution)/shard_map/ppermute | solution.py:687
  45.2 2.1 %collective-permute-start.20 = (bf16[832,128]{1,0:T(8,128)(2,1)S(1)}, bf16[832,128]{1,0:T(8,128)(2,1)S(1)}, u32[]{:S(2)}, u32[]{:S(2)}) collective-permute-start(bf16[832,128]{1,0:T(8,128)(2,1)S(1)} %add_convert_fusion.1), channel_id=1, source_target_pairs={{0,16},{1,9},{2,18},{3,11},{4,20},{5,13},{6,22},{7,15},{8,24},{9,1... | collective-permute-start | bytes 638984 | tf_op jit(solution)/shard_map/ppermute | solution.py:687
  47.3 3.3 %collective-permute-done.13 = bf16[608,128]{1,0:T(8,128)(2,1)S(1)} collective-permute-done((bf16[608,128]{1,0:T(8,128)(2,1)S(1)}, bf16[608,128]{1,0:T(8,128)(2,1)S(1)}, u32[]{:S(2)}, u32[]{:S(2)}) %collective-permute-start.13) | collective-permute-done | bytes 155680 | tf_op jit(solution)/shard_map/ppermute | solution.py:651
  50.6 0.1 constant_dynamic-update-slice_fusion.4
  50.8 0.7 collective-permute-start.18
  51.5 0.5 collective-permute-start.16
  52.0 1.8 %collective-permute-done.20 = bf16[832,128]{1,0:T(8,128)(2,1)S(1)} collective-permute-done((bf16[832,128]{1,0:T(8,128)(2,1)S(1)}, bf16[832,128]{1,0:T(8,128)(2,1)S(1)}, u32[]{:S(2)}, u32[]{:S(2)}) %collective-permute-start.20) | collective-permute-done | bytes 213024 | tf_op jit(solution)/shard_map/ppermute | solution.py:687
  53.8 1.6 %collective-permute-start.21 = (bf16[832,128]{1,0:T(8,128)(2,1)S(1)}, bf16[832,128]{1,0:T(8,128)(2,1)S(1)}, u32[]{:S(2)}, u32[]{:S(2)}) collective-permute-start(bf16[832,128]{1,0:T(8,128)(2,1)S(1)} %add_convert_fusion.refs_0_), channel_id=1, source_target_pairs={{0,2},{1,5},{2,0},{3,7},{4,6},{5,1},{6,4},{7,3},{8,10},{9,13},{10,... | collective-permute-start | bytes 638984 | tf_op jit(solution)/shard_map/ppermute | solution.py:712
  55.5 2.8 %collective-permute-done.18 = bf16[704,128]{1,0:T(8,128)(2,1)S(1)} collective-permute-done((bf16[704,128]{1,0:T(8,128)(2,1)S(1)}, bf16[704,128]{1,0:T(8,128)(2,1)S(1)}, u32[]{:S(2)}, u32[]{:S(2)}) %collective-permute-start.18) | collective-permute-done | bytes 180256 | tf_op jit(solution)/shard_map/ppermute | solution.py:687
  58.4 1.9 %collective-permute-start.19 = (bf16[832,128]{1,0:T(8,128)(2,1)S(1)}, bf16[832,128]{1,0:T(8,128)(2,1)S(1)}, u32[]{:S(2)}, u32[]{:S(2)}) collective-permute-start(bf16[832,128]{1,0:T(8,128)(2,1)S(1)} %get-tuple-element.148), channel_id=1, source_target_pairs={{0,16},{1,9},{2,18},{3,11},{4,20},{5,13},{6,22},{7,15},{8,24},{9,1... | collective-permute-start | bytes 638984 | tf_op jit(solution)/shard_map/ppermute | solution.py:687
  60.4 0.1 convert_select_fusion.3
  60.5 1.1 %pad_maximum_fusion.1 = f32[8,128,256]{2,1,0:T(8,128)} fusion(f32[4,128,256]{2,1,0:T(8,128)S(1)} %get-tuple-element.141, f32[4,128,256]{2,1,0:T(8,128)S(1)} %get-tuple-element.140), kind=kLoop, calls=%fused_computation.4 | loop fusion | flops 262144 | bytes 2097152 | tf_op jit(solution)/shard_map/concatenate | solution.py:984
  61.6 1.1 %pad_maximum_fusion = f32[8,128,256]{2,1,0:T(8,128)} fusion(f32[4,128,256]{2,1,0:T(8,128)S(1)} %get-tuple-element.143, f32[4,128,256]{2,1,0:T(8,128)S(1)} %get-tuple-element.142), kind=kLoop, calls=%fused_computation.3 | loop fusion | flops 262144 | bytes 2097152 | tf_op jit(solution)/shard_map/concatenate | solution.py:984
  62.7 1.3 %collective-permute-start.26 = (bf16[1664,128]{1,0:T(8,128)(2,1)S(1)}, bf16[1664,128]{1,0:T(8,128)(2,1)S(1)}, u32[]{:S(2)}, u32[]{:S(2)}) collective-permute-start(bf16[1664,128]{1,0:T(8,128)(2,1)S(1)} %pad_maximum_fusion.2), channel_id=1, source_target_pairs={{0,4},{1,3},{2,6},{3,1},{4,0},{5,7},{6,2},{7,5},{8,12},{9,11},{10,... | collective-permute-start | bytes 1277960 | tf_op jit(solution)/shard_map/ppermute | solution.py:712
  64.0 3.5 %collective-permute-done.19 = bf16[832,128]{1,0:T(8,128)(2,1)S(1)} collective-permute-done((bf16[832,128]{1,0:T(8,128)(2,1)S(1)}, bf16[832,128]{1,0:T(8,128)(2,1)S(1)}, u32[]{:S(2)}, u32[]{:S(2)}) %collective-permute-start.19) | collective-permute-done | bytes 213024 | tf_op jit(solution)/shard_map/ppermute | solution.py:687
  67.7 1.6 %collective-permute-start.24 = (bf16[576,128]{1,0:T(8,128)(2,1)S(1)}, bf16[576,128]{1,0:T(8,128)(2,1)S(1)}, u32[]{:S(2)}, u32[]{:S(2)}) collective-permute-start(bf16[576,128]{1,0:T(8,128)(2,1)S(1)} %add_convert_fusion.5.refs_0_), channel_id=1, source_target_pairs={{0,4},{2,6},{4,0},{6,2},{8,12},{10,14},{12,8},{14,10},{16,20},{18,... | collective-permute-start | bytes 442376 | tf_op jit(solution)/shard_map/ppermute | solution.py:651
  69.4 1.8 %collective-permute-start.25 = (bf16[576,128]{1,0:T(8,128)(2,1)S(1)}, bf16[576,128]{1,0:T(8,128)(2,1)S(1)}, u32[]{:S(2)}, u32[]{:S(2)}) collective-permute-start(bf16[576,128]{1,0:T(8,128)(2,1)S(1)} %add_convert_fusion.5.refs_0_), channel_id=1, source_target_pairs={{0,6},{2,4},{4,2},{6,0},{8,14},{10,12},{12,10},{14,8},{16,22},{18,... | collective-permute-start | bytes 442376 | tf_op jit(solution)/shard_map/ppermute | solution.py:651
  71.5 0.1 eq.11
  71.6 0.3 fusion.2
  72.1 2.0 %fusion.1 = f32[1024,512]{1,0:T(8,128)} fusion(bf16[128,256]{1,0:T(8,128)(2,1)S(1)} %reshape.104, bf16[512,128]{1,0:T(8,128)(2,1)S(1)} %collective-permute-done.5.refs_12_, bf16[512,128]{1,0:T(8,128)(2,1)S(1)} %copy-done.4, f32[128,512]{1,0:T(8,128)S(1)} %fusion.2, s32[128]{0:T(128)S(1)} %eq.11, pred[]{:T(512)S(6)} %eq.10), kind=kOutput, calls=%fused_computation.2 | convolution fusion | flops 169672704 | bytes 2687489 | tf_op jit(solution)/shard_map/dot_general | solution.py:1064
  74.1 0.9 %fusion.33 = f32[512,128]{1,0:T(8,128)} fusion(f32[128,512]{1,0:T(8,128)S(1)} %fusion.2, bf16[128,256]{1,0:T(8,128)(2,1)S(1)} %reshape.104, s32[]{:T(128)S(6)} %select_n.81), kind=kOutput, calls=%fused_computation.56 | convolution fusion | flops 17104896 | bytes 557060 | tf_op jit(solution)/shard_map/dot_general | solution.py:1054
  75.0 0.6 slice_bitcast_fusion
  75.6 1.3 %unpack_second.1 = (f32[9,128,256]{2,1,0:T(8,128)}, f32[128,256]{1,0:T(8,128)}, f32[3,256,128]{2,1,0:T(8,128)}) custom-call(bf16[832,128]{1,0:T(8,128)(2,1)S(1)} %add_convert_fusion.refs_0_, bf16[832,128]{1,0:T(8,128)(2,1)S(1)} %collective-permute-done.21.refs_1_, bf16[1664,128]{1,0:T(8,128)(2,1)S(1)} %collective-permute-done.26.refs_2_), custom_call_target="tpu_custom_call" | custom-call | tf_op jit(solution)/shard_map/unpack_second/pallas_call | solution.py:1004
  76.9 1.2 %collective-permute-done.25.refs_3_ = bf16[576,128]{1,0:T(8,128)(2,1)S(1)} collective-permute-done((bf16[576,128]{1,0:T(8,128)(2,1)S(1)}, bf16[576,128]{1,0:T(8,128)(2,1)S(1)}, u32[]{:S(2)}, u32[]{:S(2)}) %collective-permute-start.25) | collective-permute-done | bytes 147488 | tf_op jit(solution)/shard_map/ppermute | solution.py:651
  78.1 1.1 %unpack_first.1 = f32[9,256,128]{2,1,0:T(8,128)} custom-call(bf16[576,128]{1,0:T(8,128)(2,1)S(1)} %add_convert_fusion.5.refs_0_, bf16[576,128]{1,0:T(8,128)(2,1)S(1)} %collective-permute-done.23.refs_1_, bf16[576,128]{1,0:T(8,128)(2,1)S(1)} %collective-permute-done.24.refs_2_, bf16[576,128]{1,0:T(8,128)(2,1)S(1)} %collective-permute-done.25.refs_3_), custom_call_target="tpu_custom_call" | custom-call | tf_op jit(solution)/shard_map/unpack_first/pallas_call | solution.py:1004
  (64 shorter events, 1.3 us)
Async XLA Ops:
  0.7 5.8 %collective-permute-start.1 = (bf16[9,256,128]{2,1,0:T(8,128)(2,1)}, bf16[9,256,128]{2,1,0:T(8,128)(2,1)S(1)}, u32[]{:S(2)}, u32[]{:S(2)}) collective-permute-start(bf16[9,256,128]{2,1,0:T(8,128)(2,1)} %refs_3_.3), channel_id=1, source_target_pairs={{0,1},{1,0},{2,3},{3,2},{4,5},{5,4},{6,7},{7,6},{8,9},{9,8},{10,11... | collective-permute-start | bytes 1769480 | tf_op jit(solution)/shard_map/ppermute | solution.py:651
  1.2 5.3 %collective-permute-start.2 = (bf16[9,128,256]{2,1,0:T(8,128)(2,1)}, bf16[9,128,256]{2,1,0:T(8,128)(2,1)S(1)}, u32[]{:S(2)}, u32[]{:S(2)}) collective-permute-start(bf16[9,128,256]{2,1,0:T(8,128)(2,1)} %refs_5_.3), channel_id=1, source_target_pairs={{0,1},{1,0},{2,3},{3,2},{4,5},{5,4},{6,7},{7,6},{8,9},{9,8},{10,11... | collective-permute-start | bytes 1769480 | tf_op jit(solution)/shard_map/ppermute | solution.py:651
  2.4 4.0 %copy-start = (f32[16,128]{1,0:T(8,128)}, f32[16,128]{1,0:T(8,128)S(1)}, u32[]{:S(2)}) copy-start(f32[16,128]{1,0:T(8,128)S(1)} %get-tuple-element.77.refs_13_) | copy-start | bytes 24580
  2.5 4.0 %collective-permute-start = (bf16[2,4,128,256]{3,2,1,0:T(8,128)(2,1)S(1)}, bf16[2,4,128,256]{3,2,1,0:T(8,128)(2,1)S(1)}, u32[]{:S(2)}, u32[]{:S(2)}) collective-permute-start(bf16[2,4,128,256]{3,2,1,0:T(8,128)(2,1)S(1)} %get-tuple-element.76), channel_id=1, source_target_pairs={{0,1},{1,0},{2,3},{3,2},{4,5},{5,4},{6,7},{7,6},{8,9},{9,8},{10,11... | collective-permute-start | bytes 1572872 | tf_op jit(solution)/shard_map/ppermute | solution.py:651
  2.9 1.6 %collective-permute-start.6 = (f32[16,128]{1,0:T(8,128)S(1)}, f32[16,128]{1,0:T(8,128)S(1)}, u32[]{:S(2)}, u32[]{:S(2)}) collective-permute-start(f32[16,128]{1,0:T(8,128)S(1)} %get-tuple-element.77.refs_13_), channel_id=1, source_target_pairs={{0,1},{1,0},{2,3},{3,2},{4,5},{5,4},{6,7},{7,6},{8,9},{9,8},{10,11... | collective-permute-start | bytes 24584 | tf_op jit(solution)/shard_map/ppermute | solution.py:651
  3.0 1.9 %collective-permute-start.4 = (bf16[128,256]{1,0:T(8,128)(2,1)}, bf16[128,256]{1,0:T(8,128)(2,1)S(1)}, u32[]{:S(2)}, u32[]{:S(2)}) collective-permute-start(bf16[128,256]{1,0:T(8,128)(2,1)} %refs_9_.3), channel_id=1, source_target_pairs={{0,1},{1,0},{2,3},{3,2},{4,5},{5,4},{6,7},{7,6},{8,9},{9,8},{10,11... | collective-permute-start | bytes 196616 | tf_op jit(solution)/shard_map/ppermute | solution.py:651
  4.5 1.9 %collective-permute-start.3 = (bf16[3,256,128]{2,1,0:T(8,128)(2,1)}, bf16[3,256,128]{2,1,0:T(8,128)(2,1)S(1)}, u32[]{:S(2)}, u32[]{:S(2)}) collective-permute-start(bf16[3,256,128]{2,1,0:T(8,128)(2,1)} %refs_7_.3), channel_id=1, source_target_pairs={{0,1},{1,0},{2,3},{3,2},{4,5},{5,4},{6,7},{7,6},{8,9},{9,8},{10,11... | collective-permute-start | bytes 589832 | tf_op jit(solution)/shard_map/ppermute | solution.py:651
  4.9 1.6 %collective-permute-start.5 = (bf16[512,128]{1,0:T(8,128)(2,1)}, bf16[512,128]{1,0:T(8,128)(2,1)S(1)}, u32[]{:S(2)}, u32[]{:S(2)}) collective-permute-start(bf16[512,128]{1,0:T(8,128)(2,1)} %refs_11_.3), channel_id=1, source_target_pairs={{0,1},{1,0},{2,3},{3,2},{4,5},{5,4},{6,7},{7,6},{8,9},{9,8},{10,11... | collective-permute-start | bytes 393224 | tf_op jit(solution)/shard_map/ppermute | solution.py:651
  19.0 2.4 %collective-permute-start.7 = (bf16[3328,128]{1,0:T(8,128)(2,1)S(1)}, bf16[3328,128]{1,0:T(8,128)(2,1)S(1)}, u32[]{:S(2)}, u32[]{:S(2)}) collective-permute-start(bf16[3328,128]{1,0:T(8,128)(2,1)S(1)} %get-tuple-element.92), channel_id=1, source_target_pairs={{0,1},{1,0},{2,3},{3,2},{4,5},{5,4},{6,7},{7,6},{8,9},{9,8},{10,11... | collective-permute-start | bytes 2555912 | tf_op jit(solution)/shard_map/ppermute | solution.py:651
  21.6 13.3 %collective-permute-start.10 = (bf16[832,128]{1,0:T(8,128)(2,1)S(1)}, bf16[832,128]{1,0:T(8,128)(2,1)S(1)}, u32[]{:S(2)}, u32[]{:S(2)}) collective-permute-start(bf16[832,128]{1,0:T(8,128)(2,1)S(1)} %get-tuple-element.101), channel_id=1, source_target_pairs={{0,6},{2,4},{4,2},{6,0},{8,14},{10,12},{12,10},{14,8},{16,22},{18,... | collective-permute-start | bytes 638984 | tf_op jit(solution)/shard_map/ppermute | solution.py:651
  25.4 10.5 %collective-permute-start.8 = (bf16[832,128]{1,0:T(8,128)(2,1)S(1)}, bf16[832,128]{1,0:T(8,128)(2,1)S(1)}, u32[]{:S(2)}, u32[]{:S(2)}) collective-permute-start(bf16[832,128]{1,0:T(8,128)(2,1)S(1)} %get-tuple-element.99), channel_id=1, source_target_pairs={{0,2},{2,0},{4,6},{6,4},{8,10},{10,8},{12,14},{14,12},{16,18},{18,... | collective-permute-start | bytes 638984 | tf_op jit(solution)/shard_map/ppermute | solution.py:651
  25.9 10.0 %collective-permute-start.9 = (bf16[832,128]{1,0:T(8,128)(2,1)S(1)}, bf16[832,128]{1,0:T(8,128)(2,1)}, u32[]{:S(2)}, u32[]{:S(2)}) collective-permute-start(bf16[832,128]{1,0:T(8,128)(2,1)S(1)} %get-tuple-element.100), channel_id=1, source_target_pairs={{0,4},{2,6},{4,0},{6,2},{8,12},{10,14},{12,8},{14,10},{16,20},{18,... | collective-permute-start | bytes 638984 | tf_op jit(solution)/shard_map/ppermute | solution.py:651
  35.9 2.7 %collective-permute-start.11 = (bf16[2304,128]{1,0:T(8,128)(2,1)}, bf16[2304,128]{1,0:T(8,128)(2,1)S(1)}, u32[]{:S(2)}, u32[]{:S(2)}) collective-permute-start(bf16[2304,128]{1,0:T(8,128)(2,1)} %get-tuple-element.106), channel_id=1, source_target_pairs={{0,1},{1,0},{2,3},{3,2},{4,5},{5,4},{6,7},{7,6},{8,9},{9,8},{10,11... | collective-permute-start | bytes 1769480 | tf_op jit(solution)/shard_map/ppermute | solution.py:651
  37.0 8.1 %collective-permute-start.15 = (bf16[832,128]{1,0:T(8,128)(2,1)S(1)}, bf16[832,128]{1,0:T(8,128)(2,1)S(1)}, u32[]{:S(2)}, u32[]{:S(2)}) collective-permute-start(bf16[832,128]{1,0:T(8,128)(2,1)S(1)} %fusion.5), channel_id=1, source_target_pairs={{0,8},{1,17},{2,10},{3,19},{4,12},{5,21},{6,14},{7,23},{8,0},{9,25... | collective-permute-start | bytes 638984 | tf_op jit(solution)/shard_map/ppermute | solution.py:687
  38.8 12.7 %copy-start.6 = (bf16[4,128,256]{2,1,0:T(8,128)(2,1)S(1)}, bf16[4,128,256]{2,1,0:T(8,128)(2,1)}, u32[]{:S(2)}) copy-start(bf16[4,128,256]{2,1,0:T(8,128)(2,1)} %get-tuple-element.119) | copy-start | bytes 786436
  38.8 12.7 %copy-start.5 = (bf16[4,128,256]{2,1,0:T(8,128)(2,1)S(1)}, bf16[4,128,256]{2,1,0:T(8,128)(2,1)}, u32[]{:S(2)}) copy-start(bf16[4,128,256]{2,1,0:T(8,128)(2,1)} %get-tuple-element.117) | copy-start | bytes 786436
  38.8 8.5 %collective-permute-start.12 = (bf16[608,128]{1,0:T(8,128)(2,1)S(1)}, bf16[608,128]{1,0:T(8,128)(2,1)S(1)}, u32[]{:S(2)}, u32[]{:S(2)}) collective-permute-start(bf16[608,128]{1,0:T(8,128)(2,1)S(1)} %get-tuple-element.175), channel_id=1, source_target_pairs={{0,2},{2,0},{4,6},{6,4},{8,10},{10,8},{12,14},{14,12},{16,18},{18,... | collective-permute-start | bytes 466952 | tf_op jit(solution)/shard_map/ppermute | solution.py:651
  40.4 10.2 %collective-permute-start.13 = (bf16[608,128]{1,0:T(8,128)(2,1)S(1)}, bf16[608,128]{1,0:T(8,128)(2,1)S(1)}, u32[]{:S(2)}, u32[]{:S(2)}) collective-permute-start(bf16[608,128]{1,0:T(8,128)(2,1)S(1)} %get-tuple-element.174), channel_id=1, source_target_pairs={{0,4},{2,6},{4,0},{6,2},{8,12},{10,14},{12,8},{14,10},{16,20},{18,... | collective-permute-start | bytes 466952 | tf_op jit(solution)/shard_map/ppermute | solution.py:651
  41.9 8.7 %collective-permute-start.14 = (bf16[608,128]{1,0:T(8,128)(2,1)S(1)}, bf16[608,128]{1,0:T(8,128)(2,1)S(1)}, u32[]{:S(2)}, u32[]{:S(2)}) collective-permute-start(bf16[608,128]{1,0:T(8,128)(2,1)S(1)} %get-tuple-element.173), channel_id=1, source_target_pairs={{0,6},{2,4},{4,2},{6,0},{8,14},{10,12},{12,10},{14,8},{16,22},{18,... | collective-permute-start | bytes 466952 | tf_op jit(solution)/shard_map/ppermute | solution.py:651
  45.2 15.1 %copy-start.3 = (f32[4,128,256]{2,1,0:T(8,128)S(1)}, f32[4,128,256]{2,1,0:T(8,128)}, u32[]{:S(2)}) copy-start(f32[4,128,256]{2,1,0:T(8,128)} %get-tuple-element.118) | copy-start | bytes 1572868
  45.2 8.6 %collective-permute-start.20 = (bf16[832,128]{1,0:T(8,128)(2,1)S(1)}, bf16[832,128]{1,0:T(8,128)(2,1)S(1)}, u32[]{:S(2)}, u32[]{:S(2)}) collective-permute-start(bf16[832,128]{1,0:T(8,128)(2,1)S(1)} %add_convert_fusion.1), channel_id=1, source_target_pairs={{0,16},{1,9},{2,18},{3,11},{4,20},{5,13},{6,22},{7,15},{8,24},{9,1... | collective-permute-start | bytes 638984 | tf_op jit(solution)/shard_map/ppermute | solution.py:687
  50.8 7.5 %collective-permute-start.18 = (bf16[704,128]{1,0:T(8,128)(2,1)S(1)}, bf16[704,128]{1,0:T(8,128)(2,1)S(1)}, u32[]{:S(2)}, u32[]{:S(2)}) collective-permute-start(bf16[704,128]{1,0:T(8,128)(2,1)S(1)} %constant_dynamic-update-slice_fusion), channel_id=1, source_target_pairs={{0,8},{1,17},{2,10},{3,19},{4,12},{5,21},{6,14},{7,23},{8,0},{9,25... | collective-permute-start | bytes 540680 | tf_op jit(solution)/shard_map/ppermute | solution.py:687
  51.5 8.8 %collective-permute-start.17 = (bf16[4,128,256]{2,1,0:T(8,128)(2,1)S(1)}, bf16[4,128,256]{2,1,0:T(8,128)(2,1)S(1)}, u32[]{:S(2)}, u32[]{:S(2)}) collective-permute-start(bf16[4,128,256]{2,1,0:T(8,128)(2,1)S(1)} %copy-done.6), channel_id=1, source_target_pairs={{0,1},{1,0},{2,3},{3,2},{4,5},{5,4},{6,7},{7,6},{8,9},{9,8},{10,11... | collective-permute-start | bytes 786440 | tf_op jit(solution)/shard_map/ppermute | solution.py:651
  51.5 8.9 %collective-permute-start.16 = (bf16[4,128,256]{2,1,0:T(8,128)(2,1)S(1)}, bf16[4,128,256]{2,1,0:T(8,128)(2,1)S(1)}, u32[]{:S(2)}, u32[]{:S(2)}) collective-permute-start(bf16[4,128,256]{2,1,0:T(8,128)(2,1)S(1)} %copy-done.5), channel_id=1, source_target_pairs={{0,1},{1,0},{2,3},{3,2},{4,5},{5,4},{6,7},{7,6},{8,9},{9,8},{10,11... | collective-permute-start | bytes 786440 | tf_op jit(solution)/shard_map/ppermute | solution.py:651
  53.8 6.6 %copy-start.2 = (f32[4,128,256]{2,1,0:T(8,128)S(1)}, f32[4,128,256]{2,1,0:T(8,128)}, u32[]{:S(2)}) copy-start(f32[4,128,256]{2,1,0:T(8,128)} %get-tuple-element.116) | copy-start | bytes 1572868
  53.8 8.8 %collective-permute-start.21 = (bf16[832,128]{1,0:T(8,128)(2,1)S(1)}, bf16[832,128]{1,0:T(8,128)(2,1)S(1)}, u32[]{:S(2)}, u32[]{:S(2)}) collective-permute-start(bf16[832,128]{1,0:T(8,128)(2,1)S(1)} %add_convert_fusion.refs_0_), channel_id=1, source_target_pairs={{0,2},{1,5},{2,0},{3,7},{4,6},{5,1},{6,4},{7,3},{8,10},{9,13},{10,... | collective-permute-start | bytes 638984 | tf_op jit(solution)/shard_map/ppermute | solution.py:712
  58.4 9.1 %collective-permute-start.19 = (bf16[832,128]{1,0:T(8,128)(2,1)S(1)}, bf16[832,128]{1,0:T(8,128)(2,1)S(1)}, u32[]{:S(2)}, u32[]{:S(2)}) collective-permute-start(bf16[832,128]{1,0:T(8,128)(2,1)S(1)} %get-tuple-element.148), channel_id=1, source_target_pairs={{0,16},{1,9},{2,18},{3,11},{4,20},{5,13},{6,22},{7,15},{8,24},{9,1... | collective-permute-start | bytes 638984 | tf_op jit(solution)/shard_map/ppermute | solution.py:687
  62.7 8.9 %copy-start.1 = (bf16[1024,512]{1,0:T(8,128)(2,1)S(1)}, bf16[1024,512]{1,0:T(8,128)(2,1)}, u32[]{:S(2)}) copy-start(bf16[1024,512]{1,0:T(8,128)(2,1)} %refs_16_.1) | copy-start | bytes 3145732
  62.7 12.9 %collective-permute-start.26 = (bf16[1664,128]{1,0:T(8,128)(2,1)S(1)}, bf16[1664,128]{1,0:T(8,128)(2,1)S(1)}, u32[]{:S(2)}, u32[]{:S(2)}) collective-permute-start(bf16[1664,128]{1,0:T(8,128)(2,1)S(1)} %pad_maximum_fusion.2), channel_id=1, source_target_pairs={{0,4},{1,3},{2,6},{3,1},{4,0},{5,7},{6,2},{7,5},{8,12},{9,11},{10,... | collective-permute-start | bytes 1277960 | tf_op jit(solution)/shard_map/ppermute | solution.py:712
  67.5 3.7 %collective-permute-start.22 = (bf16[512,128]{1,0:T(8,128)(2,1)S(1)}, bf16[512,128]{1,0:T(8,128)(2,1)S(1)}, u32[]{:S(2)}, u32[]{:S(2)}) collective-permute-start(bf16[512,128]{1,0:T(8,128)(2,1)S(1)} %get-tuple-element.144), channel_id=1, source_target_pairs={{0,1},{1,0},{2,3},{3,2},{4,5},{5,4},{6,7},{7,6},{8,9},{9,8},{10,11... | collective-permute-start | bytes 393224 | tf_op jit(solution)/shard_map/ppermute | solution.py:651
  67.7 9.3 %collective-permute-start.23 = (bf16[576,128]{1,0:T(8,128)(2,1)S(1)}, bf16[576,128]{1,0:T(8,128)(2,1)S(1)}, u32[]{:S(2)}, u32[]{:S(2)}) collective-permute-start(bf16[576,128]{1,0:T(8,128)(2,1)S(1)} %add_convert_fusion.5.refs_0_), channel_id=1, source_target_pairs={{0,2},{2,0},{4,6},{6,4},{8,10},{10,8},{12,14},{14,12},{16,18},{18,... | collective-permute-start | bytes 442376 | tf_op jit(solution)/shard_map/ppermute | solution.py:651
  67.7 9.2 %collective-permute-start.24 = (bf16[576,128]{1,0:T(8,128)(2,1)S(1)}, bf16[576,128]{1,0:T(8,128)(2,1)S(1)}, u32[]{:S(2)}, u32[]{:S(2)}) collective-permute-start(bf16[576,128]{1,0:T(8,128)(2,1)S(1)} %add_convert_fusion.5.refs_0_), channel_id=1, source_target_pairs={{0,4},{2,6},{4,0},{6,2},{8,12},{10,14},{12,8},{14,10},{16,20},{18,... | collective-permute-start | bytes 442376 | tf_op jit(solution)/shard_map/ppermute | solution.py:651
  69.4 8.8 %collective-permute-start.25 = (bf16[576,128]{1,0:T(8,128)(2,1)S(1)}, bf16[576,128]{1,0:T(8,128)(2,1)S(1)}, u32[]{:S(2)}, u32[]{:S(2)}) collective-permute-start(bf16[576,128]{1,0:T(8,128)(2,1)S(1)} %add_convert_fusion.5.refs_0_), channel_id=1, source_target_pairs={{0,6},{2,4},{4,2},{6,0},{8,14},{10,12},{12,10},{14,8},{16,22},{18,... | collective-permute-start | bytes 442376 | tf_op jit(solution)/shard_map/ppermute | solution.py:651
  71.2 0.9 %copy-start.4 = (bf16[512,128]{1,0:T(8,128)(2,1)S(1)}, bf16[512,128]{1,0:T(8,128)(2,1)}, u32[]{:S(2)}) copy-start(bf16[512,128]{1,0:T(8,128)(2,1)} %refs_11_.3) | copy-start | bytes 393220

commit v6 on v5

--- a/solution.py
+++ b/solution.py
@@ -177,7 +177,7 @@
 
 def pack_kernel(n_vec, *refs):
     vectors, arrays = refs[:n_vec], refs[n_vec : n_vec + 2]
-    vec, halves, sems = refs[n_vec + 2 :]
+    tw, pi, po, vec, halves, small, sems = refs[n_vec + 2 :]
     cps = Copies(sems)
     count = halves.shape[1]
     first = pl.multiple_of((1 - lax.axis_index("tensor")) * count, count)
@@ -186,6 +186,15 @@
         for j, src in enumerate(arrays)
     ]
     copies += [cps.start(v, vec.at[j]) for j, v in enumerate(vectors)]
+    at = tw.shape[0]
+    copies.append(cps.start(tw, small.at[0:at]))
+    for j in range(3):
+        copies.append(cps.start(pi.at[j], small.at[at : at + pi.shape[1]]))
+        at += pi.shape[1]
+    half = po.shape[0]
+    for j in range(2):
+        copies.append(cps.start(po.at[:, j * half : (j + 1) * half], small.at[at : at + half]))
+        at += half
     vec[n_vec:, :] = jnp.zeros((16 - n_vec, vec.shape[1]), f32)
     wait_all(copies)
 
@@ -225,8 +234,9 @@
     def take(n):
         return [next(it) for _ in range(n)]
 
-    x_in, g_in = take(pieces), take(1)
-    w1_in, w2_in, pi_in, po_in, tw_in, vec_in = (take(pieces) for _ in range(6))
+    x_in, w1_in, w2_in, vec_in = (take(pieces) for _ in range(4))
+    g_in, pi_in, po_in, tw_in = (take(1) for _ in range(4))
+    small_in = take(pieces - 1)
     if pieces == 2:
         x_in, g_in = [x_in[0], x_in[1].at[0]], [g_in[0], x_in[1].at[1]]
     steps_ref, table_ref = take(2)
@@ -261,10 +271,22 @@
         row_cp.append(
             cps.start(table_ref.at[pl.ds(pl.multiple_of(step // 16 * 16, 16), 16), :], rows.at[b])
         )
-    tw_cp = load_split(cps, tw_in, tw, 1, places)
+    tw_cp = load_split(cps, tw_in, tw, 1, places[:1])
     w2_cp = load_split(cps, w2_in, w2, 1, places)
-    pi_cp = load_split(cps, pi_in, pi, 2, places)
-    po_cp = load_split(cps, po_in, po, 0, places)
+    pi_cp = load_split(cps, pi_in, pi, 2, places[:1])
+    po_cp = load_split(cps, po_in, po, 0, places[:1])
+    if pieces == 2:
+        half = chans // 2
+        theirs = pl.ds(pl.multiple_of(places[1] * half, half), half)
+        embed = tw.shape[0]
+        tw_cp.append(cps.start(small_in[0].at[0:embed], tw.at[:, theirs]))
+        for j in range(3):
+            rows_of = pl.ds(embed + j * chans, chans)
+            pi_cp.append(cps.start(small_in[0].at[rows_of], pi.at[j, :, theirs]))
+        for j in range(2):
+            rows_of = pl.ds(embed + 3 * chans + j * half, half)
+            lanes = pl.ds(j * half, half)
+            po_cp.append(cps.start(small_in[0].at[rows_of], po.at[theirs, lanes]))
     g_cp = load_images(cps, g_in, gin, places, count)
 
     zero_pads(apad, side, points)
@@ -788,18 +810,19 @@
 
     n_vec = len(vectors)
     if pieces == 2:
-        vec, halves = pl.pallas_call(
+        vec, halves, small = pl.pallas_call(
             functools.partial(pack_kernel, n_vec),
             out_shape=[
                 jax.ShapeDtypeStruct((16, local), f32),
                 jax.ShapeDtypeStruct((2, count, local, points), bf16),
+                jax.ShapeDtypeStruct((embed + 4 * chans, local), bf16),
             ],
-            in_specs=[ANY] * (n_vec + 2),
-            out_specs=[VMEM] * 2,
-            scratch_shapes=[pltpu.SemaphoreType.DMA((n_vec + 2,))],
+            in_specs=[ANY] * (n_vec + 5),
+            out_specs=[VMEM] * 3,
+            scratch_shapes=[pltpu.SemaphoreType.DMA((n_vec + 8,))],
             compiler_params=pltpu.CompilerParams(vmem_limit_bytes=4 * MIB),
             name="pack",
-        )(*(in_hbm(v) for v in vectors + [images, cotangent]))
+        )(*(in_hbm(v) for v in vectors + [images, cotangent, time_weight, project_in, project_out]))
     else:
         vec = jnp.stack(vectors + [output_bias] * 4, axis=0)
 
@@ -810,16 +833,17 @@
 
     if pieces == 2:
         x_in, g_in = [images, swap(halves, "tensor", 2, 1)], [cotangent]
+        tw_in, pi_in, po_in = [time_weight], [project_in], [project_out]
+        small_in = [swap(small, "tensor", 2, 1)]
     else:
         x_in, g_in = (
             [lax.all_to_all(v, "tensor", 0, 1, tiled=True)] for v in (images, cotangent)
         )
+        tw_in, pi_in, po_in = whole(time_weight, 1), whole(project_in, 2), whole(project_out, 0)
+        small_in = []
     vec_in = whole(vec, 1)
-    tw_in = whole(time_weight, 1)
     w1_in = whole(first_conv, 2)
     w2_in = whole(second_conv, 1)
-    pi_in = whole(project_in, 2)
-    po_in = whole(project_out, 0)
     my_steps = timesteps if pieces == 2 else lax.dynamic_slice_in_dim(timesteps, me * count, count)
 
     side = side_of(points)
@@ -870,7 +894,7 @@
         functools.partial(front_kernel, pieces, count),
         out_shape=grads_a
         + [pltpu.HBM(*v) for v in kept],
-        in_specs=[ANY, VMEM][:pieces] + [ANY] + [ANY, VMEM][:pieces] * 6 + [SMEM, ANY],
+        in_specs=[ANY, VMEM][:pieces] * 4 + [ANY] * 4 + [VMEM] * (pieces - 1) + [SMEM, ANY],
         out_specs=[VMEM] * n_grad + [ANY] * len(kept),
         scratch_shapes=scratch_a
         + [pltpu.VMEM(*v) for v in kept]
@@ -881,7 +905,7 @@
             pltpu.VMEM((count, 16, embed), bf16),
             pltpu.VMEM(pads, bf16),
             pltpu.VMEM(pads, bf16),
-            pltpu.SemaphoreType.DMA((8 * pieces + 3 * count + 19,)),
+            pltpu.SemaphoreType.DMA((8 * pieces + 3 * count + 22,)),
         ],
         compiler_params=params(28),
         cost_estimate=cost(54, 12 << 20),
@@ -889,9 +913,11 @@
     )(
         *(
             place(v)
-            for pair in (x_in, g_in, w1_in, w2_in, pi_in, po_in, tw_in, vec_in)
+            for pair in (x_in, w1_in, w2_in, vec_in)
             for v, place in zip(pair, (in_hbm, lambda v: v))
         ),
+        *(in_hbm(v) for v in g_in + pi_in + po_in + tw_in),
+        *small_in,
         steps_in,
         in_hbm(embed_table),
     )
@@ -1055,8 +1081,11 @@
         act, my_times, (((0,), (0,)), ((), ())), preferred_element_type=f32
     )
     if pieces == 2:
+        theirs = small_in[0][:embed]
         tw = jnp.where(
-            me == 0, jnp.concatenate(tw_in, axis=1), jnp.concatenate(tw_in[::-1], axis=1)
+            me == 0,
+            jnp.concatenate([time_weight, theirs], axis=1),
+            jnp.concatenate([theirs, time_weight], axis=1),
         )
     else:
         tw = tw_in[0]

time: 79.7 us -> 78.1 us (0.980)
  waiting for transfers between devices: 20.7 us -> 16.7 us
  local copies, waits for them, and re-layouts: 0.93 us -> 3.13 us
    ppermute x4, waiting for transfers between devices: 10.8 us -> 8.69 us  [send_far(): return lax.ppermute(mine, ('batch', 'tensor'), pairs)]
    ppermute x21 -> x19, waiting for transfers between devices: 9.91 us -> 7.96 us  [swap(): return lax.ppermute(value, axis, [(i, i ^ bit) for i in range(size)])]
    reshape x1, local copies, waits for them, and re-layouts: 0.03 us -> 0.86 us  [per_device(): all_times = blocks[:, n_sum:n_sum + wide * count].reshape(-1, chans)]
    ppermute x21 -> x19, starting transfers between devices: 14.7 us -> 14.3 us  [swap(): return lax.ppermute(value, axis, [(i, i ^ bit) for i in range(size)])]
  transfers between devices with their start and end apart: 27 -> 25, of which waited for: 10 -> 9; matrix products, arithmetic and copies ran while one was open for 10% -> 13% of each run, Pallas kernels for 14% -> 15%
where the time goes in v6:
time: 78.1 us; the launch traced here: 77.6 us
  Pallas kernels  25.1 us (32%)
  starting transfers between devices  23.7 us (30%)
  waiting for transfers between devices  16.7 us (21%)
  other arithmetic  4.49 us (6%)
  matrix products  3.24 us (4%)
  local copies, waits for them, and re-layouts  3.13 us (4%)
  between operations  1.15 us (1%)
    ppermute x19, starting transfers between devices, swap(): return lax.ppermute(value, axis, [(i, i ^ bit) for i in range(size)])  14.3 us
    pallas_call x1, Pallas kernels, per_device(): pl.pallas_call(functools.partial(front_kernel, pieces, count), out_shape=...  12.5 us
    pallas_call x1, Pallas kernels, per_device(): pl.pallas_call(functools.partial(back_kernel, pieces, count), out_shape=o...  8.83 us
    ppermute x4, waiting for transfers between devices, send_far(): return lax.ppermute(mine, ('batch', 'tensor'), pairs)  8.69 us
    ppermute x19, waiting for transfers between devices, swap(): return lax.ppermute(value, axis, [(i, i ^ bit) for i in range(size)])  7.96 us
    ppermute x4, starting transfers between devices, send_far(): return lax.ppermute(mine, ('batch', 'tensor'), pairs)  6.62 us
    ppermute x2, starting transfers between devices, cross(): return lax.ppermute(value, ('batch', 'tensor'), pairs)  2.81 us
    pallas_call x2, Pallas kernels, unpacked(): pl.pallas_call(kernel, out_shape=outs, in_specs=[VMEM] * len(got), out_sp...  2.41 us
  transfers between devices with their start and end apart: 25, of which 9 were waited for; matrix products, arithmetic and copies ran while one was open for 13% of the time, Pallas kernels for 15%

profile of v6, /device:TPU:0, one launch (start us, length us, event | category | flops | bytes accessed | tf_op | source)
XLA Modules:
  0.0 77.6 jit_solution(11391376203244828194)
XLA Ops:
  0.7 0.5 collective-permute-start.1
  1.3 1.4 %pack.1 = (f32[16,128]{1,0:T(8,128)S(1)}, bf16[2,4,128,256]{3,2,1,0:T(8,128)(2,1)S(1)}, bf16[1536,128]{1,0:T(8,128)(2,1)S(1)}) custom-call(f32[128]{0:T(128)} %refs_0_.2, f32[128]{0:T(128)} %refs_1_.1, f32[128]{0:T(128)} %refs_2_.2, f32[128]{0:T(128)} %refs_3_.1, f32[128]{0:T(128)} %refs_4_.2, f32[128]{0:T(128)} %refs_5_.1, f32[128]{0:T(128)} %refs_6_.1, ...), custom_call_target="tpu_custom_call" | custom-call | tf_op jit(solution)/shard_map/pack/pallas_call | solution.py:813
  2.7 0.5 collective-permute-start
  3.2 0.4 collective-permute-start.3
  3.7 1.6 %collective-permute-done.3.refs_7_ = f32[16,128]{1,0:T(8,128)S(1)} collective-permute-done((f32[16,128]{1,0:T(8,128)S(1)}, f32[16,128]{1,0:T(8,128)S(1)}, u32[]{:S(2)}, u32[]{:S(2)}) %collective-permute-start.3) | collective-permute-done | bytes 8224 | tf_op jit(solution)/shard_map/ppermute | solution.py:673
  5.3 12.5 %front.1 = (bf16[3328,128]{1,0:T(8,128)(2,1)S(1)}, bf16[3328,128]{1,0:T(8,128)(2,1)S(1)}, bf16[9,256,256]{2,1,0:T(8,128)(2,1)}, bf16[9,256,256]{2,1,0:T(8,128)(2...) custom-call(bf16[8,128,256]{2,1,0:T(8,128)(2,1)} %refs_0_.3, ...), custom_call_target="tpu_custom_call" | custom-call | flops 7247757312 | bytes 12582912 | tf_op jit(solution)/shard_map/front/pallas_call | solution.py:893
  17.8 0.5 collective-permute-start.5
  18.3 2.0 %collective-permute-done.5 = bf16[3328,128]{1,0:T(8,128)(2,1)S(1)} collective-permute-done((bf16[3328,128]{1,0:T(8,128)(2,1)S(1)}, bf16[3328,128]{1,0:T(8,128)(2,1)S(1)}, u32[]{:S(2)}, u32[]{:S(2)}) %collective-permute-start.5) | collective-permute-done | bytes 852000 | tf_op jit(solution)/shard_map/ppermute | solution.py:673
  20.3 0.2 fusion.29
  20.5 2.9 %collective-permute-start.6 = (bf16[832,128]{1,0:T(8,128)(2,1)S(1)}, bf16[832,128]{1,0:T(8,128)(2,1)S(1)}, u32[]{:S(2)}, u32[]{:S(2)}) collective-permute-start(bf16[832,128]{1,0:T(8,128)(2,1)S(1)} %get-tuple-element.101), channel_id=1, source_target_pairs={{0,2},{2,0},{4,6},{6,4},{8,10},{10,8},{12,14},{14,12},{16,18},{18,... | collective-permute-start | bytes 638984 | tf_op jit(solution)/shard_map/ppermute | solution.py:673
  23.4 1.5 %collective-permute-start.7 = (bf16[832,128]{1,0:T(8,128)(2,1)S(1)}, bf16[832,128]{1,0:T(8,128)(2,1)S(1)}, u32[]{:S(2)}, u32[]{:S(2)}) collective-permute-start(bf16[832,128]{1,0:T(8,128)(2,1)S(1)} %get-tuple-element.102), channel_id=1, source_target_pairs={{0,4},{2,6},{4,0},{6,2},{8,12},{10,14},{12,8},{14,10},{16,20},{18,... | collective-permute-start | bytes 638984 | tf_op jit(solution)/shard_map/ppermute | solution.py:673
  24.9 8.8 %back.1 = (bf16[2304,128]{1,0:T(8,128)(2,1)S(1)}, bf16[2304,128]{1,0:T(8,128)(2,1)}, f32[4,128,256]{2,1,0:T(8,128)}, bf16[4,128,256]{2,1,0:T(8,128)(2,1)}, f32[4...) custom-call(bf16[9,256,256]{2,1,0:T(8,128)(2,1)} %get-tuple-element.80.refs_0_, ...), custom_call_target="tpu_custom_call" | custom-call | flops 4429185024 | bytes 12582912 | tf_op jit(solution)/shard_map/back/pallas_call | solution.py:963
  33.8 1.2 %collective-permute-done.7 = bf16[832,128]{1,0:T(8,128)(2,1)S(1)} collective-permute-done((bf16[832,128]{1,0:T(8,128)(2,1)S(1)}, bf16[832,128]{1,0:T(8,128)(2,1)S(1)}, u32[]{:S(2)}, u32[]{:S(2)}) %collective-permute-start.7) | collective-permute-done | bytes 213024 | tf_op jit(solution)/shard_map/ppermute | solution.py:673
  35.0 0.7 copy-done.6
  35.7 1.2 %fusion.5 = bf16[832,128]{1,0:T(8,128)(2,1)S(1)} fusion(bf16[832,128]{1,0:T(8,128)(2,1)} %copy-done.7, bf16[832,128]{1,0:T(8,128)(2,1)} %copy-done.6, bf16[832,128]{1,0:T(8,128)(2,1)S(1)} %collective-permute-done.6, bf16[4,832,128]{2,1,0:T(8,128)(2,1)S(1)} %bitcast.71, s32[]{:T(128)S(6)} %select_n.72, bf16[4,832,128]{2,1,0:T(8,128)(2,1)S(1)} %bitcast.64), kind=kLoop, calls=%fused_computation.15 | loop fusion | flops 1064960 | bytes 1277956 | tf_op jit(solution)/shard_map/convert_element_type | solution.py:693
  36.9 1.6 %collective-permute-start.13 = (bf16[832,128]{1,0:T(8,128)(2,1)S(1)}, bf16[832,128]{1,0:T(8,128)(2,1)S(1)}, u32[]{:S(2)}, u32[]{:S(2)}) collective-permute-start(bf16[832,128]{1,0:T(8,128)(2,1)S(1)} %fusion.5), channel_id=1, source_target_pairs={{0,8},{1,17},{2,10},{3,19},{4,12},{5,21},{6,14},{7,23},{8,0},{9,25... | collective-permute-start | bytes 638984 | tf_op jit(solution)/shard_map/ppermute | solution.py:709
  38.5 0.1 fusion.32
  38.7 1.8 %collective-permute-start.12 = (bf16[608,128]{1,0:T(8,128)(2,1)S(1)}, bf16[608,128]{1,0:T(8,128)(2,1)S(1)}, u32[]{:S(2)}, u32[]{:S(2)}) collective-permute-start(bf16[608,128]{1,0:T(8,128)(2,1)S(1)} %get-tuple-element.175), channel_id=1, source_target_pairs={{0,6},{2,4},{4,2},{6,0},{8,14},{10,12},{12,10},{14,8},{16,22},{18,... | collective-permute-start | bytes 466952 | tf_op jit(solution)/shard_map/ppermute | solution.py:673
  40.5 0.9 %collective-permute-start.11 = (bf16[608,128]{1,0:T(8,128)(2,1)S(1)}, bf16[608,128]{1,0:T(8,128)(2,1)S(1)}, u32[]{:S(2)}, u32[]{:S(2)}) collective-permute-start(bf16[608,128]{1,0:T(8,128)(2,1)S(1)} %get-tuple-element.176), channel_id=1, source_target_pairs={{0,4},{2,6},{4,0},{6,2},{8,12},{10,14},{12,8},{14,10},{16,20},{18,... | collective-permute-start | bytes 466952 | tf_op jit(solution)/shard_map/ppermute | solution.py:673
  41.4 0.8 %collective-permute-start.10 = (bf16[608,128]{1,0:T(8,128)(2,1)S(1)}, bf16[608,128]{1,0:T(8,128)(2,1)S(1)}, u32[]{:S(2)}, u32[]{:S(2)}) collective-permute-start(bf16[608,128]{1,0:T(8,128)(2,1)S(1)} %get-tuple-element.177), channel_id=1, source_target_pairs={{0,2},{2,0},{4,6},{6,4},{8,10},{10,8},{12,14},{14,12},{16,18},{18,... | collective-permute-start | bytes 466952 | tf_op jit(solution)/shard_map/ppermute | solution.py:673
  42.3 2.8 %collective-permute-done.13 = bf16[832,128]{1,0:T(8,128)(2,1)S(1)} collective-permute-done((bf16[832,128]{1,0:T(8,128)(2,1)S(1)}, bf16[832,128]{1,0:T(8,128)(2,1)S(1)}, u32[]{:S(2)}, u32[]{:S(2)}) %collective-permute-start.13) | collective-permute-done | bytes 213024 | tf_op jit(solution)/shard_map/ppermute | solution.py:709
  45.1 2.1 %collective-permute-start.18 = (bf16[832,128]{1,0:T(8,128)(2,1)S(1)}, bf16[832,128]{1,0:T(8,128)(2,1)S(1)}, u32[]{:S(2)}, u32[]{:S(2)}) collective-permute-start(bf16[832,128]{1,0:T(8,128)(2,1)S(1)} %add_convert_fusion.1), channel_id=1, source_target_pairs={{0,16},{1,9},{2,18},{3,11},{4,20},{5,13},{6,22},{7,15},{8,24},{9,1... | collective-permute-start | bytes 638984 | tf_op jit(solution)/shard_map/ppermute | solution.py:709
  47.2 2.7 %collective-permute-done.11 = bf16[608,128]{1,0:T(8,128)(2,1)S(1)} collective-permute-done((bf16[608,128]{1,0:T(8,128)(2,1)S(1)}, bf16[608,128]{1,0:T(8,128)(2,1)S(1)}, u32[]{:S(2)}, u32[]{:S(2)}) %collective-permute-start.11) | collective-permute-done | bytes 155680 | tf_op jit(solution)/shard_map/ppermute | solution.py:673
  49.9 0.1 constant_dynamic-update-slice_fusion.4
  50.1 1.0 %collective-permute-start.16 = (bf16[704,128]{1,0:T(8,128)(2,1)S(1)}, bf16[704,128]{1,0:T(8,128)(2,1)S(1)}, u32[]{:S(2)}, u32[]{:S(2)}) collective-permute-start(bf16[704,128]{1,0:T(8,128)(2,1)S(1)} %constant_dynamic-update-slice_fusion), channel_id=1, source_target_pairs={{0,8},{1,17},{2,10},{3,19},{4,12},{5,21},{6,14},{7,23},{8,0},{9,25... | collective-permute-start | bytes 540680 | tf_op jit(solution)/shard_map/ppermute | solution.py:709
  51.1 0.5 collective-permute-start.15
  51.6 2.1 %collective-permute-done.18 = bf16[832,128]{1,0:T(8,128)(2,1)S(1)} collective-permute-done((bf16[832,128]{1,0:T(8,128)(2,1)S(1)}, bf16[832,128]{1,0:T(8,128)(2,1)S(1)}, u32[]{:S(2)}, u32[]{:S(2)}) %collective-permute-start.18) | collective-permute-done | bytes 213024 | tf_op jit(solution)/shard_map/ppermute | solution.py:709
  53.8 1.2 %collective-permute-start.19 = (bf16[832,128]{1,0:T(8,128)(2,1)S(1)}, bf16[832,128]{1,0:T(8,128)(2,1)S(1)}, u32[]{:S(2)}, u32[]{:S(2)}) collective-permute-start(bf16[832,128]{1,0:T(8,128)(2,1)S(1)} %add_convert_fusion.refs_0_), channel_id=1, source_target_pairs={{0,2},{1,5},{2,0},{3,7},{4,6},{5,1},{6,4},{7,3},{8,10},{9,13},{10,... | collective-permute-start | bytes 638984 | tf_op jit(solution)/shard_map/ppermute | solution.py:734
  55.0 2.3 %collective-permute-done.16 = bf16[704,128]{1,0:T(8,128)(2,1)S(1)} collective-permute-done((bf16[704,128]{1,0:T(8,128)(2,1)S(1)}, bf16[704,128]{1,0:T(8,128)(2,1)S(1)}, u32[]{:S(2)}, u32[]{:S(2)}) %collective-permute-start.16) | collective-permute-done | bytes 180256 | tf_op jit(solution)/shard_map/ppermute | solution.py:709
  57.4 1.9 %collective-permute-start.17 = (bf16[832,128]{1,0:T(8,128)(2,1)S(1)}, bf16[832,128]{1,0:T(8,128)(2,1)S(1)}, u32[]{:S(2)}, u32[]{:S(2)}) collective-permute-start(bf16[832,128]{1,0:T(8,128)(2,1)S(1)} %get-tuple-element.150), channel_id=1, source_target_pairs={{0,16},{1,9},{2,18},{3,11},{4,20},{5,13},{6,22},{7,15},{8,24},{9,1... | collective-permute-start | bytes 638984 | tf_op jit(solution)/shard_map/ppermute | solution.py:709
  59.6 1.1 %pad_maximum_fusion = f32[8,128,256]{2,1,0:T(8,128)} fusion(f32[4,128,256]{2,1,0:T(8,128)S(1)} %get-tuple-element.145, f32[4,128,256]{2,1,0:T(8,128)S(1)} %get-tuple-element.144), kind=kLoop, calls=%fused_computation.3 | loop fusion | flops 262144 | bytes 2097152 | tf_op jit(solution)/shard_map/concatenate | solution.py:1010
  60.6 1.1 %pad_maximum_fusion.1 = f32[8,128,256]{2,1,0:T(8,128)} fusion(f32[4,128,256]{2,1,0:T(8,128)S(1)} %get-tuple-element.143, f32[4,128,256]{2,1,0:T(8,128)S(1)} %get-tuple-element.142), kind=kLoop, calls=%fused_computation.4 | loop fusion | flops 262144 | bytes 2097152 | tf_op jit(solution)/shard_map/concatenate | solution.py:1010
  61.8 1.6 %collective-permute-start.24 = (bf16[1664,128]{1,0:T(8,128)(2,1)S(1)}, bf16[1664,128]{1,0:T(8,128)(2,1)S(1)}, u32[]{:S(2)}, u32[]{:S(2)}) collective-permute-start(bf16[1664,128]{1,0:T(8,128)(2,1)S(1)} %pad_maximum_fusion.2), channel_id=1, source_target_pairs={{0,4},{1,3},{2,6},{3,1},{4,0},{5,7},{6,2},{7,5},{8,12},{9,11},{10,... | collective-permute-start | bytes 1277960 | tf_op jit(solution)/shard_map/ppermute | solution.py:734
  63.4 1.5 %collective-permute-done.17 = bf16[832,128]{1,0:T(8,128)(2,1)S(1)} collective-permute-done((bf16[832,128]{1,0:T(8,128)(2,1)S(1)}, bf16[832,128]{1,0:T(8,128)(2,1)S(1)}, u32[]{:S(2)}, u32[]{:S(2)}) %collective-permute-start.17) | collective-permute-done | bytes 213024 | tf_op jit(solution)/shard_map/ppermute | solution.py:709
  64.9 0.2 collective-permute-start.20
  65.1 1.8 %collective-permute-start.23 = (bf16[576,128]{1,0:T(8,128)(2,1)S(1)}, bf16[576,128]{1,0:T(8,128)(2,1)S(1)}, u32[]{:S(2)}, u32[]{:S(2)}) collective-permute-start(bf16[576,128]{1,0:T(8,128)(2,1)S(1)} %add_convert_fusion.5.refs_0_), channel_id=1, source_target_pairs={{0,6},{2,4},{4,2},{6,0},{8,14},{10,12},{12,10},{14,8},{16,22},{18,... | collective-permute-start | bytes 442376 | tf_op jit(solution)/shard_map/ppermute | solution.py:673
  66.9 1.1 %collective-permute-start.22 = (bf16[576,128]{1,0:T(8,128)(2,1)S(1)}, bf16[576,128]{1,0:T(8,128)(2,1)S(1)}, u32[]{:S(2)}, u32[]{:S(2)}) collective-permute-start(bf16[576,128]{1,0:T(8,128)(2,1)S(1)} %add_convert_fusion.5.refs_0_), channel_id=1, source_target_pairs={{0,4},{2,6},{4,0},{6,2},{8,12},{10,14},{12,8},{14,10},{16,20},{18,... | collective-permute-start | bytes 442376 | tf_op jit(solution)/shard_map/ppermute | solution.py:673
  68.1 0.6 collective-permute-start.21
  68.9 0.7 slice.125
  69.5 0.9 %reshape.104 = bf16[128,256]{1,0:T(8,128)(2,1)S(1)} reshape(bf16[32,8,128]{2,1,0:T(8,128)(2,1)} %slice.125) | data formatting | bytes 131072 | tf_op jit(solution)/shard_map/reshape | solution.py:1071
  70.5 0.1 eq.11
  70.6 0.3 fusion.2
  71.0 2.0 %fusion.1 = f32[1024,512]{1,0:T(8,128)} fusion(bf16[128,256]{1,0:T(8,128)(2,1)S(1)} %reshape.104, bf16[512,128]{1,0:T(8,128)(2,1)S(1)} %slice-done, bf16[512,128]{1,0:T(8,128)(2,1)S(1)} %copy-done.5, f32[128,512]{1,0:T(8,128)S(1)} %fusion.2, s32[128]{0:T(128)S(1)} %eq.11, pred[]{:T(512)S(6)} %eq.10), kind=kOutput, calls=%fused_computation.2 | convolution fusion | flops 169672704 | bytes 2687489 | tf_op jit(solution)/shard_map/dot_general | solution.py:1093
  73.0 0.9 %fusion.33 = f32[512,128]{1,0:T(8,128)} fusion(f32[128,512]{1,0:T(8,128)S(1)} %fusion.2, bf16[128,256]{1,0:T(8,128)(2,1)S(1)} %reshape.104, s32[]{:T(128)S(6)} %select_n.81), kind=kOutput, calls=%fused_computation.56 | convolution fusion | flops 17104896 | bytes 557060 | tf_op jit(solution)/shard_map/dot_general | solution.py:1080
  73.9 0.6 slice_bitcast_fusion
  74.5 1.3 %unpack_second.1 = (f32[9,128,256]{2,1,0:T(8,128)}, f32[128,256]{1,0:T(8,128)}, f32[3,256,128]{2,1,0:T(8,128)}) custom-call(bf16[832,128]{1,0:T(8,128)(2,1)S(1)} %add_convert_fusion.refs_0_, bf16[832,128]{1,0:T(8,128)(2,1)S(1)} %collective-permute-done.19.refs_1_, bf16[1664,128]{1,0:T(8,128)(2,1)S(1)} %collective-permute-done.24.refs_2_), custom_call_target="tpu_custom_call" | custom-call | tf_op jit(solution)/shard_map/unpack_second/pallas_call | solution.py:1030
  75.8 0.5 collective-permute-done.22.refs_2_
  76.3 1.1 %unpack_first.1 = f32[9,256,128]{2,1,0:T(8,128)} custom-call(bf16[576,128]{1,0:T(8,128)(2,1)S(1)} %add_convert_fusion.5.refs_0_, bf16[576,128]{1,0:T(8,128)(2,1)S(1)} %collective-permute-done.21.refs_1_, bf16[576,128]{1,0:T(8,128)(2,1)S(1)} %collective-permute-done.22.refs_2_, bf16[576,128]{1,0:T(8,128)(2,1)S(1)} %collective-permute-done.23.refs_3_), custom_call_target="tpu_custom_call" | custom-call | tf_op jit(solution)/shard_map/unpack_first/pallas_call | solution.py:1030
  (68 shorter events, 1.3 us)
Async XLA Ops:
  0.7 4.6 %collective-permute-start.1 = (bf16[9,256,128]{2,1,0:T(8,128)(2,1)}, bf16[9,256,128]{2,1,0:T(8,128)(2,1)S(1)}, u32[]{:S(2)}, u32[]{:S(2)}) collective-permute-start(bf16[9,256,128]{2,1,0:T(8,128)(2,1)} %refs_2_.3), channel_id=1, source_target_pairs={{0,1},{1,0},{2,3},{3,2},{4,5},{5,4},{6,7},{7,6},{8,9},{9,8},{10,11... | collective-permute-start | bytes 1769480 | tf_op jit(solution)/shard_map/ppermute | solution.py:673
  1.2 4.1 %collective-permute-start.2 = (bf16[9,128,256]{2,1,0:T(8,128)(2,1)}, bf16[9,128,256]{2,1,0:T(8,128)(2,1)S(1)}, u32[]{:S(2)}, u32[]{:S(2)}) collective-permute-start(bf16[9,128,256]{2,1,0:T(8,128)(2,1)} %refs_4_.3), channel_id=1, source_target_pairs={{0,1},{1,0},{2,3},{3,2},{4,5},{5,4},{6,7},{7,6},{8,9},{9,8},{10,11... | collective-permute-start | bytes 1769480 | tf_op jit(solution)/shard_map/ppermute | solution.py:673
  2.6 2.6 %copy-start.1 = (f32[16,128]{1,0:T(8,128)}, f32[16,128]{1,0:T(8,128)S(1)}, u32[]{:S(2)}) copy-start(f32[16,128]{1,0:T(8,128)S(1)} %get-tuple-element.78.refs_6_) | copy-start | bytes 24580
  2.7 2.6 %collective-permute-start = (bf16[2,4,128,256]{3,2,1,0:T(8,128)(2,1)S(1)}, bf16[2,4,128,256]{3,2,1,0:T(8,128)(2,1)S(1)}, u32[]{:S(2)}, u32[]{:S(2)}) collective-permute-start(bf16[2,4,128,256]{3,2,1,0:T(8,128)(2,1)S(1)} %get-tuple-element.77), channel_id=1, source_target_pairs={{0,1},{1,0},{2,3},{3,2},{4,5},{5,4},{6,7},{7,6},{8,9},{9,8},{10,11... | collective-permute-start | bytes 1572872 | tf_op jit(solution)/shard_map/ppermute | solution.py:673
  3.1 2.1 %collective-permute-start.4 = (bf16[1536,128]{1,0:T(8,128)(2,1)S(1)}, bf16[1536,128]{1,0:T(8,128)(2,1)S(1)}, u32[]{:S(2)}, u32[]{:S(2)}) collective-permute-start(bf16[1536,128]{1,0:T(8,128)(2,1)S(1)} %get-tuple-element.79), channel_id=1, source_target_pairs={{0,1},{1,0},{2,3},{3,2},{4,5},{5,4},{6,7},{7,6},{8,9},{9,8},{10,11... | collective-permute-start | bytes 1179656 | tf_op jit(solution)/shard_map/ppermute | solution.py:673
  3.2 2.0 %collective-permute-start.3 = (f32[16,128]{1,0:T(8,128)S(1)}, f32[16,128]{1,0:T(8,128)S(1)}, u32[]{:S(2)}, u32[]{:S(2)}) collective-permute-start(f32[16,128]{1,0:T(8,128)S(1)} %get-tuple-element.78.refs_6_), channel_id=1, source_target_pairs={{0,1},{1,0},{2,3},{3,2},{4,5},{5,4},{6,7},{7,6},{8,9},{9,8},{10,11... | collective-permute-start | bytes 24584 | tf_op jit(solution)/shard_map/ppermute | solution.py:673
  5.3 30.5 %copy-start = (bf16[1536,128]{1,0:T(8,128)(2,1)}, bf16[1536,128]{1,0:T(8,128)(2,1)S(1)}, u32[]{:S(2)}) copy-start(bf16[1536,128]{1,0:T(8,128)(2,1)S(1)} %collective-permute-done.4.refs_12_) | copy-start | bytes 1179652
  17.8 2.5 %collective-permute-start.5 = (bf16[3328,128]{1,0:T(8,128)(2,1)S(1)}, bf16[3328,128]{1,0:T(8,128)(2,1)S(1)}, u32[]{:S(2)}, u32[]{:S(2)}) collective-permute-start(bf16[3328,128]{1,0:T(8,128)(2,1)S(1)} %get-tuple-element.94), channel_id=1, source_target_pairs={{0,1},{1,0},{2,3},{3,2},{4,5},{5,4},{6,7},{7,6},{8,9},{9,8},{10,11... | collective-permute-start | bytes 2555912 | tf_op jit(solution)/shard_map/ppermute | solution.py:673
  20.5 13.3 %collective-permute-start.6 = (bf16[832,128]{1,0:T(8,128)(2,1)S(1)}, bf16[832,128]{1,0:T(8,128)(2,1)S(1)}, u32[]{:S(2)}, u32[]{:S(2)}) collective-permute-start(bf16[832,128]{1,0:T(8,128)(2,1)S(1)} %get-tuple-element.101), channel_id=1, source_target_pairs={{0,2},{2,0},{4,6},{6,4},{8,10},{10,8},{12,14},{14,12},{16,18},{18,... | collective-permute-start | bytes 638984 | tf_op jit(solution)/shard_map/ppermute | solution.py:673
  23.4 11.6 %collective-permute-start.7 = (bf16[832,128]{1,0:T(8,128)(2,1)S(1)}, bf16[832,128]{1,0:T(8,128)(2,1)S(1)}, u32[]{:S(2)}, u32[]{:S(2)}) collective-permute-start(bf16[832,128]{1,0:T(8,128)(2,1)S(1)} %get-tuple-element.102), channel_id=1, source_target_pairs={{0,4},{2,6},{4,0},{6,2},{8,12},{10,14},{12,8},{14,10},{16,20},{18,... | collective-permute-start | bytes 638984 | tf_op jit(solution)/shard_map/ppermute | solution.py:673
  24.9 10.1 %collective-permute-start.8 = (bf16[832,128]{1,0:T(8,128)(2,1)S(1)}, bf16[832,128]{1,0:T(8,128)(2,1)S(1)}, u32[]{:S(2)}, u32[]{:S(2)}) collective-permute-start(bf16[832,128]{1,0:T(8,128)(2,1)S(1)} %get-tuple-element.103), channel_id=1, source_target_pairs={{0,6},{2,4},{4,2},{6,0},{8,14},{10,12},{12,10},{14,8},{16,22},{18,... | collective-permute-start | bytes 638984 | tf_op jit(solution)/shard_map/ppermute | solution.py:673
  35.0 0.7 copy-start.6
  35.0 0.7 copy-start.7
  35.7 2.8 %collective-permute-start.9 = (bf16[2304,128]{1,0:T(8,128)(2,1)}, bf16[2304,128]{1,0:T(8,128)(2,1)S(1)}, u32[]{:S(2)}, u32[]{:S(2)}) collective-permute-start(bf16[2304,128]{1,0:T(8,128)(2,1)} %get-tuple-element.108), channel_id=1, source_target_pairs={{0,1},{1,0},{2,3},{3,2},{4,5},{5,4},{6,7},{7,6},{8,9},{9,8},{10,11... | collective-permute-start | bytes 1769480 | tf_op jit(solution)/shard_map/ppermute | solution.py:673
  36.9 8.2 %collective-permute-start.13 = (bf16[832,128]{1,0:T(8,128)(2,1)S(1)}, bf16[832,128]{1,0:T(8,128)(2,1)S(1)}, u32[]{:S(2)}, u32[]{:S(2)}) collective-permute-start(bf16[832,128]{1,0:T(8,128)(2,1)S(1)} %fusion.5), channel_id=1, source_target_pairs={{0,8},{1,17},{2,10},{3,19},{4,12},{5,21},{6,14},{7,23},{8,0},{9,25... | collective-permute-start | bytes 638984 | tf_op jit(solution)/shard_map/ppermute | solution.py:709
  38.7 12.4 %copy-start.9 = (bf16[4,128,256]{2,1,0:T(8,128)(2,1)S(1)}, bf16[4,128,256]{2,1,0:T(8,128)(2,1)}, u32[]{:S(2)}) copy-start(bf16[4,128,256]{2,1,0:T(8,128)(2,1)} %get-tuple-element.119) | copy-start | bytes 786436
  38.7 12.4 %copy-start.8 = (bf16[4,128,256]{2,1,0:T(8,128)(2,1)S(1)}, bf16[4,128,256]{2,1,0:T(8,128)(2,1)}, u32[]{:S(2)}) copy-start(bf16[4,128,256]{2,1,0:T(8,128)(2,1)} %get-tuple-element.121) | copy-start | bytes 786436
  38.7 8.5 %collective-permute-start.12 = (bf16[608,128]{1,0:T(8,128)(2,1)S(1)}, bf16[608,128]{1,0:T(8,128)(2,1)S(1)}, u32[]{:S(2)}, u32[]{:S(2)}) collective-permute-start(bf16[608,128]{1,0:T(8,128)(2,1)S(1)} %get-tuple-element.175), channel_id=1, source_target_pairs={{0,6},{2,4},{4,2},{6,0},{8,14},{10,12},{12,10},{14,8},{16,22},{18,... | collective-permute-start | bytes 466952 | tf_op jit(solution)/shard_map/ppermute | solution.py:673
  40.5 9.4 %collective-permute-start.11 = (bf16[608,128]{1,0:T(8,128)(2,1)S(1)}, bf16[608,128]{1,0:T(8,128)(2,1)S(1)}, u32[]{:S(2)}, u32[]{:S(2)}) collective-permute-start(bf16[608,128]{1,0:T(8,128)(2,1)S(1)} %get-tuple-element.176), channel_id=1, source_target_pairs={{0,4},{2,6},{4,0},{6,2},{8,12},{10,14},{12,8},{14,10},{16,20},{18,... | collective-permute-start | bytes 466952 | tf_op jit(solution)/shard_map/ppermute | solution.py:673
  41.4 8.5 %collective-permute-start.10 = (bf16[608,128]{1,0:T(8,128)(2,1)S(1)}, bf16[608,128]{1,0:T(8,128)(2,1)S(1)}, u32[]{:S(2)}, u32[]{:S(2)}) collective-permute-start(bf16[608,128]{1,0:T(8,128)(2,1)S(1)} %get-tuple-element.177), channel_id=1, source_target_pairs={{0,2},{2,0},{4,6},{6,4},{8,10},{10,8},{12,14},{14,12},{16,18},{18,... | collective-permute-start | bytes 466952 | tf_op jit(solution)/shard_map/ppermute | solution.py:673
  45.1 14.2 %copy-start.4 = (f32[4,128,256]{2,1,0:T(8,128)S(1)}, f32[4,128,256]{2,1,0:T(8,128)}, u32[]{:S(2)}) copy-start(f32[4,128,256]{2,1,0:T(8,128)} %get-tuple-element.118) | copy-start | bytes 1572868
  45.1 8.5 %collective-permute-start.18 = (bf16[832,128]{1,0:T(8,128)(2,1)S(1)}, bf16[832,128]{1,0:T(8,128)(2,1)S(1)}, u32[]{:S(2)}, u32[]{:S(2)}) collective-permute-start(bf16[832,128]{1,0:T(8,128)(2,1)S(1)} %add_convert_fusion.1), channel_id=1, source_target_pairs={{0,16},{1,9},{2,18},{3,11},{4,20},{5,13},{6,22},{7,15},{8,24},{9,1... | collective-permute-start | bytes 638984 | tf_op jit(solution)/shard_map/ppermute | solution.py:709
  50.1 7.2 %collective-permute-start.16 = (bf16[704,128]{1,0:T(8,128)(2,1)S(1)}, bf16[704,128]{1,0:T(8,128)(2,1)S(1)}, u32[]{:S(2)}, u32[]{:S(2)}) collective-permute-start(bf16[704,128]{1,0:T(8,128)(2,1)S(1)} %constant_dynamic-update-slice_fusion), channel_id=1, source_target_pairs={{0,8},{1,17},{2,10},{3,19},{4,12},{5,21},{6,14},{7,23},{8,0},{9,25... | collective-permute-start | bytes 540680 | tf_op jit(solution)/shard_map/ppermute | solution.py:709
  51.1 8.3 %collective-permute-start.14 = (bf16[4,128,256]{2,1,0:T(8,128)(2,1)S(1)}, bf16[4,128,256]{2,1,0:T(8,128)(2,1)S(1)}, u32[]{:S(2)}, u32[]{:S(2)}) collective-permute-start(bf16[4,128,256]{2,1,0:T(8,128)(2,1)S(1)} %copy-done.9), channel_id=1, source_target_pairs={{0,1},{1,0},{2,3},{3,2},{4,5},{5,4},{6,7},{7,6},{8,9},{9,8},{10,11... | collective-permute-start | bytes 786440 | tf_op jit(solution)/shard_map/ppermute | solution.py:673
  51.1 8.4 %collective-permute-start.15 = (bf16[4,128,256]{2,1,0:T(8,128)(2,1)S(1)}, bf16[4,128,256]{2,1,0:T(8,128)(2,1)S(1)}, u32[]{:S(2)}, u32[]{:S(2)}) collective-permute-start(bf16[4,128,256]{2,1,0:T(8,128)(2,1)S(1)} %copy-done.8), channel_id=1, source_target_pairs={{0,1},{1,0},{2,3},{3,2},{4,5},{5,4},{6,7},{7,6},{8,9},{9,8},{10,11... | collective-permute-start | bytes 786440 | tf_op jit(solution)/shard_map/ppermute | solution.py:673
  53.8 5.7 %copy-start.3 = (f32[4,128,256]{2,1,0:T(8,128)S(1)}, f32[4,128,256]{2,1,0:T(8,128)}, u32[]{:S(2)}) copy-start(f32[4,128,256]{2,1,0:T(8,128)} %get-tuple-element.120) | copy-start | bytes 1572868
  53.8 8.0 %collective-permute-start.19 = (bf16[832,128]{1,0:T(8,128)(2,1)S(1)}, bf16[832,128]{1,0:T(8,128)(2,1)S(1)}, u32[]{:S(2)}, u32[]{:S(2)}) collective-permute-start(bf16[832,128]{1,0:T(8,128)(2,1)S(1)} %add_convert_fusion.refs_0_), channel_id=1, source_target_pairs={{0,2},{1,5},{2,0},{3,7},{4,6},{5,1},{6,4},{7,3},{8,10},{9,13},{10,... | collective-permute-start | bytes 638984 | tf_op jit(solution)/shard_map/ppermute | solution.py:734
  57.4 7.4 %collective-permute-start.17 = (bf16[832,128]{1,0:T(8,128)(2,1)S(1)}, bf16[832,128]{1,0:T(8,128)(2,1)S(1)}, u32[]{:S(2)}, u32[]{:S(2)}) collective-permute-start(bf16[832,128]{1,0:T(8,128)(2,1)S(1)} %get-tuple-element.150), channel_id=1, source_target_pairs={{0,16},{1,9},{2,18},{3,11},{4,20},{5,13},{6,22},{7,15},{8,24},{9,1... | collective-permute-start | bytes 638984 | tf_op jit(solution)/shard_map/ppermute | solution.py:709
  61.8 8.8 %copy-start.2 = (bf16[1024,512]{1,0:T(8,128)(2,1)S(1)}, bf16[1024,512]{1,0:T(8,128)(2,1)}, u32[]{:S(2)}) copy-start(bf16[1024,512]{1,0:T(8,128)(2,1)} %refs_14_.3) | copy-start | bytes 3145732
  61.8 12.7 %collective-permute-start.24 = (bf16[1664,128]{1,0:T(8,128)(2,1)S(1)}, bf16[1664,128]{1,0:T(8,128)(2,1)S(1)}, u32[]{:S(2)}, u32[]{:S(2)}) collective-permute-start(bf16[1664,128]{1,0:T(8,128)(2,1)S(1)} %pad_maximum_fusion.2), channel_id=1, source_target_pairs={{0,4},{1,3},{2,6},{3,1},{4,0},{5,7},{6,2},{7,5},{8,12},{9,11},{10,... | collective-permute-start | bytes 1277960 | tf_op jit(solution)/shard_map/ppermute | solution.py:734
  64.9 3.8 %collective-permute-start.20 = (bf16[512,128]{1,0:T(8,128)(2,1)S(1)}, bf16[512,128]{1,0:T(8,128)(2,1)S(1)}, u32[]{:S(2)}, u32[]{:S(2)}) collective-permute-start(bf16[512,128]{1,0:T(8,128)(2,1)S(1)} %get-tuple-element.146), channel_id=1, source_target_pairs={{0,1},{1,0},{2,3},{3,2},{4,5},{5,4},{6,7},{7,6},{8,9},{9,8},{10,11... | collective-permute-start | bytes 393224 | tf_op jit(solution)/shard_map/ppermute | solution.py:673
  65.1 10.7 %collective-permute-start.23 = (bf16[576,128]{1,0:T(8,128)(2,1)S(1)}, bf16[576,128]{1,0:T(8,128)(2,1)S(1)}, u32[]{:S(2)}, u32[]{:S(2)}) collective-permute-start(bf16[576,128]{1,0:T(8,128)(2,1)S(1)} %add_convert_fusion.5.refs_0_), channel_id=1, source_target_pairs={{0,6},{2,4},{4,2},{6,0},{8,14},{10,12},{12,10},{14,8},{16,22},{18,... | collective-permute-start | bytes 442376 | tf_op jit(solution)/shard_map/ppermute | solution.py:673
  66.9 9.3 %collective-permute-start.22 = (bf16[576,128]{1,0:T(8,128)(2,1)S(1)}, bf16[576,128]{1,0:T(8,128)(2,1)S(1)}, u32[]{:S(2)}, u32[]{:S(2)}) collective-permute-start(bf16[576,128]{1,0:T(8,128)(2,1)S(1)} %add_convert_fusion.5.refs_0_), channel_id=1, source_target_pairs={{0,4},{2,6},{4,0},{6,2},{8,12},{10,14},{12,8},{14,10},{16,20},{18,... | collective-permute-start | bytes 442376 | tf_op jit(solution)/shard_map/ppermute | solution.py:673
  68.1 8.2 %collective-permute-start.21 = (bf16[576,128]{1,0:T(8,128)(2,1)S(1)}, bf16[576,128]{1,0:T(8,128)(2,1)S(1)}, u32[]{:S(2)}, u32[]{:S(2)}) collective-permute-start(bf16[576,128]{1,0:T(8,128)(2,1)S(1)} %add_convert_fusion.5.refs_0_), channel_id=1, source_target_pairs={{0,2},{2,0},{4,6},{6,4},{8,10},{10,8},{12,14},{14,12},{16,18},{18,... | collective-permute-start | bytes 442376 | tf_op jit(solution)/shard_map/ppermute | solution.py:673
  68.7 2.3 %slice-start = ((bf16[1536,128]{1,0:T(8,128)(2,1)}), bf16[512,128]{1,0:T(8,128)(2,1)S(1)}, s32[]{:S(2)}) async-start(bf16[1536,128]{1,0:T(8,128)(2,1)} %copy-done), calls=%async_computation | async-start | bytes 262144 | tf_op jit(solution)/shard_map/slice | solution.py:1084
  68.7 2.3 %copy-start.5 = (bf16[512,128]{1,0:T(8,128)(2,1)S(1)}, bf16[512,128]{1,0:T(8,128)(2,1)}, u32[]{:S(2)}) copy-start(bf16[512,128]{1,0:T(8,128)(2,1)} %refs_11_.3) | copy-start | bytes 393220

commit v7 on v6

--- a/solution.py
+++ b/solution.py
@@ -15,7 +15,6 @@
 MIB = 1024 * 1024
 ANY = pl.BlockSpec(memory_space=pl.ANY)
 VMEM = pl.BlockSpec(memory_space=pltpu.VMEM)
-SMEM = pl.BlockSpec(memory_space=pltpu.SMEM)
 f32 = jnp.float32
 bf16 = jnp.bfloat16
 
@@ -239,7 +238,7 @@
     small_in = take(pieces - 1)
     if pieces == 2:
         x_in, g_in = [x_in[0], x_in[1].at[0]], [g_in[0], x_in[1].at[1]]
-    steps_ref, table_ref = take(2)
+    steps_in, table_ref = take(2)
     if pieces == 2:
         own, send = take(2)
     else:
@@ -250,7 +249,7 @@
     w1, w2, po, vec, xin = take(5)
     gpad, sum_one, a1t, resid, gres, mix = take(6)
     stat, sums = take(2)
-    gin, pi, tw, rows, apad, bpad = take(6)
+    gin, pi, tw, rows, apad, bpad, steps_ref = take(7)
     sems = next(it)
 
     cps = Copies(sems)
@@ -262,9 +261,12 @@
     scale = chans ** (-0.5)
     images = range(count)
 
+    steps_cp = cps.start(steps_in, steps_ref)
     x_cp = load_images(cps, x_in, xin, places, count)
     vec_cp = load_split(cps, vec_in, vec, 1, places)
     w1_cp = load_split(cps, w1_in, w1, 2, places)
+    w2_cp = load_split(cps, w2_in, w2, 1, places)
+    steps_cp.wait()
     row_cp = []
     for b in images:
         step = steps_ref[places[0] * count + b]
@@ -272,7 +274,6 @@
             cps.start(table_ref.at[pl.ds(pl.multiple_of(step // 16 * 16, 16), 16), :], rows.at[b])
         )
     tw_cp = load_split(cps, tw_in, tw, 1, places[:1])
-    w2_cp = load_split(cps, w2_in, w2, 1, places)
     pi_cp = load_split(cps, pi_in, pi, 2, places[:1])
     po_cp = load_split(cps, po_in, po, 0, places[:1])
     if pieces == 2:
@@ -894,7 +895,7 @@
         functools.partial(front_kernel, pieces, count),
         out_shape=grads_a
         + [pltpu.HBM(*v) for v in kept],
-        in_specs=[ANY, VMEM][:pieces] * 4 + [ANY] * 4 + [VMEM] * (pieces - 1) + [SMEM, ANY],
+        in_specs=[ANY, VMEM][:pieces] * 4 + [ANY] * 4 + [VMEM] * (pieces - 1) + [ANY] * 2,
         out_specs=[VMEM] * n_grad + [ANY] * len(kept),
         scratch_shapes=scratch_a
         + [pltpu.VMEM(*v) for v in kept]
@@ -905,7 +906,8 @@
             pltpu.VMEM((count, 16, embed), bf16),
             pltpu.VMEM(pads, bf16),
             pltpu.VMEM(pads, bf16),
-            pltpu.SemaphoreType.DMA((8 * pieces + 3 * count + 22,)),
+            pltpu.SMEM(my_steps.shape, jnp.int32),
+            pltpu.SemaphoreType.DMA((8 * pieces + 3 * count + 23,)),
         ],
         compiler_params=params(28),
         cost_estimate=cost(54, 12 << 20),

time: 78.1 us -> 77.5 us (level)
  no operation moved by 1% of the time
where the time goes in v7:
time: 77.5 us; the launch traced here: 76.9 us
  Pallas kernels  24.5 us (32%)
  starting transfers between devices  23.8 us (31%)
  waiting for transfers between devices  16.6 us (21%)
  other arithmetic  4.49 us (6%)
  matrix products  3.24 us (4%)
  local copies, waits for them, and re-layouts  3.13 us (4%)
  between operations  1.15 us (1%)
    ppermute x19, starting transfers between devices, swap(): return lax.ppermute(value, axis, [(i, i ^ bit) for i in range(size)])  14.3 us
    pallas_call x1, Pallas kernels, per_device(): pl.pallas_call(functools.partial(front_kernel, pieces, count), out_shape=...  11.9 us
    pallas_call x1, Pallas kernels, per_device(): pl.pallas_call(functools.partial(back_kernel, pieces, count), out_shape=o...  8.83 us
    ppermute x4, waiting for transfers between devices, send_far(): return lax.ppermute(mine, ('batch', 'tensor'), pairs)  8.59 us
    ppermute x19, waiting for transfers between devices, swap(): return lax.ppermute(value, axis, [(i, i ^ bit) for i in range(size)])  8.01 us
    ppermute x4, starting transfers between devices, send_far(): return lax.ppermute(mine, ('batch', 'tensor'), pairs)  6.66 us
    ppermute x2, starting transfers between devices, cross(): return lax.ppermute(value, ('batch', 'tensor'), pairs)  2.81 us
    pallas_call x2, Pallas kernels, unpacked(): pl.pallas_call(kernel, out_shape=outs, in_specs=[VMEM] * len(got), out_sp...  2.41 us
  transfers between devices with their start and end apart: 25, of which 9 were waited for; matrix products, arithmetic and copies ran while one was open for 13% of the time, Pallas kernels for 15%

profile of v7, /device:TPU:0, one launch (start us, length us, event | category | flops | bytes accessed | tf_op | source)
XLA Modules:
  0.0 76.9 jit_solution(7492723189403183914)
XLA Ops:
  0.7 0.5 collective-permute-start.1
  1.3 1.4 %pack.1 = (f32[16,128]{1,0:T(8,128)S(1)}, bf16[2,4,128,256]{3,2,1,0:T(8,128)(2,1)S(1)}, bf16[1536,128]{1,0:T(8,128)(2,1)S(1)}) custom-call(f32[128]{0:T(128)} %refs_0_.2, f32[128]{0:T(128)} %refs_1_.1, f32[128]{0:T(128)} %refs_2_.2, f32[128]{0:T(128)} %refs_3_.1, f32[128]{0:T(128)} %refs_4_.2, f32[128]{0:T(128)} %refs_5_.1, f32[128]{0:T(128)} %refs_6_.1, ...), custom_call_target="tpu_custom_call" | custom-call | tf_op jit(solution)/shard_map/pack/pallas_call | solution.py:814
  2.7 0.5 collective-permute-start
  3.2 0.4 collective-permute-start.3
  3.7 1.6 %collective-permute-done.3.refs_7_ = f32[16,128]{1,0:T(8,128)S(1)} collective-permute-done((f32[16,128]{1,0:T(8,128)S(1)}, f32[16,128]{1,0:T(8,128)S(1)}, u32[]{:S(2)}, u32[]{:S(2)}) %collective-permute-start.3) | collective-permute-done | bytes 8224 | tf_op jit(solution)/shard_map/ppermute | solution.py:674
  5.3 11.9 %front.1 = (bf16[3328,128]{1,0:T(8,128)(2,1)S(1)}, bf16[3328,128]{1,0:T(8,128)(2,1)S(1)}, bf16[9,256,256]{2,1,0:T(8,128)(2,1)}, bf16[9,256,256]{2,1,0:T(8,128)(2...) custom-call(bf16[8,128,256]{2,1,0:T(8,128)(2,1)} %refs_0_.3, ...), custom_call_target="tpu_custom_call" | custom-call | flops 7247757312 | bytes 12582912 | tf_op jit(solution)/shard_map/front/pallas_call | solution.py:894
  17.2 0.4 collective-permute-start.5
  17.6 2.0 %collective-permute-done.5 = bf16[3328,128]{1,0:T(8,128)(2,1)S(1)} collective-permute-done((bf16[3328,128]{1,0:T(8,128)(2,1)S(1)}, bf16[3328,128]{1,0:T(8,128)(2,1)S(1)}, u32[]{:S(2)}, u32[]{:S(2)}) %collective-permute-start.5) | collective-permute-done | bytes 852000 | tf_op jit(solution)/shard_map/ppermute | solution.py:674
  19.6 0.2 fusion.29
  19.8 2.9 %collective-permute-start.6 = (bf16[832,128]{1,0:T(8,128)(2,1)S(1)}, bf16[832,128]{1,0:T(8,128)(2,1)S(1)}, u32[]{:S(2)}, u32[]{:S(2)}) collective-permute-start(bf16[832,128]{1,0:T(8,128)(2,1)S(1)} %get-tuple-element.101), channel_id=1, source_target_pairs={{0,2},{2,0},{4,6},{6,4},{8,10},{10,8},{12,14},{14,12},{16,18},{18,... | collective-permute-start | bytes 638984 | tf_op jit(solution)/shard_map/ppermute | solution.py:674
  22.7 1.5 %collective-permute-start.7 = (bf16[832,128]{1,0:T(8,128)(2,1)S(1)}, bf16[832,128]{1,0:T(8,128)(2,1)S(1)}, u32[]{:S(2)}, u32[]{:S(2)}) collective-permute-start(bf16[832,128]{1,0:T(8,128)(2,1)S(1)} %get-tuple-element.102), channel_id=1, source_target_pairs={{0,4},{2,6},{4,0},{6,2},{8,12},{10,14},{12,8},{14,10},{16,20},{18,... | collective-permute-start | bytes 638984 | tf_op jit(solution)/shard_map/ppermute | solution.py:674
  24.3 8.8 %back.1 = (bf16[2304,128]{1,0:T(8,128)(2,1)S(1)}, bf16[2304,128]{1,0:T(8,128)(2,1)}, f32[4,128,256]{2,1,0:T(8,128)}, bf16[4,128,256]{2,1,0:T(8,128)(2,1)}, f32[4...) custom-call(bf16[9,256,256]{2,1,0:T(8,128)(2,1)} %get-tuple-element.80.refs_0_, ...), custom_call_target="tpu_custom_call" | custom-call | flops 4429185024 | bytes 12582912 | tf_op jit(solution)/shard_map/back/pallas_call | solution.py:965
  33.1 1.2 %collective-permute-done.7 = bf16[832,128]{1,0:T(8,128)(2,1)S(1)} collective-permute-done((bf16[832,128]{1,0:T(8,128)(2,1)S(1)}, bf16[832,128]{1,0:T(8,128)(2,1)S(1)}, u32[]{:S(2)}, u32[]{:S(2)}) %collective-permute-start.7) | collective-permute-done | bytes 213024 | tf_op jit(solution)/shard_map/ppermute | solution.py:674
  34.3 0.7 copy-done.6
  35.1 1.2 %fusion.5 = bf16[832,128]{1,0:T(8,128)(2,1)S(1)} fusion(bf16[832,128]{1,0:T(8,128)(2,1)} %copy-done.7, bf16[832,128]{1,0:T(8,128)(2,1)} %copy-done.6, bf16[832,128]{1,0:T(8,128)(2,1)S(1)} %collective-permute-done.6, bf16[4,832,128]{2,1,0:T(8,128)(2,1)S(1)} %bitcast.71, s32[]{:T(128)S(6)} %select_n.72, bf16[4,832,128]{2,1,0:T(8,128)(2,1)S(1)} %bitcast.64), kind=kLoop, calls=%fused_computation.15 | loop fusion | flops 1064960 | bytes 1277956 | tf_op jit(solution)/shard_map/convert_element_type | solution.py:694
  36.3 1.6 %collective-permute-start.13 = (bf16[832,128]{1,0:T(8,128)(2,1)S(1)}, bf16[832,128]{1,0:T(8,128)(2,1)S(1)}, u32[]{:S(2)}, u32[]{:S(2)}) collective-permute-start(bf16[832,128]{1,0:T(8,128)(2,1)S(1)} %fusion.5), channel_id=1, source_target_pairs={{0,8},{1,17},{2,10},{3,19},{4,12},{5,21},{6,14},{7,23},{8,0},{9,25... | collective-permute-start | bytes 638984 | tf_op jit(solution)/shard_map/ppermute | solution.py:710
  37.9 0.1 fusion.32
  38.1 1.8 %collective-permute-start.12 = (bf16[608,128]{1,0:T(8,128)(2,1)S(1)}, bf16[608,128]{1,0:T(8,128)(2,1)S(1)}, u32[]{:S(2)}, u32[]{:S(2)}) collective-permute-start(bf16[608,128]{1,0:T(8,128)(2,1)S(1)} %get-tuple-element.175), channel_id=1, source_target_pairs={{0,6},{2,4},{4,2},{6,0},{8,14},{10,12},{12,10},{14,8},{16,22},{18,... | collective-permute-start | bytes 466952 | tf_op jit(solution)/shard_map/ppermute | solution.py:674
  39.9 0.9 %collective-permute-start.11 = (bf16[608,128]{1,0:T(8,128)(2,1)S(1)}, bf16[608,128]{1,0:T(8,128)(2,1)S(1)}, u32[]{:S(2)}, u32[]{:S(2)}) collective-permute-start(bf16[608,128]{1,0:T(8,128)(2,1)S(1)} %get-tuple-element.176), channel_id=1, source_target_pairs={{0,4},{2,6},{4,0},{6,2},{8,12},{10,14},{12,8},{14,10},{16,20},{18,... | collective-permute-start | bytes 466952 | tf_op jit(solution)/shard_map/ppermute | solution.py:674
  40.8 0.9 %collective-permute-start.10 = (bf16[608,128]{1,0:T(8,128)(2,1)S(1)}, bf16[608,128]{1,0:T(8,128)(2,1)S(1)}, u32[]{:S(2)}, u32[]{:S(2)}) collective-permute-start(bf16[608,128]{1,0:T(8,128)(2,1)S(1)} %get-tuple-element.177), channel_id=1, source_target_pairs={{0,2},{2,0},{4,6},{6,4},{8,10},{10,8},{12,14},{14,12},{16,18},{18,... | collective-permute-start | bytes 466952 | tf_op jit(solution)/shard_map/ppermute | solution.py:674
  41.6 2.8 %collective-permute-done.13 = bf16[832,128]{1,0:T(8,128)(2,1)S(1)} collective-permute-done((bf16[832,128]{1,0:T(8,128)(2,1)S(1)}, bf16[832,128]{1,0:T(8,128)(2,1)S(1)}, u32[]{:S(2)}, u32[]{:S(2)}) %collective-permute-start.13) | collective-permute-done | bytes 213024 | tf_op jit(solution)/shard_map/ppermute | solution.py:710
  44.5 2.1 %collective-permute-start.18 = (bf16[832,128]{1,0:T(8,128)(2,1)S(1)}, bf16[832,128]{1,0:T(8,128)(2,1)S(1)}, u32[]{:S(2)}, u32[]{:S(2)}) collective-permute-start(bf16[832,128]{1,0:T(8,128)(2,1)S(1)} %add_convert_fusion.1), channel_id=1, source_target_pairs={{0,16},{1,9},{2,18},{3,11},{4,20},{5,13},{6,22},{7,15},{8,24},{9,1... | collective-permute-start | bytes 638984 | tf_op jit(solution)/shard_map/ppermute | solution.py:710
  46.6 2.7 %collective-permute-done.11 = bf16[608,128]{1,0:T(8,128)(2,1)S(1)} collective-permute-done((bf16[608,128]{1,0:T(8,128)(2,1)S(1)}, bf16[608,128]{1,0:T(8,128)(2,1)S(1)}, u32[]{:S(2)}, u32[]{:S(2)}) %collective-permute-start.11) | collective-permute-done | bytes 155680 | tf_op jit(solution)/shard_map/ppermute | solution.py:674
  49.3 0.1 constant_dynamic-update-slice_fusion.4
  49.4 1.0 %collective-permute-start.16 = (bf16[704,128]{1,0:T(8,128)(2,1)S(1)}, bf16[704,128]{1,0:T(8,128)(2,1)S(1)}, u32[]{:S(2)}, u32[]{:S(2)}) collective-permute-start(bf16[704,128]{1,0:T(8,128)(2,1)S(1)} %constant_dynamic-update-slice_fusion), channel_id=1, source_target_pairs={{0,8},{1,17},{2,10},{3,19},{4,12},{5,21},{6,14},{7,23},{8,0},{9,25... | collective-permute-start | bytes 540680 | tf_op jit(solution)/shard_map/ppermute | solution.py:710
  50.4 0.5 collective-permute-start.15
  50.9 2.1 %collective-permute-done.18 = bf16[832,128]{1,0:T(8,128)(2,1)S(1)} collective-permute-done((bf16[832,128]{1,0:T(8,128)(2,1)S(1)}, bf16[832,128]{1,0:T(8,128)(2,1)S(1)}, u32[]{:S(2)}, u32[]{:S(2)}) %collective-permute-start.18) | collective-permute-done | bytes 213024 | tf_op jit(solution)/shard_map/ppermute | solution.py:710
  53.1 1.2 %collective-permute-start.19 = (bf16[832,128]{1,0:T(8,128)(2,1)S(1)}, bf16[832,128]{1,0:T(8,128)(2,1)S(1)}, u32[]{:S(2)}, u32[]{:S(2)}) collective-permute-start(bf16[832,128]{1,0:T(8,128)(2,1)S(1)} %add_convert_fusion.refs_0_), channel_id=1, source_target_pairs={{0,2},{1,5},{2,0},{3,7},{4,6},{5,1},{6,4},{7,3},{8,10},{9,13},{10,... | collective-permute-start | bytes 638984 | tf_op jit(solution)/shard_map/ppermute | solution.py:735
  54.3 2.3 %collective-permute-done.16 = bf16[704,128]{1,0:T(8,128)(2,1)S(1)} collective-permute-done((bf16[704,128]{1,0:T(8,128)(2,1)S(1)}, bf16[704,128]{1,0:T(8,128)(2,1)S(1)}, u32[]{:S(2)}, u32[]{:S(2)}) %collective-permute-start.16) | collective-permute-done | bytes 180256 | tf_op jit(solution)/shard_map/ppermute | solution.py:710
  56.7 1.9 %collective-permute-start.17 = (bf16[832,128]{1,0:T(8,128)(2,1)S(1)}, bf16[832,128]{1,0:T(8,128)(2,1)S(1)}, u32[]{:S(2)}, u32[]{:S(2)}) collective-permute-start(bf16[832,128]{1,0:T(8,128)(2,1)S(1)} %get-tuple-element.150), channel_id=1, source_target_pairs={{0,16},{1,9},{2,18},{3,11},{4,20},{5,13},{6,22},{7,15},{8,24},{9,1... | collective-permute-start | bytes 638984 | tf_op jit(solution)/shard_map/ppermute | solution.py:710
  58.9 1.1 %pad_maximum_fusion = f32[8,128,256]{2,1,0:T(8,128)} fusion(f32[4,128,256]{2,1,0:T(8,128)S(1)} %get-tuple-element.145, f32[4,128,256]{2,1,0:T(8,128)S(1)} %get-tuple-element.144), kind=kLoop, calls=%fused_computation.3 | loop fusion | flops 262144 | bytes 2097152 | tf_op jit(solution)/shard_map/concatenate | solution.py:1012
  60.0 1.1 %pad_maximum_fusion.1 = f32[8,128,256]{2,1,0:T(8,128)} fusion(f32[4,128,256]{2,1,0:T(8,128)S(1)} %get-tuple-element.143, f32[4,128,256]{2,1,0:T(8,128)S(1)} %get-tuple-element.142), kind=kLoop, calls=%fused_computation.4 | loop fusion | flops 262144 | bytes 2097152 | tf_op jit(solution)/shard_map/concatenate | solution.py:1012
  61.1 1.6 %collective-permute-start.24 = (bf16[1664,128]{1,0:T(8,128)(2,1)S(1)}, bf16[1664,128]{1,0:T(8,128)(2,1)S(1)}, u32[]{:S(2)}, u32[]{:S(2)}) collective-permute-start(bf16[1664,128]{1,0:T(8,128)(2,1)S(1)} %pad_maximum_fusion.2), channel_id=1, source_target_pairs={{0,4},{1,3},{2,6},{3,1},{4,0},{5,7},{6,2},{7,5},{8,12},{9,11},{10,... | collective-permute-start | bytes 1277960 | tf_op jit(solution)/shard_map/ppermute | solution.py:735
  62.7 1.4 %collective-permute-done.17 = bf16[832,128]{1,0:T(8,128)(2,1)S(1)} collective-permute-done((bf16[832,128]{1,0:T(8,128)(2,1)S(1)}, bf16[832,128]{1,0:T(8,128)(2,1)S(1)}, u32[]{:S(2)}, u32[]{:S(2)}) %collective-permute-start.17) | collective-permute-done | bytes 213024 | tf_op jit(solution)/shard_map/ppermute | solution.py:710
  64.2 0.2 collective-permute-start.20
  64.4 1.9 %collective-permute-start.23 = (bf16[576,128]{1,0:T(8,128)(2,1)S(1)}, bf16[576,128]{1,0:T(8,128)(2,1)S(1)}, u32[]{:S(2)}, u32[]{:S(2)}) collective-permute-start(bf16[576,128]{1,0:T(8,128)(2,1)S(1)} %add_convert_fusion.5.refs_0_), channel_id=1, source_target_pairs={{0,6},{2,4},{4,2},{6,0},{8,14},{10,12},{12,10},{14,8},{16,22},{18,... | collective-permute-start | bytes 442376 | tf_op jit(solution)/shard_map/ppermute | solution.py:674
  66.3 1.2 %collective-permute-start.22 = (bf16[576,128]{1,0:T(8,128)(2,1)S(1)}, bf16[576,128]{1,0:T(8,128)(2,1)S(1)}, u32[]{:S(2)}, u32[]{:S(2)}) collective-permute-start(bf16[576,128]{1,0:T(8,128)(2,1)S(1)} %add_convert_fusion.5.refs_0_), channel_id=1, source_target_pairs={{0,4},{2,6},{4,0},{6,2},{8,12},{10,14},{12,8},{14,10},{16,20},{18,... | collective-permute-start | bytes 442376 | tf_op jit(solution)/shard_map/ppermute | solution.py:674
  67.5 0.5 collective-permute-start.21
  68.2 0.7 slice.125
  68.9 0.9 %reshape.104 = bf16[128,256]{1,0:T(8,128)(2,1)S(1)} reshape(bf16[32,8,128]{2,1,0:T(8,128)(2,1)} %slice.125) | data formatting | bytes 131072 | tf_op jit(solution)/shard_map/reshape | solution.py:1073
  69.8 0.1 eq.11
  69.9 0.3 fusion.2
  70.4 2.0 %fusion.1 = f32[1024,512]{1,0:T(8,128)} fusion(bf16[128,256]{1,0:T(8,128)(2,1)S(1)} %reshape.104, bf16[512,128]{1,0:T(8,128)(2,1)S(1)} %slice-done, bf16[512,128]{1,0:T(8,128)(2,1)S(1)} %copy-done.5, f32[128,512]{1,0:T(8,128)S(1)} %fusion.2, s32[128]{0:T(128)S(1)} %eq.11, pred[]{:T(512)S(6)} %eq.10), kind=kOutput, calls=%fused_computation.2 | convolution fusion | flops 169672704 | bytes 2687489 | tf_op jit(solution)/shard_map/dot_general | solution.py:1095
  72.3 0.9 %fusion.33 = f32[512,128]{1,0:T(8,128)} fusion(f32[128,512]{1,0:T(8,128)S(1)} %fusion.2, bf16[128,256]{1,0:T(8,128)(2,1)S(1)} %reshape.104, s32[]{:T(128)S(6)} %select_n.81), kind=kOutput, calls=%fused_computation.56 | convolution fusion | flops 17104896 | bytes 557060 | tf_op jit(solution)/shard_map/dot_general | solution.py:1082
  73.3 0.6 slice_bitcast_fusion
  73.8 1.3 %unpack_second.1 = (f32[9,128,256]{2,1,0:T(8,128)}, f32[128,256]{1,0:T(8,128)}, f32[3,256,128]{2,1,0:T(8,128)}) custom-call(bf16[832,128]{1,0:T(8,128)(2,1)S(1)} %add_convert_fusion.refs_0_, bf16[832,128]{1,0:T(8,128)(2,1)S(1)} %collective-permute-done.19.refs_1_, bf16[1664,128]{1,0:T(8,128)(2,1)S(1)} %collective-permute-done.24.refs_2_), custom_call_target="tpu_custom_call" | custom-call | tf_op jit(solution)/shard_map/unpack_second/pallas_call | solution.py:1032
  75.1 0.5 collective-permute-done.22.refs_2_
  75.6 1.1 %unpack_first.1 = f32[9,256,128]{2,1,0:T(8,128)} custom-call(bf16[576,128]{1,0:T(8,128)(2,1)S(1)} %add_convert_fusion.5.refs_0_, bf16[576,128]{1,0:T(8,128)(2,1)S(1)} %collective-permute-done.21.refs_1_, bf16[576,128]{1,0:T(8,128)(2,1)S(1)} %collective-permute-done.22.refs_2_, bf16[576,128]{1,0:T(8,128)(2,1)S(1)} %collective-permute-done.23.refs_3_), custom_call_target="tpu_custom_call" | custom-call | tf_op jit(solution)/shard_map/unpack_first/pallas_call | solution.py:1032
  (68 shorter events, 1.3 us)
Async XLA Ops:
  0.7 4.6 %collective-permute-start.1 = (bf16[9,256,128]{2,1,0:T(8,128)(2,1)}, bf16[9,256,128]{2,1,0:T(8,128)(2,1)S(1)}, u32[]{:S(2)}, u32[]{:S(2)}) collective-permute-start(bf16[9,256,128]{2,1,0:T(8,128)(2,1)} %refs_2_.3), channel_id=1, source_target_pairs={{0,1},{1,0},{2,3},{3,2},{4,5},{5,4},{6,7},{7,6},{8,9},{9,8},{10,11... | collective-permute-start | bytes 1769480 | tf_op jit(solution)/shard_map/ppermute | solution.py:674
  1.2 4.1 %collective-permute-start.2 = (bf16[9,128,256]{2,1,0:T(8,128)(2,1)}, bf16[9,128,256]{2,1,0:T(8,128)(2,1)S(1)}, u32[]{:S(2)}, u32[]{:S(2)}) collective-permute-start(bf16[9,128,256]{2,1,0:T(8,128)(2,1)} %refs_4_.3), channel_id=1, source_target_pairs={{0,1},{1,0},{2,3},{3,2},{4,5},{5,4},{6,7},{7,6},{8,9},{9,8},{10,11... | collective-permute-start | bytes 1769480 | tf_op jit(solution)/shard_map/ppermute | solution.py:674
  2.6 2.6 %copy-start.1 = (f32[16,128]{1,0:T(8,128)}, f32[16,128]{1,0:T(8,128)S(1)}, u32[]{:S(2)}) copy-start(f32[16,128]{1,0:T(8,128)S(1)} %get-tuple-element.78.refs_6_) | copy-start | bytes 24580
  2.7 2.6 %collective-permute-start = (bf16[2,4,128,256]{3,2,1,0:T(8,128)(2,1)S(1)}, bf16[2,4,128,256]{3,2,1,0:T(8,128)(2,1)S(1)}, u32[]{:S(2)}, u32[]{:S(2)}) collective-permute-start(bf16[2,4,128,256]{3,2,1,0:T(8,128)(2,1)S(1)} %get-tuple-element.77), channel_id=1, source_target_pairs={{0,1},{1,0},{2,3},{3,2},{4,5},{5,4},{6,7},{7,6},{8,9},{9,8},{10,11... | collective-permute-start | bytes 1572872 | tf_op jit(solution)/shard_map/ppermute | solution.py:674
  3.1 2.1 %collective-permute-start.4 = (bf16[1536,128]{1,0:T(8,128)(2,1)S(1)}, bf16[1536,128]{1,0:T(8,128)(2,1)S(1)}, u32[]{:S(2)}, u32[]{:S(2)}) collective-permute-start(bf16[1536,128]{1,0:T(8,128)(2,1)S(1)} %get-tuple-element.79), channel_id=1, source_target_pairs={{0,1},{1,0},{2,3},{3,2},{4,5},{5,4},{6,7},{7,6},{8,9},{9,8},{10,11... | collective-permute-start | bytes 1179656 | tf_op jit(solution)/shard_map/ppermute | solution.py:674
  3.2 2.0 %collective-permute-start.3 = (f32[16,128]{1,0:T(8,128)S(1)}, f32[16,128]{1,0:T(8,128)S(1)}, u32[]{:S(2)}, u32[]{:S(2)}) collective-permute-start(f32[16,128]{1,0:T(8,128)S(1)} %get-tuple-element.78.refs_6_), channel_id=1, source_target_pairs={{0,1},{1,0},{2,3},{3,2},{4,5},{5,4},{6,7},{7,6},{8,9},{9,8},{10,11... | collective-permute-start | bytes 24584 | tf_op jit(solution)/shard_map/ppermute | solution.py:674
  5.3 29.8 %copy-start = (bf16[1536,128]{1,0:T(8,128)(2,1)}, bf16[1536,128]{1,0:T(8,128)(2,1)S(1)}, u32[]{:S(2)}) copy-start(bf16[1536,128]{1,0:T(8,128)(2,1)S(1)} %collective-permute-done.4.refs_12_) | copy-start | bytes 1179652
  17.2 2.4 %collective-permute-start.5 = (bf16[3328,128]{1,0:T(8,128)(2,1)S(1)}, bf16[3328,128]{1,0:T(8,128)(2,1)S(1)}, u32[]{:S(2)}, u32[]{:S(2)}) collective-permute-start(bf16[3328,128]{1,0:T(8,128)(2,1)S(1)} %get-tuple-element.94), channel_id=1, source_target_pairs={{0,1},{1,0},{2,3},{3,2},{4,5},{5,4},{6,7},{7,6},{8,9},{9,8},{10,11... | collective-permute-start | bytes 2555912 | tf_op jit(solution)/shard_map/ppermute | solution.py:674
  19.8 13.3 %collective-permute-start.6 = (bf16[832,128]{1,0:T(8,128)(2,1)S(1)}, bf16[832,128]{1,0:T(8,128)(2,1)S(1)}, u32[]{:S(2)}, u32[]{:S(2)}) collective-permute-start(bf16[832,128]{1,0:T(8,128)(2,1)S(1)} %get-tuple-element.101), channel_id=1, source_target_pairs={{0,2},{2,0},{4,6},{6,4},{8,10},{10,8},{12,14},{14,12},{16,18},{18,... | collective-permute-start | bytes 638984 | tf_op jit(solution)/shard_map/ppermute | solution.py:674
  22.7 11.6 %collective-permute-start.7 = (bf16[832,128]{1,0:T(8,128)(2,1)S(1)}, bf16[832,128]{1,0:T(8,128)(2,1)S(1)}, u32[]{:S(2)}, u32[]{:S(2)}) collective-permute-start(bf16[832,128]{1,0:T(8,128)(2,1)S(1)} %get-tuple-element.102), channel_id=1, source_target_pairs={{0,4},{2,6},{4,0},{6,2},{8,12},{10,14},{12,8},{14,10},{16,20},{18,... | collective-permute-start | bytes 638984 | tf_op jit(solution)/shard_map/ppermute | solution.py:674
  24.2 10.1 %collective-permute-start.8 = (bf16[832,128]{1,0:T(8,128)(2,1)S(1)}, bf16[832,128]{1,0:T(8,128)(2,1)S(1)}, u32[]{:S(2)}, u32[]{:S(2)}) collective-permute-start(bf16[832,128]{1,0:T(8,128)(2,1)S(1)} %get-tuple-element.103), channel_id=1, source_target_pairs={{0,6},{2,4},{4,2},{6,0},{8,14},{10,12},{12,10},{14,8},{16,22},{18,... | collective-permute-start | bytes 638984 | tf_op jit(solution)/shard_map/ppermute | solution.py:674
  34.3 0.7 copy-start.6
  34.3 0.7 copy-start.7
  35.1 2.8 %collective-permute-start.9 = (bf16[2304,128]{1,0:T(8,128)(2,1)}, bf16[2304,128]{1,0:T(8,128)(2,1)S(1)}, u32[]{:S(2)}, u32[]{:S(2)}) collective-permute-start(bf16[2304,128]{1,0:T(8,128)(2,1)} %get-tuple-element.108), channel_id=1, source_target_pairs={{0,1},{1,0},{2,3},{3,2},{4,5},{5,4},{6,7},{7,6},{8,9},{9,8},{10,11... | collective-permute-start | bytes 1769480 | tf_op jit(solution)/shard_map/ppermute | solution.py:674
  36.3 8.2 %collective-permute-start.13 = (bf16[832,128]{1,0:T(8,128)(2,1)S(1)}, bf16[832,128]{1,0:T(8,128)(2,1)S(1)}, u32[]{:S(2)}, u32[]{:S(2)}) collective-permute-start(bf16[832,128]{1,0:T(8,128)(2,1)S(1)} %fusion.5), channel_id=1, source_target_pairs={{0,8},{1,17},{2,10},{3,19},{4,12},{5,21},{6,14},{7,23},{8,0},{9,25... | collective-permute-start | bytes 638984 | tf_op jit(solution)/shard_map/ppermute | solution.py:710
  38.0 12.4 %copy-start.9 = (bf16[4,128,256]{2,1,0:T(8,128)(2,1)S(1)}, bf16[4,128,256]{2,1,0:T(8,128)(2,1)}, u32[]{:S(2)}) copy-start(bf16[4,128,256]{2,1,0:T(8,128)(2,1)} %get-tuple-element.119) | copy-start | bytes 786436
  38.0 12.4 %copy-start.8 = (bf16[4,128,256]{2,1,0:T(8,128)(2,1)S(1)}, bf16[4,128,256]{2,1,0:T(8,128)(2,1)}, u32[]{:S(2)}) copy-start(bf16[4,128,256]{2,1,0:T(8,128)(2,1)} %get-tuple-element.121) | copy-start | bytes 786436
  38.1 8.5 %collective-permute-start.12 = (bf16[608,128]{1,0:T(8,128)(2,1)S(1)}, bf16[608,128]{1,0:T(8,128)(2,1)S(1)}, u32[]{:S(2)}, u32[]{:S(2)}) collective-permute-start(bf16[608,128]{1,0:T(8,128)(2,1)S(1)} %get-tuple-element.175), channel_id=1, source_target_pairs={{0,6},{2,4},{4,2},{6,0},{8,14},{10,12},{12,10},{14,8},{16,22},{18,... | collective-permute-start | bytes 466952 | tf_op jit(solution)/shard_map/ppermute | solution.py:674
  39.9 9.4 %collective-permute-start.11 = (bf16[608,128]{1,0:T(8,128)(2,1)S(1)}, bf16[608,128]{1,0:T(8,128)(2,1)S(1)}, u32[]{:S(2)}, u32[]{:S(2)}) collective-permute-start(bf16[608,128]{1,0:T(8,128)(2,1)S(1)} %get-tuple-element.176), channel_id=1, source_target_pairs={{0,4},{2,6},{4,0},{6,2},{8,12},{10,14},{12,8},{14,10},{16,20},{18,... | collective-permute-start | bytes 466952 | tf_op jit(solution)/shard_map/ppermute | solution.py:674
  40.8 8.5 %collective-permute-start.10 = (bf16[608,128]{1,0:T(8,128)(2,1)S(1)}, bf16[608,128]{1,0:T(8,128)(2,1)S(1)}, u32[]{:S(2)}, u32[]{:S(2)}) collective-permute-start(bf16[608,128]{1,0:T(8,128)(2,1)S(1)} %get-tuple-element.177), channel_id=1, source_target_pairs={{0,2},{2,0},{4,6},{6,4},{8,10},{10,8},{12,14},{14,12},{16,18},{18,... | collective-permute-start | bytes 466952 | tf_op jit(solution)/shard_map/ppermute | solution.py:674
  44.5 14.2 %copy-start.4 = (f32[4,128,256]{2,1,0:T(8,128)S(1)}, f32[4,128,256]{2,1,0:T(8,128)}, u32[]{:S(2)}) copy-start(f32[4,128,256]{2,1,0:T(8,128)} %get-tuple-element.118) | copy-start | bytes 1572868
  44.5 8.5 %collective-permute-start.18 = (bf16[832,128]{1,0:T(8,128)(2,1)S(1)}, bf16[832,128]{1,0:T(8,128)(2,1)S(1)}, u32[]{:S(2)}, u32[]{:S(2)}) collective-permute-start(bf16[832,128]{1,0:T(8,128)(2,1)S(1)} %add_convert_fusion.1), channel_id=1, source_target_pairs={{0,16},{1,9},{2,18},{3,11},{4,20},{5,13},{6,22},{7,15},{8,24},{9,1... | collective-permute-start | bytes 638984 | tf_op jit(solution)/shard_map/ppermute | solution.py:710
  49.4 7.2 %collective-permute-start.16 = (bf16[704,128]{1,0:T(8,128)(2,1)S(1)}, bf16[704,128]{1,0:T(8,128)(2,1)S(1)}, u32[]{:S(2)}, u32[]{:S(2)}) collective-permute-start(bf16[704,128]{1,0:T(8,128)(2,1)S(1)} %constant_dynamic-update-slice_fusion), channel_id=1, source_target_pairs={{0,8},{1,17},{2,10},{3,19},{4,12},{5,21},{6,14},{7,23},{8,0},{9,25... | collective-permute-start | bytes 540680 | tf_op jit(solution)/shard_map/ppermute | solution.py:710
  50.4 8.3 %collective-permute-start.14 = (bf16[4,128,256]{2,1,0:T(8,128)(2,1)S(1)}, bf16[4,128,256]{2,1,0:T(8,128)(2,1)S(1)}, u32[]{:S(2)}, u32[]{:S(2)}) collective-permute-start(bf16[4,128,256]{2,1,0:T(8,128)(2,1)S(1)} %copy-done.9), channel_id=1, source_target_pairs={{0,1},{1,0},{2,3},{3,2},{4,5},{5,4},{6,7},{7,6},{8,9},{9,8},{10,11... | collective-permute-start | bytes 786440 | tf_op jit(solution)/shard_map/ppermute | solution.py:674
  50.4 8.4 %collective-permute-start.15 = (bf16[4,128,256]{2,1,0:T(8,128)(2,1)S(1)}, bf16[4,128,256]{2,1,0:T(8,128)(2,1)S(1)}, u32[]{:S(2)}, u32[]{:S(2)}) collective-permute-start(bf16[4,128,256]{2,1,0:T(8,128)(2,1)S(1)} %copy-done.8), channel_id=1, source_target_pairs={{0,1},{1,0},{2,3},{3,2},{4,5},{5,4},{6,7},{7,6},{8,9},{9,8},{10,11... | collective-permute-start | bytes 786440 | tf_op jit(solution)/shard_map/ppermute | solution.py:674
  53.1 5.7 %copy-start.3 = (f32[4,128,256]{2,1,0:T(8,128)S(1)}, f32[4,128,256]{2,1,0:T(8,128)}, u32[]{:S(2)}) copy-start(f32[4,128,256]{2,1,0:T(8,128)} %get-tuple-element.120) | copy-start | bytes 1572868
  53.1 8.0 %collective-permute-start.19 = (bf16[832,128]{1,0:T(8,128)(2,1)S(1)}, bf16[832,128]{1,0:T(8,128)(2,1)S(1)}, u32[]{:S(2)}, u32[]{:S(2)}) collective-permute-start(bf16[832,128]{1,0:T(8,128)(2,1)S(1)} %add_convert_fusion.refs_0_), channel_id=1, source_target_pairs={{0,2},{1,5},{2,0},{3,7},{4,6},{5,1},{6,4},{7,3},{8,10},{9,13},{10,... | collective-permute-start | bytes 638984 | tf_op jit(solution)/shard_map/ppermute | solution.py:735
  56.7 7.4 %collective-permute-start.17 = (bf16[832,128]{1,0:T(8,128)(2,1)S(1)}, bf16[832,128]{1,0:T(8,128)(2,1)S(1)}, u32[]{:S(2)}, u32[]{:S(2)}) collective-permute-start(bf16[832,128]{1,0:T(8,128)(2,1)S(1)} %get-tuple-element.150), channel_id=1, source_target_pairs={{0,16},{1,9},{2,18},{3,11},{4,20},{5,13},{6,22},{7,15},{8,24},{9,1... | collective-permute-start | bytes 638984 | tf_op jit(solution)/shard_map/ppermute | solution.py:710
  61.1 8.8 %copy-start.2 = (bf16[1024,512]{1,0:T(8,128)(2,1)S(1)}, bf16[1024,512]{1,0:T(8,128)(2,1)}, u32[]{:S(2)}) copy-start(bf16[1024,512]{1,0:T(8,128)(2,1)} %refs_14_.3) | copy-start | bytes 3145732
  61.1 12.7 %collective-permute-start.24 = (bf16[1664,128]{1,0:T(8,128)(2,1)S(1)}, bf16[1664,128]{1,0:T(8,128)(2,1)S(1)}, u32[]{:S(2)}, u32[]{:S(2)}) collective-permute-start(bf16[1664,128]{1,0:T(8,128)(2,1)S(1)} %pad_maximum_fusion.2), channel_id=1, source_target_pairs={{0,4},{1,3},{2,6},{3,1},{4,0},{5,7},{6,2},{7,5},{8,12},{9,11},{10,... | collective-permute-start | bytes 1277960 | tf_op jit(solution)/shard_map/ppermute | solution.py:735
  64.2 3.8 %collective-permute-start.20 = (bf16[512,128]{1,0:T(8,128)(2,1)S(1)}, bf16[512,128]{1,0:T(8,128)(2,1)S(1)}, u32[]{:S(2)}, u32[]{:S(2)}) collective-permute-start(bf16[512,128]{1,0:T(8,128)(2,1)S(1)} %get-tuple-element.146), channel_id=1, source_target_pairs={{0,1},{1,0},{2,3},{3,2},{4,5},{5,4},{6,7},{7,6},{8,9},{9,8},{10,11... | collective-permute-start | bytes 393224 | tf_op jit(solution)/shard_map/ppermute | solution.py:674
  64.4 10.7 %collective-permute-start.23 = (bf16[576,128]{1,0:T(8,128)(2,1)S(1)}, bf16[576,128]{1,0:T(8,128)(2,1)S(1)}, u32[]{:S(2)}, u32[]{:S(2)}) collective-permute-start(bf16[576,128]{1,0:T(8,128)(2,1)S(1)} %add_convert_fusion.5.refs_0_), channel_id=1, source_target_pairs={{0,6},{2,4},{4,2},{6,0},{8,14},{10,12},{12,10},{14,8},{16,22},{18,... | collective-permute-start | bytes 442376 | tf_op jit(solution)/shard_map/ppermute | solution.py:674
  66.3 9.4 %collective-permute-start.22 = (bf16[576,128]{1,0:T(8,128)(2,1)S(1)}, bf16[576,128]{1,0:T(8,128)(2,1)S(1)}, u32[]{:S(2)}, u32[]{:S(2)}) collective-permute-start(bf16[576,128]{1,0:T(8,128)(2,1)S(1)} %add_convert_fusion.5.refs_0_), channel_id=1, source_target_pairs={{0,4},{2,6},{4,0},{6,2},{8,12},{10,14},{12,8},{14,10},{16,20},{18,... | collective-permute-start | bytes 442376 | tf_op jit(solution)/shard_map/ppermute | solution.py:674
  67.5 8.2 %collective-permute-start.21 = (bf16[576,128]{1,0:T(8,128)(2,1)S(1)}, bf16[576,128]{1,0:T(8,128)(2,1)S(1)}, u32[]{:S(2)}, u32[]{:S(2)}) collective-permute-start(bf16[576,128]{1,0:T(8,128)(2,1)S(1)} %add_convert_fusion.5.refs_0_), channel_id=1, source_target_pairs={{0,2},{2,0},{4,6},{6,4},{8,10},{10,8},{12,14},{14,12},{16,18},{18,... | collective-permute-start | bytes 442376 | tf_op jit(solution)/shard_map/ppermute | solution.py:674
  68.0 2.3 %slice-start = ((bf16[1536,128]{1,0:T(8,128)(2,1)}), bf16[512,128]{1,0:T(8,128)(2,1)S(1)}, s32[]{:S(2)}) async-start(bf16[1536,128]{1,0:T(8,128)(2,1)} %copy-done), calls=%async_computation | async-start | bytes 262144 | tf_op jit(solution)/shard_map/slice | solution.py:1086
  68.0 2.3 %copy-start.5 = (bf16[512,128]{1,0:T(8,128)(2,1)S(1)}, bf16[512,128]{1,0:T(8,128)(2,1)}, u32[]{:S(2)}) copy-start(bf16[512,128]{1,0:T(8,128)(2,1)} %refs_11_.3) | copy-start | bytes 393220

commit v8 on v7

--- a/solution.py
+++ b/solution.py
@@ -262,8 +262,8 @@
     images = range(count)
 
     steps_cp = cps.start(steps_in, steps_ref)
+    vec_cp = load_split(cps, vec_in, vec, 1, places)
     x_cp = load_images(cps, x_in, xin, places, count)
-    vec_cp = load_split(cps, vec_in, vec, 1, places)
     w1_cp = load_split(cps, w1_in, w1, 2, places)
     w2_cp = load_split(cps, w2_in, w2, 1, places)
     steps_cp.wait()
@@ -638,8 +638,8 @@
     chans = dw1.shape[1]
     for tap in range(dw1.shape[0]):
         dw1[tap] = flat[tap * chans : (tap + 1) * chans, :].astype(f32)
-        if tap % 3 == 2:
-            part = slice(tap - 2, tap + 1)
+        if tap in (3, 8):
+            part = slice(0, 4) if tap == 3 else slice(4, 9)
             outs.append(cps.start(dw1.at[part], dw1_out.at[part]))
     wait_all(outs)
 

time: 77.5 us -> 77.5 us (level)
  no operation moved by 1% of the time
where the time goes in v8:
time: 77.5 us; the launch traced here: 76.9 us
  Pallas kernels  24.5 us (32%)
  starting transfers between devices  23.7 us (31%)
  waiting for transfers between devices  16.7 us (22%)
  other arithmetic  4.49 us (6%)
  matrix products  3.25 us (4%)
  local copies, waits for them, and re-layouts  3.13 us (4%)
  between operations  1.15 us (1%)
    ppermute x19, starting transfers between devices, swap(): return lax.ppermute(value, axis, [(i, i ^ bit) for i in range(size)])  14.3 us
    pallas_call x1, Pallas kernels, per_device(): pl.pallas_call(functools.partial(front_kernel, pieces, count), out_shape=...  11.9 us
    pallas_call x1, Pallas kernels, per_device(): pl.pallas_call(functools.partial(back_kernel, pieces, count), out_shape=o...  8.83 us
    ppermute x4, waiting for transfers between devices, send_far(): return lax.ppermute(mine, ('batch', 'tensor'), pairs)  8.7 us
    ppermute x19, waiting for transfers between devices, swap(): return lax.ppermute(value, axis, [(i, i ^ bit) for i in range(size)])  7.96 us
    ppermute x4, starting transfers between devices, send_far(): return lax.ppermute(mine, ('batch', 'tensor'), pairs)  6.64 us
    ppermute x2, starting transfers between devices, cross(): return lax.ppermute(value, ('batch', 'tensor'), pairs)  2.81 us
    pallas_call x2, Pallas kernels, unpacked(): pl.pallas_call(kernel, out_shape=outs, in_specs=[VMEM] * len(got), out_sp...  2.42 us
  transfers between devices with their start and end apart: 25, of which 9 were waited for; matrix products, arithmetic and copies ran while one was open for 13% of the time, Pallas kernels for 15%

profile of v8, /device:TPU:0, one launch (start us, length us, event | category | flops | bytes accessed | tf_op | source)
XLA Modules:
  0.0 76.9 jit_solution(5280749861910000455)
XLA Ops:
  0.7 0.5 collective-permute-start.1
  1.3 1.4 %pack.1 = (f32[16,128]{1,0:T(8,128)S(1)}, bf16[2,4,128,256]{3,2,1,0:T(8,128)(2,1)S(1)}, bf16[1536,128]{1,0:T(8,128)(2,1)S(1)}) custom-call(f32[128]{0:T(128)} %refs_0_.2, f32[128]{0:T(128)} %refs_1_.1, f32[128]{0:T(128)} %refs_2_.2, f32[128]{0:T(128)} %refs_3_.1, f32[128]{0:T(128)} %refs_4_.2, f32[128]{0:T(128)} %refs_5_.1, f32[128]{0:T(128)} %refs_6_.1, ...), custom_call_target="tpu_custom_call" | custom-call | tf_op jit(solution)/shard_map/pack/pallas_call | solution.py:814
  2.7 0.5 collective-permute-start
  3.2 0.4 collective-permute-start.3
  3.7 1.6 %collective-permute-done.3.refs_7_ = f32[16,128]{1,0:T(8,128)S(1)} collective-permute-done((f32[16,128]{1,0:T(8,128)S(1)}, f32[16,128]{1,0:T(8,128)S(1)}, u32[]{:S(2)}, u32[]{:S(2)}) %collective-permute-start.3) | collective-permute-done | bytes 8224 | tf_op jit(solution)/shard_map/ppermute | solution.py:674
  5.3 11.9 %front.1 = (bf16[3328,128]{1,0:T(8,128)(2,1)S(1)}, bf16[3328,128]{1,0:T(8,128)(2,1)S(1)}, bf16[9,256,256]{2,1,0:T(8,128)(2,1)}, bf16[9,256,256]{2,1,0:T(8,128)(2...) custom-call(bf16[8,128,256]{2,1,0:T(8,128)(2,1)} %refs_0_.3, ...), custom_call_target="tpu_custom_call" | custom-call | flops 7247757312 | bytes 12582912 | tf_op jit(solution)/shard_map/front/pallas_call | solution.py:894
  17.2 0.4 collective-permute-start.5
  17.6 2.0 %collective-permute-done.5 = bf16[3328,128]{1,0:T(8,128)(2,1)S(1)} collective-permute-done((bf16[3328,128]{1,0:T(8,128)(2,1)S(1)}, bf16[3328,128]{1,0:T(8,128)(2,1)S(1)}, u32[]{:S(2)}, u32[]{:S(2)}) %collective-permute-start.5) | collective-permute-done | bytes 852000 | tf_op jit(solution)/shard_map/ppermute | solution.py:674
  19.6 0.2 fusion.29
  19.8 2.9 %collective-permute-start.6 = (bf16[832,128]{1,0:T(8,128)(2,1)S(1)}, bf16[832,128]{1,0:T(8,128)(2,1)S(1)}, u32[]{:S(2)}, u32[]{:S(2)}) collective-permute-start(bf16[832,128]{1,0:T(8,128)(2,1)S(1)} %get-tuple-element.101), channel_id=1, source_target_pairs={{0,2},{2,0},{4,6},{6,4},{8,10},{10,8},{12,14},{14,12},{16,18},{18,... | collective-permute-start | bytes 638984 | tf_op jit(solution)/shard_map/ppermute | solution.py:674
  22.7 1.5 %collective-permute-start.7 = (bf16[832,128]{1,0:T(8,128)(2,1)S(1)}, bf16[832,128]{1,0:T(8,128)(2,1)S(1)}, u32[]{:S(2)}, u32[]{:S(2)}) collective-permute-start(bf16[832,128]{1,0:T(8,128)(2,1)S(1)} %get-tuple-element.102), channel_id=1, source_target_pairs={{0,4},{2,6},{4,0},{6,2},{8,12},{10,14},{12,8},{14,10},{16,20},{18,... | collective-permute-start | bytes 638984 | tf_op jit(solution)/shard_map/ppermute | solution.py:674
  24.3 8.8 %back.1 = (bf16[2304,128]{1,0:T(8,128)(2,1)S(1)}, bf16[2304,128]{1,0:T(8,128)(2,1)}, f32[4,128,256]{2,1,0:T(8,128)}, bf16[4,128,256]{2,1,0:T(8,128)(2,1)}, f32[4...) custom-call(bf16[9,256,256]{2,1,0:T(8,128)(2,1)} %get-tuple-element.80.refs_0_, ...), custom_call_target="tpu_custom_call" | custom-call | flops 4429185024 | bytes 12582912 | tf_op jit(solution)/shard_map/back/pallas_call | solution.py:965
  33.1 1.2 %collective-permute-done.7 = bf16[832,128]{1,0:T(8,128)(2,1)S(1)} collective-permute-done((bf16[832,128]{1,0:T(8,128)(2,1)S(1)}, bf16[832,128]{1,0:T(8,128)(2,1)S(1)}, u32[]{:S(2)}, u32[]{:S(2)}) %collective-permute-start.7) | collective-permute-done | bytes 213024 | tf_op jit(solution)/shard_map/ppermute | solution.py:674
  34.3 0.7 copy-done.6
  35.1 1.2 %fusion.5 = bf16[832,128]{1,0:T(8,128)(2,1)S(1)} fusion(bf16[832,128]{1,0:T(8,128)(2,1)} %copy-done.7, bf16[832,128]{1,0:T(8,128)(2,1)} %copy-done.6, bf16[832,128]{1,0:T(8,128)(2,1)S(1)} %collective-permute-done.6, bf16[4,832,128]{2,1,0:T(8,128)(2,1)S(1)} %bitcast.71, s32[]{:T(128)S(6)} %select_n.72, bf16[4,832,128]{2,1,0:T(8,128)(2,1)S(1)} %bitcast.64), kind=kLoop, calls=%fused_computation.15 | loop fusion | flops 1064960 | bytes 1277956 | tf_op jit(solution)/shard_map/convert_element_type | solution.py:694
  36.3 1.6 %collective-permute-start.13 = (bf16[832,128]{1,0:T(8,128)(2,1)S(1)}, bf16[832,128]{1,0:T(8,128)(2,1)S(1)}, u32[]{:S(2)}, u32[]{:S(2)}) collective-permute-start(bf16[832,128]{1,0:T(8,128)(2,1)S(1)} %fusion.5), channel_id=1, source_target_pairs={{0,8},{1,17},{2,10},{3,19},{4,12},{5,21},{6,14},{7,23},{8,0},{9,25... | collective-permute-start | bytes 638984 | tf_op jit(solution)/shard_map/ppermute | solution.py:710
  37.9 0.1 fusion.32
  38.1 1.8 %collective-permute-start.12 = (bf16[608,128]{1,0:T(8,128)(2,1)S(1)}, bf16[608,128]{1,0:T(8,128)(2,1)S(1)}, u32[]{:S(2)}, u32[]{:S(2)}) collective-permute-start(bf16[608,128]{1,0:T(8,128)(2,1)S(1)} %get-tuple-element.175), channel_id=1, source_target_pairs={{0,6},{2,4},{4,2},{6,0},{8,14},{10,12},{12,10},{14,8},{16,22},{18,... | collective-permute-start | bytes 466952 | tf_op jit(solution)/shard_map/ppermute | solution.py:674
  39.9 0.9 %collective-permute-start.11 = (bf16[608,128]{1,0:T(8,128)(2,1)S(1)}, bf16[608,128]{1,0:T(8,128)(2,1)S(1)}, u32[]{:S(2)}, u32[]{:S(2)}) collective-permute-start(bf16[608,128]{1,0:T(8,128)(2,1)S(1)} %get-tuple-element.176), channel_id=1, source_target_pairs={{0,4},{2,6},{4,0},{6,2},{8,12},{10,14},{12,8},{14,10},{16,20},{18,... | collective-permute-start | bytes 466952 | tf_op jit(solution)/shard_map/ppermute | solution.py:674
  40.8 0.9 %collective-permute-start.10 = (bf16[608,128]{1,0:T(8,128)(2,1)S(1)}, bf16[608,128]{1,0:T(8,128)(2,1)S(1)}, u32[]{:S(2)}, u32[]{:S(2)}) collective-permute-start(bf16[608,128]{1,0:T(8,128)(2,1)S(1)} %get-tuple-element.177), channel_id=1, source_target_pairs={{0,2},{2,0},{4,6},{6,4},{8,10},{10,8},{12,14},{14,12},{16,18},{18,... | collective-permute-start | bytes 466952 | tf_op jit(solution)/shard_map/ppermute | solution.py:674
  41.6 2.8 %collective-permute-done.13 = bf16[832,128]{1,0:T(8,128)(2,1)S(1)} collective-permute-done((bf16[832,128]{1,0:T(8,128)(2,1)S(1)}, bf16[832,128]{1,0:T(8,128)(2,1)S(1)}, u32[]{:S(2)}, u32[]{:S(2)}) %collective-permute-start.13) | collective-permute-done | bytes 213024 | tf_op jit(solution)/shard_map/ppermute | solution.py:710
  44.5 2.1 %collective-permute-start.18 = (bf16[832,128]{1,0:T(8,128)(2,1)S(1)}, bf16[832,128]{1,0:T(8,128)(2,1)S(1)}, u32[]{:S(2)}, u32[]{:S(2)}) collective-permute-start(bf16[832,128]{1,0:T(8,128)(2,1)S(1)} %add_convert_fusion.1), channel_id=1, source_target_pairs={{0,16},{1,9},{2,18},{3,11},{4,20},{5,13},{6,22},{7,15},{8,24},{9,1... | collective-permute-start | bytes 638984 | tf_op jit(solution)/shard_map/ppermute | solution.py:710
  46.6 2.7 %collective-permute-done.11 = bf16[608,128]{1,0:T(8,128)(2,1)S(1)} collective-permute-done((bf16[608,128]{1,0:T(8,128)(2,1)S(1)}, bf16[608,128]{1,0:T(8,128)(2,1)S(1)}, u32[]{:S(2)}, u32[]{:S(2)}) %collective-permute-start.11) | collective-permute-done | bytes 155680 | tf_op jit(solution)/shard_map/ppermute | solution.py:674
  49.3 0.1 constant_dynamic-update-slice_fusion.4
  49.4 1.0 %collective-permute-start.16 = (bf16[704,128]{1,0:T(8,128)(2,1)S(1)}, bf16[704,128]{1,0:T(8,128)(2,1)S(1)}, u32[]{:S(2)}, u32[]{:S(2)}) collective-permute-start(bf16[704,128]{1,0:T(8,128)(2,1)S(1)} %constant_dynamic-update-slice_fusion), channel_id=1, source_target_pairs={{0,8},{1,17},{2,10},{3,19},{4,12},{5,21},{6,14},{7,23},{8,0},{9,25... | collective-permute-start | bytes 540680 | tf_op jit(solution)/shard_map/ppermute | solution.py:710
  50.4 0.5 collective-permute-start.15
  50.9 2.1 %collective-permute-done.18 = bf16[832,128]{1,0:T(8,128)(2,1)S(1)} collective-permute-done((bf16[832,128]{1,0:T(8,128)(2,1)S(1)}, bf16[832,128]{1,0:T(8,128)(2,1)S(1)}, u32[]{:S(2)}, u32[]{:S(2)}) %collective-permute-start.18) | collective-permute-done | bytes 213024 | tf_op jit(solution)/shard_map/ppermute | solution.py:710
  53.1 1.2 %collective-permute-start.19 = (bf16[832,128]{1,0:T(8,128)(2,1)S(1)}, bf16[832,128]{1,0:T(8,128)(2,1)S(1)}, u32[]{:S(2)}, u32[]{:S(2)}) collective-permute-start(bf16[832,128]{1,0:T(8,128)(2,1)S(1)} %add_convert_fusion.refs_0_), channel_id=1, source_target_pairs={{0,2},{1,5},{2,0},{3,7},{4,6},{5,1},{6,4},{7,3},{8,10},{9,13},{10,... | collective-permute-start | bytes 638984 | tf_op jit(solution)/shard_map/ppermute | solution.py:735
  54.3 2.3 %collective-permute-done.16 = bf16[704,128]{1,0:T(8,128)(2,1)S(1)} collective-permute-done((bf16[704,128]{1,0:T(8,128)(2,1)S(1)}, bf16[704,128]{1,0:T(8,128)(2,1)S(1)}, u32[]{:S(2)}, u32[]{:S(2)}) %collective-permute-start.16) | collective-permute-done | bytes 180256 | tf_op jit(solution)/shard_map/ppermute | solution.py:710
  56.8 1.9 %collective-permute-start.17 = (bf16[832,128]{1,0:T(8,128)(2,1)S(1)}, bf16[832,128]{1,0:T(8,128)(2,1)S(1)}, u32[]{:S(2)}, u32[]{:S(2)}) collective-permute-start(bf16[832,128]{1,0:T(8,128)(2,1)S(1)} %get-tuple-element.150), channel_id=1, source_target_pairs={{0,16},{1,9},{2,18},{3,11},{4,20},{5,13},{6,22},{7,15},{8,24},{9,1... | collective-permute-start | bytes 638984 | tf_op jit(solution)/shard_map/ppermute | solution.py:710
  58.9 1.1 %pad_maximum_fusion = f32[8,128,256]{2,1,0:T(8,128)} fusion(f32[4,128,256]{2,1,0:T(8,128)S(1)} %get-tuple-element.145, f32[4,128,256]{2,1,0:T(8,128)S(1)} %get-tuple-element.144), kind=kLoop, calls=%fused_computation.3 | loop fusion | flops 262144 | bytes 2097152 | tf_op jit(solution)/shard_map/concatenate | solution.py:1012
  60.0 1.1 %pad_maximum_fusion.1 = f32[8,128,256]{2,1,0:T(8,128)} fusion(f32[4,128,256]{2,1,0:T(8,128)S(1)} %get-tuple-element.143, f32[4,128,256]{2,1,0:T(8,128)S(1)} %get-tuple-element.142), kind=kLoop, calls=%fused_computation.4 | loop fusion | flops 262144 | bytes 2097152 | tf_op jit(solution)/shard_map/concatenate | solution.py:1012
  61.1 1.6 %collective-permute-start.24 = (bf16[1664,128]{1,0:T(8,128)(2,1)S(1)}, bf16[1664,128]{1,0:T(8,128)(2,1)S(1)}, u32[]{:S(2)}, u32[]{:S(2)}) collective-permute-start(bf16[1664,128]{1,0:T(8,128)(2,1)S(1)} %pad_maximum_fusion.2), channel_id=1, source_target_pairs={{0,4},{1,3},{2,6},{3,1},{4,0},{5,7},{6,2},{7,5},{8,12},{9,11},{10,... | collective-permute-start | bytes 1277960 | tf_op jit(solution)/shard_map/ppermute | solution.py:735
  62.7 1.5 %collective-permute-done.17 = bf16[832,128]{1,0:T(8,128)(2,1)S(1)} collective-permute-done((bf16[832,128]{1,0:T(8,128)(2,1)S(1)}, bf16[832,128]{1,0:T(8,128)(2,1)S(1)}, u32[]{:S(2)}, u32[]{:S(2)}) %collective-permute-start.17) | collective-permute-done | bytes 213024 | tf_op jit(solution)/shard_map/ppermute | solution.py:710
  64.3 0.2 collective-permute-start.20
  64.5 1.8 %collective-permute-start.23 = (bf16[576,128]{1,0:T(8,128)(2,1)S(1)}, bf16[576,128]{1,0:T(8,128)(2,1)S(1)}, u32[]{:S(2)}, u32[]{:S(2)}) collective-permute-start(bf16[576,128]{1,0:T(8,128)(2,1)S(1)} %add_convert_fusion.5.refs_0_), channel_id=1, source_target_pairs={{0,6},{2,4},{4,2},{6,0},{8,14},{10,12},{12,10},{14,8},{16,22},{18,... | collective-permute-start | bytes 442376 | tf_op jit(solution)/shard_map/ppermute | solution.py:674
  66.3 1.1 %collective-permute-start.22 = (bf16[576,128]{1,0:T(8,128)(2,1)S(1)}, bf16[576,128]{1,0:T(8,128)(2,1)S(1)}, u32[]{:S(2)}, u32[]{:S(2)}) collective-permute-start(bf16[576,128]{1,0:T(8,128)(2,1)S(1)} %add_convert_fusion.5.refs_0_), channel_id=1, source_target_pairs={{0,4},{2,6},{4,0},{6,2},{8,12},{10,14},{12,8},{14,10},{16,20},{18,... | collective-permute-start | bytes 442376 | tf_op jit(solution)/shard_map/ppermute | solution.py:674
  67.5 0.6 collective-permute-start.21
  68.3 0.7 slice.125
  68.9 0.9 %reshape.104 = bf16[128,256]{1,0:T(8,128)(2,1)S(1)} reshape(bf16[32,8,128]{2,1,0:T(8,128)(2,1)} %slice.125) | data formatting | bytes 131072 | tf_op jit(solution)/shard_map/reshape | solution.py:1073
  69.9 0.1 eq.11
  70.0 0.3 fusion.2
  70.4 2.0 %fusion.1 = f32[1024,512]{1,0:T(8,128)} fusion(bf16[128,256]{1,0:T(8,128)(2,1)S(1)} %reshape.104, bf16[512,128]{1,0:T(8,128)(2,1)S(1)} %slice-done, bf16[512,128]{1,0:T(8,128)(2,1)S(1)} %copy-done.5, f32[128,512]{1,0:T(8,128)S(1)} %fusion.2, s32[128]{0:T(128)S(1)} %eq.11, pred[]{:T(512)S(6)} %eq.10), kind=kOutput, calls=%fused_computation.2 | convolution fusion | flops 169672704 | bytes 2687489 | tf_op jit(solution)/shard_map/dot_general | solution.py:1095
  72.4 0.9 %fusion.33 = f32[512,128]{1,0:T(8,128)} fusion(f32[128,512]{1,0:T(8,128)S(1)} %fusion.2, bf16[128,256]{1,0:T(8,128)(2,1)S(1)} %reshape.104, s32[]{:T(128)S(6)} %select_n.81), kind=kOutput, calls=%fused_computation.56 | convolution fusion | flops 17104896 | bytes 557060 | tf_op jit(solution)/shard_map/dot_general | solution.py:1082
  73.3 0.6 slice_bitcast_fusion
  73.9 1.3 %unpack_second.1 = (f32[9,128,256]{2,1,0:T(8,128)}, f32[128,256]{1,0:T(8,128)}, f32[3,256,128]{2,1,0:T(8,128)}) custom-call(bf16[832,128]{1,0:T(8,128)(2,1)S(1)} %add_convert_fusion.refs_0_, bf16[832,128]{1,0:T(8,128)(2,1)S(1)} %collective-permute-done.19.refs_1_, bf16[1664,128]{1,0:T(8,128)(2,1)S(1)} %collective-permute-done.24.refs_2_), custom_call_target="tpu_custom_call" | custom-call | tf_op jit(solution)/shard_map/unpack_second/pallas_call | solution.py:1032
  75.2 0.4 collective-permute-done.22.refs_2_
  75.7 1.1 %unpack_first.1 = f32[9,256,128]{2,1,0:T(8,128)} custom-call(bf16[576,128]{1,0:T(8,128)(2,1)S(1)} %add_convert_fusion.5.refs_0_, bf16[576,128]{1,0:T(8,128)(2,1)S(1)} %collective-permute-done.21.refs_1_, bf16[576,128]{1,0:T(8,128)(2,1)S(1)} %collective-permute-done.22.refs_2_, bf16[576,128]{1,0:T(8,128)(2,1)S(1)} %collective-permute-done.23.refs_3_), custom_call_target="tpu_custom_call" | custom-call | tf_op jit(solution)/shard_map/unpack_first/pallas_call | solution.py:1032
  (68 shorter events, 1.2 us)
Async XLA Ops:
  0.7 4.6 %collective-permute-start.1 = (bf16[9,256,128]{2,1,0:T(8,128)(2,1)}, bf16[9,256,128]{2,1,0:T(8,128)(2,1)S(1)}, u32[]{:S(2)}, u32[]{:S(2)}) collective-permute-start(bf16[9,256,128]{2,1,0:T(8,128)(2,1)} %refs_2_.3), channel_id=1, source_target_pairs={{0,1},{1,0},{2,3},{3,2},{4,5},{5,4},{6,7},{7,6},{8,9},{9,8},{10,11... | collective-permute-start | bytes 1769480 | tf_op jit(solution)/shard_map/ppermute | solution.py:674
  1.2 4.1 %collective-permute-start.2 = (bf16[9,128,256]{2,1,0:T(8,128)(2,1)}, bf16[9,128,256]{2,1,0:T(8,128)(2,1)S(1)}, u32[]{:S(2)}, u32[]{:S(2)}) collective-permute-start(bf16[9,128,256]{2,1,0:T(8,128)(2,1)} %refs_4_.3), channel_id=1, source_target_pairs={{0,1},{1,0},{2,3},{3,2},{4,5},{5,4},{6,7},{7,6},{8,9},{9,8},{10,11... | collective-permute-start | bytes 1769480 | tf_op jit(solution)/shard_map/ppermute | solution.py:674
  2.6 2.6 %copy-start.1 = (f32[16,128]{1,0:T(8,128)}, f32[16,128]{1,0:T(8,128)S(1)}, u32[]{:S(2)}) copy-start(f32[16,128]{1,0:T(8,128)S(1)} %get-tuple-element.78.refs_6_) | copy-start | bytes 24580
  2.7 2.6 %collective-permute-start = (bf16[2,4,128,256]{3,2,1,0:T(8,128)(2,1)S(1)}, bf16[2,4,128,256]{3,2,1,0:T(8,128)(2,1)S(1)}, u32[]{:S(2)}, u32[]{:S(2)}) collective-permute-start(bf16[2,4,128,256]{3,2,1,0:T(8,128)(2,1)S(1)} %get-tuple-element.77), channel_id=1, source_target_pairs={{0,1},{1,0},{2,3},{3,2},{4,5},{5,4},{6,7},{7,6},{8,9},{9,8},{10,11... | collective-permute-start | bytes 1572872 | tf_op jit(solution)/shard_map/ppermute | solution.py:674
  3.1 2.1 %collective-permute-start.4 = (bf16[1536,128]{1,0:T(8,128)(2,1)S(1)}, bf16[1536,128]{1,0:T(8,128)(2,1)S(1)}, u32[]{:S(2)}, u32[]{:S(2)}) collective-permute-start(bf16[1536,128]{1,0:T(8,128)(2,1)S(1)} %get-tuple-element.79), channel_id=1, source_target_pairs={{0,1},{1,0},{2,3},{3,2},{4,5},{5,4},{6,7},{7,6},{8,9},{9,8},{10,11... | collective-permute-start | bytes 1179656 | tf_op jit(solution)/shard_map/ppermute | solution.py:674
  3.2 2.0 %collective-permute-start.3 = (f32[16,128]{1,0:T(8,128)S(1)}, f32[16,128]{1,0:T(8,128)S(1)}, u32[]{:S(2)}, u32[]{:S(2)}) collective-permute-start(f32[16,128]{1,0:T(8,128)S(1)} %get-tuple-element.78.refs_6_), channel_id=1, source_target_pairs={{0,1},{1,0},{2,3},{3,2},{4,5},{5,4},{6,7},{7,6},{8,9},{9,8},{10,11... | collective-permute-start | bytes 24584 | tf_op jit(solution)/shard_map/ppermute | solution.py:674
  5.3 29.8 %copy-start = (bf16[1536,128]{1,0:T(8,128)(2,1)}, bf16[1536,128]{1,0:T(8,128)(2,1)S(1)}, u32[]{:S(2)}) copy-start(bf16[1536,128]{1,0:T(8,128)(2,1)S(1)} %collective-permute-done.4.refs_12_) | copy-start | bytes 1179652
  17.2 2.4 %collective-permute-start.5 = (bf16[3328,128]{1,0:T(8,128)(2,1)S(1)}, bf16[3328,128]{1,0:T(8,128)(2,1)S(1)}, u32[]{:S(2)}, u32[]{:S(2)}) collective-permute-start(bf16[3328,128]{1,0:T(8,128)(2,1)S(1)} %get-tuple-element.94), channel_id=1, source_target_pairs={{0,1},{1,0},{2,3},{3,2},{4,5},{5,4},{6,7},{7,6},{8,9},{9,8},{10,11... | collective-permute-start | bytes 2555912 | tf_op jit(solution)/shard_map/ppermute | solution.py:674
  19.8 13.3 %collective-permute-start.6 = (bf16[832,128]{1,0:T(8,128)(2,1)S(1)}, bf16[832,128]{1,0:T(8,128)(2,1)S(1)}, u32[]{:S(2)}, u32[]{:S(2)}) collective-permute-start(bf16[832,128]{1,0:T(8,128)(2,1)S(1)} %get-tuple-element.101), channel_id=1, source_target_pairs={{0,2},{2,0},{4,6},{6,4},{8,10},{10,8},{12,14},{14,12},{16,18},{18,... | collective-permute-start | bytes 638984 | tf_op jit(solution)/shard_map/ppermute | solution.py:674
  22.7 11.6 %collective-permute-start.7 = (bf16[832,128]{1,0:T(8,128)(2,1)S(1)}, bf16[832,128]{1,0:T(8,128)(2,1)S(1)}, u32[]{:S(2)}, u32[]{:S(2)}) collective-permute-start(bf16[832,128]{1,0:T(8,128)(2,1)S(1)} %get-tuple-element.102), channel_id=1, source_target_pairs={{0,4},{2,6},{4,0},{6,2},{8,12},{10,14},{12,8},{14,10},{16,20},{18,... | collective-permute-start | bytes 638984 | tf_op jit(solution)/shard_map/ppermute | solution.py:674
  24.3 10.1 %collective-permute-start.8 = (bf16[832,128]{1,0:T(8,128)(2,1)S(1)}, bf16[832,128]{1,0:T(8,128)(2,1)S(1)}, u32[]{:S(2)}, u32[]{:S(2)}) collective-permute-start(bf16[832,128]{1,0:T(8,128)(2,1)S(1)} %get-tuple-element.103), channel_id=1, source_target_pairs={{0,6},{2,4},{4,2},{6,0},{8,14},{10,12},{12,10},{14,8},{16,22},{18,... | collective-permute-start | bytes 638984 | tf_op jit(solution)/shard_map/ppermute | solution.py:674
  34.3 0.7 copy-start.6
  34.3 0.7 copy-start.7
  35.1 2.8 %collective-permute-start.9 = (bf16[2304,128]{1,0:T(8,128)(2,1)}, bf16[2304,128]{1,0:T(8,128)(2,1)S(1)}, u32[]{:S(2)}, u32[]{:S(2)}) collective-permute-start(bf16[2304,128]{1,0:T(8,128)(2,1)} %get-tuple-element.108), channel_id=1, source_target_pairs={{0,1},{1,0},{2,3},{3,2},{4,5},{5,4},{6,7},{7,6},{8,9},{9,8},{10,11... | collective-permute-start | bytes 1769480 | tf_op jit(solution)/shard_map/ppermute | solution.py:674
  36.3 8.2 %collective-permute-start.13 = (bf16[832,128]{1,0:T(8,128)(2,1)S(1)}, bf16[832,128]{1,0:T(8,128)(2,1)S(1)}, u32[]{:S(2)}, u32[]{:S(2)}) collective-permute-start(bf16[832,128]{1,0:T(8,128)(2,1)S(1)} %fusion.5), channel_id=1, source_target_pairs={{0,8},{1,17},{2,10},{3,19},{4,12},{5,21},{6,14},{7,23},{8,0},{9,25... | collective-permute-start | bytes 638984 | tf_op jit(solution)/shard_map/ppermute | solution.py:710
  38.0 12.4 %copy-start.9 = (bf16[4,128,256]{2,1,0:T(8,128)(2,1)S(1)}, bf16[4,128,256]{2,1,0:T(8,128)(2,1)}, u32[]{:S(2)}) copy-start(bf16[4,128,256]{2,1,0:T(8,128)(2,1)} %get-tuple-element.119) | copy-start | bytes 786436
  38.0 12.4 %copy-start.8 = (bf16[4,128,256]{2,1,0:T(8,128)(2,1)S(1)}, bf16[4,128,256]{2,1,0:T(8,128)(2,1)}, u32[]{:S(2)}) copy-start(bf16[4,128,256]{2,1,0:T(8,128)(2,1)} %get-tuple-element.121) | copy-start | bytes 786436
  38.1 8.5 %collective-permute-start.12 = (bf16[608,128]{1,0:T(8,128)(2,1)S(1)}, bf16[608,128]{1,0:T(8,128)(2,1)S(1)}, u32[]{:S(2)}, u32[]{:S(2)}) collective-permute-start(bf16[608,128]{1,0:T(8,128)(2,1)S(1)} %get-tuple-element.175), channel_id=1, source_target_pairs={{0,6},{2,4},{4,2},{6,0},{8,14},{10,12},{12,10},{14,8},{16,22},{18,... | collective-permute-start | bytes 466952 | tf_op jit(solution)/shard_map/ppermute | solution.py:674
  39.9 9.4 %collective-permute-start.11 = (bf16[608,128]{1,0:T(8,128)(2,1)S(1)}, bf16[608,128]{1,0:T(8,128)(2,1)S(1)}, u32[]{:S(2)}, u32[]{:S(2)}) collective-permute-start(bf16[608,128]{1,0:T(8,128)(2,1)S(1)} %get-tuple-element.176), channel_id=1, source_target_pairs={{0,4},{2,6},{4,0},{6,2},{8,12},{10,14},{12,8},{14,10},{16,20},{18,... | collective-permute-start | bytes 466952 | tf_op jit(solution)/shard_map/ppermute | solution.py:674
  40.8 8.5 %collective-permute-start.10 = (bf16[608,128]{1,0:T(8,128)(2,1)S(1)}, bf16[608,128]{1,0:T(8,128)(2,1)S(1)}, u32[]{:S(2)}, u32[]{:S(2)}) collective-permute-start(bf16[608,128]{1,0:T(8,128)(2,1)S(1)} %get-tuple-element.177), channel_id=1, source_target_pairs={{0,2},{2,0},{4,6},{6,4},{8,10},{10,8},{12,14},{14,12},{16,18},{18,... | collective-permute-start | bytes 466952 | tf_op jit(solution)/shard_map/ppermute | solution.py:674
  44.5 14.2 %copy-start.4 = (f32[4,128,256]{2,1,0:T(8,128)S(1)}, f32[4,128,256]{2,1,0:T(8,128)}, u32[]{:S(2)}) copy-start(f32[4,128,256]{2,1,0:T(8,128)} %get-tuple-element.118) | copy-start | bytes 1572868
  44.5 8.5 %collective-permute-start.18 = (bf16[832,128]{1,0:T(8,128)(2,1)S(1)}, bf16[832,128]{1,0:T(8,128)(2,1)S(1)}, u32[]{:S(2)}, u32[]{:S(2)}) collective-permute-start(bf16[832,128]{1,0:T(8,128)(2,1)S(1)} %add_convert_fusion.1), channel_id=1, source_target_pairs={{0,16},{1,9},{2,18},{3,11},{4,20},{5,13},{6,22},{7,15},{8,24},{9,1... | collective-permute-start | bytes 638984 | tf_op jit(solution)/shard_map/ppermute | solution.py:710
  49.4 7.2 %collective-permute-start.16 = (bf16[704,128]{1,0:T(8,128)(2,1)S(1)}, bf16[704,128]{1,0:T(8,128)(2,1)S(1)}, u32[]{:S(2)}, u32[]{:S(2)}) collective-permute-start(bf16[704,128]{1,0:T(8,128)(2,1)S(1)} %constant_dynamic-update-slice_fusion), channel_id=1, source_target_pairs={{0,8},{1,17},{2,10},{3,19},{4,12},{5,21},{6,14},{7,23},{8,0},{9,25... | collective-permute-start | bytes 540680 | tf_op jit(solution)/shard_map/ppermute | solution.py:710
  50.4 8.3 %collective-permute-start.14 = (bf16[4,128,256]{2,1,0:T(8,128)(2,1)S(1)}, bf16[4,128,256]{2,1,0:T(8,128)(2,1)S(1)}, u32[]{:S(2)}, u32[]{:S(2)}) collective-permute-start(bf16[4,128,256]{2,1,0:T(8,128)(2,1)S(1)} %copy-done.9), channel_id=1, source_target_pairs={{0,1},{1,0},{2,3},{3,2},{4,5},{5,4},{6,7},{7,6},{8,9},{9,8},{10,11... | collective-permute-start | bytes 786440 | tf_op jit(solution)/shard_map/ppermute | solution.py:674
  50.4 8.4 %collective-permute-start.15 = (bf16[4,128,256]{2,1,0:T(8,128)(2,1)S(1)}, bf16[4,128,256]{2,1,0:T(8,128)(2,1)S(1)}, u32[]{:S(2)}, u32[]{:S(2)}) collective-permute-start(bf16[4,128,256]{2,1,0:T(8,128)(2,1)S(1)} %copy-done.8), channel_id=1, source_target_pairs={{0,1},{1,0},{2,3},{3,2},{4,5},{5,4},{6,7},{7,6},{8,9},{9,8},{10,11... | collective-permute-start | bytes 786440 | tf_op jit(solution)/shard_map/ppermute | solution.py:674
  53.1 5.7 %copy-start.3 = (f32[4,128,256]{2,1,0:T(8,128)S(1)}, f32[4,128,256]{2,1,0:T(8,128)}, u32[]{:S(2)}) copy-start(f32[4,128,256]{2,1,0:T(8,128)} %get-tuple-element.120) | copy-start | bytes 1572868
  53.1 8.0 %collective-permute-start.19 = (bf16[832,128]{1,0:T(8,128)(2,1)S(1)}, bf16[832,128]{1,0:T(8,128)(2,1)S(1)}, u32[]{:S(2)}, u32[]{:S(2)}) collective-permute-start(bf16[832,128]{1,0:T(8,128)(2,1)S(1)} %add_convert_fusion.refs_0_), channel_id=1, source_target_pairs={{0,2},{1,5},{2,0},{3,7},{4,6},{5,1},{6,4},{7,3},{8,10},{9,13},{10,... | collective-permute-start | bytes 638984 | tf_op jit(solution)/shard_map/ppermute | solution.py:735
  56.8 7.4 %collective-permute-start.17 = (bf16[832,128]{1,0:T(8,128)(2,1)S(1)}, bf16[832,128]{1,0:T(8,128)(2,1)S(1)}, u32[]{:S(2)}, u32[]{:S(2)}) collective-permute-start(bf16[832,128]{1,0:T(8,128)(2,1)S(1)} %get-tuple-element.150), channel_id=1, source_target_pairs={{0,16},{1,9},{2,18},{3,11},{4,20},{5,13},{6,22},{7,15},{8,24},{9,1... | collective-permute-start | bytes 638984 | tf_op jit(solution)/shard_map/ppermute | solution.py:710
  61.1 8.9 %copy-start.2 = (bf16[1024,512]{1,0:T(8,128)(2,1)S(1)}, bf16[1024,512]{1,0:T(8,128)(2,1)}, u32[]{:S(2)}) copy-start(bf16[1024,512]{1,0:T(8,128)(2,1)} %refs_14_.3) | copy-start | bytes 3145732
  61.1 12.8 %collective-permute-start.24 = (bf16[1664,128]{1,0:T(8,128)(2,1)S(1)}, bf16[1664,128]{1,0:T(8,128)(2,1)S(1)}, u32[]{:S(2)}, u32[]{:S(2)}) collective-permute-start(bf16[1664,128]{1,0:T(8,128)(2,1)S(1)} %pad_maximum_fusion.2), channel_id=1, source_target_pairs={{0,4},{1,3},{2,6},{3,1},{4,0},{5,7},{6,2},{7,5},{8,12},{9,11},{10,... | collective-permute-start | bytes 1277960 | tf_op jit(solution)/shard_map/ppermute | solution.py:735
  64.3 3.8 %collective-permute-start.20 = (bf16[512,128]{1,0:T(8,128)(2,1)S(1)}, bf16[512,128]{1,0:T(8,128)(2,1)S(1)}, u32[]{:S(2)}, u32[]{:S(2)}) collective-permute-start(bf16[512,128]{1,0:T(8,128)(2,1)S(1)} %get-tuple-element.146), channel_id=1, source_target_pairs={{0,1},{1,0},{2,3},{3,2},{4,5},{5,4},{6,7},{7,6},{8,9},{9,8},{10,11... | collective-permute-start | bytes 393224 | tf_op jit(solution)/shard_map/ppermute | solution.py:674
  64.5 10.7 %collective-permute-start.23 = (bf16[576,128]{1,0:T(8,128)(2,1)S(1)}, bf16[576,128]{1,0:T(8,128)(2,1)S(1)}, u32[]{:S(2)}, u32[]{:S(2)}) collective-permute-start(bf16[576,128]{1,0:T(8,128)(2,1)S(1)} %add_convert_fusion.5.refs_0_), channel_id=1, source_target_pairs={{0,6},{2,4},{4,2},{6,0},{8,14},{10,12},{12,10},{14,8},{16,22},{18,... | collective-permute-start | bytes 442376 | tf_op jit(solution)/shard_map/ppermute | solution.py:674
  66.3 9.3 %collective-permute-start.22 = (bf16[576,128]{1,0:T(8,128)(2,1)S(1)}, bf16[576,128]{1,0:T(8,128)(2,1)S(1)}, u32[]{:S(2)}, u32[]{:S(2)}) collective-permute-start(bf16[576,128]{1,0:T(8,128)(2,1)S(1)} %add_convert_fusion.5.refs_0_), channel_id=1, source_target_pairs={{0,4},{2,6},{4,0},{6,2},{8,12},{10,14},{12,8},{14,10},{16,20},{18,... | collective-permute-start | bytes 442376 | tf_op jit(solution)/shard_map/ppermute | solution.py:674
  67.5 8.2 %collective-permute-start.21 = (bf16[576,128]{1,0:T(8,128)(2,1)S(1)}, bf16[576,128]{1,0:T(8,128)(2,1)S(1)}, u32[]{:S(2)}, u32[]{:S(2)}) collective-permute-start(bf16[576,128]{1,0:T(8,128)(2,1)S(1)} %add_convert_fusion.5.refs_0_), channel_id=1, source_target_pairs={{0,2},{2,0},{4,6},{6,4},{8,10},{10,8},{12,14},{14,12},{16,18},{18,... | collective-permute-start | bytes 442376 | tf_op jit(solution)/shard_map/ppermute | solution.py:674
  68.1 2.3 %slice-start = ((bf16[1536,128]{1,0:T(8,128)(2,1)}), bf16[512,128]{1,0:T(8,128)(2,1)S(1)}, s32[]{:S(2)}) async-start(bf16[1536,128]{1,0:T(8,128)(2,1)} %copy-done), calls=%async_computation | async-start | bytes 262144 | tf_op jit(solution)/shard_map/slice | solution.py:1086
  68.1 2.3 %copy-start.5 = (bf16[512,128]{1,0:T(8,128)(2,1)S(1)}, bf16[512,128]{1,0:T(8,128)(2,1)}, u32[]{:S(2)}) copy-start(bf16[512,128]{1,0:T(8,128)(2,1)} %refs_11_.3) | copy-start | bytes 393220
